TPU v7x, 32 devices: a whole 2x2x4 slice. The times are simulated.
32 devices in a mesh: seq: 8 (over z, y), head: 4 (over x, core).
Axes of the slice: x: 2, y: 2, z: 4, core: 2. Of those that a mesh axis runs over, the one named last changes fastest.
Arguments:
- tokens: bfloat16 [4096, 2048], P(('seq', 'head'))
- ln_gain: float32 [2048], replicated, may hold values from 0.1 to 1.9
- w_qkv: bfloat16 [2048, 3, 2048], P(None, None, 'head')
- slopes: float32 [16], P('head')
- w_out: bfloat16 [2048, 2048], P('head'), may hold values from -0.125 to 0.125
- seg_ids: int32 [4096], P('seq'), may hold values from 0 to 3, never falling along the last dimension, each value on 1 to 2048 neighbouring positions
Outputs:
- hidden: bfloat16 [4096, 2048], P(('seq', 'head'))
- key_cache: bfloat16 [4096, 2048], P('seq', 'head')
- value_cache: bfloat16 [4096, 2048], P('seq', 'head')
Inputs may be any that keep to these rules, and one draw needn't show every extreme that they name: `seg_ids`: Non-decreasing along the stream; each prompt number names 1 to 2048 consecutive tokens, one prompt exactly 2048.
All inputs are finite; a program needn't handle non-finite values.
Results may differ from a plain program's by a relative error of at most 0.0075.
Values may be sent and summed in bfloat16 or wider, within the bound.
No kernel may reach another device: no remote copies, remote signals or barrier semaphores. Data moves between devices by JAX's collectives and lax.ppermute only.
A program may use at most 128 MiB of HBM per device.

v0:
```python
import jax
import jax.numpy as jnp
from jax import lax
from jax.sharding import PartitionSpec as P

HD = 128
SPAN = 4


EPSILON = 1e-05
NEG_FILL = -1e30


def shifted(value, axis, steps):
    count = lax.axis_size(axis)
    leading, last = (max(0, -steps), min(count, count - steps))
    return lax.ppermute(value, axis, [(source, source + steps) for source in range(leading, last)])


def layer_norm(inputs, ln_gain):
    row_mean = jnp.mean(inputs, axis=-1, keepdims=True)
    centred = inputs - row_mean
    variance = jnp.mean(centred * centred, axis=-1, keepdims=True)
    return (centred * lax.rsqrt(variance + EPSILON) * ln_gain).astype(jnp.bfloat16)


def attend_one(
    run_state, queries, q_pos, seg_query, slopes_dev, key_rows, value_rows, seg_key, k_pos
):
    prev_max, prev_sum, prev_acc = run_state
    scores = jnp.einsum(
        "qhe,khe->qhk", queries, key_rows, preferred_element_type=jnp.float32
    ) * HD ** (-0.5)
    distance = (q_pos[:, None] - k_pos[None, :]).astype(jnp.float32)
    scores = scores - slopes_dev[None, :, None] * distance[:, None, :]
    valid_mask = (
        (seg_query[:, None] == seg_key[None, :])
        & (k_pos[None, :] <= q_pos[:, None])
        & (k_pos[None, :] >= 0)
    )[:, None, :]
    scores = jnp.where(valid_mask, scores, NEG_FILL)
    row_max = jnp.maximum(prev_max, jnp.max(scores, axis=-1))
    expo = jnp.where(valid_mask, jnp.exp(scores - row_max[..., None]), 0.0)
    rescale = jnp.exp(prev_max - row_max)
    new_sum = prev_sum * rescale + jnp.sum(expo, axis=-1)
    new_acc = prev_acc * rescale[..., None] + jnp.einsum(
        "qhk,khe->qhe", expo.astype(jnp.bfloat16), value_rows, preferred_element_type=jnp.float32
    )
    return (row_max, new_sum, new_acc)


def on_device(tokens, ln_gain, w_qkv, slopes, w_out, seg_ids):
    inputs = tokens.astype(jnp.float32)
    normed = layer_norm(inputs, ln_gain)
    width_local = w_qkv.shape[2]
    heads_dev = slopes.shape[0]
    joined = w_qkv.reshape(w_qkv.shape[0], 3 * width_local)
    qkv_rows = jnp.dot(
        lax.all_gather(normed, "head", axis=0, tiled=True),
        joined,
        preferred_element_type=jnp.float32,
    ).astype(jnp.bfloat16)
    block_len = qkv_rows.shape[0]
    queries = qkv_rows[:, :width_local].reshape(block_len, heads_dev, HD)
    key_cache = qkv_rows[:, width_local : 2 * width_local]
    value_cache = qkv_rows[:, 2 * width_local :]
    seq_index = lax.axis_index("seq")
    offsets = jnp.arange(block_len, dtype=jnp.int32)
    q_pos = seq_index * block_len + offsets
    own_kv = jnp.stack([key_cache, value_cache])

    def visit_block(run_state, kv_pair, seg_key, steps_back):
        k_pos = (seq_index - steps_back) * block_len + offsets

        def compute(current):
            return attend_one(
                current,
                queries,
                q_pos,
                seg_ids,
                slopes,
                kv_pair[0].reshape(block_len, heads_dev, HD),
                kv_pair[1].reshape(block_len, heads_dev, HD),
                seg_key,
                k_pos,
            )

        if steps_back == 0:
            return compute(run_state)
        live = (seg_key[-1] == seg_ids[0]) & (seq_index - steps_back >= 0)
        return lax.cond(live, compute, lambda current: current, run_state)

    initial = (
        jnp.full((block_len, heads_dev), NEG_FILL, jnp.float32),
        jnp.zeros((block_len, heads_dev), jnp.float32),
        jnp.zeros((block_len, heads_dev, HD), jnp.float32),
    )
    run_state = visit_block(initial, own_kv, seg_ids, 0)
    carried = (own_kv, seg_ids)
    for steps_back in range(1, SPAN + 1):
        carried = shifted((carried[0], carried[1]), "seq", 1)
        run_state = visit_block(run_state, carried[0], carried[1], steps_back)
    context = (
        (run_state[2] / run_state[1][..., None])
        .astype(jnp.bfloat16)
        .reshape(block_len, width_local)
    )
    summed = lax.psum_scatter(
        jnp.dot(context, w_out, preferred_element_type=jnp.float32).astype(jnp.bfloat16),
        "head",
        scatter_dimension=0,
        tiled=True,
    ).astype(jnp.float32)
    hidden = (inputs + summed).astype(jnp.bfloat16)
    return (hidden, key_cache, value_cache)


def solution(mesh):
    in_specs = (
        P(("seq", "head"), None),
        P(),
        P(None, None, "head"),
        P("head"),
        P("head", None),
        P("seq"),
    )
    out_specs = (P(("seq", "head"), None), P("seq", "head"), P("seq", "head"))
    return jax.shard_map(
        on_device, mesh=mesh, in_specs=in_specs, out_specs=out_specs, check_vma=False
    )
```

profile of v0, /device:TPU:12, one launch (start us, length us, event | category | flops | bytes accessed | tf_op | source)
XLA Modules:
  0.0 236.0 jit_solution(1863122676806560535)
XLA Ops:
  7.2 1.3 convert_reduce_fusion
  8.6 1.3 fusion.82
  9.9 2.2 fusion.84
  12.2 8.9 %copy.35 = bf16[2048,3,512]{0,2,1:T(8,128)(2,1)} copy(bf16[2048,3,512]{2,0,1:T(8,128)(2,1)} %param.16) | data formatting | bytes 12582912 | tf_op args[2]
  21.1 14.9 %all-gather.2.cloned.1.call-done = bf16[512,2048]{1,0:T(8,128)(2,1)} async-done(((bf16[128,2048]{1,0:T(8,128)(2,1)}), bf16[512,2048]{1,0:T(8,128)(2,1)}) %all-gather.2.cloned.1.call-update) | async-done | bytes 2097168 | tf_op jit(solution)/shard_map/all_gather | solution.py:59
  36.0 6.9 %convolution_convert_fusion.1 = bf16[512,1536]{1,0:T(8,128)(2,1)S(1)} fusion(bf16[512,2048]{1,0:T(8,128)(2,1)} %all-gather.2.cloned.1.call-done, bf16[2048,1536]{0,1:T(8,128)(2,1)} %bitcast.141), kind=kOutput, calls=%fused_computation.84 | convolution fusion | flops 3222011904 | bytes 9961472 | tf_op jit(solution)/shard_map/dot_general | solution.py:58
  44.8 3.4 %collective-permute-start.4 = (bf16[2,512,512]{2,1,0:T(8,128)(2,1)S(1)}, bf16[2,512,512]{2,1,0:T(8,128)(2,1)}, u32[]{:S(2)}, u32[]{:S(2)}) collective-permute-start(bf16[2,512,512]{2,1,0:T(8,128)(2,1)S(1)} %pad_maximum_fusion), channel_id=1, source_target_pairs={{0,4},{4,8},{8,12},{12,16},{16,20},{20,24},{24,28},{1,5},{5,9},{9,... | collective-permute-start | bytes 3145736 | tf_op jit(solution)/shard_map/ppermute | solution.py:17
  48.2 23.9 %collective-permute-done.4 = bf16[2,512,512]{2,1,0:T(8,128)(2,1)} collective-permute-done((bf16[2,512,512]{2,1,0:T(8,128)(2,1)S(1)}, bf16[2,512,512]{2,1,0:T(8,128)(2,1)}, u32[]{:S(2)}, u32[]{:S(2)}) %collective-permute-start.4) | collective-permute-done | bytes 1048608 | tf_op jit(solution)/shard_map/ppermute | solution.py:17
  72.1 4.3 %collective-permute-start.5 = (bf16[2,512,512]{2,1,0:T(8,128)(2,1)}, bf16[2,512,512]{2,1,0:T(8,128)(2,1)}, u32[]{:S(2)}, u32[]{:S(2)}) collective-permute-start(bf16[2,512,512]{2,1,0:T(8,128)(2,1)} %collective-permute-done.4), channel_id=1, source_target_pairs={{0,4},{4,8},{8,12},{12,16},{16,20},{20,24},{24,28},{1,5},{5,9},{9,... | collective-permute-start | bytes 3145736 | tf_op jit(solution)/shard_map/ppermute | solution.py:17
  76.3 2.5 %collective-permute-start = (s32[512]{0:T(512)S(1)}, s32[512]{0:T(512)S(1)}, u32[]{:S(2)}, u32[]{:S(2)}) collective-permute-start(s32[512]{0:T(512)S(1)} %copy-done.16), channel_id=1, source_target_pairs={{0,4},{4,8},{8,12},{12,16},{16,20},{20,24},{24,28},{1,5},{5,9},{9,... | collective-permute-start | bytes 6152 | tf_op jit(solution)/shard_map/ppermute | solution.py:17
  78.9 1.1 subtract_convert_fusion.4
  80.0 18.8 %collective-permute-done = s32[512]{0:T(512)S(1)} collective-permute-done((s32[512]{0:T(512)S(1)}, s32[512]{0:T(512)S(1)}, u32[]{:S(2)}, u32[]{:S(2)}) %collective-permute-start) | collective-permute-done | bytes 2080 | tf_op jit(solution)/shard_map/ppermute | solution.py:17
  98.8 5.2 %collective-permute-start.1 = (s32[512]{0:T(512)S(1)}, s32[512]{0:T(512)S(1)}, u32[]{:S(2)}, u32[]{:S(2)}) collective-permute-start(s32[512]{0:T(512)S(1)} %collective-permute-done), channel_id=1, source_target_pairs={{0,4},{4,8},{8,12},{12,16},{16,20},{20,24},{24,28},{1,5},{5,9},{9,... | collective-permute-start | bytes 6152 | tf_op jit(solution)/shard_map/ppermute | solution.py:17
  103.9 1.9 collective-permute-start.6
  106.2 4.8 %collective-permute-start.2 = (s32[512]{0:T(512)S(1)}, s32[512]{0:T(512)S(1)}, u32[]{:S(2)}, u32[]{:S(2)}) collective-permute-start(s32[512]{0:T(512)S(1)} %collective-permute-done.1), channel_id=1, source_target_pairs={{0,4},{4,8},{8,12},{12,16},{16,20},{20,24},{24,28},{1,5},{5,9},{9,... | collective-permute-start | bytes 6152 | tf_op jit(solution)/shard_map/ppermute | solution.py:17
  111.1 18.4 %collective-permute-done.2 = s32[512]{0:T(512)S(1)} collective-permute-done((s32[512]{0:T(512)S(1)}, s32[512]{0:T(512)S(1)}, u32[]{:S(2)}, u32[]{:S(2)}) %collective-permute-start.2) | collective-permute-done | bytes 2080 | tf_op jit(solution)/shard_map/ppermute | solution.py:17
  129.5 3.1 %collective-permute-start.3 = (s32[512]{0:T(512)S(1)}, s32[512]{0:T(512)S(1)}, u32[]{:S(2)}, u32[]{:S(2)}) collective-permute-start(s32[512]{0:T(512)S(1)} %collective-permute-done.2), channel_id=1, source_target_pairs={{0,4},{4,8},{8,12},{12,16},{16,20},{20,24},{24,28},{1,5},{5,9},{9,... | collective-permute-start | bytes 6152 | tf_op jit(solution)/shard_map/ppermute | solution.py:17
  140.4 1.0 copy.64
  142.3 2.7 %fusion.71 = (f32[512,4]{0,1:T(4,128)S(1)}, f32[4,512,512]{2,1,0:T(8,128)S(1)}) fusion(f32[512,512]{0,1:T(8,128)} %subtract_convert_fusion.4, f32[4]{0:T(128)S(1)} %copy-done.17, pred[512,512]{0,1:T(8,128)(4,1)S(1)} %and_and_fusion.4, bf16[64,4,8,128]{3,2,1,0:T(8,128)(2,1)} %get-tuple-element.303, bf16[512,512]{1,0:T(8,128)(2,1)} %copy-done.14), kind=kOutput, calls=%fused_computation.85 | convolution fusion | flops 273676288 | bytes 6561808 | tf_op jit(solution)/shard_map/qhe,khe->qhk/dot_general | solution.py:31
  145.1 3.8 %collective-permute-start.7 = (bf16[2,512,512]{2,1,0:T(8,128)(2,1)}, bf16[2,512,512]{2,1,0:T(8,128)(2,1)}, u32[]{:S(2)}, u32[]{:S(2)}) collective-permute-start(bf16[2,512,512]{2,1,0:T(8,128)(2,1)} %collective-permute-done.6), channel_id=1, source_target_pairs={{0,4},{4,8},{8,12},{12,16},{16,20},{20,24},{24,28},{1,5},{5,9},{9,... | collective-permute-start | bytes 3145736 | tf_op jit(solution)/shard_map/ppermute | solution.py:17
  148.9 1.4 fusion.70
  150.3 1.8 fusion.77
  152.1 19.6 %conditional.4 = (f32[512,4]{0,1:T(4,128)S(1)}, f32[512,4]{0,1:T(4,128)S(1)}, f32[512,4,128]{2,0,1:T(8,128)}) conditional(s32[]{:T(128)} %convert_element_type.87, (f32[512,4]{0,1:T(4,128)S(1)}, f32[512,4]{0,1:T(4,128)S(1)}, f32[512,4,128]{0,2,1:T(8,128)S(1)}) %tuple.34, (s32[512]{0:T(512)S(1)}, s32[512]{0:T(512)S(1)}, s32[512]{0:T(512)S(1)}, ...), branch_computations={%region_4.5_spmd, %region_5.8_spmd} | conditional | flops 558895616 | bytes 48905344 | solution.py:91
  152.7 1.2 subtract_convert_fusion
  153.9 2.3 copy.41
  156.2 2.1 fusion.95
  158.2 2.9 %fusion.3 = (f32[512,4]{0,1:T(4,128)S(1)}, f32[4,512,512]{2,1,0:T(8,128)S(1)}) fusion(f32[512,512]{0,1:T(8,128)} %subtract_convert_fusion, f32[4]{0:T(128)S(1)} %get-tuple-element.121, pred[512,512]{0,1:T(8,128)(4,1)S(1)} %and_and_fusion, bf16[512,4,128]{0,2,1:T(8,128)(2,1)S(1)} %bitcast.150, bf16[512,4,128]{2,1,0:T(4,128)(2,1)} %get-tuple-element.234), kind=kOutput, calls=%fused_computation.5 | convolution fusion | flops 273676288 | bytes 6561808 | tf_op jit(solution)/shard_map/cond/branch_1_fun/qhe,khe->qhk/dot_general | solution.py:31
  161.1 1.9 copy-done.3
  163.1 1.4 fusion.2
  164.5 1.3 copy.43
  165.8 5.9 %fusion.9 = f32[512,4,128]{2,0,1:T(8,128)} fusion(bf16[512,4,128]{0,2,1:T(8,128)(2,1)} %bitcast.146, f32[4,512,512]{2,1,0:T(8,128)} %copy-done.3, f32[512,4]{0,1:T(4,128)S(1)} %max.8, f32[512,512]{0,1:T(8,128)} %subtract_convert_fusion, f32[4]{0:T(128)S(1)} %get-tuple-element.121, pred[512,512]{0,1:T(8,128)(4,1)S(1)} %and_and_fusion, ...), kind=kOutput, calls=%fused_computation.8 | convolution fusion | flops 276299776 | bytes 8142864 | tf_op jit(solution)/shard_map/cond/branch_1_fun/qhk,khe->qhe/dot_general | solution.py:46
  171.7 10.7 %conditional.5 = ((f32[512,4]{0,1:T(4,128)S(1)}, f32[512,4]{0,1:T(4,128)S(1)}, f32[512,4,128]{2,0,1:T(8,128)})) conditional(s32[]{:T(128)} %convert_element_type.86, (f32[512,4]{0,1:T(4,128)S(1)}, f32[512,4]{0,1:T(4,128)S(1)}, f32[512,4,128]{2,0,1:T(8,128)}) %conditional.4, (s32[512]{0:T(512)S(1)}, s32[512]{0:T(512)S(1)}, s32[512]{0:T(512)S(1)}, ...), branch_computations={%region_8.9_spmd, %region_9.12_spmd} | conditional | flops 558895616 | bytes 38419620 | solution.py:91
  172.0 1.1 subtract_convert_fusion.1
  173.2 1.5 copy.44
  174.7 2.9 %fusion.20 = (f32[512,4]{0,1:T(4,128)S(1)}, f32[4,512,512]{2,1,0:T(8,128)S(1)}) fusion(f32[512,512]{0,1:T(8,128)} %subtract_convert_fusion.1, f32[4]{0:T(128)S(1)} %get-tuple-element.131, pred[512,512]{0,1:T(8,128)(4,1)S(1)} %and_and_fusion.1, bf16[512,4,128]{0,2,1:T(8,128)(2,1)S(1)} %bitcast.151, bf16[512,4,128]{2,1,0:T(4,128)(2,1)} %get-tuple-element.244), kind=kOutput, calls=%fused_computation.24 | convolution fusion | flops 273676288 | bytes 6561808 | tf_op jit(solution)/shard_map/cond/branch_1_fun/qhe,khe->qhk/dot_general | solution.py:31
  177.7 1.4 fusion.19
  179.1 2.3 fusion.26
  182.4 10.7 %conditional.6 = ((f32[512,4]{0,1:T(4,128)S(1)}, f32[512,4]{0,1:T(4,128)S(1)}, f32[512,4,128]{2,0,1:T(8,128)})) conditional(s32[]{:T(128)} %convert_element_type.85, (f32[512,4]{0,1:T(4,128)S(1)}, f32[512,4]{0,1:T(4,128)S(1)}, f32[512,4,128]{2,0,1:T(8,128)}) %get-tuple-element.332, (s32[512]{0:T(512)S(1)}, s32[512]{0:T(512)S(1)}, s32[]{:T(128)}, ...), branch_computations={%region_12.13_spmd, %region_13.16_spmd} | conditional | flops 558896128 | bytes 38421684 | solution.py:91
  182.7 1.1 subtract_convert_fusion.2
  183.9 1.5 copy.46
  185.5 2.9 %fusion.37 = (f32[512,4]{0,1:T(4,128)S(1)}, f32[4,512,512]{2,1,0:T(8,128)S(1)}) fusion(f32[512,512]{0,1:T(8,128)} %subtract_convert_fusion.2, f32[4]{0:T(128)S(1)} %get-tuple-element.142, pred[512,512]{0,1:T(8,128)(4,1)S(1)} %and_and_fusion.2, bf16[512,4,128]{0,2,1:T(8,128)(2,1)S(1)} %bitcast.152, bf16[512,4,128]{2,1,0:T(4,128)(2,1)} %get-tuple-element.255), kind=kOutput, calls=%fused_computation.43 | convolution fusion | flops 273676288 | bytes 6561808 | tf_op jit(solution)/shard_map/cond/branch_1_fun/qhe,khe->qhk/dot_general | solution.py:31
  188.4 1.4 fusion.36
  189.9 2.3 fusion.43
  193.1 1.6 conditional.7
  193.1 1.6 copy.65
  194.9 2.6 %convolution_convert_fusion = bf16[512,2048]{1,0:T(8,128)(2,1)} fusion(bf16[512,512]{0,1:T(8,128)(2,1)S(1)} %bitcast.144, bf16[512,2048]{1,0:T(8,128)(2,1)S(1)} %copy-done), kind=kOutput, calls=%fused_computation.83 | convolution fusion | flops 1074790400 | bytes 4718592 | tf_op jit(solution)/shard_map/dot_general | solution.py:109
  197.5 29.7 %reduce-scatter.2.cloned.1.call-done = bf16[128,2048]{1,0:T(8,128)(2,1)} async-done(((bf16[512,2048]{1,0:T(8,128)(2,1)}), bf16[128,2048]{1,0:T(8,128)(2,1)}) %reduce-scatter.2.cloned.1.call-update) | async-done | bytes 524304 | tf_op jit(solution)/shard_map/reduce_scatter | solution.py:108
  227.2 2.0 fusion.85
  (77 shorter events, 9.5 us)
Async XLA Ops:
  7.2 187.7 %copy-start = (bf16[512,2048]{1,0:T(8,128)(2,1)S(1)}, bf16[512,2048]{1,0:T(8,128)(2,1)}, u32[]{:S(2)}) copy-start(bf16[512,2048]{1,0:T(8,128)(2,1)} %param.18) | copy-start | bytes 6291460
  7.2 28.8 %all-gather.2.cloned.1.call-start = ((), (), s32[]{:S(2)}) async-start(), calls=%async_computation.1 | async-start | bytes 2621440 | tf_op jit(solution)/shard_map/all_gather | solution.py:59
  12.1 215.1 %reduce-scatter.2.cloned.1.call-start = ((), (), s32[]{:S(2)}) async-start(), calls=%async_computation.2 | async-start | bytes 2621440 | tf_op jit(solution)/shard_map/reduce_scatter | solution.py:108
  42.9 33.5 %copy-start.16 = (s32[512]{0:T(512)S(1)}, s32[512]{0:T(512)}, u32[]{:S(2)}) copy-start(s32[512]{0:T(512)} %param.19) | copy-start | bytes 6148
  42.9 99.4 %copy-start.17 = (f32[4]{0:T(128)S(1)}, f32[4]{0:T(128)}, u32[]{:S(2)}) copy-start(f32[4]{0:T(128)} %param.17) | copy-start | bytes 52
  43.9 0.8 copy-start.14
  43.9 101.2 %copy-start.2 = (bf16[512,512]{1,0:T(8,128)(2,1)}, bf16[512,512]{1,0:T(8,128)(2,1)S(1)}, u32[]{:S(2)}) copy-start(bf16[512,512]{1,0:T(8,128)(2,1)S(1)} %get-tuple-element.304) | copy-start | bytes 1572868
  44.8 27.3 %collective-permute-start.4 = (bf16[2,512,512]{2,1,0:T(8,128)(2,1)S(1)}, bf16[2,512,512]{2,1,0:T(8,128)(2,1)}, u32[]{:S(2)}, u32[]{:S(2)}) collective-permute-start(bf16[2,512,512]{2,1,0:T(8,128)(2,1)S(1)} %pad_maximum_fusion), channel_id=1, source_target_pairs={{0,4},{4,8},{8,12},{12,16},{16,20},{20,24},{24,28},{1,5},{5,9},{9,... | collective-permute-start | bytes 3145736 | tf_op jit(solution)/shard_map/ppermute | solution.py:17
  72.1 31.9 %collective-permute-start.5 = (bf16[2,512,512]{2,1,0:T(8,128)(2,1)}, bf16[2,512,512]{2,1,0:T(8,128)(2,1)}, u32[]{:S(2)}, u32[]{:S(2)}) collective-permute-start(bf16[2,512,512]{2,1,0:T(8,128)(2,1)} %collective-permute-done.4), channel_id=1, source_target_pairs={{0,4},{4,8},{8,12},{12,16},{16,20},{20,24},{24,28},{1,5},{5,9},{9,... | collective-permute-start | bytes 3145736 | tf_op jit(solution)/shard_map/ppermute | solution.py:17
  76.3 22.4 %collective-permute-start = (s32[512]{0:T(512)S(1)}, s32[512]{0:T(512)S(1)}, u32[]{:S(2)}, u32[]{:S(2)}) collective-permute-start(s32[512]{0:T(512)S(1)} %copy-done.16), channel_id=1, source_target_pairs={{0,4},{4,8},{8,12},{12,16},{16,20},{20,24},{24,28},{1,5},{5,9},{9,... | collective-permute-start | bytes 6152 | tf_op jit(solution)/shard_map/ppermute | solution.py:17
  98.8 7.4 %collective-permute-start.1 = (s32[512]{0:T(512)S(1)}, s32[512]{0:T(512)S(1)}, u32[]{:S(2)}, u32[]{:S(2)}) collective-permute-start(s32[512]{0:T(512)S(1)} %collective-permute-done), channel_id=1, source_target_pairs={{0,4},{4,8},{8,12},{12,16},{16,20},{20,24},{24,28},{1,5},{5,9},{9,... | collective-permute-start | bytes 6152 | tf_op jit(solution)/shard_map/ppermute | solution.py:17
  103.9 41.2 %collective-permute-start.6 = (bf16[2,512,512]{2,1,0:T(8,128)(2,1)}, bf16[2,512,512]{2,1,0:T(8,128)(2,1)}, u32[]{:S(2)}, u32[]{:S(2)}) collective-permute-start(bf16[2,512,512]{2,1,0:T(8,128)(2,1)} %collective-permute-done.5), channel_id=1, source_target_pairs={{0,4},{4,8},{8,12},{12,16},{16,20},{20,24},{24,28},{1,5},{5,9},{9,... | collective-permute-start | bytes 3145736 | tf_op jit(solution)/shard_map/ppermute | solution.py:17
  106.2 23.3 %collective-permute-start.2 = (s32[512]{0:T(512)S(1)}, s32[512]{0:T(512)S(1)}, u32[]{:S(2)}, u32[]{:S(2)}) collective-permute-start(s32[512]{0:T(512)S(1)} %collective-permute-done.1), channel_id=1, source_target_pairs={{0,4},{4,8},{8,12},{12,16},{16,20},{20,24},{24,28},{1,5},{5,9},{9,... | collective-permute-start | bytes 6152 | tf_op jit(solution)/shard_map/ppermute | solution.py:17
  129.5 9.0 %collective-permute-start.3 = (s32[512]{0:T(512)S(1)}, s32[512]{0:T(512)S(1)}, u32[]{:S(2)}, u32[]{:S(2)}) collective-permute-start(s32[512]{0:T(512)S(1)} %collective-permute-done.2), channel_id=1, source_target_pairs={{0,4},{4,8},{8,12},{12,16},{16,20},{20,24},{24,28},{1,5},{5,9},{9,... | collective-permute-start | bytes 6152 | tf_op jit(solution)/shard_map/ppermute | solution.py:17
  142.3 6.6 %copy-start.9 = (f32[512,512]{0,1:T(8,128)S(1)}, f32[512,512]{0,1:T(8,128)}, u32[]{:S(2)}) copy-start(f32[512,512]{0,1:T(8,128)} %subtract_convert_fusion.4) | copy-start | bytes 3145732
  145.1 5.2 %copy-start.15 = (bf16[512,512]{0,1:T(8,128)(2,1)S(1)}, bf16[512,512]{0,1:T(8,128)(2,1)}, u32[]{:S(2)}) copy-start(bf16[512,512]{0,1:T(8,128)(2,1)} %copy.64) | copy-start | bytes 1572868
  145.1 48.0 %collective-permute-start.7 = (bf16[2,512,512]{2,1,0:T(8,128)(2,1)}, bf16[2,512,512]{2,1,0:T(8,128)(2,1)}, u32[]{:S(2)}, u32[]{:S(2)}) collective-permute-start(bf16[2,512,512]{2,1,0:T(8,128)(2,1)} %collective-permute-done.6), channel_id=1, source_target_pairs={{0,4},{4,8},{8,12},{12,16},{16,20},{20,24},{24,28},{1,5},{5,9},{9,... | collective-permute-start | bytes 3145736 | tf_op jit(solution)/shard_map/ppermute | solution.py:17
  158.2 4.8 %copy-start.11 = (f32[512,512]{0,1:T(8,128)S(1)}, f32[512,512]{0,1:T(8,128)}, u32[]{:S(2)}) copy-start(f32[512,512]{0,1:T(8,128)} %subtract_convert_fusion) | copy-start | bytes 3145732 | tf_op jit(solution)/shard_map/cond
  161.1 1.9 copy-start.3
  174.7 3.0 %copy-start.12 = (f32[512,512]{0,1:T(8,128)S(1)}, f32[512,512]{0,1:T(8,128)}, u32[]{:S(2)}) copy-start(f32[512,512]{0,1:T(8,128)} %subtract_convert_fusion.1) | copy-start | bytes 3145732 | tf_op jit(solution)/shard_map/cond
  177.7 1.4 copy-start.4
  181.4 1.0 copy-start.5
  185.5 3.0 %copy-start.10 = (f32[512,512]{0,1:T(8,128)S(1)}, f32[512,512]{0,1:T(8,128)}, u32[]{:S(2)}) copy-start(f32[512,512]{0,1:T(8,128)} %subtract_convert_fusion.2) | copy-start | bytes 3145732 | tf_op jit(solution)/shard_map/cond
  188.4 1.4 copy-start.6
  192.2 1.0 copy-start.7
  194.9 32.4 %copy-start.1 = (bf16[128,2048]{1,0:T(8,128)(2,1)S(1)}, bf16[128,2048]{1,0:T(8,128)(2,1)}, u32[]{:S(2)}) copy-start(bf16[128,2048]{1,0:T(8,128)(2,1)} %param.14) | copy-start | bytes 1572868
Sparse Core Ops, SparseCore 0:
  12.3 23.6 all-gather.1
  197.6 29.5 reduce-scatter.1
where the time goes:
time: 239 us; the launch traced here: 236 us
  waiting for transfers between devices  106 us (44%)
  matrix products  33.3 us (14%)
  local copies, waits for them, and re-layouts  29.8 us (12%)
  starting transfers between devices  29 us (12%)
  between operations  19.1 us (8%)
  other arithmetic  18.5 us (8%)
    ppermute x8, waiting for transfers between devices, shifted(): lax.ppermute(value, axis, [(source, source + steps) for source in range(l...  61.1 us
    reduce_scatter x1, waiting for transfers between devices, on_device(): lax.psum_scatter(jnp.dot(context, w_out, preferred_element_type=jnp.float...  29.7 us
    ppermute x8, starting transfers between devices, shifted(): lax.ppermute(value, axis, [(source, source + steps) for source in range(l...  28.9 us
    all_gather x1, waiting for transfers between devices, on_device(): lax.all_gather(normed, 'head', axis=0, tiled=True)  14.9 us
    dot_general x4, matrix products, attend_one(): jnp.einsum('qhk,khe->qhe', expo.astype(jnp.bfloat16), value_rows, preferr...  12.3 us
    dot_general x4, matrix products, attend_one(): jnp.einsum('qhe,khe->qhk', queries, key_rows, preferred_element_type=jnp....  11.5 us
    unnamed x17, local copies, waits for them, and re-layouts  9.72 us
    dot_general x1, matrix products, on_device(): jnp.dot(lax.all_gather(normed, 'head', axis=0, tiled=True), joined, prefe...  6.86 us
  transfers between devices with their start and end apart: 10, of which 5 were waited for; matrix products, arithmetic and copies ran while one was open for 25% of the time, Pallas kernels for 0%

commit v1 on v0

v1 whole, which is shorter than its diff:
```python
import functools

import jax
import jax.numpy as jnp
from jax import lax
from jax.experimental import pallas as pl
from jax.experimental.pallas import tpu as pltpu
from jax.sharding import PartitionSpec as P

HD = 128
PIECE = 128
EPSILON = 1e-05
NEG_FILL = -1e30
MASKED = -2e38
LOG2E = 1.4426950408889634
VMEM_LIMIT = 56 * 2**20

BF16 = jnp.bfloat16
F32 = jnp.float32
ANY = pl.BlockSpec(memory_space=pl.ANY)
SMEM = pl.BlockSpec(memory_space=pltpu.SMEM)
VMEM = pl.BlockSpec(memory_space=pltpu.VMEM)


def params():
    return pltpu.CompilerParams(vmem_limit_bytes=VMEM_LIMIT)


def cost(macs, nbytes, exps=0):
    return pl.CostEstimate(flops=2 * macs, bytes_accessed=nbytes, transcendentals=exps)


def dot(lhs, rhs):
    return jnp.dot(lhs, rhs, preferred_element_type=F32)


def layer_norm(tokens, ln_gain):
    def body(tokens_ref, gain_ref, out_ref):
        inputs = tokens_ref[...].astype(F32)
        centred = inputs - jnp.mean(inputs, axis=-1, keepdims=True)
        variance = jnp.mean(centred * centred, axis=-1, keepdims=True)
        out_ref[...] = (centred * lax.rsqrt(variance + EPSILON) * gain_ref[...]).astype(BF16)

    return pl.pallas_call(
        body,
        out_shape=jax.ShapeDtypeStruct(tokens.shape, BF16),
        in_specs=[VMEM, VMEM],
        out_specs=VMEM,
        compiler_params=params(),
        cost_estimate=cost(0, 2 * tokens.size * 2, tokens.size),
    )(tokens, ln_gain.reshape(1, -1))


def set_masks(info_ref, lo_ref, key_base, keys, mask_ref, dist_ref):
    block_base = info_ref[0]
    lane = lax.broadcasted_iota(jnp.int32, (1, PIECE), 1)
    row = lax.broadcasted_iota(jnp.int32, (PIECE, PIECE), 0)
    for piece in range(keys):
        k_pos = row + key_base(piece)
        rows = pl.ds(piece * PIECE, PIECE)
        dist_ref[rows, :] = (k_pos - block_base).astype(F32)
        for place in range(4):
            head = info_ref[1 + place]
            q_pos = lane + (block_base + head * PIECE)
            first = lo_ref[pl.ds(head, 1), :]
            kept = (k_pos >= first) & (k_pos <= q_pos)
            mask_ref[rows, pl.ds(place * PIECE, PIECE)] = jnp.where(kept, 0.0, MASKED)


def attend(group, k_rows, v_t, q_ref, slopes_ref, mask_ref, dist_ref, stat_ref, acc_ref, fresh):
    heads = k_rows.shape[1] // HD
    for local in range(heads):
        head = group * heads + local
        cols = slice(local * HD, (local + 1) * HD)
        wide = pl.ds(head * HD, HD)
        bias = dist_ref[...] * (slopes_ref[head] * LOG2E)
        bias = jnp.concatenate([bias] * (q_ref.shape[1] // PIECE), axis=1)
        scores = dot(k_rows[:, cols], q_ref[wide, :]) * (HD**-0.5 * LOG2E)
        scores = scores + bias + mask_ref[...]
        top = jnp.max(scores, axis=0, keepdims=True)
        prev = jnp.full_like(top, NEG_FILL) if fresh else stat_ref[head : head + 1, :]
        row_max = jnp.maximum(prev, top)
        expo = jnp.exp2(scores - row_max)
        total = jnp.sum(expo, axis=0, keepdims=True)
        update = dot(v_t[cols, :], expo.astype(BF16))
        stat_ref[head : head + 1, :] = row_max
        if fresh:
            stat_ref[8 + head : 9 + head, :] = total
            acc_ref[wide, :] = update
        else:
            rescale = jnp.exp2(prev - row_max)
            stat_ref[8 + head : 9 + head, :] = stat_ref[8 + head : 9 + head, :] * rescale + total
            acc_ref[wide, :] = acc_ref[wide, :] * rescale + update


def own_block(info, slopes, lo, pieces, w_own, w_pair):
    depth, width = w_own.shape[1:]
    block = 4 * PIECE

    def body(info_ref, slopes_ref, lo_ref, a, b, c, d, w0, w1, q_out, stat_out, acc_out, k_out, v_out,
             x, w, q, k_cache, v_cache, stat, acc, mask, dist, sems, out_sems):
        loads = [pltpu.make_async_copy(src, x.at[pl.ds(i * PIECE, PIECE)], sems.at[i])
                 for i, src in enumerate((a, b, c, d))]
        w_loads = [pltpu.make_async_copy(src.at[part], w.at[3 * g + part], sems.at[4 + 3 * g + part])
                   for g, src in enumerate((w0, w1)) for part in range(3)]
        for copy in loads + w_loads:
            copy.start()
        set_masks(info_ref, lo_ref, lambda i: info_ref[0] + info_ref[1 + i] * PIECE, 2, mask, dist)
        for copy in loads:
            copy.wait()
        for group in range(2):
            rows = block if group == 0 else 2 * PIECE
            w_loads[3 * group].wait()
            q[pl.ds(group * width, width), :] = dot(x[...], w[3 * group]).T.astype(BF16)
            w_loads[3 * group + 1].wait()
            keys = dot(x[:rows, :], w[3 * group + 1]).astype(BF16)
            w_loads[3 * group + 2].wait()
            values = dot(x[:rows, :], w[3 * group + 2])
            if group == 0:
                for place in range(4):
                    to = pl.ds(pl.multiple_of(info_ref[1 + place] * PIECE, PIECE), PIECE)
                    k_cache[to, :] = keys[place * PIECE : (place + 1) * PIECE]
                    v_cache[to, :] = values[place * PIECE : (place + 1) * PIECE].astype(BF16)
                caches = [pltpu.make_async_copy(k_cache, k_out, out_sems.at[0]),
                          pltpu.make_async_copy(v_cache, v_out, out_sems.at[1])]
                for copy in caches:
                    copy.start()
            v_t = values[: 2 * PIECE].T.astype(BF16)
            attend(group, keys[: 2 * PIECE], v_t, q, slopes_ref, mask, dist, stat, acc, True)
        last = [pltpu.make_async_copy(q, q_out, out_sems.at[2]),
                pltpu.make_async_copy(stat, stat_out, out_sems.at[3]),
                pltpu.make_async_copy(acc, acc_out, out_sems.at[4])]
        for copy in last:
            copy.start()
        for copy in caches + last:
            copy.wait()

    return pl.pallas_call(
        body,
        out_shape=(
            jax.ShapeDtypeStruct((2 * width, block), BF16),
            jax.ShapeDtypeStruct((16, block), F32),
            jax.ShapeDtypeStruct((2 * width, block), F32),
            jax.ShapeDtypeStruct((block, width), BF16),
            jax.ShapeDtypeStruct((block, width), BF16),
        ),
        in_specs=[SMEM, SMEM, VMEM] + [ANY] * 6,
        out_specs=(ANY,) * 5,
        scratch_shapes=[
            pltpu.VMEM((block, depth), BF16),
            pltpu.VMEM((6, depth, width), BF16),
            pltpu.VMEM((2 * width, block), BF16),
            pltpu.VMEM((block, width), BF16),
            pltpu.VMEM((block, width), BF16),
            pltpu.VMEM((16, block), F32),
            pltpu.VMEM((2 * width, block), F32),
            pltpu.VMEM((2 * PIECE, block), F32),
            pltpu.VMEM((2 * PIECE, PIECE), F32),
            pltpu.SemaphoreType.DMA((10,)),
            pltpu.SemaphoreType.DMA((5,)),
        ],
        compiler_params=params(),
        cost_estimate=cost(5 * block * depth * width, 20 * 2**20, 8 * block * 2 * PIECE),
    )(info, slopes, lo, *pieces, w_own, w_pair)


def earlier_pieces(info, bases, slopes, lo, pieces, w_own, w_pair, q_t, stat_in, acc_in):
    depth, width = w_own.shape[1:]
    block = 4 * PIECE
    count = len(pieces)
    rows = count * PIECE

    def body(info_ref, bases_ref, slopes_ref, lo_ref, *refs):
        sources, refs = refs[:count], refs[count:]
        w0, w1, q_in, stat_src, acc_src, stat_out, acc_out, x, w, q, stat, acc, mask, dist, sems = refs
        live = bases_ref[0] + PIECE > info_ref[5]
        for i in range(1, count):
            live = live | (bases_ref[i] + PIECE > info_ref[5])

        keep = [pltpu.make_async_copy(stat_src, stat, sems.at[0]),
                pltpu.make_async_copy(acc_src, acc, sems.at[1])]
        for copy in keep:
            copy.start()

        @pl.when(live)
        def _():
            loads = [pltpu.make_async_copy(src, x.at[pl.ds(i * PIECE, PIECE)], sems.at[7 + i])
                     for i, src in enumerate(sources)]
            w_loads = [pltpu.make_async_copy(src.at[1 + part], w.at[2 * g + part], sems.at[3 + 2 * g + part])
                       for g, src in enumerate((w0, w1)) for part in range(2)]
            q_load = pltpu.make_async_copy(q_in, q, sems.at[2])
            for copy in loads + w_loads[:2] + [q_load] + w_loads[2:]:
                copy.start()
            set_masks(info_ref, lo_ref, lambda i: bases_ref[i], count, mask, dist)
            for copy in loads:
                copy.wait()
            for group in range(2):
                w_loads[2 * group].wait()
                keys = dot(x[...], w[2 * group]).astype(BF16)
                w_loads[2 * group + 1].wait()
                v_t = dot(x[...], w[2 * group + 1]).T.astype(BF16)
                if group == 0:
                    for copy in keep + [q_load]:
                        copy.wait()
                attend(group, keys, v_t, q, slopes_ref, mask, dist, stat, acc, False)

        @pl.when(jnp.logical_not(live))
        def _():
            for copy in keep:
                copy.wait()

        last = [pltpu.make_async_copy(stat, stat_out, sems.at[0]),
                pltpu.make_async_copy(acc, acc_out, sems.at[1])]
        for copy in last:
            copy.start()
        for copy in last:
            copy.wait()

    return pl.pallas_call(
        body,
        out_shape=(
            jax.ShapeDtypeStruct(stat_in.shape, F32),
            jax.ShapeDtypeStruct(acc_in.shape, F32),
        ),
        in_specs=[SMEM, SMEM, SMEM, VMEM] + [ANY] * (count + 5),
        out_specs=(ANY,) * 2,
        scratch_shapes=[
            pltpu.VMEM((rows, depth), BF16),
            pltpu.VMEM((4, depth, width), BF16),
            pltpu.VMEM((2 * width, block), BF16),
            pltpu.VMEM((16, block), F32),
            pltpu.VMEM((2 * width, block), F32),
            pltpu.VMEM((rows, block), F32),
            pltpu.VMEM((rows, PIECE), F32),
            pltpu.SemaphoreType.DMA((7 + count,)),
        ],
        compiler_params=params(),
        cost_estimate=cost(4 * rows * depth * width, 16 * 2**20, 8 * block * rows),
    )(info, bases, slopes, lo, *pieces, w_own, w_pair, q_t, stat_in, acc_in)


def close_half(stat, acc):
    wide, block = acc.shape
    half = block // 2

    def body(stat_ref, acc_ref, send_ref, lse_ref, out_ref):
        total = stat_ref[8:16, :]
        some = total > 0.0
        lse = jnp.where(some, stat_ref[0:8, :] + jnp.log2(jnp.where(some, total, 1.0)), NEG_FILL)
        scale = jnp.where(some, 1.0 / jnp.where(some, total, 1.0), 0.0)
        lse_ref[...] = lse[:, :half]
        for head in range(8):
            rows = pl.ds(head * HD, HD)
            normal = acc_ref[rows, :] * scale[head : head + 1, :]
            out_ref[rows, :] = normal[:, :half]
            send_ref[rows, :] = normal[:, half:].astype(BF16)
        rest = lse[:, half:]
        high = rest.astype(BF16)
        rest = rest - high.astype(F32)
        middle = rest.astype(BF16)
        low = (rest - middle.astype(F32)).astype(BF16)
        parts = [part.astype(F32) for part in (high, middle, low)]
        parts.append(jnp.zeros_like(parts[0]))
        send_ref[pl.ds(wide, 32), :] = jnp.concatenate(parts, axis=0).astype(BF16)

    return pl.pallas_call(
        body,
        out_shape=(
            jax.ShapeDtypeStruct((wide + 32, half), BF16),
            jax.ShapeDtypeStruct((8, half), F32),
            jax.ShapeDtypeStruct((wide, half), F32),
        ),
        in_specs=[VMEM] * 2,
        out_specs=(VMEM,) * 3,
        compiler_params=params(),
        cost_estimate=cost(0, 4 * 2**20, 0),
    )(stat, acc)


def project(place, lse, out, got, wo_own, wo_pair, tokens):
    wide = out.shape[0]
    width, model = wo_own.shape

    def body(lse_ref, out_ref, got_ref, w0, w1, *refs):
        tokens_ref, (y_ref, w, ctx, sems) = (refs[0], refs[1:]) if tokens is not None else (None, refs)
        loads = [pltpu.make_async_copy(src, w.at[pl.ds(i * width, width)], sems.at[i])
                 for i, src in enumerate((w0, w1))]
        for copy in loads:
            copy.start()
        lanes = pl.ds(place * PIECE, PIECE)
        other = got_ref[pl.ds(wide, 32), lanes].astype(F32)
        other = other[0:8] + other[8:16] + other[16:24]
        for head in range(8):
            swapped = (head + 4) % 8
            mine, theirs = lse_ref[head : head + 1, lanes], other[swapped : swapped + 1]
            top = jnp.maximum(mine, theirs)
            weigh, weigh_other = jnp.exp2(mine - top), jnp.exp2(theirs - top)
            joined = (out_ref[pl.ds(head * HD, HD), lanes] * weigh
                      + got_ref[pl.ds(swapped * HD, HD), lanes].astype(F32) * weigh_other)
            joined = joined / (weigh + weigh_other)
            ctx[:, head * HD : (head + 1) * HD] = joined.T.astype(BF16)
        for copy in loads:
            copy.wait()
        result = dot(ctx[...], w[...])
        if tokens is not None:
            result = result + tokens_ref[...].astype(F32)
        y_ref[...] = result.astype(y_ref.dtype)

    extra = () if tokens is None else (tokens,)
    return pl.pallas_call(
        body,
        out_shape=jax.ShapeDtypeStruct((PIECE, model), BF16 if tokens is None else F32),
        in_specs=[VMEM] * 3 + [ANY] * 2 + [VMEM] * len(extra),
        out_specs=VMEM,
        scratch_shapes=[
            pltpu.VMEM((2 * width, model), BF16),
            pltpu.VMEM((PIECE, wide), BF16),
            pltpu.SemaphoreType.DMA((2,)),
        ],
        compiler_params=params(),
        cost_estimate=cost(PIECE * wide * model, 6 * 2**20, 0),
    )(lse, out, got, wo_own, wo_pair, *extra)


def on_device(tokens, ln_gain, w_qkv, slopes, w_out, seg_ids):
    blocks = lax.axis_size("seq")
    block_num = lax.axis_index("seq")
    head_num = lax.axis_index("head")
    block = seg_ids.shape[0]
    odd = (block_num % 2) == 1

    def over_core(value):
        return lax.ppermute(value, "head", [(i, i ^ 1) for i in range(4)])

    def over_x(value):
        return lax.ppermute(value, "head", [(i, i ^ 2) for i in range(4)])

    def over_seq(value, pairs):
        return lax.ppermute(value, "seq", pairs)

    two_on = [(i, i + 2) for i in range(blocks - 2)]
    even_to_odd = [(i, i + 1) for i in range(0, blocks, 2)]
    odd_to_even = [(i + 1, i) for i in range(0, blocks, 2)]

    w_own = jnp.transpose(w_qkv, (1, 0, 2))

    base = block_num * block
    all_seg = lax.all_gather(seg_ids, "seq", axis=0, tiled=True)
    all_slopes = lax.all_gather(slopes, "head", axis=0, tiled=True)
    first_seg = seg_ids[0]
    start = jnp.sum((all_seg < first_seg).astype(jnp.int32))
    inside = base + jnp.sum((seg_ids[None, :] < seg_ids[:, None]).astype(jnp.int32), axis=1)
    lo = jnp.where(seg_ids == first_seg, start, inside).reshape(4, PIECE)
    heads = [head_num, head_num ^ 2, head_num ^ 1, head_num ^ 3]
    info = jnp.stack([base] + heads + [start]).astype(jnp.int32)
    slopes_pair = jnp.concatenate([
        slopes, lax.dynamic_slice_in_dim(all_slopes, (head_num ^ 1) * 4, 4)])

    def key_base(steps, place):
        return (block_num - steps) * block + heads[place] * PIECE

    def bases(*which):
        return jnp.stack([key_base(*w) for w in which]).astype(jnp.int32)

    a0 = layer_norm(tokens, ln_gain)
    a2 = over_seq(a0, two_on)
    b0 = over_x(a0)
    a1_odd = over_seq(a0, even_to_odd)
    c0 = over_core(a0)
    w_tied, wo_tied, _ = lax.optimization_barrier((w_own, w_out, a0))
    w_pair = over_core(w_tied)
    wo_pair = over_core(wo_tied)
    d0 = over_core(b0)

    a4 = over_seq(a2, two_on)
    b2 = over_x(a2)
    crossed = over_seq(a2, even_to_odd + odd_to_even)
    a1 = jnp.where(odd, a1_odd, crossed)

    b1 = over_x(a1)
    b4 = over_seq(b2, two_on)
    a3_even = over_seq(a4, odd_to_even)
    a3 = jnp.where(odd, crossed, a3_even)
    b3 = over_x(a3)

    q_t, stat, acc, key_cache, value_cache = own_block(
        info, slopes_pair, lo, (a0, b0, c0, d0), w_own, w_pair)
    for pieces, which in (
        ((a2, b2, a1, a4), ((2, 0), (2, 1), (1, 0), (4, 0))),
        ((b1, b4, a3), ((1, 1), (4, 1), (3, 0))),
        ((b3,), ((3, 1),)),
    ):
        stat, acc = earlier_pieces(
            info, bases(*which), slopes_pair, lo, pieces, w_own, w_pair, q_t, stat, acc)
    send, lse, out = close_half(stat, acc)
    got = over_core(send)
    y_pair = project(1, lse, out, got, w_out, wo_pair, None)
    y_got = over_x(y_pair)
    y_own = project(0, lse, out, got, w_out, wo_pair, tokens)
    hidden = (y_own + y_got.astype(F32)).astype(BF16)
    return (hidden, key_cache, value_cache)


def solution(mesh):
    in_specs = (
        P(("seq", "head"), None),
        P(),
        P(None, None, "head"),
        P("head"),
        P("head", None),
        P("seq"),
    )
    out_specs = (P(("seq", "head"), None), P("seq", "head"), P("seq", "head"))
    return jax.shard_map(
        on_device, mesh=mesh, in_specs=in_specs, out_specs=out_specs, check_vma=False
    )
```

time: 239 us -> 166 us (0.69)
  the two profiles are of different devices: /device:TPU:12 before, /device:TPU:20 now
where the time goes in v1:
time: 166 us; the launch traced here: 165 us
  Pallas kernels  64.7 us (39%)
  blocking collectives  33.1 us (20%)
  waiting for transfers between devices  25.5 us (15%)
  starting transfers between devices  22.7 us (14%)
  other arithmetic  9.7 us (6%)
  local copies, waits for them, and re-layouts  7.33 us (4%)
    pallas_call x3, Pallas kernels, earlier_pieces(): pl.pallas_call(body, out_shape=(jax.ShapeDtypeStruct(stat_in.shape, F32),...  35.5 us
    all_gather x1, blocking collectives, on_device(): all_seg = lax.all_gather(seg_ids, 'seq', axis=0, tiled=True)  22.5 us
    ppermute x6, starting transfers between devices, over_seq(): return lax.ppermute(value, 'seq', pairs)  16.7 us
    ppermute x6, waiting for transfers between devices, over_seq(): return lax.ppermute(value, 'seq', pairs)  15.9 us
    pallas_call x1, Pallas kernels, own_block(): pl.pallas_call(body, out_shape=(jax.ShapeDtypeStruct((2 * width, block),...  13.5 us
    pallas_call x2, Pallas kernels, project(): pl.pallas_call(body, out_shape=jax.ShapeDtypeStruct((PIECE, model), BF16...  10.6 us
    unnamed x1, blocking collectives  10.6 us
    ppermute x5, waiting for transfers between devices, over_x(): return lax.ppermute(value, 'head', [(i, i ^ 2) for i in range(4)])  7.46 us
  transfers between devices with their start and end apart: 16, of which 5 were waited for; matrix products, arithmetic and copies ran while one was open for 8% of the time, Pallas kernels for 35%

profile of v1, /device:TPU:20, one launch (start us, length us, event | category | flops | bytes accessed | tf_op | source)
XLA Modules:
  0.0 164.6 jit_solution(14087809307013496198)
XLA Ops:
  0.6 2.2 %shard_map.85.a = bf16[128,2048]{1,0:T(8,128)(2,1)} custom-call(bf16[128,2048]{1,0:T(8,128)(2,1)} %refs_0_.1, f32[1,2048]{1,0:T(1,128)} %bitcast.27), custom_call_target="tpu_custom_call" | custom-call | bytes 1048576 | tf_op jit(solution)/shard_map/pallas_call | solution.py:44
  2.8 3.5 %collective-permute-start = (bf16[128,2048]{1,0:T(8,128)(2,1)}, bf16[128,2048]{1,0:T(8,128)(2,1)S(1)}, u32[]{:S(2)}, u32[]{:S(2)}) collective-permute-start(bf16[128,2048]{1,0:T(8,128)(2,1)} %shard_map.85.a), channel_id=1, source_target_pairs={{0,8},{4,12},{8,16},{12,20},{16,24},{20,28},{1,9},{5,13},{9,17},{1... | collective-permute-start | bytes 1572872 | tf_op jit(solution)/shard_map/ppermute | solution.py:339
  6.3 1.3 collective-permute-start.9
  7.6 11.6 %collective-permute-done.refs_0_ = bf16[128,2048]{1,0:T(8,128)(2,1)S(1)} collective-permute-done((bf16[128,2048]{1,0:T(8,128)(2,1)}, bf16[128,2048]{1,0:T(8,128)(2,1)S(1)}, u32[]{:S(2)}, u32[]{:S(2)}) %collective-permute-start) | collective-permute-done | bytes 524320 | tf_op jit(solution)/shard_map/ppermute | solution.py:339
  19.3 3.5 %collective-permute-start.2 = (bf16[128,2048]{1,0:T(8,128)(2,1)S(1)}, bf16[128,2048]{1,0:T(8,128)(2,1)S(1)}, u32[]{:S(2)}, u32[]{:S(2)}) collective-permute-start(bf16[128,2048]{1,0:T(8,128)(2,1)S(1)} %collective-permute-done.refs_0_), channel_id=1, source_target_pairs={{0,8},{4,12},{8,16},{12,20},{16,24},{20,28},{1,9},{5,13},{9,17},{1... | collective-permute-start | bytes 1572872 | tf_op jit(solution)/shard_map/ppermute | solution.py:339
  22.8 1.6 collective-permute-start.6
  24.3 1.3 slice.3
  25.6 1.3 dynamic-slice
  27.5 0.9 dynamic-update-slice
  28.4 10.6 %all-reduce = f32[16]{0:T(128)S(1)} all-reduce(f32[16]{0:T(128)S(1)} %dynamic-update-slice), channel_id=1, replica_groups=mesh['seq'=8,'head'=4] {'head'}, use_global_device_ids=true, to_apply=%add | all-reduce | flops 16 | bytes 128
  39.0 0.1 dynamic_slice.3
  39.1 22.5 %all-gather = s32[8,1,512]{2,1,0:T(1,128)S(1)} all-gather(s32[1,1,512]{2,1,0:T(1,128)} %bitcast.26), channel_id=1, replica_groups=mesh['seq'=8,'head'=4] {'seq'}, dimensions={0}, use_global_device_ids=true | all-gather | bytes 18432 | tf_op jit(solution)/shard_map/all_gather | solution.py:348
  61.6 1.3 fusion
  62.9 1.5 collective-permute-start.1
  64.4 1.3 pad_maximum_fusion.slopes_ref
  65.7 0.0 collective-permute-done.9
  65.7 0.5 collective-permute-start.11
  66.2 0.0 collective-permute-done.2.refs_3_
  66.3 2.5 %collective-permute-start.3 = (bf16[128,2048]{1,0:T(8,128)(2,1)S(1)}, bf16[128,2048]{1,0:T(8,128)(2,1)S(1)}, u32[]{:S(2)}, u32[]{:S(2)}) collective-permute-start(bf16[128,2048]{1,0:T(8,128)(2,1)S(1)} %collective-permute-done.2.refs_3_), channel_id=1, source_target_pairs={{4,0},{12,8},{20,16},{28,24},{5,1},{13,9},{21,17},{29,25},{6,2},{1... | collective-permute-start | bytes 1572872 | tf_op jit(solution)/shard_map/ppermute | solution.py:339
  68.7 0.6 pad_add_fusion.bases_ref
  69.3 1.0 convert_reduce_fusion
  70.3 2.6 %select_bitcast_fusion.lo_ref = s32[4,128]{1,0:T(4,128)} fusion(s32[512]{0:T(512)S(1)} %convert_reduce_fusion, s32[512]{0:T(512)} %param.11, s32[]{:T(128)} %mul.16, s32[]{:T(128)} %fusion, s32[]{:T(128)} %bitcast.6), kind=kLoop, calls=%fused_computation.6 | loop fusion | flops 1536 | bytes 6156 | tf_op jit(solution)/shard_map/reshape | solution.py:353
  72.9 1.1 collective-permute-done.1
  74.0 0.7 pad_add_fusion.1.bases_ref
  74.7 1.3 stack.57.info_ref
  76.0 0.5 collective-permute-start.14
  76.5 3.1 %collective-permute-done.3 = bf16[128,2048]{1,0:T(8,128)(2,1)S(1)} collective-permute-done((bf16[128,2048]{1,0:T(8,128)(2,1)S(1)}, bf16[128,2048]{1,0:T(8,128)(2,1)S(1)}, u32[]{:S(2)}, u32[]{:S(2)}) %collective-permute-start.3) | collective-permute-done | bytes 524320 | tf_op jit(solution)/shard_map/ppermute | solution.py:339
  79.6 4.5 %collective-permute-start.12 = (bf16[128,2048]{1,0:T(8,128)(2,1)S(1)}, bf16[128,2048]{1,0:T(8,128)(2,1)S(1)}, u32[]{:S(2)}, u32[]{:S(2)}) collective-permute-start(bf16[128,2048]{1,0:T(8,128)(2,1)S(1)} %collective-permute-done.11.refs_1_), channel_id=1, source_target_pairs={{0,8},{4,12},{8,16},{12,20},{16,24},{20,28},{1,9},{5,13},{9,17},{1... | collective-permute-start | bytes 1572872 | tf_op jit(solution)/shard_map/ppermute | solution.py:339
  84.1 0.1 broadcast_select_fusion
  84.2 1.3 collective-permute-start.10
  85.5 0.8 collective-permute-start.4
  86.3 13.5 %shard_map.86 = (bf16[1024,512]{1,0:T(8,128)(2,1)}, f32[16,512]{1,0:T(8,128)}, f32[1024,512]{1,0:T(8,128)}, bf16[512,512]{1,0:T(8,128)(2,1)}, bf16[512,512]{1,0:T(8,128)(2,1)}) custom-call(s32[6]{0:T(128)} %stack.57.info_ref, f32[8]{0:T(128)} %pad_maximum_fusion.slopes_ref, s32[4,128]{1,0:T(4,128)} %select_bitcast_fusion.lo_ref, ...), custom_call_target="tpu_custom_call" | custom-call | flops 5368709120 | bytes 20971520 | tf_op jit(solution)/shard_map/pallas_call | solution.py:138
  99.9 14.4 %shard_map.87 = (f32[16,512]{1,0:T(8,128)}, f32[1024,512]{1,0:T(8,128)}) custom-call(s32[6]{0:T(128)} %stack.57.info_ref, s32[4]{0:T(128)} %pad_add_fusion.1.bases_ref, f32[8]{0:T(128)} %pad_maximum_fusion.slopes_ref, s32[4,128]{1,0:T(4,128)} %select_bitcast_fusion.lo_ref, bf16[128,2048]{1,0:T(8,128)(2,1)} %copy-done.4, bf16[128,2048]{1,0:T(8,128)(2,1)} %copy-done.6, ...), custom_call_target="tpu_custom_call" | custom-call | flops 4294967296 | bytes 16777216 | tf_op jit(solution)/shard_map/pallas_call | solution.py:219
  114.3 0.0 copy-start.8
  114.3 0.7 copy-done.7
  115.1 0.2 copy-done.8
  115.3 12.3 %shard_map.88 = (f32[16,512]{1,0:T(8,128)}, f32[1024,512]{1,0:T(8,128)}) custom-call(s32[6]{0:T(128)} %stack.57.info_ref, s32[3]{0:T(128)} %pad_add_fusion.bases_ref, f32[8]{0:T(128)} %pad_maximum_fusion.slopes_ref, s32[4,128]{1,0:T(4,128)} %select_bitcast_fusion.lo_ref, bf16[128,2048]{1,0:T(8,128)(2,1)} %copy-done.8, bf16[128,2048]{1,0:T(8,128)(2,1)} %copy-done.7, ...), custom_call_target="tpu_custom_call" | custom-call | flops 3221225472 | bytes 16777216 | tf_op jit(solution)/shard_map/pallas_call | solution.py:219
  127.6 0.0 copy-start.9
  127.6 0.8 copy-done.9
  128.4 8.8 %shard_map.89 = (f32[16,512]{1,0:T(8,128)}, f32[1024,512]{1,0:T(8,128)}) custom-call(s32[6]{0:T(128)} %stack.57.info_ref, s32[1]{0:T(128)} %bitcast.8.bases_ref, f32[8]{0:T(128)} %pad_maximum_fusion.slopes_ref, s32[4,128]{1,0:T(4,128)} %select_bitcast_fusion.lo_ref, bf16[128,2048]{1,0:T(8,128)(2,1)} %copy-done.9, bf16[3,2048,512]{2,1,0:T(8,128)(2,1)} %bitcast.25, ...), custom_call_target="tpu_custom_call" | custom-call | flops 1073741824 | bytes 16777216 | tf_op jit(solution)/shard_map/pallas_call | solution.py:219
  137.2 2.9 %shard_map.90 = (bf16[1056,256]{1,0:T(8,128)(2,1)}, f32[8,256]{1,0:T(8,128)}, f32[1024,256]{1,0:T(8,128)}) custom-call(f32[16,512]{1,0:T(8,128)} %get-tuple-element.27.stat_ref, f32[1024,512]{1,0:T(8,128)} %get-tuple-element.28.acc_ref), custom_call_target="tpu_custom_call" | custom-call | bytes 4194304 | tf_op jit(solution)/shard_map/pallas_call | solution.py:266
  140.1 2.1 %collective-permute-done.13.got_ref = bf16[1056,256]{1,0:T(8,128)(2,1)S(1)} collective-permute-done((bf16[1056,256]{1,0:T(8,128)(2,1)}, bf16[1056,256]{1,0:T(8,128)(2,1)S(1)}, u32[]{:S(2)}, u32[]{:S(2)}) %collective-permute-start.13) | collective-permute-done | bytes 540704 | tf_op jit(solution)/shard_map/ppermute | solution.py:333
  142.3 0.8 copy-done.1
  143.1 5.1 %shard_map.92 = bf16[128,2048]{1,0:T(8,128)(2,1)} custom-call(f32[8,256]{1,0:T(8,128)} %get-tuple-element.29.lse_ref, f32[1024,256]{1,0:T(8,128)} %get-tuple-element.30.out_ref, bf16[1056,256]{1,0:T(8,128)(2,1)} %copy-done.1, bf16[512,2048]{1,0:T(8,128)(2,1)} %w0.3, bf16[512,2048]{1,0:T(8,128)(2,1)} %copy-done), custom_call_target="tpu_custom_call" | custom-call | flops 536870912 | bytes 6291456 | tf_op jit(solution)/shard_map/pallas_call | solution.py:310
  148.2 1.3 collective-permute-start.15
  149.5 5.5 %shard_map.91 = f32[128,2048]{1,0:T(8,128)} custom-call(f32[8,256]{1,0:T(8,128)} %get-tuple-element.29.lse_ref, f32[1024,256]{1,0:T(8,128)} %get-tuple-element.30.out_ref, bf16[1056,256]{1,0:T(8,128)(2,1)} %copy-done.1, bf16[512,2048]{1,0:T(8,128)(2,1)} %w0.3, bf16[512,2048]{1,0:T(8,128)(2,1)} %copy-done, bf16[128,2048]{1,0:T(8,128)(2,1)} %refs_0_.1), custom_call_target="tpu_custom_call" | custom-call | flops 536870912 | bytes 6291456 | tf_op jit(solution)/shard_map/pallas_call | solution.py:310
  155.0 7.4 %collective-permute-done.15 = bf16[128,2048]{1,0:T(8,128)(2,1)S(1)} collective-permute-done((bf16[128,2048]{1,0:T(8,128)(2,1)}, bf16[128,2048]{1,0:T(8,128)(2,1)S(1)}, u32[]{:S(2)}, u32[]{:S(2)}) %collective-permute-start.15) | collective-permute-done | bytes 524320 | tf_op jit(solution)/shard_map/ppermute | solution.py:336
  162.4 2.1 %add_convert_fusion = bf16[128,2048]{1,0:T(8,128)(2,1)} fusion(f32[128,2048]{1,0:T(8,128)} %shard_map.91, bf16[128,2048]{1,0:T(8,128)(2,1)S(1)} %collective-permute-done.15), kind=kLoop, calls=%fused_computation | loop fusion | flops 786432 | bytes 2097152 | tf_op jit(solution)/shard_map/convert_element_type | solution.py:400
  (28 shorter events, 0.1 us)
Async XLA Ops:
  2.8 83.5 %collective-permute-start.5 = (bf16[3,2048,512]{2,1,0:T(8,128)(2,1)}, bf16[3,2048,512]{2,1,0:T(8,128)(2,1)}, u32[]{:S(2)}, u32[]{:S(2)}) collective-permute-start(bf16[3,2048,512]{2,1,0:T(8,128)(2,1)} %bitcast.21), channel_id=1, source_target_pairs={{0,1},{1,0},{2,3},{3,2},{4,5},{5,4},{6,7},{7,6},{8,9},{9,8},{10,11... | collective-permute-start | bytes 18874376 | tf_op jit(solution)/shard_map/ppermute | solution.py:333
  2.8 16.4 %collective-permute-start = (bf16[128,2048]{1,0:T(8,128)(2,1)}, bf16[128,2048]{1,0:T(8,128)(2,1)S(1)}, u32[]{:S(2)}, u32[]{:S(2)}) collective-permute-start(bf16[128,2048]{1,0:T(8,128)(2,1)} %shard_map.85.a), channel_id=1, source_target_pairs={{0,8},{4,12},{8,16},{12,20},{16,24},{20,28},{1,9},{5,13},{9,17},{1... | collective-permute-start | bytes 1572872 | tf_op jit(solution)/shard_map/ppermute | solution.py:339
  6.3 59.4 %collective-permute-start.9 = (bf16[128,2048]{1,0:T(8,128)(2,1)}, bf16[128,2048]{1,0:T(8,128)(2,1)S(1)}, u32[]{:S(2)}, u32[]{:S(2)}) collective-permute-start(bf16[128,2048]{1,0:T(8,128)(2,1)} %shard_map.85.a), channel_id=1, source_target_pairs={{0,4},{8,12},{16,20},{24,28},{1,5},{9,13},{17,21},{25,29},{2,6},{1... | collective-permute-start | bytes 1572872 | tf_op jit(solution)/shard_map/ppermute | solution.py:339
  19.3 80.6 %copy-start.4 = (bf16[128,2048]{1,0:T(8,128)(2,1)}, bf16[128,2048]{1,0:T(8,128)(2,1)S(1)}, u32[]{:S(2)}) copy-start(bf16[128,2048]{1,0:T(8,128)(2,1)S(1)} %collective-permute-done.refs_0_) | copy-start | bytes 1572868
  19.3 47.0 %collective-permute-start.2 = (bf16[128,2048]{1,0:T(8,128)(2,1)S(1)}, bf16[128,2048]{1,0:T(8,128)(2,1)S(1)}, u32[]{:S(2)}, u32[]{:S(2)}) collective-permute-start(bf16[128,2048]{1,0:T(8,128)(2,1)S(1)} %collective-permute-done.refs_0_), channel_id=1, source_target_pairs={{0,8},{4,12},{8,16},{12,20},{16,24},{20,28},{1,9},{5,13},{9,17},{1... | collective-permute-start | bytes 1572872 | tf_op jit(solution)/shard_map/ppermute | solution.py:339
  22.8 50.1 %collective-permute-start.6 = (bf16[128,2048]{1,0:T(8,128)(2,1)}, bf16[128,2048]{1,0:T(8,128)(2,1)}, u32[]{:S(2)}, u32[]{:S(2)}) collective-permute-start(bf16[128,2048]{1,0:T(8,128)(2,1)} %shard_map.85.a), channel_id=1, source_target_pairs={{0,2},{1,3},{2,0},{3,1},{4,6},{5,7},{6,4},{7,5},{8,10},{9,11},{10,... | collective-permute-start | bytes 1572872 | tf_op jit(solution)/shard_map/ppermute | solution.py:336
  62.9 11.1 %collective-permute-start.1 = (bf16[128,2048]{1,0:T(8,128)(2,1)S(1)}, bf16[128,2048]{1,0:T(8,128)(2,1)S(1)}, u32[]{:S(2)}, u32[]{:S(2)}) collective-permute-start(bf16[128,2048]{1,0:T(8,128)(2,1)S(1)} %collective-permute-done.refs_0_), channel_id=1, source_target_pairs={{0,4},{8,12},{16,20},{24,28},{4,0},{12,8},{20,16},{28,24},{1,5},{9... | collective-permute-start | bytes 1572872 | tf_op jit(solution)/shard_map/ppermute | solution.py:339
  65.7 10.2 %collective-permute-start.11 = (bf16[128,2048]{1,0:T(8,128)(2,1)S(1)}, bf16[128,2048]{1,0:T(8,128)(2,1)S(1)}, u32[]{:S(2)}, u32[]{:S(2)}) collective-permute-start(bf16[128,2048]{1,0:T(8,128)(2,1)S(1)} %collective-permute-done.refs_0_), channel_id=1, source_target_pairs={{0,2},{1,3},{2,0},{3,1},{4,6},{5,7},{6,4},{7,5},{8,10},{9,11},{10,... | collective-permute-start | bytes 1572872 | tf_op jit(solution)/shard_map/ppermute | solution.py:336
  66.3 33.6 %copy-start.5 = (bf16[128,2048]{1,0:T(8,128)(2,1)}, bf16[128,2048]{1,0:T(8,128)(2,1)S(1)}, u32[]{:S(2)}) copy-start(bf16[128,2048]{1,0:T(8,128)(2,1)S(1)} %collective-permute-done.2.refs_3_) | copy-start | bytes 1572868
  66.3 13.4 %collective-permute-start.3 = (bf16[128,2048]{1,0:T(8,128)(2,1)S(1)}, bf16[128,2048]{1,0:T(8,128)(2,1)S(1)}, u32[]{:S(2)}, u32[]{:S(2)}) collective-permute-start(bf16[128,2048]{1,0:T(8,128)(2,1)S(1)} %collective-permute-done.2.refs_3_), channel_id=1, source_target_pairs={{4,0},{12,8},{20,16},{28,24},{5,1},{13,9},{21,17},{29,25},{6,2},{1... | collective-permute-start | bytes 1572872 | tf_op jit(solution)/shard_map/ppermute | solution.py:339
  72.9 11.3 %collective-permute-start.7 = (bf16[128,2048]{1,0:T(8,128)(2,1)}, bf16[128,2048]{1,0:T(8,128)(2,1)}, u32[]{:S(2)}, u32[]{:S(2)}) collective-permute-start(bf16[128,2048]{1,0:T(8,128)(2,1)} %shard_map.85.a), channel_id=1, source_target_pairs={{0,1},{1,0},{2,3},{3,2},{4,5},{5,4},{6,7},{7,6},{8,9},{9,8},{10,11... | collective-permute-start | bytes 1572872 | tf_op jit(solution)/shard_map/ppermute | solution.py:333
  74.0 11.6 %collective-permute-start.8 = (bf16[128,2048]{1,0:T(8,128)(2,1)}, bf16[128,2048]{1,0:T(8,128)(2,1)}, u32[]{:S(2)}, u32[]{:S(2)}) collective-permute-start(bf16[128,2048]{1,0:T(8,128)(2,1)} %collective-permute-done.6.b), channel_id=1, source_target_pairs={{0,1},{1,0},{2,3},{3,2},{4,5},{5,4},{6,7},{7,6},{8,9},{9,8},{10,11... | collective-permute-start | bytes 1572872 | tf_op jit(solution)/shard_map/ppermute | solution.py:333
  75.9 24.0 %copy-start.6 = (bf16[128,2048]{1,0:T(8,128)(2,1)}, bf16[128,2048]{1,0:T(8,128)(2,1)S(1)}, u32[]{:S(2)}) copy-start(bf16[128,2048]{1,0:T(8,128)(2,1)S(1)} %collective-permute-done.11.refs_1_) | copy-start | bytes 1572868
  76.0 64.2 %collective-permute-start.14 = (bf16[512,2048]{1,0:T(8,128)(2,1)}, bf16[512,2048]{1,0:T(8,128)(2,1)S(1)}, u32[]{:S(2)}, u32[]{:S(2)}) collective-permute-start(bf16[512,2048]{1,0:T(8,128)(2,1)} %w0.3), channel_id=1, source_target_pairs={{0,1},{1,0},{2,3},{3,2},{4,5},{5,4},{6,7},{7,6},{8,9},{9,8},{10,11... | collective-permute-start | bytes 6291464 | tf_op jit(solution)/shard_map/ppermute | solution.py:333
  79.6 34.7 %collective-permute-start.12 = (bf16[128,2048]{1,0:T(8,128)(2,1)S(1)}, bf16[128,2048]{1,0:T(8,128)(2,1)S(1)}, u32[]{:S(2)}, u32[]{:S(2)}) collective-permute-start(bf16[128,2048]{1,0:T(8,128)(2,1)S(1)} %collective-permute-done.11.refs_1_), channel_id=1, source_target_pairs={{0,8},{4,12},{8,16},{12,20},{16,24},{20,28},{1,9},{5,13},{9,17},{1... | collective-permute-start | bytes 1572872 | tf_op jit(solution)/shard_map/ppermute | solution.py:339
  84.2 15.7 %copy-start.2 = (bf16[128,2048]{1,0:T(8,128)(2,1)}, bf16[128,2048]{1,0:T(8,128)(2,1)S(1)}, u32[]{:S(2)}) copy-start(bf16[128,2048]{1,0:T(8,128)(2,1)S(1)} %get-tuple-element.36.refs_2_) | copy-start | bytes 1572868
  84.2 15.7 %copy-start.3 = (bf16[128,2048]{1,0:T(8,128)(2,1)}, bf16[128,2048]{1,0:T(8,128)(2,1)S(1)}, u32[]{:S(2)}) copy-start(bf16[128,2048]{1,0:T(8,128)(2,1)S(1)} %get-tuple-element.35.refs_2_) | copy-start | bytes 1572868
  84.2 30.1 %collective-permute-start.10 = (bf16[128,2048]{1,0:T(8,128)(2,1)S(1)}, bf16[128,2048]{1,0:T(8,128)(2,1)S(1)}, u32[]{:S(2)}, u32[]{:S(2)}) collective-permute-start(bf16[128,2048]{1,0:T(8,128)(2,1)S(1)} %get-tuple-element.35.refs_2_), channel_id=1, source_target_pairs={{0,2},{1,3},{2,0},{3,1},{4,6},{5,7},{6,4},{7,5},{8,10},{9,11},{10,... | collective-permute-start | bytes 1572872 | tf_op jit(solution)/shard_map/ppermute | solution.py:336
  85.5 42.0 %collective-permute-start.4 = (bf16[128,2048]{1,0:T(8,128)(2,1)S(1)}, bf16[128,2048]{1,0:T(8,128)(2,1)S(1)}, u32[]{:S(2)}, u32[]{:S(2)}) collective-permute-start(bf16[128,2048]{1,0:T(8,128)(2,1)S(1)} %get-tuple-element.36.refs_2_), channel_id=1, source_target_pairs={{0,2},{1,3},{2,0},{3,1},{4,6},{5,7},{6,4},{7,5},{8,10},{9,11},{10,... | collective-permute-start | bytes 1572872 | tf_op jit(solution)/shard_map/ppermute | solution.py:336
  114.3 0.8 copy-start.7
  114.3 0.9 copy-start.8
  127.6 0.8 copy-start.9
  140.1 2.1 %collective-permute-start.13 = (bf16[1056,256]{1,0:T(8,128)(2,1)}, bf16[1056,256]{1,0:T(8,128)(2,1)S(1)}, u32[]{:S(2)}, u32[]{:S(2)}) collective-permute-start(bf16[1056,256]{1,0:T(8,128)(2,1)} %get-tuple-element.31), channel_id=1, source_target_pairs={{0,1},{1,0},{2,3},{3,2},{4,5},{5,4},{6,7},{7,6},{8,9},{9,8},{10,11... | collective-permute-start | bytes 1622024 | tf_op jit(solution)/shard_map/ppermute | solution.py:333
  140.1 2.1 %copy-start = (bf16[512,2048]{1,0:T(8,128)(2,1)}, bf16[512,2048]{1,0:T(8,128)(2,1)S(1)}, u32[]{:S(2)}) copy-start(bf16[512,2048]{1,0:T(8,128)(2,1)S(1)} %collective-permute-done.14.w1) | copy-start | bytes 6291460
  142.3 0.8 copy-start.1
  148.2 14.2 %collective-permute-start.15 = (bf16[128,2048]{1,0:T(8,128)(2,1)}, bf16[128,2048]{1,0:T(8,128)(2,1)S(1)}, u32[]{:S(2)}, u32[]{:S(2)}) collective-permute-start(bf16[128,2048]{1,0:T(8,128)(2,1)} %shard_map.92), channel_id=1, source_target_pairs={{0,2},{1,3},{2,0},{3,1},{4,6},{5,7},{6,4},{7,5},{8,10},{9,11},{10,... | collective-permute-start | bytes 1572872 | tf_op jit(solution)/shard_map/ppermute | solution.py:336

commit v2 on v1

v2 whole, which is shorter than its diff:
```python
import jax
import jax.numpy as jnp
from jax import lax
from jax.experimental import pallas as pl
from jax.experimental.pallas import tpu as pltpu
from jax.sharding import PartitionSpec as P

HD = 128
SPAN = 4
PIECE = 128
EPSILON = 1e-05
NEG_FILL = -1e30
MASKED = -2e38
LOG2E = 1.4426950408889634

BF16 = jnp.bfloat16
F32 = jnp.float32
SMEM = pl.BlockSpec(memory_space=pltpu.SMEM)
VMEM = pl.BlockSpec(memory_space=pltpu.VMEM)


def params(mebibytes):
    return pltpu.CompilerParams(vmem_limit_bytes=mebibytes * 2**20)


def cost(macs, nbytes, exps=0):
    return pl.CostEstimate(flops=2 * macs, bytes_accessed=nbytes, transcendentals=exps)


def dot(lhs, rhs):
    return jnp.dot(lhs, rhs, preferred_element_type=F32)


def layer_norm(tokens, ln_gain):
    def body(tokens_ref, gain_ref, out_ref):
        inputs = tokens_ref[...].astype(F32)
        centred = inputs - jnp.mean(inputs, axis=-1, keepdims=True)
        variance = jnp.mean(centred * centred, axis=-1, keepdims=True)
        out_ref[...] = (centred * lax.rsqrt(variance + EPSILON) * gain_ref[...]).astype(BF16)

    return pl.pallas_call(
        body,
        out_shape=jax.ShapeDtypeStruct(tokens.shape, BF16),
        in_specs=[VMEM, VMEM],
        out_specs=VMEM,
        compiler_params=params(8),
        cost_estimate=cost(0, 2 * tokens.size * 2, tokens.size),
    )(tokens, ln_gain.reshape(1, -1))


def place_of(place):
    return lax.axis_index("head") ^ (0, 2, 1, 3)[place]


def set_distance(block_base, key_base, keys, dist_ref):
    row = lax.broadcasted_iota(jnp.int32, (PIECE, PIECE), 0)
    for piece in range(keys):
        dist_ref[pl.ds(piece * PIECE, PIECE), :] = (row + (key_base(piece) - block_base)).astype(F32)


def set_own_masks(seg_ref, mask_ref, dist_ref):
    lane = lax.broadcasted_iota(jnp.int32, (1, PIECE), 1)
    row = lax.broadcasted_iota(jnp.int32, (PIECE, PIECE), 0)
    set_distance(0, lambda i: place_of(i) * PIECE, 2, dist_ref)
    for piece in range(2):
        rows = pl.ds(piece * PIECE, PIECE)
        k_pos = row + place_of(piece) * PIECE
        key_seg = seg_ref[pl.ds(place_of(piece), 1), :]
        key_seg = jnp.broadcast_to(key_seg, (PIECE, PIECE)).T
        for place in range(4):
            q_pos = lane + place_of(place) * PIECE
            kept = (key_seg == seg_ref[pl.ds(place_of(place), 1), :]) & (k_pos <= q_pos)
            mask_ref[rows, pl.ds(place * PIECE, PIECE)] = jnp.where(kept, 0.0, MASKED)


def set_earlier_masks(seg_ref, start, block_base, key_base, keys, mask_ref, dist_ref):
    row = lax.broadcasted_iota(jnp.int32, (PIECE, PIECE), 0)
    set_distance(block_base, key_base, keys, dist_ref)
    first_seg = seg_ref[0:1, 0:1]
    for piece in range(keys):
        rows = pl.ds(piece * PIECE, PIECE)
        late = row + key_base(piece) >= start
        for place in range(4):
            kept = late & (seg_ref[pl.ds(place_of(place), 1), :] == first_seg)
            mask_ref[rows, pl.ds(place * PIECE, PIECE)] = jnp.where(kept, 0.0, MASKED)


def attend(group, k_rows, v_t, q_ref, slopes_ref, mask_ref, dist_ref, before, stat_ref, acc_ref):
    heads = k_rows.shape[1] // HD
    for local in range(heads):
        head = group * heads + local
        cols = slice(local * HD, (local + 1) * HD)
        wide = pl.ds(head * HD, HD)
        bias = dist_ref[...] * (slopes_ref[local] * LOG2E)
        bias = jnp.concatenate([bias] * (q_ref.shape[1] // PIECE), axis=1)
        scores = dot(k_rows[:, cols], q_ref[wide, :]) * (HD**-0.5 * LOG2E)
        scores = scores + bias + mask_ref[...]
        top = jnp.max(scores, axis=0, keepdims=True)
        prev = jnp.full_like(top, NEG_FILL) if before is None else before[0][head : head + 1, :]
        row_max = jnp.maximum(prev, top)
        expo = jnp.exp2(scores - row_max)
        total = jnp.sum(expo, axis=0, keepdims=True)
        update = dot(v_t[cols, :], expo.astype(BF16))
        if before is not None:
            rescale = jnp.exp2(prev - row_max)
            total = before[0][8 + head : 9 + head, :] * rescale + total
            update = before[1][wide, :] * rescale + update
        stat_ref[head : head + 1, :] = row_max
        stat_ref[8 + head : 9 + head, :] = total
        acc_ref[wide, :] = update


def own_block(slopes, slopes_pair, seg, pieces, w_own, w_pair):
    depth, width = w_own.shape[1:]
    block = 4 * PIECE

    def body(s0, s1, seg_ref, a, b, c, d, w0, w1, q, stat, acc, k_cache, v_cache, mask, dist):
        set_own_masks(seg_ref, mask, dist)
        x = jnp.concatenate([a[...], b[...], c[...], d[...]], axis=0)
        for group, w in enumerate((w0, w1)):
            rows = block if group == 0 else 2 * PIECE
            q[pl.ds(group * width, width), :] = dot(x, w[0]).T.astype(BF16)
            keys = dot(x[:rows], w[1]).astype(BF16)
            values = dot(x[:rows], w[2])
            if group == 0:
                for place in range(4):
                    to = pl.ds(pl.multiple_of(place_of(place) * PIECE, PIECE), PIECE)
                    k_cache[to, :] = keys[place * PIECE : (place + 1) * PIECE]
                    v_cache[to, :] = values[place * PIECE : (place + 1) * PIECE].astype(BF16)
            v_t = values[: 2 * PIECE].T.astype(BF16)
            attend(group, keys[: 2 * PIECE], v_t, q, (s0, s1)[group], mask, dist, None, stat, acc)

    return pl.pallas_call(
        body,
        out_shape=(
            jax.ShapeDtypeStruct((2 * width, block), BF16),
            jax.ShapeDtypeStruct((16, block), F32),
            jax.ShapeDtypeStruct((2 * width, block), F32),
            jax.ShapeDtypeStruct((block, width), BF16),
            jax.ShapeDtypeStruct((block, width), BF16),
        ),
        in_specs=[SMEM, SMEM] + [VMEM] * 7,
        out_specs=(VMEM,) * 5,
        scratch_shapes=[
            pltpu.VMEM((2 * PIECE, block), F32),
            pltpu.VMEM((2 * PIECE, PIECE), F32),
        ],
        compiler_params=params(26),
        cost_estimate=cost(5 * block * depth * width, 2**20, 0),
    )(slopes, slopes_pair, seg, *pieces, w_own, w_pair)


def write_closed(stat, acc, send_ref, lse_ref, out_ref):
    wide, block = acc.shape
    half = block // 2
    total = stat[8:16, :]
    some = total > 0.0
    lse = jnp.where(some, stat[0:8, :] + jnp.log2(jnp.where(some, total, 1.0)), NEG_FILL)
    scale = jnp.where(some, 1.0 / jnp.where(some, total, 1.0), 0.0)
    lse_ref[...] = lse[:, :half]
    for head in range(8):
        rows = pl.ds(head * HD, HD)
        normal = acc[rows, :] * scale[head : head + 1, :]
        out_ref[rows, :] = normal[:, :half]
        send_ref[rows, :] = normal[:, half:].astype(BF16)
    rest = lse[:, half:]
    high = rest.astype(BF16)
    rest = rest - high.astype(F32)
    middle = rest.astype(BF16)
    low = (rest - middle.astype(F32)).astype(BF16)
    parts = [part.astype(F32) for part in (high, middle, low)]
    parts.append(jnp.zeros_like(parts[0]))
    send_ref[pl.ds(wide, 32), :] = jnp.concatenate(parts, axis=0).astype(BF16)


def earlier_pieces(which, closing, slopes, slopes_pair, seg, segs, pieces, w_own, w_pair, q_t, stat_in, acc_in):
    depth, width = w_own.shape[1:]
    block = 4 * PIECE
    count = len(pieces)
    rows = count * PIECE
    n_out = 3 if closing else 2

    def body(s0, s1, seg_ref, *refs):
        seg_refs, refs = refs[: len(segs)], refs[len(segs) :]
        sources, refs = refs[:count], refs[count:]
        (w0, w1, q, stat_src, acc_src), refs = refs[:5], refs[5:]
        outs, scratch = refs[:n_out], refs[n_out:]
        mask, dist = scratch[:2]
        stat, acc = scratch[2:] if closing else outs
        block_num = lax.axis_index("seq")
        block_base = block_num * block
        same = jnp.zeros(seg_ref.shape, jnp.int32)
        for back, ref in enumerate(seg_refs, 1):
            same = same + jnp.where((ref[...] == seg_ref[0:1, 0:1]) & (block_num >= back), 1, 0)
        start = block_base - jnp.sum(same)

        def key_base(i):
            back, place = which[i]
            return block_base - back * block + place_of(place) * PIECE

        live = key_base(0) + PIECE > start
        for i in range(1, count):
            live = live | (key_base(i) + PIECE > start)

        @pl.when(live)
        def _():
            set_earlier_masks(seg_ref, start, block_base, key_base, count, mask, dist)
            x = jnp.concatenate([source[...] for source in sources], axis=0)
            for group, w in enumerate((w0, w1)):
                keys = dot(x, w[1]).astype(BF16)
                v_t = dot(x, w[2]).T.astype(BF16)
                attend(group, keys, v_t, q, (s0, s1)[group], mask, dist, (stat_src, acc_src), stat, acc)

        @pl.when(jnp.logical_not(live))
        def _():
            stat[...] = stat_src[...]
            acc[...] = acc_src[...]

        if closing:
            write_closed(stat, acc, *outs)

    scratch = [pltpu.VMEM((rows, block), F32), pltpu.VMEM((rows, PIECE), F32)]
    if closing:
        scratch += [pltpu.VMEM(stat_in.shape, F32), pltpu.VMEM(acc_in.shape, F32)]
        out_shape = (
            jax.ShapeDtypeStruct((2 * width + 32, block // 2), BF16),
            jax.ShapeDtypeStruct((8, block // 2), F32),
            jax.ShapeDtypeStruct((2 * width, block // 2), F32),
        )
    else:
        out_shape = (
            jax.ShapeDtypeStruct(stat_in.shape, F32),
            jax.ShapeDtypeStruct(acc_in.shape, F32),
        )
    return pl.pallas_call(
        body,
        out_shape=out_shape,
        in_specs=[SMEM, SMEM] + [VMEM] * (6 + len(segs) + count),
        out_specs=(VMEM,) * n_out,
        scratch_shapes=scratch,
        compiler_params=params(26),
        cost_estimate=cost(4 * rows * depth * width, 2**20, 0),
    )(slopes, slopes_pair, seg, *segs, *pieces, w_own, w_pair, q_t, stat_in, acc_in)


def project(place, lse, out, got, wo_own, wo_pair, tokens):
    wide = out.shape[0]
    width, model = wo_own.shape

    def body(lse_ref, out_ref, got_ref, w0, w1, *refs):
        y_ref, ctx = refs[-2:]
        lanes = pl.ds(place * PIECE, PIECE)
        other = got_ref[pl.ds(wide, 32), lanes].astype(F32)
        other = other[0:8] + other[8:16] + other[16:24]
        for head in range(8):
            swapped = (head + 4) % 8
            mine, theirs = lse_ref[head : head + 1, lanes], other[swapped : swapped + 1]
            top = jnp.maximum(mine, theirs)
            weigh, weigh_other = jnp.exp2(mine - top), jnp.exp2(theirs - top)
            joined = (out_ref[pl.ds(head * HD, HD), lanes] * weigh
                      + got_ref[pl.ds(swapped * HD, HD), lanes].astype(F32) * weigh_other)
            joined = joined / (weigh + weigh_other)
            ctx[:, head * HD : (head + 1) * HD] = joined.T.astype(BF16)
        result = dot(ctx[:, :width], w0[...]) + dot(ctx[:, width:], w1[...])
        if tokens is not None:
            result = result + refs[0][...].astype(F32)
        y_ref[...] = result.astype(y_ref.dtype)

    extra = () if tokens is None else (tokens,)
    return pl.pallas_call(
        body,
        out_shape=jax.ShapeDtypeStruct((PIECE, model), BF16 if tokens is None else F32),
        in_specs=[VMEM] * (5 + len(extra)),
        out_specs=VMEM,
        scratch_shapes=[pltpu.VMEM((PIECE, wide), BF16)],
        compiler_params=params(16),
        cost_estimate=cost(PIECE * wide * model, 2**20, 0),
    )(lse, out, got, wo_own, wo_pair, *extra)


def on_device(tokens, ln_gain, w_qkv, slopes, w_out, seg_ids):
    blocks = lax.axis_size("seq")
    block_num = lax.axis_index("seq")
    odd = (block_num % 2) == 1

    def over_core(value):
        return lax.ppermute(value, "head", [(i, i ^ 1) for i in range(4)])

    def over_x(value):
        return lax.ppermute(value, "head", [(i, i ^ 2) for i in range(4)])

    def over_seq(value, pairs):
        return lax.ppermute(value, "seq", pairs)

    two_on = [(i, i + 2) for i in range(blocks - 2)]
    even_to_odd = [(i, i + 1) for i in range(0, blocks, 2)]
    odd_to_even = [(i + 1, i) for i in range(0, blocks, 2)]

    w_own = jnp.transpose(w_qkv, (1, 0, 2))
    w_pair = over_core(w_own)
    a0 = layer_norm(tokens, ln_gain)
    a2 = over_seq(a0, two_on)
    b0 = over_x(a0)
    a1_odd = over_seq(a0, even_to_odd)
    c0 = over_core(a0)
    wo_tied, slopes_tied, seg, _ = lax.optimization_barrier(
        (w_out, slopes, seg_ids.reshape(4, PIECE), c0))
    slopes_pair = over_core(slopes_tied)
    segs = [over_seq(seg, [(i, i + back) for i in range(blocks - back)]) for back in range(1, SPAN + 1)]
    wo_pair = over_core(wo_tied)
    d0 = over_core(b0)

    a4 = over_seq(a2, two_on)
    b2 = over_x(a2)
    crossed = over_seq(a2, even_to_odd + odd_to_even)
    a1 = jnp.where(odd, a1_odd, crossed)

    def merge(closing, pieces, which, state):
        return earlier_pieces(
            which, closing, slopes, slopes_pair, seg, segs, pieces, w_own, w_pair, q_t, *state)

    q_t, stat, acc, key_cache, value_cache = own_block(
        slopes, slopes_pair, seg, (a0, b0, c0, d0), w_own, w_pair)
    a1, b2, a4, stat = lax.optimization_barrier((a1, b2, a4, stat))
    b1 = over_x(a1)
    b4 = over_seq(b2, two_on)
    a3_even = over_seq(a4, odd_to_even)
    a3 = jnp.where(odd, crossed, a3_even)
    state = merge(False, (a2, b2, a1, a4), ((2, 0), (2, 1), (1, 0), (4, 0)), (stat, acc))
    a3, tied = lax.optimization_barrier((a3, state[0]))
    b3 = over_x(a3)
    state = (tied, state[1])
    state = merge(False, (b1, b4, a3), ((1, 1), (4, 1), (3, 0)), state)
    state = merge(True, (b3,), ((3, 1),), state)
    send, lse, out = state
    got = over_core(send)
    y_pair = project(1, lse, out, got, w_out, wo_pair, None)
    y_got = over_x(y_pair)
    y_own = project(0, lse, out, got, w_out, wo_pair, tokens)
    hidden = (y_own + y_got.astype(F32)).astype(BF16)
    return (hidden, key_cache, value_cache)


def solution(mesh):
    in_specs = (
        P(("seq", "head"), None),
        P(),
        P(None, None, "head"),
        P("head"),
        P("head", None),
        P("seq"),
    )
    out_specs = (P(("seq", "head"), None), P("seq", "head"), P("seq", "head"))
    return jax.shard_map(
        on_device, mesh=mesh, in_specs=in_specs, out_specs=out_specs, check_vma=False
    )
```

time: 166 us -> 118 us (0.71)
  the two profiles are of different devices: /device:TPU:20 before, /device:TPU:12 now
where the time goes in v2:
time: 118 us
  waiting for transfers between devices  44.6 us (38%)
  Pallas kernels  42.2 us (36%)
  starting transfers between devices  23.6 us (20%)
  local copies, waits for them, and re-layouts  4.53 us (4%)
  other arithmetic  2.13 us (2%)
    pallas_call x3, Pallas kernels, earlier_pieces(): pl.pallas_call(body, out_shape=out_shape, in_specs=[SMEM, SMEM] + [VMEM]...  28.3 us
    ppermute x10, waiting for transfers between devices, over_seq(): return lax.ppermute(value, 'seq', pairs)  27 us
    ppermute x10, starting transfers between devices, over_seq(): return lax.ppermute(value, 'seq', pairs)  19 us
    ppermute x5, waiting for transfers between devices, over_x(): return lax.ppermute(value, 'head', [(i, i ^ 2) for i in range(4)])  15.7 us
    pallas_call x1, Pallas kernels, own_block(): pl.pallas_call(body, out_shape=(jax.ShapeDtypeStruct((2 * width, block),...  11.9 us
    unnamed x16, local copies, waits for them, and re-layouts  4.53 us
    ppermute x5, starting transfers between devices, over_x(): return lax.ppermute(value, 'head', [(i, i ^ 2) for i in range(4)])  3.79 us
  transfers between devices with their start and end apart: 21, of which 10 were waited for; matrix products, arithmetic and copies ran while one was open for 1% of the time, Pallas kernels for 35%

profile of v2, /device:TPU:12, one launch (start us, length us, event | category | flops | bytes accessed | tf_op | source)
XLA Modules:
  0.0 117.9 jit_solution(9285270328328366664)
XLA Ops:
  0.6 0.0 copy-start.7
  0.7 0.1 collective-permute-start.13
  0.7 0.0 copy-start.3
  0.7 1.0 copy-done.3
  1.8 0.7 copy-done.6
  2.5 0.4 shard_map.85.a
  2.9 3.5 %collective-permute-start.6 = (bf16[128,2048]{1,0:T(8,128)(2,1)S(1)}, bf16[128,2048]{1,0:T(8,128)(2,1)S(1)}, u32[]{:S(2)}, u32[]{:S(2)}) collective-permute-start(bf16[128,2048]{1,0:T(8,128)(2,1)S(1)} %shard_map.85.a), channel_id=1, source_target_pairs={{0,8},{4,12},{8,16},{12,20},{16,24},{20,28},{1,9},{5,13},{9,17},{1... | collective-permute-start | bytes 1572872 | tf_op jit(solution)/shard_map/ppermute | solution.py:293
  6.3 1.6 %collective-permute-start.11 = (bf16[128,2048]{1,0:T(8,128)(2,1)S(1)}, bf16[128,2048]{1,0:T(8,128)(2,1)S(1)}, u32[]{:S(2)}, u32[]{:S(2)}) collective-permute-start(bf16[128,2048]{1,0:T(8,128)(2,1)S(1)} %shard_map.85.a), channel_id=1, source_target_pairs={{0,2},{1,3},{2,0},{3,1},{4,6},{5,7},{6,4},{7,5},{8,10},{9,11},{10,... | collective-permute-start | bytes 1572872 | tf_op jit(solution)/shard_map/ppermute | solution.py:290
  7.9 0.0 collective-permute-start
  7.9 1.3 %collective-permute-start.8 = (bf16[128,2048]{1,0:T(8,128)(2,1)S(1)}, bf16[128,2048]{1,0:T(8,128)(2,1)}, u32[]{:S(2)}, u32[]{:S(2)}) collective-permute-start(bf16[128,2048]{1,0:T(8,128)(2,1)S(1)} %shard_map.85.a), channel_id=1, source_target_pairs={{0,4},{8,12},{16,20},{24,28},{1,5},{9,13},{17,21},{25,29},{2,6},{1... | collective-permute-start | bytes 1572872 | tf_op jit(solution)/shard_map/ppermute | solution.py:293
  9.2 9.9 %collective-permute-done.6.refs_4_ = bf16[128,2048]{1,0:T(8,128)(2,1)S(1)} collective-permute-done((bf16[128,2048]{1,0:T(8,128)(2,1)S(1)}, bf16[128,2048]{1,0:T(8,128)(2,1)S(1)}, u32[]{:S(2)}, u32[]{:S(2)}) %collective-permute-start.6) | collective-permute-done | bytes 524320 | tf_op jit(solution)/shard_map/ppermute | solution.py:293
  19.1 0.5 collective-permute-start.7
  19.6 0.9 collective-permute-done.11.b
  20.5 0.0 collective-permute-start.12
  20.5 0.0 collective-permute-done.c
  20.5 0.5 collective-permute-start.1
  21.0 3.6 %collective-permute-done.8 = bf16[128,2048]{1,0:T(8,128)(2,1)} collective-permute-done((bf16[128,2048]{1,0:T(8,128)(2,1)S(1)}, bf16[128,2048]{1,0:T(8,128)(2,1)}, u32[]{:S(2)}, u32[]{:S(2)}) %collective-permute-start.8) | collective-permute-done | bytes 524320 | tf_op jit(solution)/shard_map/ppermute | solution.py:293
  24.6 0.5 collective-permute-start.9
  25.1 10.2 %collective-permute-done.7 = bf16[128,2048]{1,0:T(8,128)(2,1)S(1)} collective-permute-done((bf16[128,2048]{1,0:T(8,128)(2,1)S(1)}, bf16[128,2048]{1,0:T(8,128)(2,1)S(1)}, u32[]{:S(2)}, u32[]{:S(2)}) %collective-permute-start.7) | collective-permute-done | bytes 524320 | tf_op jit(solution)/shard_map/ppermute | solution.py:293
  35.4 3.5 %collective-permute-start.10 = (bf16[128,2048]{1,0:T(8,128)(2,1)S(1)}, bf16[128,2048]{1,0:T(8,128)(2,1)S(1)}, u32[]{:S(2)}, u32[]{:S(2)}) collective-permute-start(bf16[128,2048]{1,0:T(8,128)(2,1)S(1)} %collective-permute-done.6.refs_4_), channel_id=1, source_target_pairs={{0,8},{4,12},{8,16},{12,20},{16,24},{20,28},{1,9},{5,13},{9,17},{1... | collective-permute-start | bytes 1572872 | tf_op jit(solution)/shard_map/ppermute | solution.py:293
  38.8 1.1 broadcast_select_fusion.1.refs_6_
  40.0 0.0 copy-start
  40.0 2.8 %copy-done = bf16[2048,3,512]{2,0,1:T(8,128)(2,1)S(1)} copy-done((bf16[2048,3,512]{2,0,1:T(8,128)(2,1)S(1)}, bf16[2048,3,512]{2,0,1:T(8,128)(2,1)}, u32[]{:S(2)}) %copy-start) | copy-done | bytes 6291480
  42.8 11.9 %shard_map.86 = (bf16[1024,512]{1,0:T(8,128)(2,1)S(1)}, f32[16,512]{1,0:T(8,128)S(1)}, f32[1024,512]{1,0:T(8,128)S(1)}, bf16[512,512]{1,0:T(8,128)(2,1)}, bf16[512,512]{1,0:T(8,128)(2,1)}) custom-call(f32[4]{0:T(128)S(1)} %copy-done.7, f32[4]{0:T(128)S(1)} %collective-permute-done.1.s1, s32[4,128]{1,0:T(4,128)S(1)} %bitcast.8, ...), custom_call_target="tpu_custom_call" | custom-call | flops 5368709120 | bytes 1048576 | tf_op jit(solution)/shard_map/pallas_call | solution.py:133
  54.7 1.3 %collective-permute-start.14 = (bf16[128,2048]{1,0:T(8,128)(2,1)S(1)}, bf16[128,2048]{1,0:T(8,128)(2,1)S(1)}, u32[]{:S(2)}, u32[]{:S(2)}) collective-permute-start(bf16[128,2048]{1,0:T(8,128)(2,1)S(1)} %collective-permute-done.10.refs_7_), channel_id=1, source_target_pairs={{4,0},{12,8},{20,16},{28,24},{5,1},{13,9},{21,17},{29,25},{6,2},{1... | collective-permute-start | bytes 1572872 | tf_op jit(solution)/shard_map/ppermute | solution.py:293
  56.0 0.1 collective-permute-start.19
  56.1 1.9 %collective-permute-start.2 = (s32[4,128]{1,0:T(4,128)S(1)}, s32[4,128]{1,0:T(4,128)S(1)}, u32[]{:S(2)}, u32[]{:S(2)}) collective-permute-start(s32[4,128]{1,0:T(4,128)S(1)} %bitcast.9), channel_id=1, source_target_pairs={{0,4},{4,8},{8,12},{12,16},{16,20},{20,24},{24,28},{1,5},{5,9},{9,... | collective-permute-start | bytes 6152 | tf_op jit(solution)/shard_map/ppermute | solution.py:293
  58.0 1.9 %collective-permute-start.3 = (s32[4,128]{1,0:T(4,128)S(1)}, s32[4,128]{1,0:T(4,128)S(1)}, u32[]{:S(2)}, u32[]{:S(2)}) collective-permute-start(s32[4,128]{1,0:T(4,128)S(1)} %bitcast.10), channel_id=1, source_target_pairs={{0,8},{4,12},{8,16},{12,20},{16,24},{20,28},{1,9},{5,13},{9,17},{1... | collective-permute-start | bytes 6152 | tf_op jit(solution)/shard_map/ppermute | solution.py:293
  60.0 1.9 %collective-permute-start.4 = (s32[4,128]{1,0:T(4,128)S(1)}, s32[4,128]{1,0:T(4,128)S(1)}, u32[]{:S(2)}, u32[]{:S(2)}) collective-permute-start(s32[4,128]{1,0:T(4,128)S(1)} %bitcast.11), channel_id=1, source_target_pairs={{0,12},{4,16},{8,20},{12,24},{16,28},{1,13},{5,17},{9,21},{13,25},... | collective-permute-start | bytes 6152 | tf_op jit(solution)/shard_map/ppermute | solution.py:293
  61.9 1.3 %collective-permute-start.5 = (s32[4,128]{1,0:T(4,128)S(1)}, s32[4,128]{1,0:T(4,128)S(1)}, u32[]{:S(2)}, u32[]{:S(2)}) collective-permute-start(s32[4,128]{1,0:T(4,128)S(1)} %bitcast.12), channel_id=1, source_target_pairs={{0,16},{4,20},{8,24},{12,28},{1,17},{5,21},{9,25},{13,29},{2,18},{... | collective-permute-start | bytes 6152 | tf_op jit(solution)/shard_map/ppermute | solution.py:293
  63.2 0.3 collective-permute-done.3.refs_1_
  63.5 0.5 collective-permute-start.16
  64.0 2.3 %collective-permute-done.4.refs_2_ = s32[4,128]{1,0:T(4,128)S(1)} collective-permute-done((s32[4,128]{1,0:T(4,128)S(1)}, s32[4,128]{1,0:T(4,128)S(1)}, u32[]{:S(2)}, u32[]{:S(2)}) %collective-permute-start.4) | collective-permute-done | bytes 2080 | tf_op jit(solution)/shard_map/ppermute | solution.py:293
  66.3 1.9 %collective-permute-start.17 = (bf16[128,2048]{1,0:T(8,128)(2,1)S(1)}, bf16[128,2048]{1,0:T(8,128)(2,1)S(1)}, u32[]{:S(2)}, u32[]{:S(2)}) collective-permute-start(bf16[128,2048]{1,0:T(8,128)(2,1)S(1)} %collective-permute-done.9.refs_5_), channel_id=1, source_target_pairs={{0,8},{4,12},{8,16},{12,20},{16,24},{20,28},{1,9},{5,13},{9,17},{1... | collective-permute-start | bytes 1572872 | tf_op jit(solution)/shard_map/ppermute | solution.py:293
  68.3 11.8 %shard_map.87 = (f32[16,512]{1,0:T(8,128)S(1)}, f32[1024,512]{1,0:T(8,128)S(1)}) custom-call(f32[4]{0:T(128)S(1)} %copy-done.7, f32[4]{0:T(128)S(1)} %collective-permute-done.1.s1, s32[4,128]{1,0:T(4,128)S(1)} %bitcast.13, s32[4,128]{1,0:T(4,128)S(1)} %collective-permute-done.2.refs_0_, s32[4,128]{1,0:T(4,128)S(1)} %collective-permute-done.3.refs_1_, ...), custom_call_target="tpu_custom_call" | custom-call | flops 4294967296 | bytes 1048576 | tf_op jit(solution)/shard_map/pallas_call | solution.py:235
  80.1 0.1 broadcast_select_fusion.refs_6_
  80.2 0.6 collective-permute-start.15
  80.8 0.6 collective-permute-done.17.refs_5_
  81.4 9.8 %shard_map.88 = (f32[16,512]{1,0:T(8,128)S(1)}, f32[1024,512]{1,0:T(8,128)S(1)}) custom-call(f32[4]{0:T(128)S(1)} %copy-done.7, f32[4]{0:T(128)S(1)} %collective-permute-done.1.s1, s32[4,128]{1,0:T(4,128)S(1)} %bitcast.14, s32[4,128]{1,0:T(4,128)S(1)} %collective-permute-done.2.refs_0_, s32[4,128]{1,0:T(4,128)S(1)} %collective-permute-done.3.refs_1_, ...), custom_call_target="tpu_custom_call" | custom-call | flops 3221225472 | bytes 1048576 | tf_op jit(solution)/shard_map/pallas_call | solution.py:235
  91.2 2.2 %collective-permute-done.15.refs_4_ = bf16[128,2048]{1,0:T(8,128)(2,1)S(1)} collective-permute-done((bf16[128,2048]{1,0:T(8,128)(2,1)S(1)}, bf16[128,2048]{1,0:T(8,128)(2,1)S(1)}, u32[]{:S(2)}, u32[]{:S(2)}) %collective-permute-start.15) | collective-permute-done | bytes 524320 | tf_op jit(solution)/shard_map/ppermute | solution.py:290
  93.4 6.7 %shard_map.89 = (bf16[1056,256]{1,0:T(8,128)(2,1)S(1)}, f32[8,256]{1,0:T(8,128)S(1)}, f32[1024,256]{1,0:T(8,128)S(1)}) custom-call(f32[4]{0:T(128)S(1)} %copy-done.7, f32[4]{0:T(128)S(1)} %collective-permute-done.1.s1, s32[4,128]{1,0:T(4,128)S(1)} %bitcast.15, s32[4,128]{1,0:T(4,128)S(1)} %collective-permute-done.2.refs_0_, ...), custom_call_target="tpu_custom_call" | custom-call | flops 1073741824 | bytes 1048576 | tf_op jit(solution)/shard_map/pallas_call | solution.py:235
  100.1 0.1 collective-permute-start.18
  100.2 1.9 %collective-permute-done.18.got_ref = bf16[1056,256]{1,0:T(8,128)(2,1)S(1)} collective-permute-done((bf16[1056,256]{1,0:T(8,128)(2,1)S(1)}, bf16[1056,256]{1,0:T(8,128)(2,1)S(1)}, u32[]{:S(2)}, u32[]{:S(2)}) %collective-permute-start.18) | collective-permute-done | bytes 540704 | tf_op jit(solution)/shard_map/ppermute | solution.py:287
  102.1 0.8 shard_map.91
  102.9 0.6 collective-permute-start.20
  103.5 0.8 shard_map.90
  104.3 12.6 %collective-permute-done.20 = bf16[128,2048]{1,0:T(8,128)(2,1)S(1)} collective-permute-done((bf16[128,2048]{1,0:T(8,128)(2,1)S(1)}, bf16[128,2048]{1,0:T(8,128)(2,1)S(1)}, u32[]{:S(2)}, u32[]{:S(2)}) %collective-permute-start.20) | collective-permute-done | bytes 524320 | tf_op jit(solution)/shard_map/ppermute | solution.py:290
  117.0 0.9 add_convert_fusion
  (20 shorter events, 0.0 us)
Async XLA Ops:
  0.6 39.4 %copy-start.7 = (f32[4]{0:T(128)S(1)}, f32[4]{0:T(128)}, u32[]{:S(2)}) copy-start(f32[4]{0:T(128)} %s0.7) | copy-start | bytes 52
  0.6 39.4 %copy-start.5 = (s32[512]{0:T(512)S(1)}, s32[512]{0:T(512)}, u32[]{:S(2)}) copy-start(s32[512]{0:T(512)} %param.11) | copy-start | bytes 6148
  0.7 39.3 %collective-permute-start.13 = (bf16[3,2048,512]{2,1,0:T(8,128)(2,1)}, bf16[3,2048,512]{2,1,0:T(8,128)(2,1)}, u32[]{:S(2)}, u32[]{:S(2)}) collective-permute-start(bf16[3,2048,512]{2,1,0:T(8,128)(2,1)} %bitcast.3), channel_id=1, source_target_pairs={{0,1},{1,0},{2,3},{3,2},{4,5},{5,4},{6,7},{7,6},{8,9},{9,8},{10,11... | collective-permute-start | bytes 18874376 | tf_op jit(solution)/shard_map/ppermute | solution.py:287
  0.7 1.0 copy-start.3
  1.8 0.7 copy-start.6
  2.9 16.2 %collective-permute-start.6 = (bf16[128,2048]{1,0:T(8,128)(2,1)S(1)}, bf16[128,2048]{1,0:T(8,128)(2,1)S(1)}, u32[]{:S(2)}, u32[]{:S(2)}) collective-permute-start(bf16[128,2048]{1,0:T(8,128)(2,1)S(1)} %shard_map.85.a), channel_id=1, source_target_pairs={{0,8},{4,12},{8,16},{12,20},{16,24},{20,28},{1,9},{5,13},{9,17},{1... | collective-permute-start | bytes 1572872 | tf_op jit(solution)/shard_map/ppermute | solution.py:293
  6.3 14.1 %collective-permute-start.11 = (bf16[128,2048]{1,0:T(8,128)(2,1)S(1)}, bf16[128,2048]{1,0:T(8,128)(2,1)S(1)}, u32[]{:S(2)}, u32[]{:S(2)}) collective-permute-start(bf16[128,2048]{1,0:T(8,128)(2,1)S(1)} %shard_map.85.a), channel_id=1, source_target_pairs={{0,2},{1,3},{2,0},{3,1},{4,6},{5,7},{6,4},{7,5},{8,10},{9,11},{10,... | collective-permute-start | bytes 1572872 | tf_op jit(solution)/shard_map/ppermute | solution.py:290
  7.9 12.6 %collective-permute-start = (bf16[128,2048]{1,0:T(8,128)(2,1)S(1)}, bf16[128,2048]{1,0:T(8,128)(2,1)S(1)}, u32[]{:S(2)}, u32[]{:S(2)}) collective-permute-start(bf16[128,2048]{1,0:T(8,128)(2,1)S(1)} %shard_map.85.a), channel_id=1, source_target_pairs={{0,1},{1,0},{2,3},{3,2},{4,5},{5,4},{6,7},{7,6},{8,9},{9,8},{10,11... | collective-permute-start | bytes 1572872 | tf_op jit(solution)/shard_map/ppermute | solution.py:287
  7.9 16.7 %collective-permute-start.8 = (bf16[128,2048]{1,0:T(8,128)(2,1)S(1)}, bf16[128,2048]{1,0:T(8,128)(2,1)}, u32[]{:S(2)}, u32[]{:S(2)}) collective-permute-start(bf16[128,2048]{1,0:T(8,128)(2,1)S(1)} %shard_map.85.a), channel_id=1, source_target_pairs={{0,4},{8,12},{16,20},{24,28},{1,5},{9,13},{17,21},{25,29},{2,6},{1... | collective-permute-start | bytes 1572872 | tf_op jit(solution)/shard_map/ppermute | solution.py:293
  19.1 16.3 %collective-permute-start.7 = (bf16[128,2048]{1,0:T(8,128)(2,1)S(1)}, bf16[128,2048]{1,0:T(8,128)(2,1)S(1)}, u32[]{:S(2)}, u32[]{:S(2)}) collective-permute-start(bf16[128,2048]{1,0:T(8,128)(2,1)S(1)} %collective-permute-done.6.refs_4_), channel_id=1, source_target_pairs={{0,4},{8,12},{16,20},{24,28},{4,0},{12,8},{20,16},{28,24},{1,5},{9... | collective-permute-start | bytes 1572872 | tf_op jit(solution)/shard_map/ppermute | solution.py:293
  20.5 19.5 %collective-permute-start.12 = (bf16[128,2048]{1,0:T(8,128)(2,1)S(1)}, bf16[128,2048]{1,0:T(8,128)(2,1)S(1)}, u32[]{:S(2)}, u32[]{:S(2)}) collective-permute-start(bf16[128,2048]{1,0:T(8,128)(2,1)S(1)} %collective-permute-done.11.b), channel_id=1, source_target_pairs={{0,1},{1,0},{2,3},{3,2},{4,5},{5,4},{6,7},{7,6},{8,9},{9,8},{10,11... | collective-permute-start | bytes 1572872 | tf_op jit(solution)/shard_map/ppermute | solution.py:287
  20.5 19.5 %collective-permute-start.1 = (f32[4]{0:T(128)}, f32[4]{0:T(128)S(1)}, u32[]{:S(2)}, u32[]{:S(2)}) collective-permute-start(f32[4]{0:T(128)} %s0.7), channel_id=1, source_target_pairs={{0,1},{1,0},{2,3},{3,2},{4,5},{5,4},{6,7},{7,6},{8,9},{9,8},{10,11... | collective-permute-start | bytes 56 | tf_op jit(solution)/shard_map/ppermute | solution.py:287
  24.6 30.1 %collective-permute-start.9 = (bf16[128,2048]{1,0:T(8,128)(2,1)S(1)}, bf16[128,2048]{1,0:T(8,128)(2,1)S(1)}, u32[]{:S(2)}, u32[]{:S(2)}) collective-permute-start(bf16[128,2048]{1,0:T(8,128)(2,1)S(1)} %collective-permute-done.6.refs_4_), channel_id=1, source_target_pairs={{0,2},{1,3},{2,0},{3,1},{4,6},{5,7},{6,4},{7,5},{8,10},{9,11},{10,... | collective-permute-start | bytes 1572872 | tf_op jit(solution)/shard_map/ppermute | solution.py:290
  35.4 19.3 %collective-permute-start.10 = (bf16[128,2048]{1,0:T(8,128)(2,1)S(1)}, bf16[128,2048]{1,0:T(8,128)(2,1)S(1)}, u32[]{:S(2)}, u32[]{:S(2)}) collective-permute-start(bf16[128,2048]{1,0:T(8,128)(2,1)S(1)} %collective-permute-done.6.refs_4_), channel_id=1, source_target_pairs={{0,8},{4,12},{8,16},{12,20},{16,24},{20,28},{1,9},{5,13},{9,17},{1... | collective-permute-start | bytes 1572872 | tf_op jit(solution)/shard_map/ppermute | solution.py:293
  40.0 2.8 %copy-start = (bf16[2048,3,512]{2,0,1:T(8,128)(2,1)S(1)}, bf16[2048,3,512]{2,0,1:T(8,128)(2,1)}, u32[]{:S(2)}) copy-start(bf16[2048,3,512]{2,0,1:T(8,128)(2,1)} %param.8) | copy-start | bytes 18874372
  42.8 13.2 %copy-start.2 = (bf16[512,2048]{1,0:T(8,128)(2,1)S(1)}, bf16[512,2048]{1,0:T(8,128)(2,1)}, u32[]{:S(2)}) copy-start(bf16[512,2048]{1,0:T(8,128)(2,1)} %w0.3) | copy-start | bytes 6291460
  42.8 25.5 %copy-start.1 = (bf16[2048,3,512]{2,0,1:T(8,128)(2,1)S(1)}, bf16[2048,3,512]{2,0,1:T(8,128)(2,1)}, u32[]{:S(2)}) copy-start(bf16[2048,3,512]{2,0,1:T(8,128)(2,1)} %param.8) | copy-start | bytes 18874372
  54.7 25.4 %collective-permute-start.14 = (bf16[128,2048]{1,0:T(8,128)(2,1)S(1)}, bf16[128,2048]{1,0:T(8,128)(2,1)S(1)}, u32[]{:S(2)}, u32[]{:S(2)}) collective-permute-start(bf16[128,2048]{1,0:T(8,128)(2,1)S(1)} %collective-permute-done.10.refs_7_), channel_id=1, source_target_pairs={{4,0},{12,8},{20,16},{28,24},{5,1},{13,9},{21,17},{29,25},{6,2},{1... | collective-permute-start | bytes 1572872 | tf_op jit(solution)/shard_map/ppermute | solution.py:293
  56.0 44.1 %collective-permute-start.19 = (bf16[512,2048]{1,0:T(8,128)(2,1)S(1)}, bf16[512,2048]{1,0:T(8,128)(2,1)S(1)}, u32[]{:S(2)}, u32[]{:S(2)}) collective-permute-start(bf16[512,2048]{1,0:T(8,128)(2,1)S(1)} %copy-done.2), channel_id=1, source_target_pairs={{0,1},{1,0},{2,3},{3,2},{4,5},{5,4},{6,7},{7,6},{8,9},{9,8},{10,11... | collective-permute-start | bytes 6291464 | tf_op jit(solution)/shard_map/ppermute | solution.py:287
  56.1 5.8 %collective-permute-start.2 = (s32[4,128]{1,0:T(4,128)S(1)}, s32[4,128]{1,0:T(4,128)S(1)}, u32[]{:S(2)}, u32[]{:S(2)}) collective-permute-start(s32[4,128]{1,0:T(4,128)S(1)} %bitcast.9), channel_id=1, source_target_pairs={{0,4},{4,8},{8,12},{12,16},{16,20},{20,24},{24,28},{1,5},{5,9},{9,... | collective-permute-start | bytes 6152 | tf_op jit(solution)/shard_map/ppermute | solution.py:293
  58.0 5.5 %collective-permute-start.3 = (s32[4,128]{1,0:T(4,128)S(1)}, s32[4,128]{1,0:T(4,128)S(1)}, u32[]{:S(2)}, u32[]{:S(2)}) collective-permute-start(s32[4,128]{1,0:T(4,128)S(1)} %bitcast.10), channel_id=1, source_target_pairs={{0,8},{4,12},{8,16},{12,20},{16,24},{20,28},{1,9},{5,13},{9,17},{1... | collective-permute-start | bytes 6152 | tf_op jit(solution)/shard_map/ppermute | solution.py:293
  60.0 6.4 %collective-permute-start.4 = (s32[4,128]{1,0:T(4,128)S(1)}, s32[4,128]{1,0:T(4,128)S(1)}, u32[]{:S(2)}, u32[]{:S(2)}) collective-permute-start(s32[4,128]{1,0:T(4,128)S(1)} %bitcast.11), channel_id=1, source_target_pairs={{0,12},{4,16},{8,20},{12,24},{16,28},{1,13},{5,17},{9,21},{13,25},... | collective-permute-start | bytes 6152 | tf_op jit(solution)/shard_map/ppermute | solution.py:293
  61.9 6.4 %collective-permute-start.5 = (s32[4,128]{1,0:T(4,128)S(1)}, s32[4,128]{1,0:T(4,128)S(1)}, u32[]{:S(2)}, u32[]{:S(2)}) collective-permute-start(s32[4,128]{1,0:T(4,128)S(1)} %bitcast.12), channel_id=1, source_target_pairs={{0,16},{4,20},{8,24},{12,28},{1,17},{5,21},{9,25},{13,29},{2,18},{... | collective-permute-start | bytes 6152 | tf_op jit(solution)/shard_map/ppermute | solution.py:293
  63.5 17.3 %collective-permute-start.16 = (bf16[128,2048]{1,0:T(8,128)(2,1)S(1)}, bf16[128,2048]{1,0:T(8,128)(2,1)S(1)}, u32[]{:S(2)}, u32[]{:S(2)}) collective-permute-start(bf16[128,2048]{1,0:T(8,128)(2,1)S(1)} %broadcast_select_fusion.1.refs_6_), channel_id=1, source_target_pairs={{0,2},{1,3},{2,0},{3,1},{4,6},{5,7},{6,4},{7,5},{8,10},{9,11},{10,... | collective-permute-start | bytes 1572872 | tf_op jit(solution)/shard_map/ppermute | solution.py:290
  66.3 15.0 %collective-permute-start.17 = (bf16[128,2048]{1,0:T(8,128)(2,1)S(1)}, bf16[128,2048]{1,0:T(8,128)(2,1)S(1)}, u32[]{:S(2)}, u32[]{:S(2)}) collective-permute-start(bf16[128,2048]{1,0:T(8,128)(2,1)S(1)} %collective-permute-done.9.refs_5_), channel_id=1, source_target_pairs={{0,8},{4,12},{8,16},{12,20},{16,24},{20,28},{1,9},{5,13},{9,17},{1... | collective-permute-start | bytes 1572872 | tf_op jit(solution)/shard_map/ppermute | solution.py:293
  80.2 13.2 %collective-permute-start.15 = (bf16[128,2048]{1,0:T(8,128)(2,1)S(1)}, bf16[128,2048]{1,0:T(8,128)(2,1)S(1)}, u32[]{:S(2)}, u32[]{:S(2)}) collective-permute-start(bf16[128,2048]{1,0:T(8,128)(2,1)S(1)} %broadcast_select_fusion.refs_6_), channel_id=1, source_target_pairs={{0,2},{1,3},{2,0},{3,1},{4,6},{5,7},{6,4},{7,5},{8,10},{9,11},{10,... | collective-permute-start | bytes 1572872 | tf_op jit(solution)/shard_map/ppermute | solution.py:290
  100.1 2.0 %collective-permute-start.18 = (bf16[1056,256]{1,0:T(8,128)(2,1)S(1)}, bf16[1056,256]{1,0:T(8,128)(2,1)S(1)}, u32[]{:S(2)}, u32[]{:S(2)}) collective-permute-start(bf16[1056,256]{1,0:T(8,128)(2,1)S(1)} %get-tuple-element.41), channel_id=1, source_target_pairs={{0,1},{1,0},{2,3},{3,2},{4,5},{5,4},{6,7},{7,6},{8,9},{9,8},{10,11... | collective-permute-start | bytes 1622024 | tf_op jit(solution)/shard_map/ppermute | solution.py:287
  102.1 1.4 %copy-start.4 = (bf16[128,2048]{1,0:T(8,128)(2,1)S(1)}, bf16[128,2048]{1,0:T(8,128)(2,1)}, u32[]{:S(2)}) copy-start(bf16[128,2048]{1,0:T(8,128)(2,1)} %refs_0_.1) | copy-start | bytes 1572868
  102.9 14.0 %collective-permute-start.20 = (bf16[128,2048]{1,0:T(8,128)(2,1)S(1)}, bf16[128,2048]{1,0:T(8,128)(2,1)S(1)}, u32[]{:S(2)}, u32[]{:S(2)}) collective-permute-start(bf16[128,2048]{1,0:T(8,128)(2,1)S(1)} %shard_map.91), channel_id=1, source_target_pairs={{0,2},{1,3},{2,0},{3,1},{4,6},{5,7},{6,4},{7,5},{8,10},{9,11},{10,... | collective-permute-start | bytes 1572872 | tf_op jit(solution)/shard_map/ppermute | solution.py:290

commit v3 on v2

--- a/solution.py
+++ b/solution.py
@@ -16,6 +16,7 @@
 BF16 = jnp.bfloat16
 F32 = jnp.float32
 SMEM = pl.BlockSpec(memory_space=pltpu.SMEM)
+ANY = pl.BlockSpec(memory_space=pl.ANY)
 VMEM = pl.BlockSpec(memory_space=pltpu.VMEM)
 
 
@@ -31,21 +32,58 @@
     return jnp.dot(lhs, rhs, preferred_element_type=F32)
 
 
-def layer_norm(tokens, ln_gain):
-    def body(tokens_ref, gain_ref, out_ref):
+def three_addends(value):
+    high = value.astype(BF16).astype(F32)
+    middle = (value - high).astype(BF16).astype(F32)
+    return high, middle, value - high - middle
+
+
+def layer_norm(tokens, ln_gain, slopes):
+    rows, model = tokens.shape
+
+    def body(slopes_ref, tokens_ref, gain_ref, out_ref, long_ref):
         inputs = tokens_ref[...].astype(F32)
         centred = inputs - jnp.mean(inputs, axis=-1, keepdims=True)
         variance = jnp.mean(centred * centred, axis=-1, keepdims=True)
-        out_ref[...] = (centred * lax.rsqrt(variance + EPSILON) * gain_ref[...]).astype(BF16)
+        normed = (centred * lax.rsqrt(variance + EPSILON) * gain_ref[...]).astype(BF16)
+        out_ref[...] = normed
+        long_ref[:rows, :] = normed
+        row = lax.broadcasted_iota(jnp.int32, (16, model), 0)
+        spread = jnp.zeros((16, model), F32)
+        for head in range(4):
+            spread = jnp.where(row % 4 == head, slopes_ref[head], spread)
+        high, middle, low = three_addends(spread)
+        part = jnp.where(row < 4, high, jnp.where(row < 8, middle, jnp.where(row < 12, low, 0.0)))
+        long_ref[pl.ds(rows, 16), :] = part.astype(BF16)
 
     return pl.pallas_call(
         body,
-        out_shape=jax.ShapeDtypeStruct(tokens.shape, BF16),
-        in_specs=[VMEM, VMEM],
-        out_specs=VMEM,
+        out_shape=(
+            jax.ShapeDtypeStruct((rows, model), BF16),
+            jax.ShapeDtypeStruct((rows + 16, model), BF16),
+        ),
+        in_specs=[SMEM, VMEM, VMEM],
+        out_specs=(VMEM, VMEM),
         compiler_params=params(8),
         cost_estimate=cost(0, 2 * tokens.size * 2, tokens.size),
-    )(tokens, ln_gain.reshape(1, -1))
+    )(slopes, tokens, ln_gain.reshape(1, -1))
+
+
+def stage(weights):
+    def body(source, out_ref, sem):
+        copy = pltpu.make_async_copy(source, out_ref, sem)
+        copy.start()
+        copy.wait()
+
+    return pl.pallas_call(
+        body,
+        out_shape=jax.ShapeDtypeStruct(weights.shape, weights.dtype),
+        in_specs=[ANY],
+        out_specs=VMEM,
+        scratch_shapes=[pltpu.SemaphoreType.DMA],
+        compiler_params=params(10),
+        cost_estimate=cost(0, 2 * weights.size * 2),
+    )(weights)
 
 
 def place_of(place):
@@ -87,11 +125,11 @@
 
 def attend(group, k_rows, v_t, q_ref, slopes_ref, mask_ref, dist_ref, before, stat_ref, acc_ref):
     heads = k_rows.shape[1] // HD
-    for local in range(heads):
-        head = group * heads + local
-        cols = slice(local * HD, (local + 1) * HD)
+    for head in range(heads):
+        cols = slice(head * HD, (head + 1) * HD)
         wide = pl.ds(head * HD, HD)
-        bias = dist_ref[...] * (slopes_ref[local] * LOG2E)
+        place = heads * group + head
+        bias = dist_ref[...] * (slopes_ref[place : place + 1, :] * LOG2E)
         bias = jnp.concatenate([bias] * (q_ref.shape[1] // PIECE), axis=1)
         scores = dot(k_rows[:, cols], q_ref[wide, :]) * (HD**-0.5 * LOG2E)
         scores = scores + bias + mask_ref[...]
@@ -103,90 +141,113 @@
         update = dot(v_t[cols, :], expo.astype(BF16))
         if before is not None:
             rescale = jnp.exp2(prev - row_max)
-            total = before[0][8 + head : 9 + head, :] * rescale + total
+            total = before[0][4 + head : 5 + head, :] * rescale + total
             update = before[1][wide, :] * rescale + update
         stat_ref[head : head + 1, :] = row_max
-        stat_ref[8 + head : 9 + head, :] = total
+        stat_ref[4 + head : 5 + head, :] = total
         acc_ref[wide, :] = update
 
 
-def own_block(slopes, slopes_pair, seg, pieces, w_own, w_pair):
+def state_shapes(width, block):
+    return (jax.ShapeDtypeStruct((8, block), F32), jax.ShapeDtypeStruct((width, block), F32))
+
+
+def load_weights(own, sources, held, sems):
+    copies = [pltpu.make_async_copy(source, held.at[i], sems.at[i]) for i, source in enumerate(sources)]
+    for copy in copies:
+        copy.start()
+
+    def ready(i):
+        if i < len(copies):
+            return own[i]
+        copies[i - len(copies)].wait()
+        return held[i - len(copies)]
+
+    return ready
+
+
+def own_block(slopes, seg, pieces, w_own, w_pair):
     depth, width = w_own.shape[1:]
     block = 4 * PIECE
 
-    def body(s0, s1, seg_ref, a, b, c, d, w0, w1, q, stat, acc, k_cache, v_cache, mask, dist):
+    def body(s0, seg_ref, a, b, c, d, w0, w1, q0, q1, stat0, acc0, stat1, acc1, k_cache, v_cache, slopes_out,
+             held, mask, dist, sems):
+        ready = load_weights(w0, [w1.at[part] for part in range(3)], held, sems)
         set_own_masks(seg_ref, mask, dist)
-        x = jnp.concatenate([a[...], b[...], c[...], d[...]], axis=0)
-        for group, w in enumerate((w0, w1)):
+        tail = c[PIECE : PIECE + 16, :PIECE].astype(F32)
+        for head in range(4):
+            slopes_out[head : head + 1, :] = jnp.full((1, PIECE), s0[head], F32)
+        slopes_out[4:8, :] = tail[0:4] + tail[4:8] + tail[8:12]
+        x = jnp.concatenate([a[...], b[...], c[:PIECE, :], d[...]], axis=0)
+        for group, (q, stat, acc) in enumerate(((q0, stat0, acc0), (q1, stat1, acc1))):
             rows = block if group == 0 else 2 * PIECE
-            q[pl.ds(group * width, width), :] = dot(x, w[0]).T.astype(BF16)
-            keys = dot(x[:rows], w[1]).astype(BF16)
-            values = dot(x[:rows], w[2])
+            q[...] = dot(x, ready(3 * group)).T.astype(BF16)
+            keys = dot(x[:rows], ready(3 * group + 1)).astype(BF16)
+            values = dot(x[:rows], ready(3 * group + 2))
             if group == 0:
                 for place in range(4):
                     to = pl.ds(pl.multiple_of(place_of(place) * PIECE, PIECE), PIECE)
                     k_cache[to, :] = keys[place * PIECE : (place + 1) * PIECE]
                     v_cache[to, :] = values[place * PIECE : (place + 1) * PIECE].astype(BF16)
             v_t = values[: 2 * PIECE].T.astype(BF16)
-            attend(group, keys[: 2 * PIECE], v_t, q, (s0, s1)[group], mask, dist, None, stat, acc)
+            attend(group, keys[: 2 * PIECE], v_t, q, slopes_out, mask, dist, None, stat, acc)
 
     return pl.pallas_call(
         body,
-        out_shape=(
-            jax.ShapeDtypeStruct((2 * width, block), BF16),
-            jax.ShapeDtypeStruct((16, block), F32),
-            jax.ShapeDtypeStruct((2 * width, block), F32),
+        out_shape=(jax.ShapeDtypeStruct((width, block), BF16),) * 2 + state_shapes(width, block) * 2 + (
             jax.ShapeDtypeStruct((block, width), BF16),
             jax.ShapeDtypeStruct((block, width), BF16),
+            jax.ShapeDtypeStruct((8, PIECE), F32),
         ),
-        in_specs=[SMEM, SMEM] + [VMEM] * 7,
-        out_specs=(VMEM,) * 5,
+        in_specs=[SMEM] + [VMEM] * 6 + [ANY],
+        out_specs=(VMEM,) * 9,
         scratch_shapes=[
+            pltpu.VMEM((3, depth, width), BF16),
             pltpu.VMEM((2 * PIECE, block), F32),
             pltpu.VMEM((2 * PIECE, PIECE), F32),
+            pltpu.SemaphoreType.DMA((3,)),
         ],
         compiler_params=params(26),
         cost_estimate=cost(5 * block * depth * width, 2**20, 0),
-    )(slopes, slopes_pair, seg, *pieces, w_own, w_pair)
-
-
-def write_closed(stat, acc, send_ref, lse_ref, out_ref):
-    wide, block = acc.shape
+    )(slopes, seg, *pieces, w_own, w_pair)
+
+
+def write_closed(states, send_ref, lse_ref, out_ref):
+    width, block = states[0][1].shape
     half = block // 2
-    total = stat[8:16, :]
-    some = total > 0.0
-    lse = jnp.where(some, stat[0:8, :] + jnp.log2(jnp.where(some, total, 1.0)), NEG_FILL)
-    scale = jnp.where(some, 1.0 / jnp.where(some, total, 1.0), 0.0)
-    lse_ref[...] = lse[:, :half]
-    for head in range(8):
-        rows = pl.ds(head * HD, HD)
-        normal = acc[rows, :] * scale[head : head + 1, :]
-        out_ref[rows, :] = normal[:, :half]
-        send_ref[rows, :] = normal[:, half:].astype(BF16)
-    rest = lse[:, half:]
-    high = rest.astype(BF16)
-    rest = rest - high.astype(F32)
-    middle = rest.astype(BF16)
-    low = (rest - middle.astype(F32)).astype(BF16)
-    parts = [part.astype(F32) for part in (high, middle, low)]
+    sent = []
+    for group, (stat, acc) in enumerate(states):
+        total = stat[4:8, :]
+        some = total > 0.0
+        lse = jnp.where(some, stat[0:4, :] + jnp.log2(jnp.where(some, total, 1.0)), NEG_FILL)
+        scale = jnp.where(some, 1.0 / jnp.where(some, total, 1.0), 0.0)
+        lse_ref[4 * group : 4 * group + 4, :] = lse[:, :half]
+        sent.append(lse[:, half:])
+        for head in range(4):
+            rows = pl.ds(head * HD, HD)
+            to = pl.ds(group * width + head * HD, HD)
+            normal = acc[rows, :] * scale[head : head + 1, :]
+            out_ref[to, :] = normal[:, :half]
+            send_ref[to, :] = normal[:, half:].astype(BF16)
+    parts = list(three_addends(jnp.concatenate(sent, axis=0)))
     parts.append(jnp.zeros_like(parts[0]))
-    send_ref[pl.ds(wide, 32), :] = jnp.concatenate(parts, axis=0).astype(BF16)
-
-
-def earlier_pieces(which, closing, slopes, slopes_pair, seg, segs, pieces, w_own, w_pair, q_t, stat_in, acc_in):
+    send_ref[pl.ds(2 * width, 32), :] = jnp.concatenate(parts, axis=0).astype(BF16)
+
+
+def earlier_pieces(which, closing, slopes8, seg, segs, pieces, w_own, w_pair, q_own, q_pair, state):
     depth, width = w_own.shape[1:]
     block = 4 * PIECE
     count = len(pieces)
     rows = count * PIECE
-    n_out = 3 if closing else 2
-
-    def body(s0, s1, seg_ref, *refs):
+    n_out = 3 if closing else 4
+
+    def body(slopes_ref, seg_ref, *refs):
         seg_refs, refs = refs[: len(segs)], refs[len(segs) :]
         sources, refs = refs[:count], refs[count:]
-        (w0, w1, q, stat_src, acc_src), refs = refs[:5], refs[5:]
-        outs, scratch = refs[:n_out], refs[n_out:]
-        mask, dist = scratch[:2]
-        stat, acc = scratch[2:] if closing else outs
+        (w0, w1, q0, q1), before, refs = refs[:4], (refs[4:6], refs[6:8]), refs[8:]
+        outs, (mask, dist, held, sems, *inner) = refs[:n_out], refs[n_out:]
+        after = inner if closing else outs
+        after = (after[0:2], after[2:4])
         block_num = lax.axis_index("seq")
         block_base = block_num * block
         same = jnp.zeros(seg_ref.shape, jnp.int32)
@@ -204,43 +265,46 @@
 
         @pl.when(live)
         def _():
+            ready = load_weights(w0.at[1:3], [w1.at[part] for part in (1, 2)], held, sems)
             set_earlier_masks(seg_ref, start, block_base, key_base, count, mask, dist)
             x = jnp.concatenate([source[...] for source in sources], axis=0)
-            for group, w in enumerate((w0, w1)):
-                keys = dot(x, w[1]).astype(BF16)
-                v_t = dot(x, w[2]).T.astype(BF16)
-                attend(group, keys, v_t, q, (s0, s1)[group], mask, dist, (stat_src, acc_src), stat, acc)
+            for group, q in enumerate((q0, q1)):
+                keys = dot(x, ready(2 * group)).astype(BF16)
+                v_t = dot(x, ready(2 * group + 1)).T.astype(BF16)
+                attend(group, keys, v_t, q, slopes_ref, mask, dist, before[group], *after[group])
 
         @pl.when(jnp.logical_not(live))
         def _():
-            stat[...] = stat_src[...]
-            acc[...] = acc_src[...]
+            for old, new in zip(before, after):
+                new[0][...] = old[0][...]
+                new[1][...] = old[1][...]
 
         if closing:
-            write_closed(stat, acc, *outs)
-
-    scratch = [pltpu.VMEM((rows, block), F32), pltpu.VMEM((rows, PIECE), F32)]
+            write_closed(after, *outs)
+
+    shapes = state_shapes(width, block) * 2
+    scratch = [
+        pltpu.VMEM((rows, block), F32),
+        pltpu.VMEM((rows, PIECE), F32),
+        pltpu.VMEM((2, depth, width), BF16),
+        pltpu.SemaphoreType.DMA((2,)),
+    ]
     if closing:
-        scratch += [pltpu.VMEM(stat_in.shape, F32), pltpu.VMEM(acc_in.shape, F32)]
-        out_shape = (
+        scratch += [pltpu.VMEM(shape.shape, F32) for shape in shapes]
+        shapes = (
             jax.ShapeDtypeStruct((2 * width + 32, block // 2), BF16),
             jax.ShapeDtypeStruct((8, block // 2), F32),
             jax.ShapeDtypeStruct((2 * width, block // 2), F32),
         )
-    else:
-        out_shape = (
-            jax.ShapeDtypeStruct(stat_in.shape, F32),
-            jax.ShapeDtypeStruct(acc_in.shape, F32),
-        )
     return pl.pallas_call(
         body,
-        out_shape=out_shape,
-        in_specs=[SMEM, SMEM] + [VMEM] * (6 + len(segs) + count),
+        out_shape=shapes,
+        in_specs=[VMEM] * (3 + len(segs) + count) + [ANY] + [VMEM] * 6,
         out_specs=(VMEM,) * n_out,
         scratch_shapes=scratch,
-        compiler_params=params(26),
+        compiler_params=params(24),
         cost_estimate=cost(4 * rows * depth * width, 2**20, 0),
-    )(slopes, slopes_pair, seg, *segs, *pieces, w_own, w_pair, q_t, stat_in, acc_in)
+    )(slopes8, seg, *segs, *pieces, w_own, w_pair, q_own, q_pair, *state)
 
 
 def project(place, lse, out, got, wo_own, wo_pair, tokens):
@@ -296,43 +360,53 @@
     even_to_odd = [(i, i + 1) for i in range(0, blocks, 2)]
     odd_to_even = [(i + 1, i) for i in range(0, blocks, 2)]
 
-    w_own = jnp.transpose(w_qkv, (1, 0, 2))
-    w_pair = over_core(w_own)
-    a0 = layer_norm(tokens, ln_gain)
+    tie = lax.optimization_barrier
+    w_all = jnp.transpose(w_qkv, (1, 0, 2))
+    seg = seg_ids.reshape(4, PIECE)
+    w_pair = over_core(w_all)
+    a0, a0_long = layer_norm(tokens, ln_gain, slopes)
+
+    def back(steps):
+        return [(i, i + steps) for i in range(blocks - steps)]
+
     a2 = over_seq(a0, two_on)
     b0 = over_x(a0)
     a1_odd = over_seq(a0, even_to_odd)
-    c0 = over_core(a0)
-    wo_tied, slopes_tied, seg, _ = lax.optimization_barrier(
-        (w_out, slopes, seg_ids.reshape(4, PIECE), c0))
-    slopes_pair = over_core(slopes_tied)
-    segs = [over_seq(seg, [(i, i + back) for i in range(blocks - back)]) for back in range(1, SPAN + 1)]
-    wo_pair = over_core(wo_tied)
-    d0 = over_core(b0)
-
+    c0 = over_core(a0_long)
+    seg_sent, w_staged, c0 = tie((seg, w_all, c0))
+    w_staged = stage(w_staged)
+    seg1 = over_seq(seg_sent, back(1))
+    seg4 = over_seq(seg_sent, back(SPAN))
+
+    a2, b0, a1_odd, w_pair, w_staged, seg1, seg4 = tie((a2, b0, a1_odd, w_pair, w_staged, seg1, seg4))
     a4 = over_seq(a2, two_on)
     b2 = over_x(a2)
     crossed = over_seq(a2, even_to_odd + odd_to_even)
+    d0 = over_core(b0)
+    seg23 = over_seq(jnp.concatenate([seg, seg1], axis=0), back(2))
+    segs = [seg1, seg23[:4], seg23[4:], seg4]
+    q_own, q_pair, *state, key_cache, value_cache, slopes8 = own_block(
+        slopes, seg, (a0, b0, c0, d0), w_staged, w_pair)
+
+    crossed, b2, a4, segs, state[0] = tie((crossed, b2, a4, segs, state[0]))
     a1 = jnp.where(odd, a1_odd, crossed)
-
-    def merge(closing, pieces, which, state):
-        return earlier_pieces(
-            which, closing, slopes, slopes_pair, seg, segs, pieces, w_own, w_pair, q_t, *state)
-
-    q_t, stat, acc, key_cache, value_cache = own_block(
-        slopes, slopes_pair, seg, (a0, b0, c0, d0), w_own, w_pair)
-    a1, b2, a4, stat = lax.optimization_barrier((a1, b2, a4, stat))
     b1 = over_x(a1)
     b4 = over_seq(b2, two_on)
     a3_even = over_seq(a4, odd_to_even)
+
+    def merge(closing, pieces, which, state):
+        return earlier_pieces(
+            which, closing, slopes8, seg, segs, pieces, w_staged, w_pair, q_own, q_pair, state)
+
+    state = merge(False, (a2, b2, a1, a4), ((2, 0), (2, 1), (1, 0), (4, 0)), state)
+
+    a3_even, b1, b4, wo_sent, held = tie((a3_even, b1, b4, w_out, state[0]))
+    state = (held, *state[1:])
     a3 = jnp.where(odd, crossed, a3_even)
-    state = merge(False, (a2, b2, a1, a4), ((2, 0), (2, 1), (1, 0), (4, 0)), (stat, acc))
-    a3, tied = lax.optimization_barrier((a3, state[0]))
     b3 = over_x(a3)
-    state = (tied, state[1])
+    wo_pair = over_core(wo_sent)
     state = merge(False, (b1, b4, a3), ((1, 1), (4, 1), (3, 0)), state)
-    state = merge(True, (b3,), ((3, 1),), state)
-    send, lse, out = state
+    send, lse, out = merge(True, (b3,), ((3, 1),), state)
     got = over_core(send)
     y_pair = project(1, lse, out, got, w_out, wo_pair, None)
     y_got = over_x(y_pair)

time: 118 us -> 111 us (0.941)
  waiting for transfers between devices: 44.6 us -> 28.2 us
  local copies, waits for them, and re-layouts: 4.53 us -> 16 us
  Pallas kernels: 42.2 us -> 31.3 us
  starting transfers between devices: 23.6 us -> 33.4 us
    ppermute x10 -> x9, waiting for transfers between devices: 27 us -> 7.29 us  [over_seq(): return lax.ppermute(value, 'seq', pairs)]
    unnamed x16 -> x28, local copies, waits for them, and re-layouts: 4.53 us -> 16 us
    pallas_call x5 -> x6, Pallas kernels: 40.5 us -> 29.7 us  [the longest x3 17.9 us: earlier_pieces(): pl.pallas_call(body, out_shape=shapes, in_specs=[VMEM] * (3 + len(segs) +...]
    ppermute x10 -> x9, starting transfers between devices: 19 us -> 23.3 us  [over_seq(): return lax.ppermute(value, 'seq', pairs)]
    ppermute x6 -> x5, starting transfers between devices: 0.73 us -> 4.26 us  [over_core(): return lax.ppermute(value, 'head', [(i, i ^ 1) for i in range(4)])]
    ppermute x5, waiting for transfers between devices: 15.7 us -> 18.6 us  [over_x(): return lax.ppermute(value, 'head', [(i, i ^ 2) for i in range(4)])]
    ppermute x5, starting transfers between devices: 3.79 us -> 5.81 us  [over_x(): return lax.ppermute(value, 'head', [(i, i ^ 2) for i in range(4)])]
  transfers between devices with their start and end apart: 21 -> 19, of which waited for: 10 -> 6; matrix products, arithmetic and copies ran while one was open for 1% -> 0% of each run, Pallas kernels for 35% -> 28%
where the time goes in v3:
time: 111 us
  starting transfers between devices  33.4 us (30%)
  Pallas kernels  31.3 us (28%)
  waiting for transfers between devices  28.2 us (25%)
  local copies, waits for them, and re-layouts  16 us (14%)
    ppermute x9, starting transfers between devices, over_seq(): return lax.ppermute(value, 'seq', pairs)  23.3 us
    ppermute x5, waiting for transfers between devices, over_x(): return lax.ppermute(value, 'head', [(i, i ^ 2) for i in range(4)])  18.6 us
    pallas_call x3, Pallas kernels, earlier_pieces(): pl.pallas_call(body, out_shape=shapes, in_specs=[VMEM] * (3 + len(segs) +...  17.9 us
    unnamed x28, local copies, waits for them, and re-layouts  16 us
    pallas_call x1, Pallas kernels, own_block(): pl.pallas_call(body, out_shape=(jax.ShapeDtypeStruct((width, block), BF16...  10.4 us
    ppermute x9, waiting for transfers between devices, over_seq(): return lax.ppermute(value, 'seq', pairs)  7.29 us
    ppermute x5, starting transfers between devices, over_x(): return lax.ppermute(value, 'head', [(i, i ^ 2) for i in range(4)])  5.81 us
    ppermute x5, starting transfers between devices, over_core(): return lax.ppermute(value, 'head', [(i, i ^ 1) for i in range(4)])  4.26 us
  transfers between devices with their start and end apart: 19, of which 6 were waited for; matrix products, arithmetic and copies ran while one was open for 0% of the time, Pallas kernels for 28%

profile of v3, /device:TPU:12, one launch (start us, length us, event | category | flops | bytes accessed | tf_op | source)
XLA Modules:
  0.0 111.0 jit_solution(8561332399863292324)
XLA Ops:
  0.6 0.1 collective-permute-start.3
  0.7 0.0 copy-start.8
  0.7 1.0 copy-done.8
  1.8 0.7 copy-done.11
  2.5 0.7 copy-done.12
  3.1 0.9 shard_map.85
  4.0 0.6 collective-permute-start.4
  4.6 3.5 %collective-permute-start = (bf16[128,2048]{1,0:T(8,128)(2,1)S(1)}, bf16[128,2048]{1,0:T(8,128)(2,1)S(1)}, u32[]{:S(2)}, u32[]{:S(2)}) collective-permute-start(bf16[128,2048]{1,0:T(8,128)(2,1)S(1)} %get-tuple-element.48.a), channel_id=1, source_target_pairs={{0,8},{4,12},{8,16},{12,20},{16,24},{20,28},{1,9},{5,13},{9,17},{1... | collective-permute-start | bytes 1572872 | tf_op jit(solution)/shard_map/ppermute | solution.py:357
  8.1 1.6 %collective-permute-start.1 = (bf16[128,2048]{1,0:T(8,128)(2,1)S(1)}, bf16[128,2048]{1,0:T(8,128)(2,1)S(1)}, u32[]{:S(2)}, u32[]{:S(2)}) collective-permute-start(bf16[128,2048]{1,0:T(8,128)(2,1)S(1)} %get-tuple-element.48.a), channel_id=1, source_target_pairs={{0,2},{1,3},{2,0},{3,1},{4,6},{5,7},{6,4},{7,5},{8,10},{9,11},{10,... | collective-permute-start | bytes 1572872 | tf_op jit(solution)/shard_map/ppermute | solution.py:354
  9.6 1.3 %collective-permute-start.2 = (bf16[128,2048]{1,0:T(8,128)(2,1)S(1)}, bf16[128,2048]{1,0:T(8,128)(2,1)S(1)}, u32[]{:S(2)}, u32[]{:S(2)}) collective-permute-start(bf16[128,2048]{1,0:T(8,128)(2,1)S(1)} %get-tuple-element.48.a), channel_id=1, source_target_pairs={{0,4},{8,12},{16,20},{24,28},{1,5},{9,13},{17,21},{25,29},{2,6},{1... | collective-permute-start | bytes 1572872 | tf_op jit(solution)/shard_map/ppermute | solution.py:357
  10.9 0.8 collective-permute-done.4.c
  11.7 4.8 %collective-permute-start.5 = (s32[4,128]{1,0:T(4,128)}, s32[4,128]{1,0:T(4,128)S(1)}, u32[]{:S(2)}, u32[]{:S(2)}) collective-permute-start(s32[4,128]{1,0:T(4,128)} %bitcast.5), channel_id=1, source_target_pairs={{0,4},{4,8},{8,12},{12,16},{16,20},{20,24},{24,28},{1,5},{5,9},{9,... | collective-permute-start | bytes 6152 | tf_op jit(solution)/shard_map/ppermute | solution.py:357
  16.5 3.8 %collective-permute-done.refs_4_ = bf16[128,2048]{1,0:T(8,128)(2,1)S(1)} collective-permute-done((bf16[128,2048]{1,0:T(8,128)(2,1)S(1)}, bf16[128,2048]{1,0:T(8,128)(2,1)S(1)}, u32[]{:S(2)}, u32[]{:S(2)}) %collective-permute-start) | collective-permute-done | bytes 524320 | tf_op jit(solution)/shard_map/ppermute | solution.py:357
  20.3 4.5 %collective-permute-start.6 = (s32[4,128]{1,0:T(4,128)}, s32[4,128]{1,0:T(4,128)S(1)}, u32[]{:S(2)}, u32[]{:S(2)}) collective-permute-start(s32[4,128]{1,0:T(4,128)} %bitcast.6), channel_id=1, source_target_pairs={{0,16},{4,20},{8,24},{12,28},{1,17},{5,21},{9,25},{13,29},{2,18},{... | collective-permute-start | bytes 6152 | tf_op jit(solution)/shard_map/ppermute | solution.py:357
  24.8 0.0 copy-start.7
  24.9 2.8 %copy-done.7 = bf16[2048,3,512]{2,0,1:T(8,128)(2,1)S(1)} copy-done((bf16[2048,3,512]{2,0,1:T(8,128)(2,1)S(1)}, bf16[2048,3,512]{2,0,1:T(8,128)(2,1)}, u32[]{:S(2)}) %copy-start.7) | copy-done | bytes 6291480
  27.6 0.4 shard_map.86.w0.refs_8_.refs_7_.refs_5_
  28.1 2.6 %copy-done = bf16[3,2048,512]{2,1,0:T(8,128)(2,1)} copy-done((bf16[3,2048,512]{2,1,0:T(8,128)(2,1)}, bf16[3,2048,512]{2,1,0:T(8,128)(2,1)S(1)}, u32[]{:S(2)}) %copy-start) | copy-done | bytes 6291480
  30.7 0.0 collective-permute-done.6.refs_3_
  30.7 0.0 collective-permute-done.3.w1.refs_9_.refs_8_.refs_6_
  30.7 2.6 %copy-done.3 = bf16[3,2048,512]{2,1,0:T(8,128)(2,1)} copy-done((bf16[3,2048,512]{2,1,0:T(8,128)(2,1)}, bf16[3,2048,512]{2,1,0:T(8,128)(2,1)S(1)}, u32[]{:S(2)}) %copy-start.3) | copy-done | bytes 6291480
  33.4 1.9 %collective-permute-start.11 = (s32[8,128]{1,0:T(8,128)S(1)}, s32[8,128]{1,0:T(8,128)S(1)}, u32[]{:S(2)}, u32[]{:S(2)}) collective-permute-start(s32[8,128]{1,0:T(8,128)S(1)} %pad_add_fusion), channel_id=1, source_target_pairs={{0,8},{4,12},{8,16},{12,20},{16,24},{20,28},{1,9},{5,13},{9,17},{1... | collective-permute-start | bytes 12296 | tf_op jit(solution)/shard_map/ppermute | solution.py:357
  35.3 1.9 %collective-permute-start.10 = (bf16[128,2048]{1,0:T(8,128)(2,1)S(1)}, bf16[128,2048]{1,0:T(8,128)(2,1)S(1)}, u32[]{:S(2)}, u32[]{:S(2)}) collective-permute-start(bf16[128,2048]{1,0:T(8,128)(2,1)S(1)} %collective-permute-done.refs_4_), channel_id=1, source_target_pairs={{0,8},{4,12},{8,16},{12,20},{16,24},{20,28},{1,9},{5,13},{9,17},{1... | collective-permute-start | bytes 1572872 | tf_op jit(solution)/shard_map/ppermute | solution.py:357
  37.2 0.6 collective-permute-start.8
  37.8 1.5 %collective-permute-start.9 = (bf16[128,2048]{1,0:T(8,128)(2,1)S(1)}, bf16[128,2048]{1,0:T(8,128)(2,1)S(1)}, u32[]{:S(2)}, u32[]{:S(2)}) collective-permute-start(bf16[128,2048]{1,0:T(8,128)(2,1)S(1)} %collective-permute-done.refs_4_), channel_id=1, source_target_pairs={{0,2},{1,3},{2,0},{3,1},{4,6},{5,7},{6,4},{7,5},{8,10},{9,11},{10,... | collective-permute-start | bytes 1572872 | tf_op jit(solution)/shard_map/ppermute | solution.py:354
  39.3 2.8 %copy-done.1 = bf16[3,2048,512]{2,1,0:T(8,128)(2,1)S(1)} copy-done((bf16[3,2048,512]{2,1,0:T(8,128)(2,1)S(1)}, bf16[3,2048,512]{2,1,0:T(8,128)(2,1)}, u32[]{:S(2)}) %copy-start.1) | copy-done | bytes 6291480
  42.1 2.8 %copy-done.4 = bf16[3,2048,512]{2,1,0:T(8,128)(2,1)S(1)} copy-done((bf16[3,2048,512]{2,1,0:T(8,128)(2,1)S(1)}, bf16[3,2048,512]{2,1,0:T(8,128)(2,1)}, u32[]{:S(2)}) %copy-start.4) | copy-done | bytes 6291480
  44.9 10.4 %shard_map.87 = (bf16[512,512]{1,0:T(8,128)(2,1)S(1)}, bf16[512,512]{1,0:T(8,128)(2,1)S(1)}, f32[8,512]{1,0:T(8,128)S(1)}, f32[512,512]{1,0:T(8,128)S(1)}, f32[8...) custom-call(f32[4]{0:T(128)S(1)} %copy-done.13, ...), custom_call_target="tpu_custom_call" | custom-call | flops 5368709120 | bytes 1048576 | tf_op jit(solution)/shard_map/pallas_call | solution.py:195
  55.3 0.1 broadcast_select_fusion.1.refs_6_
  55.4 1.1 %collective-permute-start.13 = (bf16[128,2048]{1,0:T(8,128)(2,1)S(1)}, bf16[128,2048]{1,0:T(8,128)(2,1)S(1)}, u32[]{:S(2)}, u32[]{:S(2)}) collective-permute-start(bf16[128,2048]{1,0:T(8,128)(2,1)S(1)} %broadcast_select_fusion.1.refs_6_), channel_id=1, source_target_pairs={{0,2},{1,3},{2,0},{3,1},{4,6},{5,7},{6,4},{7,5},{8,10},{9,11},{10,... | collective-permute-start | bytes 1572872 | tf_op jit(solution)/shard_map/ppermute | solution.py:354
  56.5 2.9 %collective-permute-start.12 = (bf16[128,2048]{1,0:T(8,128)(2,1)S(1)}, bf16[128,2048]{1,0:T(8,128)(2,1)S(1)}, u32[]{:S(2)}, u32[]{:S(2)}) collective-permute-start(bf16[128,2048]{1,0:T(8,128)(2,1)S(1)} %collective-permute-done.10.refs_7_), channel_id=1, source_target_pairs={{4,0},{12,8},{20,16},{28,24},{5,1},{13,9},{21,17},{29,25},{6,2},{1... | collective-permute-start | bytes 1572872 | tf_op jit(solution)/shard_map/ppermute | solution.py:357
  59.5 1.9 %collective-permute-start.14 = (bf16[128,2048]{1,0:T(8,128)(2,1)S(1)}, bf16[128,2048]{1,0:T(8,128)(2,1)S(1)}, u32[]{:S(2)}, u32[]{:S(2)}) collective-permute-start(bf16[128,2048]{1,0:T(8,128)(2,1)S(1)} %collective-permute-done.9.refs_5_), channel_id=1, source_target_pairs={{0,8},{4,12},{8,16},{12,20},{16,24},{20,28},{1,9},{5,13},{9,17},{1... | collective-permute-start | bytes 1572872 | tf_op jit(solution)/shard_map/ppermute | solution.py:357
  61.4 0.0 copy-start.6
  61.4 9.7 %shard_map.88 = (f32[8,512]{1,0:T(8,128)S(1)}, f32[512,512]{1,0:T(8,128)S(1)}, f32[8,512]{1,0:T(8,128)S(1)}, f32[512,512]{1,0:T(8,128)S(1)}) custom-call(f32[8,128]{1,0:T(8,128)S(1)} %get-tuple-element.56.slopes_ref, s32[4,128]{1,0:T(4,128)S(1)} %bitcast.9, s32[4,128]{1,0:T(4,128)S(1)} %collective-permute-done.5.refs_0_, ...), custom_call_target="tpu_custom_call" | custom-call | flops 4294967296 | bytes 1048576 | tf_op jit(solution)/shard_map/pallas_call | solution.py:299
  71.1 3.5 %collective-permute-done.14.refs_5_ = bf16[128,2048]{1,0:T(8,128)(2,1)S(1)} collective-permute-done((bf16[128,2048]{1,0:T(8,128)(2,1)S(1)}, bf16[128,2048]{1,0:T(8,128)(2,1)S(1)}, u32[]{:S(2)}, u32[]{:S(2)}) %collective-permute-start.14) | collective-permute-done | bytes 524320 | tf_op jit(solution)/shard_map/ppermute | solution.py:357
  74.6 0.1 broadcast_select_fusion.refs_6_
  74.7 1.6 %collective-permute-start.15 = (bf16[128,2048]{1,0:T(8,128)(2,1)S(1)}, bf16[128,2048]{1,0:T(8,128)(2,1)S(1)}, u32[]{:S(2)}, u32[]{:S(2)}) collective-permute-start(bf16[128,2048]{1,0:T(8,128)(2,1)S(1)} %broadcast_select_fusion.refs_6_), channel_id=1, source_target_pairs={{0,2},{1,3},{2,0},{3,1},{4,6},{5,7},{6,4},{7,5},{8,10},{9,11},{10,... | collective-permute-start | bytes 1572872 | tf_op jit(solution)/shard_map/ppermute | solution.py:354
  76.2 7.6 %shard_map.89 = (f32[8,512]{1,0:T(8,128)S(1)}, f32[512,512]{1,0:T(8,128)S(1)}, f32[8,512]{1,0:T(8,128)S(1)}, f32[512,512]{1,0:T(8,128)S(1)}) custom-call(f32[8,128]{1,0:T(8,128)S(1)} %get-tuple-element.56.slopes_ref, s32[4,128]{1,0:T(4,128)S(1)} %bitcast.10, s32[4,128]{1,0:T(4,128)S(1)} %collective-permute-done.5.refs_0_, ...), custom_call_target="tpu_custom_call" | custom-call | flops 3221225472 | bytes 1048576 | tf_op jit(solution)/shard_map/pallas_call | solution.py:299
  83.8 5.2 %collective-permute-done.15.refs_4_ = bf16[128,2048]{1,0:T(8,128)(2,1)S(1)} collective-permute-done((bf16[128,2048]{1,0:T(8,128)(2,1)S(1)}, bf16[128,2048]{1,0:T(8,128)(2,1)S(1)}, u32[]{:S(2)}, u32[]{:S(2)}) %collective-permute-start.15) | collective-permute-done | bytes 524320 | tf_op jit(solution)/shard_map/ppermute | solution.py:354
  89.1 0.7 shard_map.90
  89.8 0.0 copy-start.9
  89.8 3.6 %collective-permute-start.16 = (bf16[1056,256]{1,0:T(8,128)(2,1)S(1)}, bf16[1056,256]{1,0:T(8,128)(2,1)S(1)}, u32[]{:S(2)}, u32[]{:S(2)}) collective-permute-start(bf16[1056,256]{1,0:T(8,128)(2,1)S(1)} %get-tuple-element.89), channel_id=1, source_target_pairs={{0,1},{1,0},{2,3},{3,2},{4,5},{5,4},{6,7},{7,6},{8,9},{9,8},{10,11... | collective-permute-start | bytes 1622024 | tf_op jit(solution)/shard_map/ppermute | solution.py:351
  93.4 1.6 %collective-permute-done.16.got_ref = bf16[1056,256]{1,0:T(8,128)(2,1)S(1)} collective-permute-done((bf16[1056,256]{1,0:T(8,128)(2,1)S(1)}, bf16[1056,256]{1,0:T(8,128)(2,1)S(1)}, u32[]{:S(2)}, u32[]{:S(2)}) %collective-permute-start.16) | collective-permute-done | bytes 540704 | tf_op jit(solution)/shard_map/ppermute | solution.py:351
  95.0 0.8 shard_map.92
  95.8 0.1 collective-permute-start.18
  95.9 0.8 shard_map.91
  96.7 13.4 %collective-permute-done.18 = bf16[128,2048]{1,0:T(8,128)(2,1)S(1)} collective-permute-done((bf16[128,2048]{1,0:T(8,128)(2,1)S(1)}, bf16[128,2048]{1,0:T(8,128)(2,1)S(1)}, u32[]{:S(2)}, u32[]{:S(2)}) %collective-permute-start.18) | collective-permute-done | bytes 524320 | tf_op jit(solution)/shard_map/ppermute | solution.py:354
  110.0 0.9 add_convert_fusion
  (31 shorter events, 0.1 us)
Async XLA Ops:
  0.6 30.1 %collective-permute-start.3 = (bf16[3,2048,512]{2,1,0:T(8,128)(2,1)}, bf16[3,2048,512]{2,1,0:T(8,128)(2,1)S(1)}, u32[]{:S(2)}, u32[]{:S(2)}) collective-permute-start(bf16[3,2048,512]{2,1,0:T(8,128)(2,1)} %bitcast.3), channel_id=1, source_target_pairs={{0,1},{1,0},{2,3},{3,2},{4,5},{5,4},{6,7},{7,6},{8,9},{9,8},{10,11... | collective-permute-start | bytes 18874376 | tf_op jit(solution)/shard_map/ppermute | solution.py:351
  0.7 1.0 copy-start.8
  1.8 0.7 copy-start.11
  2.5 0.7 copy-start.12
  4.0 7.7 %collective-permute-start.4 = (bf16[144,2048]{1,0:T(8,128)(2,1)S(1)}, bf16[144,2048]{1,0:T(8,128)(2,1)S(1)}, u32[]{:S(2)}, u32[]{:S(2)}) collective-permute-start(bf16[144,2048]{1,0:T(8,128)(2,1)S(1)} %get-tuple-element.49), channel_id=1, source_target_pairs={{0,1},{1,0},{2,3},{3,2},{4,5},{5,4},{6,7},{7,6},{8,9},{9,8},{10,11... | collective-permute-start | bytes 1769480 | tf_op jit(solution)/shard_map/ppermute | solution.py:351
  4.6 15.8 %collective-permute-start = (bf16[128,2048]{1,0:T(8,128)(2,1)S(1)}, bf16[128,2048]{1,0:T(8,128)(2,1)S(1)}, u32[]{:S(2)}, u32[]{:S(2)}) collective-permute-start(bf16[128,2048]{1,0:T(8,128)(2,1)S(1)} %get-tuple-element.48.a), channel_id=1, source_target_pairs={{0,8},{4,12},{8,16},{12,20},{16,24},{20,28},{1,9},{5,13},{9,17},{1... | collective-permute-start | bytes 1572872 | tf_op jit(solution)/shard_map/ppermute | solution.py:357
  8.1 22.6 %collective-permute-start.1 = (bf16[128,2048]{1,0:T(8,128)(2,1)S(1)}, bf16[128,2048]{1,0:T(8,128)(2,1)S(1)}, u32[]{:S(2)}, u32[]{:S(2)}) collective-permute-start(bf16[128,2048]{1,0:T(8,128)(2,1)S(1)} %get-tuple-element.48.a), channel_id=1, source_target_pairs={{0,2},{1,3},{2,0},{3,1},{4,6},{5,7},{6,4},{7,5},{8,10},{9,11},{10,... | collective-permute-start | bytes 1572872 | tf_op jit(solution)/shard_map/ppermute | solution.py:354
  9.6 21.1 %collective-permute-start.2 = (bf16[128,2048]{1,0:T(8,128)(2,1)S(1)}, bf16[128,2048]{1,0:T(8,128)(2,1)S(1)}, u32[]{:S(2)}, u32[]{:S(2)}) collective-permute-start(bf16[128,2048]{1,0:T(8,128)(2,1)S(1)} %get-tuple-element.48.a), channel_id=1, source_target_pairs={{0,4},{8,12},{16,20},{24,28},{1,5},{9,13},{17,21},{25,29},{2,6},{1... | collective-permute-start | bytes 1572872 | tf_op jit(solution)/shard_map/ppermute | solution.py:357
  11.7 27.6 %copy-start.13 = (f32[4]{0:T(128)S(1)}, f32[4]{0:T(128)}, u32[]{:S(2)}) copy-start(f32[4]{0:T(128)} %s0.1) | copy-start | bytes 52
  11.7 19.0 %collective-permute-start.5 = (s32[4,128]{1,0:T(4,128)}, s32[4,128]{1,0:T(4,128)S(1)}, u32[]{:S(2)}, u32[]{:S(2)}) collective-permute-start(s32[4,128]{1,0:T(4,128)} %bitcast.5), channel_id=1, source_target_pairs={{0,4},{4,8},{8,12},{12,16},{16,20},{20,24},{24,28},{1,5},{5,9},{9,... | collective-permute-start | bytes 6152 | tf_op jit(solution)/shard_map/ppermute | solution.py:357
  20.3 10.4 %collective-permute-start.6 = (s32[4,128]{1,0:T(4,128)}, s32[4,128]{1,0:T(4,128)S(1)}, u32[]{:S(2)}, u32[]{:S(2)}) collective-permute-start(s32[4,128]{1,0:T(4,128)} %bitcast.6), channel_id=1, source_target_pairs={{0,16},{4,20},{8,24},{12,28},{1,17},{5,21},{9,25},{13,29},{2,18},{... | collective-permute-start | bytes 6152 | tf_op jit(solution)/shard_map/ppermute | solution.py:357
  24.8 2.8 %copy-start.7 = (bf16[2048,3,512]{2,0,1:T(8,128)(2,1)S(1)}, bf16[2048,3,512]{2,0,1:T(8,128)(2,1)}, u32[]{:S(2)}) copy-start(bf16[2048,3,512]{2,0,1:T(8,128)(2,1)} %param.8) | copy-start | bytes 18874372
  27.6 5.7 %copy-start.10 = (s32[512]{0:T(512)S(1)}, s32[512]{0:T(512)}, u32[]{:S(2)}) copy-start(s32[512]{0:T(512)} %param.11) | copy-start | bytes 6148
  28.1 2.6 %copy-start = (bf16[3,2048,512]{2,1,0:T(8,128)(2,1)}, bf16[3,2048,512]{2,1,0:T(8,128)(2,1)S(1)}, u32[]{:S(2)}) copy-start(bf16[3,2048,512]{2,1,0:T(8,128)(2,1)S(1)} %shard_map.86.w0.refs_8_.refs_7_.refs_5_) | copy-start | bytes 18874372
  30.7 2.6 %copy-start.3 = (bf16[3,2048,512]{2,1,0:T(8,128)(2,1)}, bf16[3,2048,512]{2,1,0:T(8,128)(2,1)S(1)}, u32[]{:S(2)}) copy-start(bf16[3,2048,512]{2,1,0:T(8,128)(2,1)S(1)} %collective-permute-done.3.w1.refs_9_.refs_8_.refs_6_) | copy-start | bytes 18874372
  33.3 5.9 %collective-permute-start.7 = (bf16[128,2048]{1,0:T(8,128)(2,1)S(1)}, bf16[128,2048]{1,0:T(8,128)(2,1)S(1)}, u32[]{:S(2)}, u32[]{:S(2)}) collective-permute-start(bf16[128,2048]{1,0:T(8,128)(2,1)S(1)} %collective-permute-done.1.b), channel_id=1, source_target_pairs={{0,1},{1,0},{2,3},{3,2},{4,5},{5,4},{6,7},{7,6},{8,9},{9,8},{10,11... | collective-permute-start | bytes 1572872 | tf_op jit(solution)/shard_map/ppermute | solution.py:351
  33.4 5.9 %collective-permute-start.11 = (s32[8,128]{1,0:T(8,128)S(1)}, s32[8,128]{1,0:T(8,128)S(1)}, u32[]{:S(2)}, u32[]{:S(2)}) collective-permute-start(s32[8,128]{1,0:T(8,128)S(1)} %pad_add_fusion), channel_id=1, source_target_pairs={{0,8},{4,12},{8,16},{12,20},{16,24},{20,28},{1,9},{5,13},{9,17},{1... | collective-permute-start | bytes 12296 | tf_op jit(solution)/shard_map/ppermute | solution.py:357
  35.3 20.0 %collective-permute-start.10 = (bf16[128,2048]{1,0:T(8,128)(2,1)S(1)}, bf16[128,2048]{1,0:T(8,128)(2,1)S(1)}, u32[]{:S(2)}, u32[]{:S(2)}) collective-permute-start(bf16[128,2048]{1,0:T(8,128)(2,1)S(1)} %collective-permute-done.refs_4_), channel_id=1, source_target_pairs={{0,8},{4,12},{8,16},{12,20},{16,24},{20,28},{1,9},{5,13},{9,17},{1... | collective-permute-start | bytes 1572872 | tf_op jit(solution)/shard_map/ppermute | solution.py:357
  37.2 18.1 %collective-permute-start.8 = (bf16[128,2048]{1,0:T(8,128)(2,1)S(1)}, bf16[128,2048]{1,0:T(8,128)(2,1)S(1)}, u32[]{:S(2)}, u32[]{:S(2)}) collective-permute-start(bf16[128,2048]{1,0:T(8,128)(2,1)S(1)} %collective-permute-done.refs_4_), channel_id=1, source_target_pairs={{0,4},{8,12},{16,20},{24,28},{4,0},{12,8},{20,16},{28,24},{1,5},{9... | collective-permute-start | bytes 1572872 | tf_op jit(solution)/shard_map/ppermute | solution.py:357
  37.8 17.5 %collective-permute-start.9 = (bf16[128,2048]{1,0:T(8,128)(2,1)S(1)}, bf16[128,2048]{1,0:T(8,128)(2,1)S(1)}, u32[]{:S(2)}, u32[]{:S(2)}) collective-permute-start(bf16[128,2048]{1,0:T(8,128)(2,1)S(1)} %collective-permute-done.refs_4_), channel_id=1, source_target_pairs={{0,2},{1,3},{2,0},{3,1},{4,6},{5,7},{6,4},{7,5},{8,10},{9,11},{10,... | collective-permute-start | bytes 1572872 | tf_op jit(solution)/shard_map/ppermute | solution.py:354
  39.3 2.8 %copy-start.1 = (bf16[3,2048,512]{2,1,0:T(8,128)(2,1)S(1)}, bf16[3,2048,512]{2,1,0:T(8,128)(2,1)}, u32[]{:S(2)}) copy-start(bf16[3,2048,512]{2,1,0:T(8,128)(2,1)} %copy-done) | copy-start | bytes 18874372
  42.1 2.8 %copy-start.4 = (bf16[3,2048,512]{2,1,0:T(8,128)(2,1)S(1)}, bf16[3,2048,512]{2,1,0:T(8,128)(2,1)}, u32[]{:S(2)}) copy-start(bf16[3,2048,512]{2,1,0:T(8,128)(2,1)} %copy-done.3) | copy-start | bytes 18874372
  44.9 16.5 %copy-start.2 = (bf16[3,2048,512]{2,1,0:T(8,128)(2,1)S(1)}, bf16[3,2048,512]{2,1,0:T(8,128)(2,1)}, u32[]{:S(2)}) copy-start(bf16[3,2048,512]{2,1,0:T(8,128)(2,1)} %copy-done) | copy-start | bytes 18874372
  44.9 16.6 %copy-start.5 = (bf16[3,2048,512]{2,1,0:T(8,128)(2,1)S(1)}, bf16[3,2048,512]{2,1,0:T(8,128)(2,1)}, u32[]{:S(2)}) copy-start(bf16[3,2048,512]{2,1,0:T(8,128)(2,1)} %copy-done.3) | copy-start | bytes 18874372
  55.4 15.7 %collective-permute-start.13 = (bf16[128,2048]{1,0:T(8,128)(2,1)S(1)}, bf16[128,2048]{1,0:T(8,128)(2,1)S(1)}, u32[]{:S(2)}, u32[]{:S(2)}) collective-permute-start(bf16[128,2048]{1,0:T(8,128)(2,1)S(1)} %broadcast_select_fusion.1.refs_6_), channel_id=1, source_target_pairs={{0,2},{1,3},{2,0},{3,1},{4,6},{5,7},{6,4},{7,5},{8,10},{9,11},{10,... | collective-permute-start | bytes 1572872 | tf_op jit(solution)/shard_map/ppermute | solution.py:354
  56.5 14.6 %collective-permute-start.12 = (bf16[128,2048]{1,0:T(8,128)(2,1)S(1)}, bf16[128,2048]{1,0:T(8,128)(2,1)S(1)}, u32[]{:S(2)}, u32[]{:S(2)}) collective-permute-start(bf16[128,2048]{1,0:T(8,128)(2,1)S(1)} %collective-permute-done.10.refs_7_), channel_id=1, source_target_pairs={{4,0},{12,8},{20,16},{28,24},{5,1},{13,9},{21,17},{29,25},{6,2},{1... | collective-permute-start | bytes 1572872 | tf_op jit(solution)/shard_map/ppermute | solution.py:357
  59.5 15.1 %collective-permute-start.14 = (bf16[128,2048]{1,0:T(8,128)(2,1)S(1)}, bf16[128,2048]{1,0:T(8,128)(2,1)S(1)}, u32[]{:S(2)}, u32[]{:S(2)}) collective-permute-start(bf16[128,2048]{1,0:T(8,128)(2,1)S(1)} %collective-permute-done.9.refs_5_), channel_id=1, source_target_pairs={{0,8},{4,12},{8,16},{12,20},{16,24},{20,28},{1,9},{5,13},{9,17},{1... | collective-permute-start | bytes 1572872 | tf_op jit(solution)/shard_map/ppermute | solution.py:357
  61.4 13.2 %copy-start.6 = (bf16[512,2048]{1,0:T(8,128)(2,1)S(1)}, bf16[512,2048]{1,0:T(8,128)(2,1)}, u32[]{:S(2)}) copy-start(bf16[512,2048]{1,0:T(8,128)(2,1)} %w0.3) | copy-start | bytes 6291460
  74.6 20.4 %collective-permute-start.17 = (bf16[512,2048]{1,0:T(8,128)(2,1)S(1)}, bf16[512,2048]{1,0:T(8,128)(2,1)S(1)}, u32[]{:S(2)}, u32[]{:S(2)}) collective-permute-start(bf16[512,2048]{1,0:T(8,128)(2,1)S(1)} %copy-done.6), channel_id=1, source_target_pairs={{0,1},{1,0},{2,3},{3,2},{4,5},{5,4},{6,7},{7,6},{8,9},{9,8},{10,11... | collective-permute-start | bytes 6291464 | tf_op jit(solution)/shard_map/ppermute | solution.py:351
  74.7 14.4 %collective-permute-start.15 = (bf16[128,2048]{1,0:T(8,128)(2,1)S(1)}, bf16[128,2048]{1,0:T(8,128)(2,1)S(1)}, u32[]{:S(2)}, u32[]{:S(2)}) collective-permute-start(bf16[128,2048]{1,0:T(8,128)(2,1)S(1)} %broadcast_select_fusion.refs_6_), channel_id=1, source_target_pairs={{0,2},{1,3},{2,0},{3,1},{4,6},{5,7},{6,4},{7,5},{8,10},{9,11},{10,... | collective-permute-start | bytes 1572872 | tf_op jit(solution)/shard_map/ppermute | solution.py:354
  89.8 6.1 %copy-start.9 = (bf16[128,2048]{1,0:T(8,128)(2,1)S(1)}, bf16[128,2048]{1,0:T(8,128)(2,1)}, u32[]{:S(2)}) copy-start(bf16[128,2048]{1,0:T(8,128)(2,1)} %refs_0_.1) | copy-start | bytes 1572868
  89.8 5.2 %collective-permute-start.16 = (bf16[1056,256]{1,0:T(8,128)(2,1)S(1)}, bf16[1056,256]{1,0:T(8,128)(2,1)S(1)}, u32[]{:S(2)}, u32[]{:S(2)}) collective-permute-start(bf16[1056,256]{1,0:T(8,128)(2,1)S(1)} %get-tuple-element.89), channel_id=1, source_target_pairs={{0,1},{1,0},{2,3},{3,2},{4,5},{5,4},{6,7},{7,6},{8,9},{9,8},{10,11... | collective-permute-start | bytes 1622024 | tf_op jit(solution)/shard_map/ppermute | solution.py:351
  95.8 14.3 %collective-permute-start.18 = (bf16[128,2048]{1,0:T(8,128)(2,1)S(1)}, bf16[128,2048]{1,0:T(8,128)(2,1)S(1)}, u32[]{:S(2)}, u32[]{:S(2)}) collective-permute-start(bf16[128,2048]{1,0:T(8,128)(2,1)S(1)} %shard_map.92), channel_id=1, source_target_pairs={{0,2},{1,3},{2,0},{3,1},{4,6},{5,7},{6,4},{7,5},{8,10},{9,11},{10,... | collective-permute-start | bytes 1572872 | tf_op jit(solution)/shard_map/ppermute | solution.py:354

commit v4 on v3

--- a/solution.py
+++ b/solution.py
@@ -11,12 +11,14 @@
 EPSILON = 1e-05
 NEG_FILL = -1e30
 MASKED = -2e38
+OWN_MIB = 14
+EARLIER_MIB = 14
 LOG2E = 1.4426950408889634
 
 BF16 = jnp.bfloat16
 F32 = jnp.float32
 SMEM = pl.BlockSpec(memory_space=pltpu.SMEM)
-ANY = pl.BlockSpec(memory_space=pl.ANY)
+HBM = pl.BlockSpec(memory_space=pltpu.HBM)
 VMEM = pl.BlockSpec(memory_space=pltpu.VMEM)
 
 
@@ -41,7 +43,13 @@
 def layer_norm(tokens, ln_gain, slopes):
     rows, model = tokens.shape
 
-    def body(slopes_ref, tokens_ref, gain_ref, out_ref, long_ref):
+    def body(slopes_ref, tokens_hbm, gain_hbm, out_ref, long_ref, tokens_ref, gain_ref, sems):
+        loads = [pltpu.make_async_copy(tokens_hbm, tokens_ref, sems.at[0]),
+                 pltpu.make_async_copy(gain_hbm, gain_ref, sems.at[1])]
+        for copy in loads:
+            copy.start()
+        for copy in loads:
+            copy.wait()
         inputs = tokens_ref[...].astype(F32)
         centred = inputs - jnp.mean(inputs, axis=-1, keepdims=True)
         variance = jnp.mean(centred * centred, axis=-1, keepdims=True)
@@ -62,8 +70,13 @@
             jax.ShapeDtypeStruct((rows, model), BF16),
             jax.ShapeDtypeStruct((rows + 16, model), BF16),
         ),
-        in_specs=[SMEM, VMEM, VMEM],
+        in_specs=[SMEM, HBM, HBM],
         out_specs=(VMEM, VMEM),
+        scratch_shapes=[
+            pltpu.VMEM((rows, model), BF16),
+            pltpu.VMEM((1, model), F32),
+            pltpu.SemaphoreType.DMA((2,)),
+        ],
         compiler_params=params(8),
         cost_estimate=cost(0, 2 * tokens.size * 2, tokens.size),
     )(slopes, tokens, ln_gain.reshape(1, -1))
@@ -78,10 +91,10 @@
     return pl.pallas_call(
         body,
         out_shape=jax.ShapeDtypeStruct(weights.shape, weights.dtype),
-        in_specs=[ANY],
+        in_specs=[HBM],
         out_specs=VMEM,
         scratch_shapes=[pltpu.SemaphoreType.DMA],
-        compiler_params=params(10),
+        compiler_params=params(8),
         cost_estimate=cost(0, 2 * weights.size * 2),
     )(weights)
 
@@ -152,38 +165,23 @@
     return (jax.ShapeDtypeStruct((8, block), F32), jax.ShapeDtypeStruct((width, block), F32))
 
 
-def load_weights(own, sources, held, sems):
-    copies = [pltpu.make_async_copy(source, held.at[i], sems.at[i]) for i, source in enumerate(sources)]
-    for copy in copies:
-        copy.start()
-
-    def ready(i):
-        if i < len(copies):
-            return own[i]
-        copies[i - len(copies)].wait()
-        return held[i - len(copies)]
-
-    return ready
-
-
 def own_block(slopes, seg, pieces, w_own, w_pair):
     depth, width = w_own.shape[1:]
     block = 4 * PIECE
 
     def body(s0, seg_ref, a, b, c, d, w0, w1, q0, q1, stat0, acc0, stat1, acc1, k_cache, v_cache, slopes_out,
-             held, mask, dist, sems):
-        ready = load_weights(w0, [w1.at[part] for part in range(3)], held, sems)
+             mask, dist):
         set_own_masks(seg_ref, mask, dist)
         tail = c[PIECE : PIECE + 16, :PIECE].astype(F32)
         for head in range(4):
             slopes_out[head : head + 1, :] = jnp.full((1, PIECE), s0[head], F32)
         slopes_out[4:8, :] = tail[0:4] + tail[4:8] + tail[8:12]
         x = jnp.concatenate([a[...], b[...], c[:PIECE, :], d[...]], axis=0)
-        for group, (q, stat, acc) in enumerate(((q0, stat0, acc0), (q1, stat1, acc1))):
+        for group, (w, q, stat, acc) in enumerate(((w0, q0, stat0, acc0), (w1, q1, stat1, acc1))):
             rows = block if group == 0 else 2 * PIECE
-            q[...] = dot(x, ready(3 * group)).T.astype(BF16)
-            keys = dot(x[:rows], ready(3 * group + 1)).astype(BF16)
-            values = dot(x[:rows], ready(3 * group + 2))
+            q[...] = dot(x, w[0]).T.astype(BF16)
+            keys = dot(x[:rows], w[1]).astype(BF16)
+            values = dot(x[:rows], w[2])
             if group == 0:
                 for place in range(4):
                     to = pl.ds(pl.multiple_of(place_of(place) * PIECE, PIECE), PIECE)
@@ -199,15 +197,13 @@
             jax.ShapeDtypeStruct((block, width), BF16),
             jax.ShapeDtypeStruct((8, PIECE), F32),
         ),
-        in_specs=[SMEM] + [VMEM] * 6 + [ANY],
+        in_specs=[SMEM] + [VMEM] * 7,
         out_specs=(VMEM,) * 9,
         scratch_shapes=[
-            pltpu.VMEM((3, depth, width), BF16),
             pltpu.VMEM((2 * PIECE, block), F32),
             pltpu.VMEM((2 * PIECE, PIECE), F32),
-            pltpu.SemaphoreType.DMA((3,)),
         ],
-        compiler_params=params(26),
+        compiler_params=params(OWN_MIB),
         cost_estimate=cost(5 * block * depth * width, 2**20, 0),
     )(slopes, seg, *pieces, w_own, w_pair)
 
@@ -245,7 +241,7 @@
         seg_refs, refs = refs[: len(segs)], refs[len(segs) :]
         sources, refs = refs[:count], refs[count:]
         (w0, w1, q0, q1), before, refs = refs[:4], (refs[4:6], refs[6:8]), refs[8:]
-        outs, (mask, dist, held, sems, *inner) = refs[:n_out], refs[n_out:]
+        outs, (mask, dist, *inner) = refs[:n_out], refs[n_out:]
         after = inner if closing else outs
         after = (after[0:2], after[2:4])
         block_num = lax.axis_index("seq")
@@ -265,12 +261,11 @@
 
         @pl.when(live)
         def _():
-            ready = load_weights(w0.at[1:3], [w1.at[part] for part in (1, 2)], held, sems)
             set_earlier_masks(seg_ref, start, block_base, key_base, count, mask, dist)
             x = jnp.concatenate([source[...] for source in sources], axis=0)
-            for group, q in enumerate((q0, q1)):
-                keys = dot(x, ready(2 * group)).astype(BF16)
-                v_t = dot(x, ready(2 * group + 1)).T.astype(BF16)
+            for group, (w, q) in enumerate(((w0, q0), (w1, q1))):
+                keys = dot(x, w[1]).astype(BF16)
+                v_t = dot(x, w[2]).T.astype(BF16)
                 attend(group, keys, v_t, q, slopes_ref, mask, dist, before[group], *after[group])
 
         @pl.when(jnp.logical_not(live))
@@ -286,8 +281,6 @@
     scratch = [
         pltpu.VMEM((rows, block), F32),
         pltpu.VMEM((rows, PIECE), F32),
-        pltpu.VMEM((2, depth, width), BF16),
-        pltpu.SemaphoreType.DMA((2,)),
     ]
     if closing:
         scratch += [pltpu.VMEM(shape.shape, F32) for shape in shapes]
@@ -299,10 +292,10 @@
     return pl.pallas_call(
         body,
         out_shape=shapes,
-        in_specs=[VMEM] * (3 + len(segs) + count) + [ANY] + [VMEM] * 6,
+        in_specs=[VMEM] * (10 + len(segs) + count),
         out_specs=(VMEM,) * n_out,
         scratch_shapes=scratch,
-        compiler_params=params(24),
+        compiler_params=params(EARLIER_MIB),
         cost_estimate=cost(4 * rows * depth * width, 2**20, 0),
     )(slopes8, seg, *segs, *pieces, w_own, w_pair, q_own, q_pair, *state)
 
@@ -366,25 +359,21 @@
     w_pair = over_core(w_all)
     a0, a0_long = layer_norm(tokens, ln_gain, slopes)
 
-    def back(steps):
-        return [(i, i + steps) for i in range(blocks - steps)]
-
     a2 = over_seq(a0, two_on)
     b0 = over_x(a0)
     a1_odd = over_seq(a0, even_to_odd)
     c0 = over_core(a0_long)
     seg_sent, w_staged, c0 = tie((seg, w_all, c0))
     w_staged = stage(w_staged)
-    seg1 = over_seq(seg_sent, back(1))
-    seg4 = over_seq(seg_sent, back(SPAN))
-
-    a2, b0, a1_odd, w_pair, w_staged, seg1, seg4 = tie((a2, b0, a1_odd, w_pair, w_staged, seg1, seg4))
+    seg1 = over_seq(seg_sent, [(i, i + 1) for i in range(blocks - 1)])
+
+    a2, b0, a1_odd, w_pair, w_staged, seg1 = tie((a2, b0, a1_odd, w_pair, w_staged, seg1))
     a4 = over_seq(a2, two_on)
     b2 = over_x(a2)
     crossed = over_seq(a2, even_to_odd + odd_to_even)
     d0 = over_core(b0)
-    seg23 = over_seq(jnp.concatenate([seg, seg1], axis=0), back(2))
-    segs = [seg1, seg23[:4], seg23[4:], seg4]
+    seg23 = over_seq(jnp.concatenate([seg, seg1], axis=0), two_on)
+    segs = [seg1, seg23[:4], seg23[4:]]
     q_own, q_pair, *state, key_cache, value_cache, slopes8 = own_block(
         slopes, seg, (a0, b0, c0, d0), w_staged, w_pair)
 
@@ -393,20 +382,22 @@
     b1 = over_x(a1)
     b4 = over_seq(b2, two_on)
     a3_even = over_seq(a4, odd_to_even)
-
-    def merge(closing, pieces, which, state):
+    seg4 = over_seq(segs[1], two_on)
+
+    def merge(closing, segs, pieces, which, state):
         return earlier_pieces(
             which, closing, slopes8, seg, segs, pieces, w_staged, w_pair, q_own, q_pair, state)
 
-    state = merge(False, (a2, b2, a1, a4), ((2, 0), (2, 1), (1, 0), (4, 0)), state)
-
-    a3_even, b1, b4, wo_sent, held = tie((a3_even, b1, b4, w_out, state[0]))
+    state = merge(False, segs, (a2, b2, a1), ((2, 0), (2, 1), (1, 0)), state)
+
+    a3_even, b1, b4, seg4, wo_sent, held = tie((a3_even, b1, b4, seg4, w_out, state[0]))
+    segs = [*segs, seg4]
     state = (held, *state[1:])
     a3 = jnp.where(odd, crossed, a3_even)
     b3 = over_x(a3)
     wo_pair = over_core(wo_sent)
-    state = merge(False, (b1, b4, a3), ((1, 1), (4, 1), (3, 0)), state)
-    send, lse, out = merge(True, (b3,), ((3, 1),), state)
+    state = merge(False, segs, (b1, a4, b4, a3), ((1, 1), (4, 0), (4, 1), (3, 0)), state)
+    send, lse, out = merge(True, segs, (b3,), ((3, 1),), state)
     got = over_core(send)
     y_pair = project(1, lse, out, got, w_out, wo_pair, None)
     y_got = over_x(y_pair)

time: 111 us -> 104 us (0.937); the launches traced: 111 us -> 102 us
  starting transfers between devices: 33.4 us -> 28.5 us
  Pallas kernels: 31.3 us -> 29.1 us
  waiting for transfers between devices: 28.2 us -> 26.3 us
    ppermute x5, starting transfers between devices: 4.26 us -> 0.77 us  [over_core(): return lax.ppermute(value, 'head', [(i, i ^ 1) for i in range(4)])]
    pallas_call x3, Pallas kernels: 17.9 us -> 16.6 us  [earlier_pieces(): pl.pallas_call(body, out_shape=shapes, in_specs=[VMEM] * (10 + len(segs)...]
    ppermute x5, waiting for transfers between devices: 18.6 us -> 17.4 us  [over_x(): return lax.ppermute(value, 'head', [(i, i ^ 2) for i in range(4)])]
where the time goes in v4:
time: 104 us; the launch traced here: 102 us
  Pallas kernels  29.1 us (28%)
  starting transfers between devices  28.5 us (27%)
  waiting for transfers between devices  26.3 us (25%)
  local copies, waits for them, and re-layouts  16 us (15%)
  other arithmetic  1.08 us (1%)
    ppermute x9, starting transfers between devices, over_seq(): return lax.ppermute(value, 'seq', pairs)  22.8 us
    ppermute x5, waiting for transfers between devices, over_x(): return lax.ppermute(value, 'head', [(i, i ^ 2) for i in range(4)])  17.4 us
    pallas_call x3, Pallas kernels, earlier_pieces(): pl.pallas_call(body, out_shape=shapes, in_specs=[VMEM] * (10 + len(segs)...  16.6 us
    unnamed x28, local copies, waits for them, and re-layouts  16 us
    pallas_call x1, Pallas kernels, own_block(): pl.pallas_call(body, out_shape=(jax.ShapeDtypeStruct((width, block), BF16...  9.45 us
    ppermute x9, waiting for transfers between devices, over_seq(): return lax.ppermute(value, 'seq', pairs)  6.28 us
    ppermute x5, starting transfers between devices, over_x(): return lax.ppermute(value, 'head', [(i, i ^ 2) for i in range(4)])  4.89 us
    ppermute x5, waiting for transfers between devices, over_core(): return lax.ppermute(value, 'head', [(i, i ^ 1) for i in range(4)])  2.67 us
  transfers between devices with their start and end apart: 19, of which 6 were waited for; matrix products, arithmetic and copies ran while one was open for 0% of the time, Pallas kernels for 28%

profile of v4, /device:TPU:12, one launch (start us, length us, event | category | flops | bytes accessed | tf_op | source)
XLA Modules:
  0.0 101.9 jit_solution(5889883811112767950)
XLA Ops:
  0.6 0.1 collective-permute-start.3
  0.7 0.0 copy-start.8
  0.7 1.0 %copy-done.8 = bf16[128,2048]{1,0:T(8,128)(2,1)S(1)} copy-done((bf16[128,2048]{1,0:T(8,128)(2,1)S(1)}, bf16[128,2048]{1,0:T(8,128)(2,1)}, u32[]{:S(2)}) %copy-start.8) | copy-done | bytes 524312
  1.8 0.7 copy-done.11
  2.5 0.7 copy-done.12
  3.1 1.0 shard_map.85
  4.1 0.6 collective-permute-start.4
  4.6 3.5 %collective-permute-start = (bf16[128,2048]{1,0:T(8,128)(2,1)S(1)}, bf16[128,2048]{1,0:T(8,128)(2,1)S(1)}, u32[]{:S(2)}, u32[]{:S(2)}) collective-permute-start(bf16[128,2048]{1,0:T(8,128)(2,1)S(1)} %get-tuple-element.47.a), channel_id=1, source_target_pairs={{0,8},{4,12},{8,16},{12,20},{16,24},{20,28},{1,9},{5,13},{9,17},{1... | collective-permute-start | bytes 1572872 | tf_op jit(solution)/shard_map/ppermute | solution.py:350
  8.1 1.6 %collective-permute-start.1 = (bf16[128,2048]{1,0:T(8,128)(2,1)S(1)}, bf16[128,2048]{1,0:T(8,128)(2,1)S(1)}, u32[]{:S(2)}, u32[]{:S(2)}) collective-permute-start(bf16[128,2048]{1,0:T(8,128)(2,1)S(1)} %get-tuple-element.47.a), channel_id=1, source_target_pairs={{0,2},{1,3},{2,0},{3,1},{4,6},{5,7},{6,4},{7,5},{8,10},{9,11},{10,... | collective-permute-start | bytes 1572872 | tf_op jit(solution)/shard_map/ppermute | solution.py:347
  9.7 1.3 %collective-permute-start.2 = (bf16[128,2048]{1,0:T(8,128)(2,1)S(1)}, bf16[128,2048]{1,0:T(8,128)(2,1)S(1)}, u32[]{:S(2)}, u32[]{:S(2)}) collective-permute-start(bf16[128,2048]{1,0:T(8,128)(2,1)S(1)} %get-tuple-element.47.a), channel_id=1, source_target_pairs={{0,4},{8,12},{16,20},{24,28},{1,5},{9,13},{17,21},{25,29},{2,6},{1... | collective-permute-start | bytes 1572872 | tf_op jit(solution)/shard_map/ppermute | solution.py:350
  11.0 0.7 collective-permute-done.4.c
  11.7 4.9 %collective-permute-start.5 = (s32[4,128]{1,0:T(4,128)}, s32[4,128]{1,0:T(4,128)S(1)}, u32[]{:S(2)}, u32[]{:S(2)}) collective-permute-start(s32[4,128]{1,0:T(4,128)} %bitcast.5), channel_id=1, source_target_pairs={{0,4},{4,8},{8,12},{12,16},{16,20},{20,24},{24,28},{1,5},{5,9},{9,... | collective-permute-start | bytes 6152 | tf_op jit(solution)/shard_map/ppermute | solution.py:350
  16.6 0.0 copy-start.7
  16.6 2.8 %copy-done.7 = bf16[2048,3,512]{2,0,1:T(8,128)(2,1)S(1)} copy-done((bf16[2048,3,512]{2,0,1:T(8,128)(2,1)S(1)}, bf16[2048,3,512]{2,0,1:T(8,128)(2,1)}, u32[]{:S(2)}) %copy-start.7) | copy-done | bytes 6291480
  19.4 0.4 shard_map.86.w0.refs_6_.refs_8_.refs_5_
  19.8 2.6 %copy-done = bf16[3,2048,512]{2,1,0:T(8,128)(2,1)} copy-done((bf16[3,2048,512]{2,1,0:T(8,128)(2,1)}, bf16[3,2048,512]{2,1,0:T(8,128)(2,1)S(1)}, u32[]{:S(2)}) %copy-start) | copy-done | bytes 6291480
  22.4 2.4 %collective-permute-done.2 = bf16[128,2048]{1,0:T(8,128)(2,1)S(1)} collective-permute-done((bf16[128,2048]{1,0:T(8,128)(2,1)S(1)}, bf16[128,2048]{1,0:T(8,128)(2,1)S(1)}, u32[]{:S(2)}, u32[]{:S(2)}) %collective-permute-start.2) | collective-permute-done | bytes 524320 | tf_op jit(solution)/shard_map/ppermute | solution.py:350
  24.9 0.0 collective-permute-done.5.refs_0_
  24.9 2.6 %copy-done.3 = bf16[3,2048,512]{2,1,0:T(8,128)(2,1)} copy-done((bf16[3,2048,512]{2,1,0:T(8,128)(2,1)}, bf16[3,2048,512]{2,1,0:T(8,128)(2,1)S(1)}, u32[]{:S(2)}) %copy-start.3) | copy-done | bytes 6291480
  27.5 3.5 %collective-permute-start.10 = (s32[8,128]{1,0:T(8,128)S(1)}, s32[8,128]{1,0:T(8,128)S(1)}, u32[]{:S(2)}, u32[]{:S(2)}) collective-permute-start(s32[8,128]{1,0:T(8,128)S(1)} %pad_add_fusion), channel_id=1, source_target_pairs={{0,8},{4,12},{8,16},{12,20},{16,24},{20,28},{1,9},{5,13},{9,17},{1... | collective-permute-start | bytes 12296 | tf_op jit(solution)/shard_map/ppermute | solution.py:350
  31.0 0.1 collective-permute-start.7
  31.1 0.6 collective-permute-start.8
  31.7 1.9 %collective-permute-start.9 = (bf16[128,2048]{1,0:T(8,128)(2,1)S(1)}, bf16[128,2048]{1,0:T(8,128)(2,1)S(1)}, u32[]{:S(2)}, u32[]{:S(2)}) collective-permute-start(bf16[128,2048]{1,0:T(8,128)(2,1)S(1)} %collective-permute-done.refs_3_), channel_id=1, source_target_pairs={{0,8},{4,12},{8,16},{12,20},{16,24},{20,28},{1,9},{5,13},{9,17},{1... | collective-permute-start | bytes 1572872 | tf_op jit(solution)/shard_map/ppermute | solution.py:350
  33.7 2.8 %copy-done.1 = bf16[3,2048,512]{2,1,0:T(8,128)(2,1)S(1)} copy-done((bf16[3,2048,512]{2,1,0:T(8,128)(2,1)S(1)}, bf16[3,2048,512]{2,1,0:T(8,128)(2,1)}, u32[]{:S(2)}) %copy-start.1) | copy-done | bytes 6291480
  36.5 2.8 %copy-done.4 = bf16[3,2048,512]{2,1,0:T(8,128)(2,1)S(1)} copy-done((bf16[3,2048,512]{2,1,0:T(8,128)(2,1)S(1)}, bf16[3,2048,512]{2,1,0:T(8,128)(2,1)}, u32[]{:S(2)}) %copy-start.4) | copy-done | bytes 6291480
  39.2 9.4 %shard_map.87 = (bf16[512,512]{1,0:T(8,128)(2,1)S(1)}, bf16[512,512]{1,0:T(8,128)(2,1)S(1)}, f32[8,512]{1,0:T(8,128)S(1)}, f32[512,512]{1,0:T(8,128)S(1)}, f32[8...) custom-call(f32[4]{0:T(128)S(1)} %copy-done.13, ...), custom_call_target="tpu_custom_call" | custom-call | flops 5368709120 | bytes 1048576 | tf_op jit(solution)/shard_map/pallas_call | solution.py:193
  48.7 0.1 broadcast_select_fusion.1.refs_5_
  48.8 1.5 %collective-permute-start.12 = (bf16[128,2048]{1,0:T(8,128)(2,1)S(1)}, bf16[128,2048]{1,0:T(8,128)(2,1)S(1)}, u32[]{:S(2)}, u32[]{:S(2)}) collective-permute-start(bf16[128,2048]{1,0:T(8,128)(2,1)S(1)} %broadcast_select_fusion.1.refs_5_), channel_id=1, source_target_pairs={{0,2},{1,3},{2,0},{3,1},{4,6},{5,7},{6,4},{7,5},{8,10},{9,11},{10,... | collective-permute-start | bytes 1572872 | tf_op jit(solution)/shard_map/ppermute | solution.py:347
  50.3 3.9 %collective-permute-start.11 = (bf16[128,2048]{1,0:T(8,128)(2,1)S(1)}, bf16[128,2048]{1,0:T(8,128)(2,1)S(1)}, u32[]{:S(2)}, u32[]{:S(2)}) collective-permute-start(bf16[128,2048]{1,0:T(8,128)(2,1)S(1)} %collective-permute-done.9.refs_5_), channel_id=1, source_target_pairs={{4,0},{12,8},{20,16},{28,24},{5,1},{13,9},{21,17},{29,25},{6,2},{1... | collective-permute-start | bytes 1572872 | tf_op jit(solution)/shard_map/ppermute | solution.py:350
  54.2 1.9 %collective-permute-start.13 = (bf16[128,2048]{1,0:T(8,128)(2,1)S(1)}, bf16[128,2048]{1,0:T(8,128)(2,1)S(1)}, u32[]{:S(2)}, u32[]{:S(2)}) collective-permute-start(bf16[128,2048]{1,0:T(8,128)(2,1)S(1)} %collective-permute-done.8.refs_4_), channel_id=1, source_target_pairs={{0,8},{4,12},{8,16},{12,20},{16,24},{20,28},{1,9},{5,13},{9,17},{1... | collective-permute-start | bytes 1572872 | tf_op jit(solution)/shard_map/ppermute | solution.py:350
  56.1 1.9 %collective-permute-start.14 = (s32[4,128]{1,0:T(4,128)S(1)}, s32[4,128]{1,0:T(4,128)S(1)}, u32[]{:S(2)}, u32[]{:S(2)}) collective-permute-start(s32[4,128]{1,0:T(4,128)S(1)} %get-tuple-element.60.refs_1_), channel_id=1, source_target_pairs={{0,8},{4,12},{8,16},{12,20},{16,24},{20,28},{1,9},{5,13},{9,17},{1... | collective-permute-start | bytes 6152 | tf_op jit(solution)/shard_map/ppermute | solution.py:350
  58.1 0.0 copy-start.6
  58.1 7.2 %shard_map.88 = (f32[8,512]{1,0:T(8,128)S(1)}, f32[512,512]{1,0:T(8,128)S(1)}, f32[8,512]{1,0:T(8,128)S(1)}, f32[512,512]{1,0:T(8,128)S(1)}) custom-call(f32[8,128]{1,0:T(8,128)S(1)} %get-tuple-element.55.slopes_ref, s32[4,128]{1,0:T(4,128)S(1)} %bitcast.8, s32[4,128]{1,0:T(4,128)S(1)} %collective-permute-done.5.refs_0_, ...), custom_call_target="tpu_custom_call" | custom-call | flops 3221225472 | bytes 1048576 | tf_op jit(solution)/shard_map/pallas_call | solution.py:292
  65.3 3.8 %collective-permute-done.14.refs_3_ = s32[4,128]{1,0:T(4,128)S(1)} collective-permute-done((s32[4,128]{1,0:T(4,128)S(1)}, s32[4,128]{1,0:T(4,128)S(1)}, u32[]{:S(2)}, u32[]{:S(2)}) %collective-permute-start.14) | collective-permute-done | bytes 2080 | tf_op jit(solution)/shard_map/ppermute | solution.py:350
  69.1 0.1 collective-permute-start.17
  69.2 0.1 broadcast_select_fusion.refs_7_
  69.3 0.6 collective-permute-start.15
  69.9 9.0 %shard_map.89 = (f32[8,512]{1,0:T(8,128)S(1)}, f32[512,512]{1,0:T(8,128)S(1)}, f32[8,512]{1,0:T(8,128)S(1)}, f32[512,512]{1,0:T(8,128)S(1)}) custom-call(f32[8,128]{1,0:T(8,128)S(1)} %get-tuple-element.55.slopes_ref, s32[4,128]{1,0:T(4,128)S(1)} %bitcast.9, s32[4,128]{1,0:T(4,128)S(1)} %collective-permute-done.5.refs_0_, ...), custom_call_target="tpu_custom_call" | custom-call | flops 4294967296 | bytes 1048576 | tf_op jit(solution)/shard_map/pallas_call | solution.py:292
  78.9 4.8 %collective-permute-done.15.refs_4_ = bf16[128,2048]{1,0:T(8,128)(2,1)S(1)} collective-permute-done((bf16[128,2048]{1,0:T(8,128)(2,1)S(1)}, bf16[128,2048]{1,0:T(8,128)(2,1)S(1)}, u32[]{:S(2)}, u32[]{:S(2)}) %collective-permute-start.15) | collective-permute-done | bytes 524320 | tf_op jit(solution)/shard_map/ppermute | solution.py:347
  83.7 0.4 shard_map.90
  84.1 0.0 copy-start.9
  84.1 0.1 collective-permute-start.16
  84.2 1.9 %collective-permute-done.16.got_ref = bf16[1056,256]{1,0:T(8,128)(2,1)S(1)} collective-permute-done((bf16[1056,256]{1,0:T(8,128)(2,1)S(1)}, bf16[1056,256]{1,0:T(8,128)(2,1)S(1)}, u32[]{:S(2)}, u32[]{:S(2)}) %collective-permute-start.16) | collective-permute-done | bytes 540704 | tf_op jit(solution)/shard_map/ppermute | solution.py:344
  86.1 0.8 shard_map.92
  86.9 0.6 collective-permute-start.18
  87.5 0.8 shard_map.91
  88.4 12.6 %collective-permute-done.18 = bf16[128,2048]{1,0:T(8,128)(2,1)S(1)} collective-permute-done((bf16[128,2048]{1,0:T(8,128)(2,1)S(1)}, bf16[128,2048]{1,0:T(8,128)(2,1)S(1)}, u32[]{:S(2)}, u32[]{:S(2)}) %collective-permute-start.18) | collective-permute-done | bytes 524320 | tf_op jit(solution)/shard_map/ppermute | solution.py:347
  101.0 0.9 add_convert_fusion
  (31 shorter events, 0.1 us)
Async XLA Ops:
  0.6 24.3 %collective-permute-start.3 = (bf16[3,2048,512]{2,1,0:T(8,128)(2,1)}, bf16[3,2048,512]{2,1,0:T(8,128)(2,1)S(1)}, u32[]{:S(2)}, u32[]{:S(2)}) collective-permute-start(bf16[3,2048,512]{2,1,0:T(8,128)(2,1)} %bitcast.3), channel_id=1, source_target_pairs={{0,1},{1,0},{2,3},{3,2},{4,5},{5,4},{6,7},{7,6},{8,9},{9,8},{10,11... | collective-permute-start | bytes 18874376 | tf_op jit(solution)/shard_map/ppermute | solution.py:344
  0.7 1.0 %copy-start.8 = (bf16[128,2048]{1,0:T(8,128)(2,1)S(1)}, bf16[128,2048]{1,0:T(8,128)(2,1)}, u32[]{:S(2)}) copy-start(bf16[128,2048]{1,0:T(8,128)(2,1)} %refs_0_.1) | copy-start | bytes 1572868
  1.8 0.7 copy-start.11
  2.5 0.7 copy-start.12
  4.1 7.6 %collective-permute-start.4 = (bf16[144,2048]{1,0:T(8,128)(2,1)S(1)}, bf16[144,2048]{1,0:T(8,128)(2,1)S(1)}, u32[]{:S(2)}, u32[]{:S(2)}) collective-permute-start(bf16[144,2048]{1,0:T(8,128)(2,1)S(1)} %get-tuple-element.48), channel_id=1, source_target_pairs={{0,1},{1,0},{2,3},{3,2},{4,5},{5,4},{6,7},{7,6},{8,9},{9,8},{10,11... | collective-permute-start | bytes 1769480 | tf_op jit(solution)/shard_map/ppermute | solution.py:344
  4.6 17.8 %collective-permute-start = (bf16[128,2048]{1,0:T(8,128)(2,1)S(1)}, bf16[128,2048]{1,0:T(8,128)(2,1)S(1)}, u32[]{:S(2)}, u32[]{:S(2)}) collective-permute-start(bf16[128,2048]{1,0:T(8,128)(2,1)S(1)} %get-tuple-element.47.a), channel_id=1, source_target_pairs={{0,8},{4,12},{8,16},{12,20},{16,24},{20,28},{1,9},{5,13},{9,17},{1... | collective-permute-start | bytes 1572872 | tf_op jit(solution)/shard_map/ppermute | solution.py:350
  8.1 14.3 %collective-permute-start.1 = (bf16[128,2048]{1,0:T(8,128)(2,1)S(1)}, bf16[128,2048]{1,0:T(8,128)(2,1)S(1)}, u32[]{:S(2)}, u32[]{:S(2)}) collective-permute-start(bf16[128,2048]{1,0:T(8,128)(2,1)S(1)} %get-tuple-element.47.a), channel_id=1, source_target_pairs={{0,2},{1,3},{2,0},{3,1},{4,6},{5,7},{6,4},{7,5},{8,10},{9,11},{10,... | collective-permute-start | bytes 1572872 | tf_op jit(solution)/shard_map/ppermute | solution.py:347
  9.7 15.2 %collective-permute-start.2 = (bf16[128,2048]{1,0:T(8,128)(2,1)S(1)}, bf16[128,2048]{1,0:T(8,128)(2,1)S(1)}, u32[]{:S(2)}, u32[]{:S(2)}) collective-permute-start(bf16[128,2048]{1,0:T(8,128)(2,1)S(1)} %get-tuple-element.47.a), channel_id=1, source_target_pairs={{0,4},{8,12},{16,20},{24,28},{1,5},{9,13},{17,21},{25,29},{2,6},{1... | collective-permute-start | bytes 1572872 | tf_op jit(solution)/shard_map/ppermute | solution.py:350
  11.7 13.2 %collective-permute-start.5 = (s32[4,128]{1,0:T(4,128)}, s32[4,128]{1,0:T(4,128)S(1)}, u32[]{:S(2)}, u32[]{:S(2)}) collective-permute-start(s32[4,128]{1,0:T(4,128)} %bitcast.5), channel_id=1, source_target_pairs={{0,4},{4,8},{8,12},{12,16},{16,20},{20,24},{24,28},{1,5},{5,9},{9,... | collective-permute-start | bytes 6152 | tf_op jit(solution)/shard_map/ppermute | solution.py:350
  16.6 2.8 %copy-start.7 = (bf16[2048,3,512]{2,0,1:T(8,128)(2,1)S(1)}, bf16[2048,3,512]{2,0,1:T(8,128)(2,1)}, u32[]{:S(2)}) copy-start(bf16[2048,3,512]{2,0,1:T(8,128)(2,1)} %param.8) | copy-start | bytes 18874372
  19.4 8.2 %copy-start.10 = (s32[512]{0:T(512)S(1)}, s32[512]{0:T(512)}, u32[]{:S(2)}) copy-start(s32[512]{0:T(512)} %param.11) | copy-start | bytes 6148
  19.4 14.3 %copy-start.13 = (f32[4]{0:T(128)S(1)}, f32[4]{0:T(128)}, u32[]{:S(2)}) copy-start(f32[4]{0:T(128)} %s0.1) | copy-start | bytes 52
  19.8 2.6 %copy-start = (bf16[3,2048,512]{2,1,0:T(8,128)(2,1)}, bf16[3,2048,512]{2,1,0:T(8,128)(2,1)S(1)}, u32[]{:S(2)}) copy-start(bf16[3,2048,512]{2,1,0:T(8,128)(2,1)S(1)} %shard_map.86.w0.refs_6_.refs_8_.refs_5_) | copy-start | bytes 18874372
  24.9 2.6 %copy-start.3 = (bf16[3,2048,512]{2,1,0:T(8,128)(2,1)}, bf16[3,2048,512]{2,1,0:T(8,128)(2,1)S(1)}, u32[]{:S(2)}) copy-start(bf16[3,2048,512]{2,1,0:T(8,128)(2,1)S(1)} %collective-permute-done.3.w1.refs_7_.refs_9_.refs_6_) | copy-start | bytes 18874372
  27.5 6.1 %collective-permute-start.6 = (bf16[128,2048]{1,0:T(8,128)(2,1)S(1)}, bf16[128,2048]{1,0:T(8,128)(2,1)S(1)}, u32[]{:S(2)}, u32[]{:S(2)}) collective-permute-start(bf16[128,2048]{1,0:T(8,128)(2,1)S(1)} %collective-permute-done.1.b), channel_id=1, source_target_pairs={{0,1},{1,0},{2,3},{3,2},{4,5},{5,4},{6,7},{7,6},{8,9},{9,8},{10,11... | collective-permute-start | bytes 1572872 | tf_op jit(solution)/shard_map/ppermute | solution.py:344
  27.5 6.1 %collective-permute-start.10 = (s32[8,128]{1,0:T(8,128)S(1)}, s32[8,128]{1,0:T(8,128)S(1)}, u32[]{:S(2)}, u32[]{:S(2)}) collective-permute-start(s32[8,128]{1,0:T(8,128)S(1)} %pad_add_fusion), channel_id=1, source_target_pairs={{0,8},{4,12},{8,16},{12,20},{16,24},{20,28},{1,9},{5,13},{9,17},{1... | collective-permute-start | bytes 12296 | tf_op jit(solution)/shard_map/ppermute | solution.py:350
  31.0 17.7 %collective-permute-start.7 = (bf16[128,2048]{1,0:T(8,128)(2,1)S(1)}, bf16[128,2048]{1,0:T(8,128)(2,1)S(1)}, u32[]{:S(2)}, u32[]{:S(2)}) collective-permute-start(bf16[128,2048]{1,0:T(8,128)(2,1)S(1)} %collective-permute-done.refs_3_), channel_id=1, source_target_pairs={{0,4},{8,12},{16,20},{24,28},{4,0},{12,8},{20,16},{28,24},{1,5},{9... | collective-permute-start | bytes 1572872 | tf_op jit(solution)/shard_map/ppermute | solution.py:350
  31.1 17.6 %collective-permute-start.8 = (bf16[128,2048]{1,0:T(8,128)(2,1)S(1)}, bf16[128,2048]{1,0:T(8,128)(2,1)S(1)}, u32[]{:S(2)}, u32[]{:S(2)}) collective-permute-start(bf16[128,2048]{1,0:T(8,128)(2,1)S(1)} %collective-permute-done.refs_3_), channel_id=1, source_target_pairs={{0,2},{1,3},{2,0},{3,1},{4,6},{5,7},{6,4},{7,5},{8,10},{9,11},{10,... | collective-permute-start | bytes 1572872 | tf_op jit(solution)/shard_map/ppermute | solution.py:347
  31.7 17.0 %collective-permute-start.9 = (bf16[128,2048]{1,0:T(8,128)(2,1)S(1)}, bf16[128,2048]{1,0:T(8,128)(2,1)S(1)}, u32[]{:S(2)}, u32[]{:S(2)}) collective-permute-start(bf16[128,2048]{1,0:T(8,128)(2,1)S(1)} %collective-permute-done.refs_3_), channel_id=1, source_target_pairs={{0,8},{4,12},{8,16},{12,20},{16,24},{20,28},{1,9},{5,13},{9,17},{1... | collective-permute-start | bytes 1572872 | tf_op jit(solution)/shard_map/ppermute | solution.py:350
  33.7 2.8 %copy-start.1 = (bf16[3,2048,512]{2,1,0:T(8,128)(2,1)S(1)}, bf16[3,2048,512]{2,1,0:T(8,128)(2,1)}, u32[]{:S(2)}) copy-start(bf16[3,2048,512]{2,1,0:T(8,128)(2,1)} %copy-done) | copy-start | bytes 18874372
  36.5 2.8 %copy-start.4 = (bf16[3,2048,512]{2,1,0:T(8,128)(2,1)S(1)}, bf16[3,2048,512]{2,1,0:T(8,128)(2,1)}, u32[]{:S(2)}) copy-start(bf16[3,2048,512]{2,1,0:T(8,128)(2,1)} %copy-done.3) | copy-start | bytes 18874372
  39.2 18.8 %copy-start.2 = (bf16[3,2048,512]{2,1,0:T(8,128)(2,1)S(1)}, bf16[3,2048,512]{2,1,0:T(8,128)(2,1)}, u32[]{:S(2)}) copy-start(bf16[3,2048,512]{2,1,0:T(8,128)(2,1)} %copy-done) | copy-start | bytes 18874372
  39.2 18.8 %copy-start.5 = (bf16[3,2048,512]{2,1,0:T(8,128)(2,1)S(1)}, bf16[3,2048,512]{2,1,0:T(8,128)(2,1)}, u32[]{:S(2)}) copy-start(bf16[3,2048,512]{2,1,0:T(8,128)(2,1)} %copy-done.3) | copy-start | bytes 18874372
  48.8 20.3 %collective-permute-start.12 = (bf16[128,2048]{1,0:T(8,128)(2,1)S(1)}, bf16[128,2048]{1,0:T(8,128)(2,1)S(1)}, u32[]{:S(2)}, u32[]{:S(2)}) collective-permute-start(bf16[128,2048]{1,0:T(8,128)(2,1)S(1)} %broadcast_select_fusion.1.refs_5_), channel_id=1, source_target_pairs={{0,2},{1,3},{2,0},{3,1},{4,6},{5,7},{6,4},{7,5},{8,10},{9,11},{10,... | collective-permute-start | bytes 1572872 | tf_op jit(solution)/shard_map/ppermute | solution.py:347
  50.3 18.8 %collective-permute-start.11 = (bf16[128,2048]{1,0:T(8,128)(2,1)S(1)}, bf16[128,2048]{1,0:T(8,128)(2,1)S(1)}, u32[]{:S(2)}, u32[]{:S(2)}) collective-permute-start(bf16[128,2048]{1,0:T(8,128)(2,1)S(1)} %collective-permute-done.9.refs_5_), channel_id=1, source_target_pairs={{4,0},{12,8},{20,16},{28,24},{5,1},{13,9},{21,17},{29,25},{6,2},{1... | collective-permute-start | bytes 1572872 | tf_op jit(solution)/shard_map/ppermute | solution.py:350
  54.2 14.9 %collective-permute-start.13 = (bf16[128,2048]{1,0:T(8,128)(2,1)S(1)}, bf16[128,2048]{1,0:T(8,128)(2,1)S(1)}, u32[]{:S(2)}, u32[]{:S(2)}) collective-permute-start(bf16[128,2048]{1,0:T(8,128)(2,1)S(1)} %collective-permute-done.8.refs_4_), channel_id=1, source_target_pairs={{0,8},{4,12},{8,16},{12,20},{16,24},{20,28},{1,9},{5,13},{9,17},{1... | collective-permute-start | bytes 1572872 | tf_op jit(solution)/shard_map/ppermute | solution.py:350
  56.1 13.0 %collective-permute-start.14 = (s32[4,128]{1,0:T(4,128)S(1)}, s32[4,128]{1,0:T(4,128)S(1)}, u32[]{:S(2)}, u32[]{:S(2)}) collective-permute-start(s32[4,128]{1,0:T(4,128)S(1)} %get-tuple-element.60.refs_1_), channel_id=1, source_target_pairs={{0,8},{4,12},{8,16},{12,20},{16,24},{20,28},{1,9},{5,13},{9,17},{1... | collective-permute-start | bytes 6152 | tf_op jit(solution)/shard_map/ppermute | solution.py:350
  58.1 11.0 %copy-start.6 = (bf16[512,2048]{1,0:T(8,128)(2,1)S(1)}, bf16[512,2048]{1,0:T(8,128)(2,1)}, u32[]{:S(2)}) copy-start(bf16[512,2048]{1,0:T(8,128)(2,1)} %w0.3) | copy-start | bytes 6291460
  69.1 17.0 %collective-permute-start.17 = (bf16[512,2048]{1,0:T(8,128)(2,1)S(1)}, bf16[512,2048]{1,0:T(8,128)(2,1)S(1)}, u32[]{:S(2)}, u32[]{:S(2)}) collective-permute-start(bf16[512,2048]{1,0:T(8,128)(2,1)S(1)} %copy-done.6), channel_id=1, source_target_pairs={{0,1},{1,0},{2,3},{3,2},{4,5},{5,4},{6,7},{7,6},{8,9},{9,8},{10,11... | collective-permute-start | bytes 6291464 | tf_op jit(solution)/shard_map/ppermute | solution.py:344
  69.3 14.4 %collective-permute-start.15 = (bf16[128,2048]{1,0:T(8,128)(2,1)S(1)}, bf16[128,2048]{1,0:T(8,128)(2,1)S(1)}, u32[]{:S(2)}, u32[]{:S(2)}) collective-permute-start(bf16[128,2048]{1,0:T(8,128)(2,1)S(1)} %broadcast_select_fusion.refs_7_), channel_id=1, source_target_pairs={{0,2},{1,3},{2,0},{3,1},{4,6},{5,7},{6,4},{7,5},{8,10},{9,11},{10,... | collective-permute-start | bytes 1572872 | tf_op jit(solution)/shard_map/ppermute | solution.py:347
  84.1 3.4 %copy-start.9 = (bf16[128,2048]{1,0:T(8,128)(2,1)S(1)}, bf16[128,2048]{1,0:T(8,128)(2,1)}, u32[]{:S(2)}) copy-start(bf16[128,2048]{1,0:T(8,128)(2,1)} %refs_0_.1) | copy-start | bytes 1572868
  84.1 2.0 %collective-permute-start.16 = (bf16[1056,256]{1,0:T(8,128)(2,1)S(1)}, bf16[1056,256]{1,0:T(8,128)(2,1)S(1)}, u32[]{:S(2)}, u32[]{:S(2)}) collective-permute-start(bf16[1056,256]{1,0:T(8,128)(2,1)S(1)} %get-tuple-element.87), channel_id=1, source_target_pairs={{0,1},{1,0},{2,3},{3,2},{4,5},{5,4},{6,7},{7,6},{8,9},{9,8},{10,11... | collective-permute-start | bytes 1622024 | tf_op jit(solution)/shard_map/ppermute | solution.py:344
  86.9 14.0 %collective-permute-start.18 = (bf16[128,2048]{1,0:T(8,128)(2,1)S(1)}, bf16[128,2048]{1,0:T(8,128)(2,1)S(1)}, u32[]{:S(2)}, u32[]{:S(2)}) collective-permute-start(bf16[128,2048]{1,0:T(8,128)(2,1)S(1)} %shard_map.92), channel_id=1, source_target_pairs={{0,2},{1,3},{2,0},{3,1},{4,6},{5,7},{6,4},{7,5},{8,10},{9,11},{10,... | collective-permute-start | bytes 1572872 | tf_op jit(solution)/shard_map/ppermute | solution.py:347

commit v5 on v4

--- a/solution.py
+++ b/solution.py
@@ -97,6 +97,28 @@
         compiler_params=params(8),
         cost_estimate=cost(0, 2 * weights.size * 2),
     )(weights)
+
+
+def pick(even_value, odd_value):
+    def body(even_ref, odd_ref, out_ref):
+        odd = lax.axis_index("seq") % 2 == 1
+
+        @pl.when(odd)
+        def _():
+            out_ref[...] = odd_ref[...]
+
+        @pl.when(jnp.logical_not(odd))
+        def _():
+            out_ref[...] = even_ref[...]
+
+    return pl.pallas_call(
+        body,
+        out_shape=jax.ShapeDtypeStruct(even_value.shape, even_value.dtype),
+        in_specs=[VMEM, VMEM],
+        out_specs=VMEM,
+        compiler_params=params(8),
+        cost_estimate=cost(0, 2 * even_value.size * 2),
+    )(even_value, odd_value)
 
 
 def place_of(place):
@@ -234,7 +256,7 @@
     depth, width = w_own.shape[1:]
     block = 4 * PIECE
     count = len(pieces)
-    rows = count * PIECE
+    rows = len(which) * PIECE
     n_out = 3 if closing else 4
 
     def body(slopes_ref, seg_ref, *refs):
@@ -252,16 +274,18 @@
         start = block_base - jnp.sum(same)
 
         def key_base(i):
-            back, place = which[i]
-            return block_base - back * block + place_of(place) * PIECE
+            def base(back, place):
+                return block_base - back * block + place_of(place) * PIECE if back else -SPAN * block
+
+            return jnp.where(block_num % 2 == 1, base(*which[i][1]), base(*which[i][0]))
 
         live = key_base(0) + PIECE > start
-        for i in range(1, count):
+        for i in range(1, len(which)):
             live = live | (key_base(i) + PIECE > start)
 
         @pl.when(live)
         def _():
-            set_earlier_masks(seg_ref, start, block_base, key_base, count, mask, dist)
+            set_earlier_masks(seg_ref, start, block_base, key_base, len(which), mask, dist)
             x = jnp.concatenate([source[...] for source in sources], axis=0)
             for group, (w, q) in enumerate(((w0, q0), (w1, q1))):
                 keys = dot(x, w[1]).astype(BF16)
@@ -377,27 +401,28 @@
     q_own, q_pair, *state, key_cache, value_cache, slopes8 = own_block(
         slopes, seg, (a0, b0, c0, d0), w_staged, w_pair)
 
-    crossed, b2, a4, segs, state[0] = tie((crossed, b2, a4, segs, state[0]))
-    a1 = jnp.where(odd, a1_odd, crossed)
-    b1 = over_x(a1)
+    crossed, b2, a4, b0_sent, segs, wo_sent, state[0] = tie((crossed, b2, a4, b0, segs, w_out, state[0]))
+    over_y = over_seq(pick(b0_sent, a4), even_to_odd + odd_to_even)
+    x_third = over_x(crossed)
     b4 = over_seq(b2, two_on)
-    a3_even = over_seq(a4, odd_to_even)
     seg4 = over_seq(segs[1], two_on)
+    wo_pair = over_core(wo_sent)
 
     def merge(closing, segs, pieces, which, state):
         return earlier_pieces(
             which, closing, slopes8, seg, segs, pieces, w_staged, w_pair, q_own, q_pair, state)
 
-    state = merge(False, segs, (a2, b2, a1), ((2, 0), (2, 1), (1, 0)), state)
-
-    a3_even, b1, b4, seg4, wo_sent, held = tie((a3_even, b1, b4, seg4, w_out, state[0]))
+    state = merge(
+        False, segs, (a2, b2, crossed, a1_odd), (((2, 0),) * 2, ((2, 1),) * 2, ((1, 0), (3, 0)), ((0, 0), (1, 0))), state)
+
+    over_y, x_third, b4, seg4, held = tie((over_y, x_third, b4, seg4, state[0]))
     segs = [*segs, seg4]
     state = (held, *state[1:])
-    a3 = jnp.where(odd, crossed, a3_even)
-    b3 = over_x(a3)
-    wo_pair = over_core(wo_sent)
-    state = merge(False, segs, (b1, a4, b4, a3), ((1, 1), (4, 0), (4, 1), (3, 0)), state)
-    send, lse, out = merge(True, segs, (b3,), ((3, 1),), state)
+    b3_top = over_x(over_y[: PIECE // 2])
+    b3_rest = over_seq(b4[PIECE // 2 :], odd_to_even)
+    state = merge(
+        False, segs, (a4, b4, x_third, over_y), (((4, 0),) * 2, ((4, 1),) * 2, ((1, 1), (3, 1)), ((3, 0), (1, 1))), state)
+    send, lse, out = merge(True, segs, (b3_top, b3_rest), (((3, 1), (0, 0)),), state)
     got = over_core(send)
     y_pair = project(1, lse, out, got, w_out, wo_pair, None)
     y_got = over_x(y_pair)

time: 104 us -> 94.4 us (0.908); the launches traced: 102 us -> 94 us
  local copies, waits for them, and re-layouts: 16 us -> 5.23 us
  starting transfers between devices: 28.5 us -> 33.7 us
  waiting for transfers between devices: 26.3 us -> 22.3 us
  Pallas kernels: 29.1 us -> 31 us
    unnamed x28 -> x16, local copies, waits for them, and re-layouts: 16 us -> 5.19 us
    ppermute x9 -> x10, starting transfers between devices: 22.8 us -> 27.1 us  [over_seq(): return lax.ppermute(value, 'seq', pairs)]
    ppermute x5, waiting for transfers between devices: 17.4 us -> 13 us  [over_x(): return lax.ppermute(value, 'head', [(i, i ^ 2) for i in range(4)])]
    pallas_call x3, Pallas kernels: 16.6 us -> 18.5 us  [earlier_pieces(): pl.pallas_call(body, out_shape=shapes, in_specs=[VMEM] * (10 + len(segs)...]
    ppermute x9 -> x10, waiting for transfers between devices: 6.28 us -> 6.6 us  [over_seq(): return lax.ppermute(value, 'seq', pairs)]
  transfers between devices with their start and end apart: 19 -> 20, of which waited for: 6 -> 8; matrix products, arithmetic and copies ran while one was open for 0% -> 0% of each run, Pallas kernels for 28% -> 32%
where the time goes in v5:
time: 94.4 us; the launch traced here: 94 us
  starting transfers between devices  33.7 us (36%)
  Pallas kernels  31 us (33%)
  waiting for transfers between devices  22.3 us (24%)
  local copies, waits for them, and re-layouts  5.23 us (6%)
    ppermute x10, starting transfers between devices, over_seq(): return lax.ppermute(value, 'seq', pairs)  27.1 us
    pallas_call x3, Pallas kernels, earlier_pieces(): pl.pallas_call(body, out_shape=shapes, in_specs=[VMEM] * (10 + len(segs)...  18.5 us
    ppermute x5, waiting for transfers between devices, over_x(): return lax.ppermute(value, 'head', [(i, i ^ 2) for i in range(4)])  13 us
    pallas_call x1, Pallas kernels, own_block(): pl.pallas_call(body, out_shape=(jax.ShapeDtypeStruct((width, block), BF16...  9.43 us
    ppermute x10, waiting for transfers between devices, over_seq(): return lax.ppermute(value, 'seq', pairs)  6.6 us
    ppermute x5, starting transfers between devices, over_x(): return lax.ppermute(value, 'head', [(i, i ^ 2) for i in range(4)])  5.82 us
    unnamed x16, local copies, waits for them, and re-layouts  5.19 us
    ppermute x5, waiting for transfers between devices, over_core(): return lax.ppermute(value, 'head', [(i, i ^ 1) for i in range(4)])  2.67 us
  transfers between devices with their start and end apart: 20, of which 8 were waited for; matrix products, arithmetic and copies ran while one was open for 0% of the time, Pallas kernels for 32%

profile of v5, /device:TPU:12, one launch (start us, length us, event | category | flops | bytes accessed | tf_op | source)
XLA Modules:
  0.0 94.0 jit_solution(8118154731010666883)
XLA Ops:
  0.6 0.1 collective-permute-start.3
  0.7 0.0 copy-start.2
  0.7 1.0 %copy-done.2 = bf16[128,2048]{1,0:T(8,128)(2,1)S(1)} copy-done((bf16[128,2048]{1,0:T(8,128)(2,1)S(1)}, bf16[128,2048]{1,0:T(8,128)(2,1)}, u32[]{:S(2)}) %copy-start.2) | copy-done | bytes 524312
  1.8 0.7 copy-done.5
  2.5 0.7 copy-done.6
  3.1 1.0 %shard_map.85 = (bf16[128,2048]{1,0:T(8,128)(2,1)S(1)}, bf16[144,2048]{1,0:T(8,128)(2,1)S(1)}) custom-call(f32[4]{0:T(128)S(1)} %copy-done.6, bf16[128,2048]{1,0:T(8,128)(2,1)S(1)} %copy-done.2, f32[1,2048]{1,0:T(1,128)S(1)} %bitcast.11), custom_call_target="tpu_custom_call" | custom-call | bytes 1048576 | tf_op jit(solution)/shard_map/pallas_call | solution.py:67
  4.1 0.6 collective-permute-start.4
  4.6 1.3 %collective-permute-start.2 = (bf16[128,2048]{1,0:T(8,128)(2,1)S(1)}, bf16[128,2048]{1,0:T(8,128)(2,1)S(1)}, u32[]{:S(2)}, u32[]{:S(2)}) collective-permute-start(bf16[128,2048]{1,0:T(8,128)(2,1)S(1)} %get-tuple-element.48.a), channel_id=1, source_target_pairs={{0,4},{8,12},{16,20},{24,28},{1,5},{9,13},{17,21},{25,29},{2,6},{1... | collective-permute-start | bytes 1572872 | tf_op jit(solution)/shard_map/ppermute | solution.py:374
  5.9 1.6 %collective-permute-start.1 = (bf16[128,2048]{1,0:T(8,128)(2,1)S(1)}, bf16[128,2048]{1,0:T(8,128)(2,1)S(1)}, u32[]{:S(2)}, u32[]{:S(2)}) collective-permute-start(bf16[128,2048]{1,0:T(8,128)(2,1)S(1)} %get-tuple-element.48.a), channel_id=1, source_target_pairs={{0,2},{1,3},{2,0},{3,1},{4,6},{5,7},{6,4},{7,5},{8,10},{9,11},{10,... | collective-permute-start | bytes 1572872 | tf_op jit(solution)/shard_map/ppermute | solution.py:371
  7.5 3.5 %collective-permute-start = (bf16[128,2048]{1,0:T(8,128)(2,1)S(1)}, bf16[128,2048]{1,0:T(8,128)(2,1)S(1)}, u32[]{:S(2)}, u32[]{:S(2)}) collective-permute-start(bf16[128,2048]{1,0:T(8,128)(2,1)S(1)} %get-tuple-element.48.a), channel_id=1, source_target_pairs={{0,8},{4,12},{8,16},{12,20},{16,24},{20,28},{1,9},{5,13},{9,17},{1... | collective-permute-start | bytes 1572872 | tf_op jit(solution)/shard_map/ppermute | solution.py:374
  11.0 0.7 collective-permute-done.4.c
  11.7 4.9 %collective-permute-start.5 = (s32[4,128]{1,0:T(4,128)}, s32[4,128]{1,0:T(4,128)S(1)}, u32[]{:S(2)}, u32[]{:S(2)}) collective-permute-start(s32[4,128]{1,0:T(4,128)} %bitcast.5), channel_id=1, source_target_pairs={{0,4},{4,8},{8,12},{12,16},{16,20},{20,24},{24,28},{1,5},{5,9},{9,... | collective-permute-start | bytes 6152 | tf_op jit(solution)/shard_map/ppermute | solution.py:374
  16.6 0.0 copy-start.1
  16.6 2.8 %copy-done.1 = bf16[2048,3,512]{2,0,1:T(8,128)(2,1)S(1)} copy-done((bf16[2048,3,512]{2,0,1:T(8,128)(2,1)S(1)}, bf16[2048,3,512]{2,0,1:T(8,128)(2,1)}, u32[]{:S(2)}) %copy-start.1) | copy-done | bytes 6291480
  19.4 0.4 shard_map.86.w0.refs_7_.refs_8_.refs_6_
  19.8 0.6 collective-permute-done.2.refs_6_
  20.4 0.0 collective-permute-done.1.b.even_ref
  20.4 2.6 %collective-permute-done.refs_3_ = bf16[128,2048]{1,0:T(8,128)(2,1)S(1)} collective-permute-done((bf16[128,2048]{1,0:T(8,128)(2,1)S(1)}, bf16[128,2048]{1,0:T(8,128)(2,1)S(1)}, u32[]{:S(2)}, u32[]{:S(2)}) %collective-permute-start) | collective-permute-done | bytes 524320 | tf_op jit(solution)/shard_map/ppermute | solution.py:374
  23.0 0.0 collective-permute-done.5.refs_0_
  23.0 0.0 collective-permute-done.3.w1.refs_8_.refs_9_.refs_7_
  23.0 0.0 collective-permute-start.6
  23.0 3.5 %collective-permute-start.10 = (s32[8,128]{1,0:T(8,128)S(1)}, s32[8,128]{1,0:T(8,128)S(1)}, u32[]{:S(2)}, u32[]{:S(2)}) collective-permute-start(s32[8,128]{1,0:T(8,128)S(1)} %pad_add_fusion), channel_id=1, source_target_pairs={{0,8},{4,12},{8,16},{12,20},{16,24},{20,28},{1,9},{5,13},{9,17},{1... | collective-permute-start | bytes 12296 | tf_op jit(solution)/shard_map/ppermute | solution.py:374
  26.5 3.5 %collective-permute-start.9 = (bf16[128,2048]{1,0:T(8,128)(2,1)S(1)}, bf16[128,2048]{1,0:T(8,128)(2,1)S(1)}, u32[]{:S(2)}, u32[]{:S(2)}) collective-permute-start(bf16[128,2048]{1,0:T(8,128)(2,1)S(1)} %collective-permute-done.refs_3_), channel_id=1, source_target_pairs={{0,8},{4,12},{8,16},{12,20},{16,24},{20,28},{1,9},{5,13},{9,17},{1... | collective-permute-start | bytes 1572872 | tf_op jit(solution)/shard_map/ppermute | solution.py:374
  30.0 0.6 collective-permute-start.8
  30.6 2.4 %collective-permute-start.7 = (bf16[128,2048]{1,0:T(8,128)(2,1)S(1)}, bf16[128,2048]{1,0:T(8,128)(2,1)S(1)}, u32[]{:S(2)}, u32[]{:S(2)}) collective-permute-start(bf16[128,2048]{1,0:T(8,128)(2,1)S(1)} %collective-permute-done.refs_3_), channel_id=1, source_target_pairs={{0,4},{8,12},{16,20},{24,28},{4,0},{12,8},{20,16},{28,24},{1,5},{9... | collective-permute-start | bytes 1572872 | tf_op jit(solution)/shard_map/ppermute | solution.py:374
  33.0 9.4 %shard_map.87 = (bf16[512,512]{1,0:T(8,128)(2,1)S(1)}, bf16[512,512]{1,0:T(8,128)(2,1)S(1)}, f32[8,512]{1,0:T(8,128)S(1)}, f32[512,512]{1,0:T(8,128)S(1)}, f32[8...) custom-call(f32[4]{0:T(128)S(1)} %copy-done.7, ...), custom_call_target="tpu_custom_call" | custom-call | flops 5368709120 | bytes 1048576 | tf_op jit(solution)/shard_map/pallas_call | solution.py:215
  42.4 0.0 collective-permute-done.9.odd_ref.refs_4_
  42.4 1.4 %collective-permute-done.8.refs_4_ = bf16[128,2048]{1,0:T(8,128)(2,1)S(1)} collective-permute-done((bf16[128,2048]{1,0:T(8,128)(2,1)S(1)}, bf16[128,2048]{1,0:T(8,128)(2,1)S(1)}, u32[]{:S(2)}, u32[]{:S(2)}) %collective-permute-start.8) | collective-permute-done | bytes 524320 | tf_op jit(solution)/shard_map/ppermute | solution.py:371
  43.8 0.9 collective-permute-done.7.refs_5_
  44.7 1.8 %collective-permute-start.11 = (bf16[128,2048]{1,0:T(8,128)(2,1)S(1)}, bf16[128,2048]{1,0:T(8,128)(2,1)S(1)}, u32[]{:S(2)}, u32[]{:S(2)}) collective-permute-start(bf16[128,2048]{1,0:T(8,128)(2,1)S(1)} %shard_map.88), channel_id=1, source_target_pairs={{0,4},{8,12},{16,20},{24,28},{4,0},{12,8},{20,16},{28,24},{1,5},{9... | collective-permute-start | bytes 1572872 | tf_op jit(solution)/shard_map/ppermute | solution.py:374
  46.5 1.5 %collective-permute-start.12 = (bf16[128,2048]{1,0:T(8,128)(2,1)S(1)}, bf16[128,2048]{1,0:T(8,128)(2,1)S(1)}, u32[]{:S(2)}, u32[]{:S(2)}) collective-permute-start(bf16[128,2048]{1,0:T(8,128)(2,1)S(1)} %collective-permute-done.7.refs_5_), channel_id=1, source_target_pairs={{0,2},{1,3},{2,0},{3,1},{4,6},{5,7},{6,4},{7,5},{8,10},{9,11},{10,... | collective-permute-start | bytes 1572872 | tf_op jit(solution)/shard_map/ppermute | solution.py:371
  48.0 2.2 %collective-permute-start.13 = (bf16[128,2048]{1,0:T(8,128)(2,1)S(1)}, bf16[128,2048]{1,0:T(8,128)(2,1)S(1)}, u32[]{:S(2)}, u32[]{:S(2)}) collective-permute-start(bf16[128,2048]{1,0:T(8,128)(2,1)S(1)} %collective-permute-done.8.refs_4_), channel_id=1, source_target_pairs={{0,8},{4,12},{8,16},{12,20},{16,24},{20,28},{1,9},{5,13},{9,17},{1... | collective-permute-start | bytes 1572872 | tf_op jit(solution)/shard_map/ppermute | solution.py:374
  50.2 1.9 %collective-permute-start.14 = (s32[4,128]{1,0:T(4,128)S(1)}, s32[4,128]{1,0:T(4,128)S(1)}, u32[]{:S(2)}, u32[]{:S(2)}) collective-permute-start(s32[4,128]{1,0:T(4,128)S(1)} %get-tuple-element.61.refs_1_), channel_id=1, source_target_pairs={{0,8},{4,12},{8,16},{12,20},{16,24},{20,28},{1,9},{5,13},{9,17},{1... | collective-permute-start | bytes 6152 | tf_op jit(solution)/shard_map/ppermute | solution.py:374
  52.2 9.0 %shard_map.89 = (f32[8,512]{1,0:T(8,128)S(1)}, f32[512,512]{1,0:T(8,128)S(1)}, f32[8,512]{1,0:T(8,128)S(1)}, f32[512,512]{1,0:T(8,128)S(1)}) custom-call(f32[8,128]{1,0:T(8,128)S(1)} %get-tuple-element.56.slopes_ref, s32[4,128]{1,0:T(4,128)S(1)} %bitcast.8, s32[4,128]{1,0:T(4,128)S(1)} %collective-permute-done.5.refs_0_, ...), custom_call_target="tpu_custom_call" | custom-call | flops 4294967296 | bytes 1048576 | tf_op jit(solution)/shard_map/pallas_call | solution.py:316
  61.2 2.5 %collective-permute-done.14.refs_3_ = s32[4,128]{1,0:T(4,128)S(1)} collective-permute-done((s32[4,128]{1,0:T(4,128)S(1)}, s32[4,128]{1,0:T(4,128)S(1)}, u32[]{:S(2)}, u32[]{:S(2)}) %collective-permute-start.14) | collective-permute-done | bytes 2080 | tf_op jit(solution)/shard_map/ppermute | solution.py:374
  63.7 0.0 collective-permute-done.13.refs_5_
  63.8 2.3 %collective-permute-start.16 = (bf16[64,2048]{1,0:T(8,128)(2,1)S(1)}, bf16[64,2048]{1,0:T(8,128)(2,1)S(1)}, u32[]{:S(2)}, u32[]{:S(2)}) collective-permute-start(bf16[64,2048]{1,0:T(8,128)(2,1)S(1)} %slice.15), channel_id=1, source_target_pairs={{4,0},{12,8},{20,16},{28,24},{5,1},{13,9},{21,17},{29,25},{6,2},{1... | collective-permute-start | bytes 786440 | tf_op jit(solution)/shard_map/ppermute | solution.py:374
  66.1 0.6 collective-permute-start.15
  66.7 9.0 %shard_map.90 = (f32[8,512]{1,0:T(8,128)S(1)}, f32[512,512]{1,0:T(8,128)S(1)}, f32[8,512]{1,0:T(8,128)S(1)}, f32[512,512]{1,0:T(8,128)S(1)}) custom-call(f32[8,128]{1,0:T(8,128)S(1)} %get-tuple-element.56.slopes_ref, s32[4,128]{1,0:T(4,128)S(1)} %bitcast.9, s32[4,128]{1,0:T(4,128)S(1)} %collective-permute-done.5.refs_0_, ...), custom_call_target="tpu_custom_call" | custom-call | flops 4294967296 | bytes 1048576 | tf_op jit(solution)/shard_map/pallas_call | solution.py:316
  75.8 0.5 shard_map.91
  76.2 0.0 copy-start.3
  76.2 0.1 collective-permute-start.17
  76.3 1.9 %collective-permute-done.17.got_ref = bf16[1056,256]{1,0:T(8,128)(2,1)S(1)} collective-permute-done((bf16[1056,256]{1,0:T(8,128)(2,1)S(1)}, bf16[1056,256]{1,0:T(8,128)(2,1)S(1)}, u32[]{:S(2)}, u32[]{:S(2)}) %collective-permute-start.17) | collective-permute-done | bytes 540704 | tf_op jit(solution)/shard_map/ppermute | solution.py:368
  78.2 0.8 shard_map.93
  79.0 1.6 %collective-permute-start.19 = (bf16[128,2048]{1,0:T(8,128)(2,1)S(1)}, bf16[128,2048]{1,0:T(8,128)(2,1)S(1)}, u32[]{:S(2)}, u32[]{:S(2)}) collective-permute-start(bf16[128,2048]{1,0:T(8,128)(2,1)S(1)} %shard_map.93), channel_id=1, source_target_pairs={{0,2},{1,3},{2,0},{3,1},{4,6},{5,7},{6,4},{7,5},{8,10},{9,11},{10,... | collective-permute-start | bytes 1572872 | tf_op jit(solution)/shard_map/ppermute | solution.py:371
  80.6 0.8 shard_map.92
  81.4 11.6 %collective-permute-done.19 = bf16[128,2048]{1,0:T(8,128)(2,1)S(1)} collective-permute-done((bf16[128,2048]{1,0:T(8,128)(2,1)S(1)}, bf16[128,2048]{1,0:T(8,128)(2,1)S(1)}, u32[]{:S(2)}, u32[]{:S(2)}) %collective-permute-start.19) | collective-permute-done | bytes 524320 | tf_op jit(solution)/shard_map/ppermute | solution.py:371
  93.1 0.9 add_convert_fusion
  (22 shorter events, 0.1 us)
Async XLA Ops:
  0.6 22.3 %collective-permute-start.3 = (bf16[3,2048,512]{2,1,0:T(8,128)(2,1)}, bf16[3,2048,512]{2,1,0:T(8,128)(2,1)S(1)}, u32[]{:S(2)}, u32[]{:S(2)}) collective-permute-start(bf16[3,2048,512]{2,1,0:T(8,128)(2,1)} %bitcast.3), channel_id=1, source_target_pairs={{0,1},{1,0},{2,3},{3,2},{4,5},{5,4},{6,7},{7,6},{8,9},{9,8},{10,11... | collective-permute-start | bytes 18874376 | tf_op jit(solution)/shard_map/ppermute | solution.py:368
  0.7 1.0 %copy-start.2 = (bf16[128,2048]{1,0:T(8,128)(2,1)S(1)}, bf16[128,2048]{1,0:T(8,128)(2,1)}, u32[]{:S(2)}) copy-start(bf16[128,2048]{1,0:T(8,128)(2,1)} %refs_0_.1) | copy-start | bytes 1572868
  1.8 0.7 copy-start.5
  2.5 0.7 copy-start.6
  4.1 7.6 %collective-permute-start.4 = (bf16[144,2048]{1,0:T(8,128)(2,1)S(1)}, bf16[144,2048]{1,0:T(8,128)(2,1)S(1)}, u32[]{:S(2)}, u32[]{:S(2)}) collective-permute-start(bf16[144,2048]{1,0:T(8,128)(2,1)S(1)} %get-tuple-element.49), channel_id=1, source_target_pairs={{0,1},{1,0},{2,3},{3,2},{4,5},{5,4},{6,7},{7,6},{8,9},{9,8},{10,11... | collective-permute-start | bytes 1769480 | tf_op jit(solution)/shard_map/ppermute | solution.py:368
  4.6 15.8 %collective-permute-start.2 = (bf16[128,2048]{1,0:T(8,128)(2,1)S(1)}, bf16[128,2048]{1,0:T(8,128)(2,1)S(1)}, u32[]{:S(2)}, u32[]{:S(2)}) collective-permute-start(bf16[128,2048]{1,0:T(8,128)(2,1)S(1)} %get-tuple-element.48.a), channel_id=1, source_target_pairs={{0,4},{8,12},{16,20},{24,28},{1,5},{9,13},{17,21},{25,29},{2,6},{1... | collective-permute-start | bytes 1572872 | tf_op jit(solution)/shard_map/ppermute | solution.py:374
  5.9 14.5 %collective-permute-start.1 = (bf16[128,2048]{1,0:T(8,128)(2,1)S(1)}, bf16[128,2048]{1,0:T(8,128)(2,1)S(1)}, u32[]{:S(2)}, u32[]{:S(2)}) collective-permute-start(bf16[128,2048]{1,0:T(8,128)(2,1)S(1)} %get-tuple-element.48.a), channel_id=1, source_target_pairs={{0,2},{1,3},{2,0},{3,1},{4,6},{5,7},{6,4},{7,5},{8,10},{9,11},{10,... | collective-permute-start | bytes 1572872 | tf_op jit(solution)/shard_map/ppermute | solution.py:371
  7.5 15.5 %collective-permute-start = (bf16[128,2048]{1,0:T(8,128)(2,1)S(1)}, bf16[128,2048]{1,0:T(8,128)(2,1)S(1)}, u32[]{:S(2)}, u32[]{:S(2)}) collective-permute-start(bf16[128,2048]{1,0:T(8,128)(2,1)S(1)} %get-tuple-element.48.a), channel_id=1, source_target_pairs={{0,8},{4,12},{8,16},{12,20},{16,24},{20,28},{1,9},{5,13},{9,17},{1... | collective-permute-start | bytes 1572872 | tf_op jit(solution)/shard_map/ppermute | solution.py:374
  11.7 11.3 %collective-permute-start.5 = (s32[4,128]{1,0:T(4,128)}, s32[4,128]{1,0:T(4,128)S(1)}, u32[]{:S(2)}, u32[]{:S(2)}) collective-permute-start(s32[4,128]{1,0:T(4,128)} %bitcast.5), channel_id=1, source_target_pairs={{0,4},{4,8},{8,12},{12,16},{16,20},{20,24},{24,28},{1,5},{5,9},{9,... | collective-permute-start | bytes 6152 | tf_op jit(solution)/shard_map/ppermute | solution.py:374
  16.6 2.8 %copy-start.1 = (bf16[2048,3,512]{2,0,1:T(8,128)(2,1)S(1)}, bf16[2048,3,512]{2,0,1:T(8,128)(2,1)}, u32[]{:S(2)}) copy-start(bf16[2048,3,512]{2,0,1:T(8,128)(2,1)} %param.8) | copy-start | bytes 18874372
  19.4 3.6 %copy-start.4 = (s32[512]{0:T(512)S(1)}, s32[512]{0:T(512)}, u32[]{:S(2)}) copy-start(s32[512]{0:T(512)} %param.11) | copy-start | bytes 6148
  19.4 13.6 %copy-start.7 = (f32[4]{0:T(128)S(1)}, f32[4]{0:T(128)}, u32[]{:S(2)}) copy-start(f32[4]{0:T(128)} %s0.1) | copy-start | bytes 52
  23.0 10.0 %collective-permute-start.6 = (bf16[128,2048]{1,0:T(8,128)(2,1)S(1)}, bf16[128,2048]{1,0:T(8,128)(2,1)S(1)}, u32[]{:S(2)}, u32[]{:S(2)}) collective-permute-start(bf16[128,2048]{1,0:T(8,128)(2,1)S(1)} %collective-permute-done.1.b.even_ref), channel_id=1, source_target_pairs={{0,1},{1,0},{2,3},{3,2},{4,5},{5,4},{6,7},{7,6},{8,9},{9,8},{10,11... | collective-permute-start | bytes 1572872 | tf_op jit(solution)/shard_map/ppermute | solution.py:368
  23.0 10.0 %collective-permute-start.10 = (s32[8,128]{1,0:T(8,128)S(1)}, s32[8,128]{1,0:T(8,128)S(1)}, u32[]{:S(2)}, u32[]{:S(2)}) collective-permute-start(s32[8,128]{1,0:T(8,128)S(1)} %pad_add_fusion), channel_id=1, source_target_pairs={{0,8},{4,12},{8,16},{12,20},{16,24},{20,28},{1,9},{5,13},{9,17},{1... | collective-permute-start | bytes 12296 | tf_op jit(solution)/shard_map/ppermute | solution.py:374
  26.5 15.9 %collective-permute-start.9 = (bf16[128,2048]{1,0:T(8,128)(2,1)S(1)}, bf16[128,2048]{1,0:T(8,128)(2,1)S(1)}, u32[]{:S(2)}, u32[]{:S(2)}) collective-permute-start(bf16[128,2048]{1,0:T(8,128)(2,1)S(1)} %collective-permute-done.refs_3_), channel_id=1, source_target_pairs={{0,8},{4,12},{8,16},{12,20},{16,24},{20,28},{1,9},{5,13},{9,17},{1... | collective-permute-start | bytes 1572872 | tf_op jit(solution)/shard_map/ppermute | solution.py:374
  30.0 13.8 %collective-permute-start.8 = (bf16[128,2048]{1,0:T(8,128)(2,1)S(1)}, bf16[128,2048]{1,0:T(8,128)(2,1)S(1)}, u32[]{:S(2)}, u32[]{:S(2)}) collective-permute-start(bf16[128,2048]{1,0:T(8,128)(2,1)S(1)} %collective-permute-done.refs_3_), channel_id=1, source_target_pairs={{0,2},{1,3},{2,0},{3,1},{4,6},{5,7},{6,4},{7,5},{8,10},{9,11},{10,... | collective-permute-start | bytes 1572872 | tf_op jit(solution)/shard_map/ppermute | solution.py:371
  30.6 14.1 %collective-permute-start.7 = (bf16[128,2048]{1,0:T(8,128)(2,1)S(1)}, bf16[128,2048]{1,0:T(8,128)(2,1)S(1)}, u32[]{:S(2)}, u32[]{:S(2)}) collective-permute-start(bf16[128,2048]{1,0:T(8,128)(2,1)S(1)} %collective-permute-done.refs_3_), channel_id=1, source_target_pairs={{0,4},{8,12},{16,20},{24,28},{4,0},{12,8},{20,16},{28,24},{1,5},{9... | collective-permute-start | bytes 1572872 | tf_op jit(solution)/shard_map/ppermute | solution.py:374
  33.0 11.7 %copy-start = (bf16[512,2048]{1,0:T(8,128)(2,1)S(1)}, bf16[512,2048]{1,0:T(8,128)(2,1)}, u32[]{:S(2)}) copy-start(bf16[512,2048]{1,0:T(8,128)(2,1)} %w0.3) | copy-start | bytes 6291460
  44.7 33.5 %collective-permute-start.18 = (bf16[512,2048]{1,0:T(8,128)(2,1)S(1)}, bf16[512,2048]{1,0:T(8,128)(2,1)S(1)}, u32[]{:S(2)}, u32[]{:S(2)}) collective-permute-start(bf16[512,2048]{1,0:T(8,128)(2,1)S(1)} %copy-done), channel_id=1, source_target_pairs={{0,1},{1,0},{2,3},{3,2},{4,5},{5,4},{6,7},{7,6},{8,9},{9,8},{10,11... | collective-permute-start | bytes 6291464 | tf_op jit(solution)/shard_map/ppermute | solution.py:368
  44.7 19.0 %collective-permute-start.11 = (bf16[128,2048]{1,0:T(8,128)(2,1)S(1)}, bf16[128,2048]{1,0:T(8,128)(2,1)S(1)}, u32[]{:S(2)}, u32[]{:S(2)}) collective-permute-start(bf16[128,2048]{1,0:T(8,128)(2,1)S(1)} %shard_map.88), channel_id=1, source_target_pairs={{0,4},{8,12},{16,20},{24,28},{4,0},{12,8},{20,16},{28,24},{1,5},{9... | collective-permute-start | bytes 1572872 | tf_op jit(solution)/shard_map/ppermute | solution.py:374
  46.5 17.2 %collective-permute-start.12 = (bf16[128,2048]{1,0:T(8,128)(2,1)S(1)}, bf16[128,2048]{1,0:T(8,128)(2,1)S(1)}, u32[]{:S(2)}, u32[]{:S(2)}) collective-permute-start(bf16[128,2048]{1,0:T(8,128)(2,1)S(1)} %collective-permute-done.7.refs_5_), channel_id=1, source_target_pairs={{0,2},{1,3},{2,0},{3,1},{4,6},{5,7},{6,4},{7,5},{8,10},{9,11},{10,... | collective-permute-start | bytes 1572872 | tf_op jit(solution)/shard_map/ppermute | solution.py:371
  48.0 15.7 %collective-permute-start.13 = (bf16[128,2048]{1,0:T(8,128)(2,1)S(1)}, bf16[128,2048]{1,0:T(8,128)(2,1)S(1)}, u32[]{:S(2)}, u32[]{:S(2)}) collective-permute-start(bf16[128,2048]{1,0:T(8,128)(2,1)S(1)} %collective-permute-done.8.refs_4_), channel_id=1, source_target_pairs={{0,8},{4,12},{8,16},{12,20},{16,24},{20,28},{1,9},{5,13},{9,17},{1... | collective-permute-start | bytes 1572872 | tf_op jit(solution)/shard_map/ppermute | solution.py:374
  50.2 13.5 %collective-permute-start.14 = (s32[4,128]{1,0:T(4,128)S(1)}, s32[4,128]{1,0:T(4,128)S(1)}, u32[]{:S(2)}, u32[]{:S(2)}) collective-permute-start(s32[4,128]{1,0:T(4,128)S(1)} %get-tuple-element.61.refs_1_), channel_id=1, source_target_pairs={{0,8},{4,12},{8,16},{12,20},{16,24},{20,28},{1,9},{5,13},{9,17},{1... | collective-permute-start | bytes 6152 | tf_op jit(solution)/shard_map/ppermute | solution.py:374
  63.8 11.9 %collective-permute-start.16 = (bf16[64,2048]{1,0:T(8,128)(2,1)S(1)}, bf16[64,2048]{1,0:T(8,128)(2,1)S(1)}, u32[]{:S(2)}, u32[]{:S(2)}) collective-permute-start(bf16[64,2048]{1,0:T(8,128)(2,1)S(1)} %slice.15), channel_id=1, source_target_pairs={{4,0},{12,8},{20,16},{28,24},{5,1},{13,9},{21,17},{29,25},{6,2},{1... | collective-permute-start | bytes 786440 | tf_op jit(solution)/shard_map/ppermute | solution.py:374
  66.1 9.7 %collective-permute-start.15 = (bf16[64,2048]{1,0:T(8,128)(2,1)S(1)}, bf16[64,2048]{1,0:T(8,128)(2,1)S(1)}, u32[]{:S(2)}, u32[]{:S(2)}) collective-permute-start(bf16[64,2048]{1,0:T(8,128)(2,1)S(1)} %slice.14), channel_id=1, source_target_pairs={{0,2},{1,3},{2,0},{3,1},{4,6},{5,7},{6,4},{7,5},{8,10},{9,11},{10,... | collective-permute-start | bytes 786440 | tf_op jit(solution)/shard_map/ppermute | solution.py:371
  76.2 4.4 %copy-start.3 = (bf16[128,2048]{1,0:T(8,128)(2,1)S(1)}, bf16[128,2048]{1,0:T(8,128)(2,1)}, u32[]{:S(2)}) copy-start(bf16[128,2048]{1,0:T(8,128)(2,1)} %refs_0_.1) | copy-start | bytes 1572868
  76.2 2.0 %collective-permute-start.17 = (bf16[1056,256]{1,0:T(8,128)(2,1)S(1)}, bf16[1056,256]{1,0:T(8,128)(2,1)S(1)}, u32[]{:S(2)}, u32[]{:S(2)}) collective-permute-start(bf16[1056,256]{1,0:T(8,128)(2,1)S(1)} %get-tuple-element.89), channel_id=1, source_target_pairs={{0,1},{1,0},{2,3},{3,2},{4,5},{5,4},{6,7},{7,6},{8,9},{9,8},{10,11... | collective-permute-start | bytes 1622024 | tf_op jit(solution)/shard_map/ppermute | solution.py:368
  79.0 14.0 %collective-permute-start.19 = (bf16[128,2048]{1,0:T(8,128)(2,1)S(1)}, bf16[128,2048]{1,0:T(8,128)(2,1)S(1)}, u32[]{:S(2)}, u32[]{:S(2)}) collective-permute-start(bf16[128,2048]{1,0:T(8,128)(2,1)S(1)} %shard_map.93), channel_id=1, source_target_pairs={{0,2},{1,3},{2,0},{3,1},{4,6},{5,7},{6,4},{7,5},{8,10},{9,11},{10,... | collective-permute-start | bytes 1572872 | tf_op jit(solution)/shard_map/ppermute | solution.py:371

commit v6 on v5

--- a/solution.py
+++ b/solution.py
@@ -11,8 +11,8 @@
 EPSILON = 1e-05
 NEG_FILL = -1e30
 MASKED = -2e38
-OWN_MIB = 14
-EARLIER_MIB = 14
+OWN_MIB = 16
+EARLIER_MIB = 16
 LOG2E = 1.4426950408889634
 
 BF16 = jnp.bfloat16
@@ -40,46 +40,43 @@
     return high, middle, value - high - middle
 
 
-def layer_norm(tokens, ln_gain, slopes):
-    rows, model = tokens.shape
-
-    def body(slopes_ref, tokens_hbm, gain_hbm, out_ref, long_ref, tokens_ref, gain_ref, sems):
-        loads = [pltpu.make_async_copy(tokens_hbm, tokens_ref, sems.at[0]),
-                 pltpu.make_async_copy(gain_hbm, gain_ref, sems.at[1])]
-        for copy in loads:
-            copy.start()
-        for copy in loads:
-            copy.wait()
-        inputs = tokens_ref[...].astype(F32)
-        centred = inputs - jnp.mean(inputs, axis=-1, keepdims=True)
-        variance = jnp.mean(centred * centred, axis=-1, keepdims=True)
-        normed = (centred * lax.rsqrt(variance + EPSILON) * gain_ref[...]).astype(BF16)
-        out_ref[...] = normed
-        long_ref[:rows, :] = normed
-        row = lax.broadcasted_iota(jnp.int32, (16, model), 0)
-        spread = jnp.zeros((16, model), F32)
+def normalise(tokens, gain):
+    inputs = tokens.astype(F32)
+    centred = inputs - jnp.mean(inputs, axis=-1, keepdims=True)
+    variance = jnp.mean(centred * centred, axis=-1, keepdims=True)
+    return (centred * lax.rsqrt(variance + EPSILON) * gain).astype(BF16)
+
+
+def count_back(slopes, seg, far_seg):
+    def body(slopes_ref, seg_ref, far_ref, out_ref):
+        there = lax.axis_index("seq") >= lax.axis_index("head") + 1
+        same = jnp.where((far_ref[...] == seg_ref[0:1, 0:1]) & there, 1, 0)
         for head in range(4):
-            spread = jnp.where(row % 4 == head, slopes_ref[head], spread)
-        high, middle, low = three_addends(spread)
-        part = jnp.where(row < 4, high, jnp.where(row < 8, middle, jnp.where(row < 12, low, 0.0)))
-        long_ref[pl.ds(rows, 16), :] = part.astype(BF16)
-
-    return pl.pallas_call(
-        body,
-        out_shape=(
-            jax.ShapeDtypeStruct((rows, model), BF16),
-            jax.ShapeDtypeStruct((rows + 16, model), BF16),
-        ),
-        in_specs=[SMEM, HBM, HBM],
-        out_specs=(VMEM, VMEM),
-        scratch_shapes=[
-            pltpu.VMEM((rows, model), BF16),
-            pltpu.VMEM((1, model), F32),
-            pltpu.SemaphoreType.DMA((2,)),
-        ],
-        compiler_params=params(8),
-        cost_estimate=cost(0, 2 * tokens.size * 2, tokens.size),
-    )(slopes, tokens, ln_gain.reshape(1, -1))
+            out_ref[head : head + 1, :] = jnp.full((1, PIECE), slopes_ref[head], F32)
+        out_ref[4:8, :] = jnp.full((4, PIECE), jnp.sum(same).astype(F32), F32)
+
+    return pl.pallas_call(
+        body,
+        out_shape=jax.ShapeDtypeStruct((8, PIECE), F32),
+        in_specs=[SMEM, VMEM, VMEM],
+        out_specs=VMEM,
+        compiler_params=params(4),
+        cost_estimate=cost(0, 2**13),
+    )(slopes, seg, far_seg)
+
+
+def add_counts(mine, other):
+    def body(mine_ref, other_ref, out_ref):
+        out_ref[...] = mine_ref[...] + other_ref[...]
+
+    return pl.pallas_call(
+        body,
+        out_shape=jax.ShapeDtypeStruct(mine.shape, F32),
+        in_specs=[VMEM, VMEM],
+        out_specs=VMEM,
+        compiler_params=params(4),
+        cost_estimate=cost(0, 2**13),
+    )(mine, other)
 
 
 def stage(weights):
@@ -158,13 +155,12 @@
             mask_ref[rows, pl.ds(place * PIECE, PIECE)] = jnp.where(kept, 0.0, MASKED)
 
 
-def attend(group, k_rows, v_t, q_ref, slopes_ref, mask_ref, dist_ref, before, stat_ref, acc_ref):
+def attend(k_rows, v_t, q_ref, slopes_ref, mask_ref, dist_ref, before, stat_ref, acc_ref):
     heads = k_rows.shape[1] // HD
     for head in range(heads):
         cols = slice(head * HD, (head + 1) * HD)
         wide = pl.ds(head * HD, HD)
-        place = heads * group + head
-        bias = dist_ref[...] * (slopes_ref[place : place + 1, :] * LOG2E)
+        bias = dist_ref[...] * (slopes_ref[head : head + 1, :] * LOG2E)
         bias = jnp.concatenate([bias] * (q_ref.shape[1] // PIECE), axis=1)
         scores = dot(k_rows[:, cols], q_ref[wide, :]) * (HD**-0.5 * LOG2E)
         scores = scores + bias + mask_ref[...]
@@ -187,47 +183,44 @@
     return (jax.ShapeDtypeStruct((8, block), F32), jax.ShapeDtypeStruct((width, block), F32))
 
 
-def own_block(slopes, seg, pieces, w_own, w_pair):
+def own_block(info, info_pair, seg, gain, pieces, w_own, w_pair):
     depth, width = w_own.shape[1:]
     block = 4 * PIECE
 
-    def body(s0, seg_ref, a, b, c, d, w0, w1, q0, q1, stat0, acc0, stat1, acc1, k_cache, v_cache, slopes_out,
-             mask, dist):
+    def body(s0, s1, seg_ref, gain_ref, a, b, c, d, w0, w1, q0, q1, stat0, acc0, stat1, acc1, k_cache, v_cache,
+             x, mask, dist):
         set_own_masks(seg_ref, mask, dist)
-        tail = c[PIECE : PIECE + 16, :PIECE].astype(F32)
-        for head in range(4):
-            slopes_out[head : head + 1, :] = jnp.full((1, PIECE), s0[head], F32)
-        slopes_out[4:8, :] = tail[0:4] + tail[4:8] + tail[8:12]
-        x = jnp.concatenate([a[...], b[...], c[:PIECE, :], d[...]], axis=0)
+        for place, piece in enumerate((a, b, c, d)):
+            x[pl.ds(place * PIECE, PIECE), :] = normalise(piece[...], gain_ref[...])
         for group, (w, q, stat, acc) in enumerate(((w0, q0, stat0, acc0), (w1, q1, stat1, acc1))):
             rows = block if group == 0 else 2 * PIECE
-            q[...] = dot(x, w[0]).T.astype(BF16)
-            keys = dot(x[:rows], w[1]).astype(BF16)
-            values = dot(x[:rows], w[2])
+            q[...] = dot(x[...], w[0]).T.astype(BF16)
+            keys = dot(x[:rows, :], w[1]).astype(BF16)
+            values = dot(x[:rows, :], w[2])
             if group == 0:
                 for place in range(4):
                     to = pl.ds(pl.multiple_of(place_of(place) * PIECE, PIECE), PIECE)
                     k_cache[to, :] = keys[place * PIECE : (place + 1) * PIECE]
                     v_cache[to, :] = values[place * PIECE : (place + 1) * PIECE].astype(BF16)
             v_t = values[: 2 * PIECE].T.astype(BF16)
-            attend(group, keys[: 2 * PIECE], v_t, q, slopes_out, mask, dist, None, stat, acc)
+            attend(keys[: 2 * PIECE], v_t, q, (s0, s1)[group], mask, dist, None, stat, acc)
 
     return pl.pallas_call(
         body,
         out_shape=(jax.ShapeDtypeStruct((width, block), BF16),) * 2 + state_shapes(width, block) * 2 + (
             jax.ShapeDtypeStruct((block, width), BF16),
             jax.ShapeDtypeStruct((block, width), BF16),
-            jax.ShapeDtypeStruct((8, PIECE), F32),
         ),
-        in_specs=[SMEM] + [VMEM] * 7,
-        out_specs=(VMEM,) * 9,
+        in_specs=[VMEM] * 10,
+        out_specs=(VMEM,) * 8,
         scratch_shapes=[
+            pltpu.VMEM((block, depth), BF16),
             pltpu.VMEM((2 * PIECE, block), F32),
             pltpu.VMEM((2 * PIECE, PIECE), F32),
         ],
         compiler_params=params(OWN_MIB),
         cost_estimate=cost(5 * block * depth * width, 2**20, 0),
-    )(slopes, seg, *pieces, w_own, w_pair)
+    )(info, info_pair, seg, gain, *pieces, w_own, w_pair)
 
 
 def write_closed(states, send_ref, lse_ref, out_ref):
@@ -252,26 +245,23 @@
     send_ref[pl.ds(2 * width, 32), :] = jnp.concatenate(parts, axis=0).astype(BF16)
 
 
-def earlier_pieces(which, closing, slopes8, seg, segs, pieces, w_own, w_pair, q_own, q_pair, state):
+def earlier_pieces(which, closing, infos, seg, gain, pieces, w_own, w_pair, q_own, q_pair, state):
     depth, width = w_own.shape[1:]
     block = 4 * PIECE
     count = len(pieces)
     rows = len(which) * PIECE
     n_out = 3 if closing else 4
 
-    def body(slopes_ref, seg_ref, *refs):
-        seg_refs, refs = refs[: len(segs)], refs[len(segs) :]
+    def body(s0, s1, rest_ref, seg_ref, gain_ref, *refs):
         sources, refs = refs[:count], refs[count:]
         (w0, w1, q0, q1), before, refs = refs[:4], (refs[4:6], refs[6:8]), refs[8:]
-        outs, (mask, dist, *inner) = refs[:n_out], refs[n_out:]
+        outs, (x, mask, dist, *inner) = refs[:n_out], refs[n_out:]
         after = inner if closing else outs
         after = (after[0:2], after[2:4])
         block_num = lax.axis_index("seq")
         block_base = block_num * block
-        same = jnp.zeros(seg_ref.shape, jnp.int32)
-        for back, ref in enumerate(seg_refs, 1):
-            same = same + jnp.where((ref[...] == seg_ref[0:1, 0:1]) & (block_num >= back), 1, 0)
-        start = block_base - jnp.sum(same)
+        counts = s0[4:5, :] + s1[4:5, :] + rest_ref[4:5, :]
+        start = block_base - jnp.max(counts).astype(jnp.int32)
 
         def key_base(i):
             def base(back, place):
@@ -286,11 +276,14 @@
         @pl.when(live)
         def _():
             set_earlier_masks(seg_ref, start, block_base, key_base, len(which), mask, dist)
-            x = jnp.concatenate([source[...] for source in sources], axis=0)
+            first = 0
+            for source in sources:
+                x[pl.ds(first, source.shape[0]), :] = normalise(source[...], gain_ref[...])
+                first += source.shape[0]
             for group, (w, q) in enumerate(((w0, q0), (w1, q1))):
-                keys = dot(x, w[1]).astype(BF16)
-                v_t = dot(x, w[2]).T.astype(BF16)
-                attend(group, keys, v_t, q, slopes_ref, mask, dist, before[group], *after[group])
+                keys = dot(x[...], w[1]).astype(BF16)
+                v_t = dot(x[...], w[2]).T.astype(BF16)
+                attend(keys, v_t, q, (s0, s1)[group], mask, dist, before[group], *after[group])
 
         @pl.when(jnp.logical_not(live))
         def _():
@@ -303,6 +296,7 @@
 
     shapes = state_shapes(width, block) * 2
     scratch = [
+        pltpu.VMEM((rows, depth), BF16),
         pltpu.VMEM((rows, block), F32),
         pltpu.VMEM((rows, PIECE), F32),
     ]
@@ -316,12 +310,12 @@
     return pl.pallas_call(
         body,
         out_shape=shapes,
-        in_specs=[VMEM] * (10 + len(segs) + count),
+        in_specs=[VMEM] * (13 + count),
         out_specs=(VMEM,) * n_out,
         scratch_shapes=scratch,
         compiler_params=params(EARLIER_MIB),
         cost_estimate=cost(4 * rows * depth * width, 2**20, 0),
-    )(slopes8, seg, *segs, *pieces, w_own, w_pair, q_own, q_pair, *state)
+    )(*infos, seg, gain, *pieces, w_own, w_pair, q_own, q_pair, *state)
 
 
 def project(place, lse, out, got, wo_own, wo_pair, tokens):
@@ -380,49 +374,51 @@
     tie = lax.optimization_barrier
     w_all = jnp.transpose(w_qkv, (1, 0, 2))
     seg = seg_ids.reshape(4, PIECE)
+    gain = ln_gain.reshape(1, -1)
     w_pair = over_core(w_all)
-    a0, a0_long = layer_norm(tokens, ln_gain, slopes)
-
-    a2 = over_seq(a0, two_on)
-    b0 = over_x(a0)
-    a1_odd = over_seq(a0, even_to_odd)
-    c0 = over_core(a0_long)
+
+    a2 = over_seq(tokens, two_on)
+    b0 = over_x(tokens)
+    a1_odd = over_seq(tokens, even_to_odd)
+    c0 = over_core(tokens)
     seg_sent, w_staged, c0 = tie((seg, w_all, c0))
     w_staged = stage(w_staged)
-    seg1 = over_seq(seg_sent, [(i, i + 1) for i in range(blocks - 1)])
-
-    a2, b0, a1_odd, w_pair, w_staged, seg1 = tie((a2, b0, a1_odd, w_pair, w_staged, seg1))
+    far_seg = lax.ppermute(
+        seg_sent, ("seq", "head"),
+        [(4 * i + head, 4 * (i + head + 1) + head) for head in range(SPAN) for i in range(blocks - head - 1)])
+    info = count_back(slopes, seg, far_seg)
+    info_pair = over_core(info)
+    infos = [info, info_pair, over_x(add_counts(info, info_pair))]
+
+    a2, b0, a1_odd, w_pair, w_staged, infos = tie((a2, b0, a1_odd, w_pair, w_staged, infos))
     a4 = over_seq(a2, two_on)
     b2 = over_x(a2)
     crossed = over_seq(a2, even_to_odd + odd_to_even)
     d0 = over_core(b0)
-    seg23 = over_seq(jnp.concatenate([seg, seg1], axis=0), two_on)
-    segs = [seg1, seg23[:4], seg23[4:]]
-    q_own, q_pair, *state, key_cache, value_cache, slopes8 = own_block(
-        slopes, seg, (a0, b0, c0, d0), w_staged, w_pair)
-
-    crossed, b2, a4, b0_sent, segs, wo_sent, state[0] = tie((crossed, b2, a4, b0, segs, w_out, state[0]))
+    q_own, q_pair, *state, key_cache, value_cache = own_block(
+        *infos[:2], seg, gain, (tokens, b0, c0, d0), w_staged, w_pair)
+
+    crossed, b2, a4, b0_sent, wo_sent, state[0] = tie((crossed, b2, a4, b0, w_out, state[0]))
     over_y = over_seq(pick(b0_sent, a4), even_to_odd + odd_to_even)
     x_third = over_x(crossed)
     b4 = over_seq(b2, two_on)
-    seg4 = over_seq(segs[1], two_on)
     wo_pair = over_core(wo_sent)
 
-    def merge(closing, segs, pieces, which, state):
+    def merge(closing, pieces, which, state):
         return earlier_pieces(
-            which, closing, slopes8, seg, segs, pieces, w_staged, w_pair, q_own, q_pair, state)
+            which, closing, infos, seg, gain, pieces, w_staged, w_pair, q_own, q_pair, state)
 
     state = merge(
-        False, segs, (a2, b2, crossed, a1_odd), (((2, 0),) * 2, ((2, 1),) * 2, ((1, 0), (3, 0)), ((0, 0), (1, 0))), state)
-
-    over_y, x_third, b4, seg4, held = tie((over_y, x_third, b4, seg4, state[0]))
-    segs = [*segs, seg4]
+        False, (a2, b2, a4, crossed, a1_odd),
+        (((2, 0),) * 2, ((2, 1),) * 2, ((4, 0),) * 2, ((1, 0), (3, 0)), ((0, 0), (1, 0))), state)
+
+    over_y, x_third, b4, held = tie((over_y, x_third, b4, state[0]))
     state = (held, *state[1:])
     b3_top = over_x(over_y[: PIECE // 2])
     b3_rest = over_seq(b4[PIECE // 2 :], odd_to_even)
     state = merge(
-        False, segs, (a4, b4, x_third, over_y), (((4, 0),) * 2, ((4, 1),) * 2, ((1, 1), (3, 1)), ((3, 0), (1, 1))), state)
-    send, lse, out = merge(True, segs, (b3_top, b3_rest), (((3, 1), (0, 0)),), state)
+        False, (b4, x_third, over_y), (((4, 1),) * 2, ((1, 1), (3, 1)), ((3, 0), (1, 1))), state)
+    send, lse, out = merge(True, (b3_top, b3_rest), (((3, 1), (0, 0)),), state)
     got = over_core(send)
     y_pair = project(1, lse, out, got, w_out, wo_pair, None)
     y_got = over_x(y_pair)

time: 94.4 us -> 95.1 us (level)
  starting transfers between devices: 33.7 us -> 29.6 us
  waiting for transfers between devices: 22.3 us -> 25.7 us
  Pallas kernels: 31 us -> 33.3 us
  local copies, waits for them, and re-layouts: 5.23 us -> 4.17 us
    ppermute x10 -> x7, starting transfers between devices: 27.1 us -> 17 us  [over_seq(): return lax.ppermute(value, 'seq', pairs)]
    ppermute x10 -> x7, waiting for transfers between devices: 6.6 us -> 1.72 us  [over_seq(): return lax.ppermute(value, 'seq', pairs)]
    ppermute x5 -> x6, waiting for transfers between devices: 2.67 us -> 7.36 us  [over_core(): return lax.ppermute(value, 'head', [(i, i ^ 1) for i in range(4)])]
    ppermute x0 -> x1, waiting for transfers between devices: none -> 3.76 us  [on_device(): lax.ppermute(seg_sent, ('seq', 'head'), [(4 * i + head, 4 * (i + head + 1...]
    ppermute x0 -> x1, starting transfers between devices: none -> 3.42 us  [on_device(): lax.ppermute(seg_sent, ('seq', 'head'), [(4 * i + head, 4 * (i + head + 1...]
    ppermute x5 -> x6, starting transfers between devices: 5.82 us -> 8.41 us  [over_x(): return lax.ppermute(value, 'head', [(i, i ^ 2) for i in range(4)])]
    pallas_call x4 -> x5, Pallas kernels: 19.5 us -> 21.2 us  [the longest x3 20.5 us: earlier_pieces(): pl.pallas_call(body, out_shape=shapes, in_specs=[VMEM] * (13 + count), ou...]
    unnamed x16 -> x14, local copies, waits for them, and re-layouts: 5.19 us -> 4.14 us
  transfers between devices with their start and end apart: 20 -> 20, of which waited for: 8 -> 9; matrix products, arithmetic and copies ran while one was open for 0% -> 0% of each run, Pallas kernels for 32% -> 34%
where the time goes in v6:
time: 95.1 us; the launch traced here: 94.6 us
  Pallas kernels  33.3 us (35%)
  starting transfers between devices  29.6 us (31%)
  waiting for transfers between devices  25.7 us (27%)
  local copies, waits for them, and re-layouts  4.17 us (4%)
    pallas_call x3, Pallas kernels, earlier_pieces(): pl.pallas_call(body, out_shape=shapes, in_specs=[VMEM] * (13 + count), ou...  20.5 us
    ppermute x7, starting transfers between devices, over_seq(): return lax.ppermute(value, 'seq', pairs)  17 us
    ppermute x6, waiting for transfers between devices, over_x(): return lax.ppermute(value, 'head', [(i, i ^ 2) for i in range(4)])  12.9 us
    pallas_call x1, Pallas kernels, own_block(): pl.pallas_call(body, out_shape=(jax.ShapeDtypeStruct((width, block), BF16...  9.95 us
    ppermute x6, starting transfers between devices, over_x(): return lax.ppermute(value, 'head', [(i, i ^ 2) for i in range(4)])  8.41 us
    ppermute x6, waiting for transfers between devices, over_core(): return lax.ppermute(value, 'head', [(i, i ^ 1) for i in range(4)])  7.36 us
    unnamed x14, local copies, waits for them, and re-layouts  4.14 us
    ppermute x1, waiting for transfers between devices, on_device(): lax.ppermute(seg_sent, ('seq', 'head'), [(4 * i + head, 4 * (i + head + 1...  3.76 us
  transfers between devices with their start and end apart: 20, of which 9 were waited for; matrix products, arithmetic and copies ran while one was open for 0% of the time, Pallas kernels for 34%

profile of v6, /device:TPU:12, one launch (start us, length us, event | category | flops | bytes accessed | tf_op | source)
XLA Modules:
  0.0 94.6 jit_solution(8076459645863507812)
XLA Ops:
  0.6 0.1 collective-permute-start.3
  0.7 0.5 collective-permute-start.4
  1.2 1.3 %collective-permute-start.2 = (bf16[128,2048]{1,0:T(8,128)(2,1)}, bf16[128,2048]{1,0:T(8,128)(2,1)S(1)}, u32[]{:S(2)}, u32[]{:S(2)}) collective-permute-start(bf16[128,2048]{1,0:T(8,128)(2,1)} %refs_0_.1), channel_id=1, source_target_pairs={{0,4},{8,12},{16,20},{24,28},{1,5},{9,13},{17,21},{25,29},{2,6},{1... | collective-permute-start | bytes 1572872 | tf_op jit(solution)/shard_map/ppermute | solution.py:368
  2.5 1.6 %collective-permute-start.1 = (bf16[128,2048]{1,0:T(8,128)(2,1)}, bf16[128,2048]{1,0:T(8,128)(2,1)S(1)}, u32[]{:S(2)}, u32[]{:S(2)}) collective-permute-start(bf16[128,2048]{1,0:T(8,128)(2,1)} %refs_0_.1), channel_id=1, source_target_pairs={{0,2},{1,3},{2,0},{3,1},{4,6},{5,7},{6,4},{7,5},{8,10},{9,11},{10,... | collective-permute-start | bytes 1572872 | tf_op jit(solution)/shard_map/ppermute | solution.py:365
  4.1 3.5 %collective-permute-start = (bf16[128,2048]{1,0:T(8,128)(2,1)}, bf16[128,2048]{1,0:T(8,128)(2,1)S(1)}, u32[]{:S(2)}, u32[]{:S(2)}) collective-permute-start(bf16[128,2048]{1,0:T(8,128)(2,1)} %refs_0_.1), channel_id=1, source_target_pairs={{0,8},{4,12},{8,16},{12,20},{16,24},{20,28},{1,9},{5,13},{9,17},{1... | collective-permute-start | bytes 1572872 | tf_op jit(solution)/shard_map/ppermute | solution.py:368
  7.5 4.3 %collective-permute-done.4.c = bf16[128,2048]{1,0:T(8,128)(2,1)S(1)} collective-permute-done((bf16[128,2048]{1,0:T(8,128)(2,1)}, bf16[128,2048]{1,0:T(8,128)(2,1)S(1)}, u32[]{:S(2)}, u32[]{:S(2)}) %collective-permute-start.4) | collective-permute-done | bytes 524320 | tf_op jit(solution)/shard_map/ppermute | solution.py:362
  11.8 3.4 %collective-permute-start.5 = (s32[4,128]{1,0:T(4,128)}, s32[4,128]{1,0:T(4,128)S(1)}, u32[]{:S(2)}, u32[]{:S(2)}) collective-permute-start(s32[4,128]{1,0:T(4,128)} %bitcast.9), channel_id=1, source_target_pairs={{0,4},{4,8},{8,12},{12,16},{16,20},{20,24},{24,28},{1,9},{5,13},{9... | collective-permute-start | bytes 6152 | tf_op jit(solution)/shard_map/ppermute | solution.py:386
  15.2 3.8 %collective-permute-done.5.far_ref = s32[4,128]{1,0:T(4,128)S(1)} collective-permute-done((s32[4,128]{1,0:T(4,128)}, s32[4,128]{1,0:T(4,128)S(1)}, u32[]{:S(2)}, u32[]{:S(2)}) %collective-permute-start.5) | collective-permute-done | bytes 2080 | tf_op jit(solution)/shard_map/ppermute | solution.py:386
  19.0 0.7 copy-done.4
  19.7 0.7 copy-done.6
  20.3 0.7 shard_map.86.mine_ref.s0
  21.0 0.1 collective-permute-start.6
  21.1 1.2 %collective-permute-done.6.other_ref.s1 = f32[8,128]{1,0:T(8,128)S(1)} collective-permute-done((f32[8,128]{1,0:T(8,128)S(1)}, f32[8,128]{1,0:T(8,128)S(1)}, u32[]{:S(2)}, u32[]{:S(2)}) %collective-permute-start.6) | collective-permute-done | bytes 4128 | tf_op jit(solution)/shard_map/ppermute | solution.py:362
  22.3 3.2 %collective-permute-start.7 = (f32[8,128]{1,0:T(8,128)S(1)}, f32[8,128]{1,0:T(8,128)S(1)}, u32[]{:S(2)}, u32[]{:S(2)}) collective-permute-start(f32[8,128]{1,0:T(8,128)S(1)} %shard_map.87), channel_id=1, source_target_pairs={{0,2},{1,3},{2,0},{3,1},{4,6},{5,7},{6,4},{7,5},{8,10},{9,11},{10,... | collective-permute-start | bytes 12296 | tf_op jit(solution)/shard_map/ppermute | solution.py:365
  25.5 2.8 %copy-done.1 = bf16[2048,3,512]{2,0,1:T(8,128)(2,1)S(1)} copy-done((bf16[2048,3,512]{2,0,1:T(8,128)(2,1)S(1)}, bf16[2048,3,512]{2,0,1:T(8,128)(2,1)}, u32[]{:S(2)}) %copy-start.1) | copy-done | bytes 6291480
  28.3 0.4 shard_map.85.w0.refs_5_.refs_3_.refs_2_
  28.7 0.0 collective-permute-done.2.refs_4_
  28.7 0.0 collective-permute-done.1.b.even_ref
  28.7 0.0 collective-permute-done.refs_0_
  28.7 0.0 collective-permute-done.7.rest_ref
  28.7 0.0 collective-permute-done.3.w1.refs_6_.refs_4_.refs_3_
  28.7 0.1 collective-permute-start.11
  28.8 3.5 %collective-permute-start.10 = (bf16[128,2048]{1,0:T(8,128)(2,1)S(1)}, bf16[128,2048]{1,0:T(8,128)(2,1)S(1)}, u32[]{:S(2)}, u32[]{:S(2)}) collective-permute-start(bf16[128,2048]{1,0:T(8,128)(2,1)S(1)} %collective-permute-done.refs_0_), channel_id=1, source_target_pairs={{0,8},{4,12},{8,16},{12,20},{16,24},{20,28},{1,9},{5,13},{9,17},{1... | collective-permute-start | bytes 1572872 | tf_op jit(solution)/shard_map/ppermute | solution.py:368
  32.3 0.3 collective-permute-start.9
  32.6 0.9 collective-permute-start.8
  33.5 0.0 copy-start
  33.5 10.0 %shard_map.88 = (bf16[512,512]{1,0:T(8,128)(2,1)S(1)}, bf16[512,512]{1,0:T(8,128)(2,1)S(1)}, f32[8,512]{1,0:T(8,128)S(1)}, f32[512,512]{1,0:T(8,128)S(1)}, f32[8...) custom-call(f32[8,128]{1,0:T(8,128)S(1)} %shard_map.86.mine_ref.s0, ...), custom_call_target="tpu_custom_call" | custom-call | flops 5368709120 | bytes 1048576 | tf_op jit(solution)/shard_map/pallas_call | solution.py:208
  43.5 1.5 %collective-permute-done.10.odd_ref.refs_2_ = bf16[128,2048]{1,0:T(8,128)(2,1)S(1)} collective-permute-done((bf16[128,2048]{1,0:T(8,128)(2,1)S(1)}, bf16[128,2048]{1,0:T(8,128)(2,1)S(1)}, u32[]{:S(2)}, u32[]{:S(2)}) %collective-permute-start.10) | collective-permute-done | bytes 524320 | tf_op jit(solution)/shard_map/ppermute | solution.py:368
  45.0 1.4 %collective-permute-done.9.refs_1_ = bf16[128,2048]{1,0:T(8,128)(2,1)S(1)} collective-permute-done((bf16[128,2048]{1,0:T(8,128)(2,1)S(1)}, bf16[128,2048]{1,0:T(8,128)(2,1)S(1)}, u32[]{:S(2)}, u32[]{:S(2)}) %collective-permute-start.9) | collective-permute-done | bytes 524320 | tf_op jit(solution)/shard_map/ppermute | solution.py:365
  46.4 0.1 collective-permute-done.8.refs_3_
  46.6 0.8 collective-permute-start.12
  47.4 1.2 %collective-permute-start.13 = (bf16[128,2048]{1,0:T(8,128)(2,1)S(1)}, bf16[128,2048]{1,0:T(8,128)(2,1)S(1)}, u32[]{:S(2)}, u32[]{:S(2)}) collective-permute-start(bf16[128,2048]{1,0:T(8,128)(2,1)S(1)} %collective-permute-done.8.refs_3_), channel_id=1, source_target_pairs={{0,2},{1,3},{2,0},{3,1},{4,6},{5,7},{6,4},{7,5},{8,10},{9,11},{10,... | collective-permute-start | bytes 1572872 | tf_op jit(solution)/shard_map/ppermute | solution.py:365
  48.6 3.5 %collective-permute-start.14 = (bf16[128,2048]{1,0:T(8,128)(2,1)S(1)}, bf16[128,2048]{1,0:T(8,128)(2,1)S(1)}, u32[]{:S(2)}, u32[]{:S(2)}) collective-permute-start(bf16[128,2048]{1,0:T(8,128)(2,1)S(1)} %collective-permute-done.9.refs_1_), channel_id=1, source_target_pairs={{0,8},{4,12},{8,16},{12,20},{16,24},{20,28},{1,9},{5,13},{9,17},{1... | collective-permute-start | bytes 1572872 | tf_op jit(solution)/shard_map/ppermute | solution.py:368
  52.0 12.2 %shard_map.90 = (f32[8,512]{1,0:T(8,128)S(1)}, f32[512,512]{1,0:T(8,128)S(1)}, f32[8,512]{1,0:T(8,128)S(1)}, f32[512,512]{1,0:T(8,128)S(1)}) custom-call(f32[8,128]{1,0:T(8,128)S(1)} %shard_map.86.mine_ref.s0, f32[8,128]{1,0:T(8,128)S(1)} %collective-permute-done.6.other_ref.s1, f32[8,128]{1,0:T(8,128)S(1)} %collective-permute-done.7.rest_ref, ...), custom_call_target="tpu_custom_call" | custom-call | flops 5368709120 | bytes 1048576 | tf_op jit(solution)/shard_map/pallas_call | solution.py:310
  64.2 0.0 collective-permute-done.13.refs_1_
  64.2 0.1 collective-permute-done.14.refs_0_
  64.4 3.6 %collective-permute-start.16 = (bf16[64,2048]{1,0:T(8,128)(2,1)S(1)}, bf16[64,2048]{1,0:T(8,128)(2,1)S(1)}, u32[]{:S(2)}, u32[]{:S(2)}) collective-permute-start(bf16[64,2048]{1,0:T(8,128)(2,1)S(1)} %slice.7), channel_id=1, source_target_pairs={{4,0},{12,8},{20,16},{28,24},{5,1},{13,9},{21,17},{29,25},{6,2},{1... | collective-permute-start | bytes 786440 | tf_op jit(solution)/shard_map/ppermute | solution.py:368
  68.0 0.4 collective-permute-start.15
  68.4 8.0 %shard_map.91 = (f32[8,512]{1,0:T(8,128)S(1)}, f32[512,512]{1,0:T(8,128)S(1)}, f32[8,512]{1,0:T(8,128)S(1)}, f32[512,512]{1,0:T(8,128)S(1)}) custom-call(f32[8,128]{1,0:T(8,128)S(1)} %shard_map.86.mine_ref.s0, f32[8,128]{1,0:T(8,128)S(1)} %collective-permute-done.6.other_ref.s1, f32[8,128]{1,0:T(8,128)S(1)} %collective-permute-done.7.rest_ref, ...), custom_call_target="tpu_custom_call" | custom-call | flops 3221225472 | bytes 1048576 | tf_op jit(solution)/shard_map/pallas_call | solution.py:310
  76.3 0.0 collective-permute-done.16.refs_1_
  76.4 0.4 shard_map.92
  76.8 0.1 collective-permute-start.17
  76.9 1.9 %collective-permute-done.17.got_ref = bf16[1056,256]{1,0:T(8,128)(2,1)S(1)} collective-permute-done((bf16[1056,256]{1,0:T(8,128)(2,1)S(1)}, bf16[1056,256]{1,0:T(8,128)(2,1)S(1)}, u32[]{:S(2)}, u32[]{:S(2)}) %collective-permute-start.17) | collective-permute-done | bytes 540704 | tf_op jit(solution)/shard_map/ppermute | solution.py:362
  78.8 0.8 shard_map.94
  79.6 1.7 %collective-permute-start.19 = (bf16[128,2048]{1,0:T(8,128)(2,1)S(1)}, bf16[128,2048]{1,0:T(8,128)(2,1)S(1)}, u32[]{:S(2)}, u32[]{:S(2)}) collective-permute-start(bf16[128,2048]{1,0:T(8,128)(2,1)S(1)} %shard_map.94), channel_id=1, source_target_pairs={{0,2},{1,3},{2,0},{3,1},{4,6},{5,7},{6,4},{7,5},{8,10},{9,11},{10,... | collective-permute-start | bytes 1572872 | tf_op jit(solution)/shard_map/ppermute | solution.py:365
  81.3 0.8 shard_map.93
  82.2 11.5 %collective-permute-done.19 = bf16[128,2048]{1,0:T(8,128)(2,1)S(1)} collective-permute-done((bf16[128,2048]{1,0:T(8,128)(2,1)S(1)}, bf16[128,2048]{1,0:T(8,128)(2,1)S(1)}, u32[]{:S(2)}, u32[]{:S(2)}) %collective-permute-start.19) | collective-permute-done | bytes 524320 | tf_op jit(solution)/shard_map/ppermute | solution.py:365
  93.7 0.9 add_convert_fusion
  (19 shorter events, 0.1 us)
Async XLA Ops:
  0.6 28.1 %collective-permute-start.3 = (bf16[3,2048,512]{2,1,0:T(8,128)(2,1)}, bf16[3,2048,512]{2,1,0:T(8,128)(2,1)S(1)}, u32[]{:S(2)}, u32[]{:S(2)}) collective-permute-start(bf16[3,2048,512]{2,1,0:T(8,128)(2,1)} %bitcast.3), channel_id=1, source_target_pairs={{0,1},{1,0},{2,3},{3,2},{4,5},{5,4},{6,7},{7,6},{8,9},{9,8},{10,11... | collective-permute-start | bytes 18874376 | tf_op jit(solution)/shard_map/ppermute | solution.py:362
  0.7 11.1 %collective-permute-start.4 = (bf16[128,2048]{1,0:T(8,128)(2,1)}, bf16[128,2048]{1,0:T(8,128)(2,1)S(1)}, u32[]{:S(2)}, u32[]{:S(2)}) collective-permute-start(bf16[128,2048]{1,0:T(8,128)(2,1)} %refs_0_.1), channel_id=1, source_target_pairs={{0,1},{1,0},{2,3},{3,2},{4,5},{5,4},{6,7},{7,6},{8,9},{9,8},{10,11... | collective-permute-start | bytes 1572872 | tf_op jit(solution)/shard_map/ppermute | solution.py:362
  1.2 27.5 %collective-permute-start.2 = (bf16[128,2048]{1,0:T(8,128)(2,1)}, bf16[128,2048]{1,0:T(8,128)(2,1)S(1)}, u32[]{:S(2)}, u32[]{:S(2)}) collective-permute-start(bf16[128,2048]{1,0:T(8,128)(2,1)} %refs_0_.1), channel_id=1, source_target_pairs={{0,4},{8,12},{16,20},{24,28},{1,5},{9,13},{17,21},{25,29},{2,6},{1... | collective-permute-start | bytes 1572872 | tf_op jit(solution)/shard_map/ppermute | solution.py:368
  2.5 26.2 %collective-permute-start.1 = (bf16[128,2048]{1,0:T(8,128)(2,1)}, bf16[128,2048]{1,0:T(8,128)(2,1)S(1)}, u32[]{:S(2)}, u32[]{:S(2)}) collective-permute-start(bf16[128,2048]{1,0:T(8,128)(2,1)} %refs_0_.1), channel_id=1, source_target_pairs={{0,2},{1,3},{2,0},{3,1},{4,6},{5,7},{6,4},{7,5},{8,10},{9,11},{10,... | collective-permute-start | bytes 1572872 | tf_op jit(solution)/shard_map/ppermute | solution.py:365
  4.1 24.7 %collective-permute-start = (bf16[128,2048]{1,0:T(8,128)(2,1)}, bf16[128,2048]{1,0:T(8,128)(2,1)S(1)}, u32[]{:S(2)}, u32[]{:S(2)}) collective-permute-start(bf16[128,2048]{1,0:T(8,128)(2,1)} %refs_0_.1), channel_id=1, source_target_pairs={{0,8},{4,12},{8,16},{12,20},{16,24},{20,28},{1,9},{5,13},{9,17},{1... | collective-permute-start | bytes 1572872 | tf_op jit(solution)/shard_map/ppermute | solution.py:368
  11.8 7.2 %collective-permute-start.5 = (s32[4,128]{1,0:T(4,128)}, s32[4,128]{1,0:T(4,128)S(1)}, u32[]{:S(2)}, u32[]{:S(2)}) collective-permute-start(s32[4,128]{1,0:T(4,128)} %bitcast.9), channel_id=1, source_target_pairs={{0,4},{4,8},{8,12},{12,16},{16,20},{20,24},{24,28},{1,9},{5,13},{9... | collective-permute-start | bytes 6152 | tf_op jit(solution)/shard_map/ppermute | solution.py:386
  19.0 0.7 copy-start.4
  19.7 0.7 copy-start.6
  21.0 1.2 %collective-permute-start.6 = (f32[8,128]{1,0:T(8,128)S(1)}, f32[8,128]{1,0:T(8,128)S(1)}, u32[]{:S(2)}, u32[]{:S(2)}) collective-permute-start(f32[8,128]{1,0:T(8,128)S(1)} %shard_map.86.mine_ref.s0), channel_id=1, source_target_pairs={{0,1},{1,0},{2,3},{3,2},{4,5},{5,4},{6,7},{7,6},{8,9},{9,8},{10,11... | collective-permute-start | bytes 12296 | tf_op jit(solution)/shard_map/ppermute | solution.py:362
  22.3 6.4 %collective-permute-start.7 = (f32[8,128]{1,0:T(8,128)S(1)}, f32[8,128]{1,0:T(8,128)S(1)}, u32[]{:S(2)}, u32[]{:S(2)}) collective-permute-start(f32[8,128]{1,0:T(8,128)S(1)} %shard_map.87), channel_id=1, source_target_pairs={{0,2},{1,3},{2,0},{3,1},{4,6},{5,7},{6,4},{7,5},{8,10},{9,11},{10,... | collective-permute-start | bytes 12296 | tf_op jit(solution)/shard_map/ppermute | solution.py:365
  25.5 2.8 %copy-start.1 = (bf16[2048,3,512]{2,0,1:T(8,128)(2,1)S(1)}, bf16[2048,3,512]{2,0,1:T(8,128)(2,1)}, u32[]{:S(2)}) copy-start(bf16[2048,3,512]{2,0,1:T(8,128)(2,1)} %param.8) | copy-start | bytes 18874372
  28.2 5.3 %copy-start.2 = (bf16[128,2048]{1,0:T(8,128)(2,1)S(1)}, bf16[128,2048]{1,0:T(8,128)(2,1)}, u32[]{:S(2)}) copy-start(bf16[128,2048]{1,0:T(8,128)(2,1)} %refs_0_.1) | copy-start | bytes 1572868
  28.2 5.3 %copy-start.3 = (f32[2048]{0:T(1024)S(1)}, f32[2048]{0:T(1024)}, u32[]{:S(2)}) copy-start(f32[2048]{0:T(1024)} %param.7) | copy-start | bytes 24580
  28.3 5.3 %copy-start.5 = (s32[512]{0:T(512)S(1)}, s32[512]{0:T(512)}, u32[]{:S(2)}) copy-start(s32[512]{0:T(512)} %param.11) | copy-start | bytes 6148
  28.7 4.8 %collective-permute-start.11 = (bf16[128,2048]{1,0:T(8,128)(2,1)S(1)}, bf16[128,2048]{1,0:T(8,128)(2,1)S(1)}, u32[]{:S(2)}, u32[]{:S(2)}) collective-permute-start(bf16[128,2048]{1,0:T(8,128)(2,1)S(1)} %collective-permute-done.1.b.even_ref), channel_id=1, source_target_pairs={{0,1},{1,0},{2,3},{3,2},{4,5},{5,4},{6,7},{7,6},{8,9},{9,8},{10,11... | collective-permute-start | bytes 1572872 | tf_op jit(solution)/shard_map/ppermute | solution.py:362
  28.8 16.2 %collective-permute-start.10 = (bf16[128,2048]{1,0:T(8,128)(2,1)S(1)}, bf16[128,2048]{1,0:T(8,128)(2,1)S(1)}, u32[]{:S(2)}, u32[]{:S(2)}) collective-permute-start(bf16[128,2048]{1,0:T(8,128)(2,1)S(1)} %collective-permute-done.refs_0_), channel_id=1, source_target_pairs={{0,8},{4,12},{8,16},{12,20},{16,24},{20,28},{1,9},{5,13},{9,17},{1... | collective-permute-start | bytes 1572872 | tf_op jit(solution)/shard_map/ppermute | solution.py:368
  32.3 14.1 %collective-permute-start.9 = (bf16[128,2048]{1,0:T(8,128)(2,1)S(1)}, bf16[128,2048]{1,0:T(8,128)(2,1)S(1)}, u32[]{:S(2)}, u32[]{:S(2)}) collective-permute-start(bf16[128,2048]{1,0:T(8,128)(2,1)S(1)} %collective-permute-done.refs_0_), channel_id=1, source_target_pairs={{0,2},{1,3},{2,0},{3,1},{4,6},{5,7},{6,4},{7,5},{8,10},{9,11},{10,... | collective-permute-start | bytes 1572872 | tf_op jit(solution)/shard_map/ppermute | solution.py:365
  32.6 13.9 %collective-permute-start.8 = (bf16[128,2048]{1,0:T(8,128)(2,1)S(1)}, bf16[128,2048]{1,0:T(8,128)(2,1)S(1)}, u32[]{:S(2)}, u32[]{:S(2)}) collective-permute-start(bf16[128,2048]{1,0:T(8,128)(2,1)S(1)} %collective-permute-done.refs_0_), channel_id=1, source_target_pairs={{0,4},{8,12},{16,20},{24,28},{4,0},{12,8},{20,16},{28,24},{1,5},{9... | collective-permute-start | bytes 1572872 | tf_op jit(solution)/shard_map/ppermute | solution.py:368
  33.5 13.0 %copy-start = (bf16[512,2048]{1,0:T(8,128)(2,1)S(1)}, bf16[512,2048]{1,0:T(8,128)(2,1)}, u32[]{:S(2)}) copy-start(bf16[512,2048]{1,0:T(8,128)(2,1)} %w0.3) | copy-start | bytes 6291460
  46.5 32.3 %collective-permute-start.18 = (bf16[512,2048]{1,0:T(8,128)(2,1)S(1)}, bf16[512,2048]{1,0:T(8,128)(2,1)S(1)}, u32[]{:S(2)}, u32[]{:S(2)}) collective-permute-start(bf16[512,2048]{1,0:T(8,128)(2,1)S(1)} %copy-done), channel_id=1, source_target_pairs={{0,1},{1,0},{2,3},{3,2},{4,5},{5,4},{6,7},{7,6},{8,9},{9,8},{10,11... | collective-permute-start | bytes 6291464 | tf_op jit(solution)/shard_map/ppermute | solution.py:362
  46.6 17.6 %collective-permute-start.12 = (bf16[128,2048]{1,0:T(8,128)(2,1)S(1)}, bf16[128,2048]{1,0:T(8,128)(2,1)S(1)}, u32[]{:S(2)}, u32[]{:S(2)}) collective-permute-start(bf16[128,2048]{1,0:T(8,128)(2,1)S(1)} %shard_map.89), channel_id=1, source_target_pairs={{0,4},{8,12},{16,20},{24,28},{4,0},{12,8},{20,16},{28,24},{1,5},{9... | collective-permute-start | bytes 1572872 | tf_op jit(solution)/shard_map/ppermute | solution.py:368
  47.4 16.8 %collective-permute-start.13 = (bf16[128,2048]{1,0:T(8,128)(2,1)S(1)}, bf16[128,2048]{1,0:T(8,128)(2,1)S(1)}, u32[]{:S(2)}, u32[]{:S(2)}) collective-permute-start(bf16[128,2048]{1,0:T(8,128)(2,1)S(1)} %collective-permute-done.8.refs_3_), channel_id=1, source_target_pairs={{0,2},{1,3},{2,0},{3,1},{4,6},{5,7},{6,4},{7,5},{8,10},{9,11},{10,... | collective-permute-start | bytes 1572872 | tf_op jit(solution)/shard_map/ppermute | solution.py:365
  48.6 15.7 %collective-permute-start.14 = (bf16[128,2048]{1,0:T(8,128)(2,1)S(1)}, bf16[128,2048]{1,0:T(8,128)(2,1)S(1)}, u32[]{:S(2)}, u32[]{:S(2)}) collective-permute-start(bf16[128,2048]{1,0:T(8,128)(2,1)S(1)} %collective-permute-done.9.refs_1_), channel_id=1, source_target_pairs={{0,8},{4,12},{8,16},{12,20},{16,24},{20,28},{1,9},{5,13},{9,17},{1... | collective-permute-start | bytes 1572872 | tf_op jit(solution)/shard_map/ppermute | solution.py:368
  64.4 12.0 %collective-permute-start.16 = (bf16[64,2048]{1,0:T(8,128)(2,1)S(1)}, bf16[64,2048]{1,0:T(8,128)(2,1)S(1)}, u32[]{:S(2)}, u32[]{:S(2)}) collective-permute-start(bf16[64,2048]{1,0:T(8,128)(2,1)S(1)} %slice.7), channel_id=1, source_target_pairs={{4,0},{12,8},{20,16},{28,24},{5,1},{13,9},{21,17},{29,25},{6,2},{1... | collective-permute-start | bytes 786440 | tf_op jit(solution)/shard_map/ppermute | solution.py:368
  68.0 8.4 %collective-permute-start.15 = (bf16[64,2048]{1,0:T(8,128)(2,1)S(1)}, bf16[64,2048]{1,0:T(8,128)(2,1)S(1)}, u32[]{:S(2)}, u32[]{:S(2)}) collective-permute-start(bf16[64,2048]{1,0:T(8,128)(2,1)S(1)} %slice.6), channel_id=1, source_target_pairs={{0,2},{1,3},{2,0},{3,1},{4,6},{5,7},{6,4},{7,5},{8,10},{9,11},{10,... | collective-permute-start | bytes 786440 | tf_op jit(solution)/shard_map/ppermute | solution.py:365
  76.8 2.0 %collective-permute-start.17 = (bf16[1056,256]{1,0:T(8,128)(2,1)S(1)}, bf16[1056,256]{1,0:T(8,128)(2,1)S(1)}, u32[]{:S(2)}, u32[]{:S(2)}) collective-permute-start(bf16[1056,256]{1,0:T(8,128)(2,1)S(1)} %get-tuple-element.79), channel_id=1, source_target_pairs={{0,1},{1,0},{2,3},{3,2},{4,5},{5,4},{6,7},{7,6},{8,9},{9,8},{10,11... | collective-permute-start | bytes 1622024 | tf_op jit(solution)/shard_map/ppermute | solution.py:362
  79.6 14.0 %collective-permute-start.19 = (bf16[128,2048]{1,0:T(8,128)(2,1)S(1)}, bf16[128,2048]{1,0:T(8,128)(2,1)S(1)}, u32[]{:S(2)}, u32[]{:S(2)}) collective-permute-start(bf16[128,2048]{1,0:T(8,128)(2,1)S(1)} %shard_map.94), channel_id=1, source_target_pairs={{0,2},{1,3},{2,0},{3,1},{4,6},{5,7},{6,4},{7,5},{8,10},{9,11},{10,... | collective-permute-start | bytes 1572872 | tf_op jit(solution)/shard_map/ppermute | solution.py:365

commit v7 on v6

--- a/solution.py
+++ b/solution.py
@@ -67,7 +67,8 @@
 
 def add_counts(mine, other):
     def body(mine_ref, other_ref, out_ref):
-        out_ref[...] = mine_ref[...] + other_ref[...]
+        out_ref[0:4, :] = mine_ref[0:4, :]
+        out_ref[4:8, :] = mine_ref[4:8, :] + other_ref[4:8, :]
 
     return pl.pallas_call(
         body,
@@ -252,7 +253,7 @@
     rows = len(which) * PIECE
     n_out = 3 if closing else 4
 
-    def body(s0, s1, rest_ref, seg_ref, gain_ref, *refs):
+    def body(s0, s1, seg_ref, gain_ref, *refs):
         sources, refs = refs[:count], refs[count:]
         (w0, w1, q0, q1), before, refs = refs[:4], (refs[4:6], refs[6:8]), refs[8:]
         outs, (x, mask, dist, *inner) = refs[:n_out], refs[n_out:]
@@ -260,7 +261,7 @@
         after = (after[0:2], after[2:4])
         block_num = lax.axis_index("seq")
         block_base = block_num * block
-        counts = s0[4:5, :] + s1[4:5, :] + rest_ref[4:5, :]
+        counts = s0[4:5, :] + s1[4:5, :]
         start = block_base - jnp.max(counts).astype(jnp.int32)
 
         def key_base(i):
@@ -310,7 +311,7 @@
     return pl.pallas_call(
         body,
         out_shape=shapes,
-        in_specs=[VMEM] * (13 + count),
+        in_specs=[VMEM] * (12 + count),
         out_specs=(VMEM,) * n_out,
         scratch_shapes=scratch,
         compiler_params=params(EARLIER_MIB),
@@ -375,20 +376,21 @@
     w_all = jnp.transpose(w_qkv, (1, 0, 2))
     seg = seg_ids.reshape(4, PIECE)
     gain = ln_gain.reshape(1, -1)
+    far_seg = lax.ppermute(
+        seg, ("seq", "head"),
+        [(4 * i + head, 4 * (i + head + 1) + head) for head in range(SPAN) for i in range(blocks - head - 1)])
     w_pair = over_core(w_all)
 
     a2 = over_seq(tokens, two_on)
     b0 = over_x(tokens)
     a1_odd = over_seq(tokens, even_to_odd)
     c0 = over_core(tokens)
-    seg_sent, w_staged, c0 = tie((seg, w_all, c0))
+    info = count_back(slopes, seg, far_seg)
+    info_x = over_x(info)
+    info_x, w_staged = tie((info_x, w_all))
     w_staged = stage(w_staged)
-    far_seg = lax.ppermute(
-        seg_sent, ("seq", "head"),
-        [(4 * i + head, 4 * (i + head + 1) + head) for head in range(SPAN) for i in range(blocks - head - 1)])
-    info = count_back(slopes, seg, far_seg)
-    info_pair = over_core(info)
-    infos = [info, info_pair, over_x(add_counts(info, info_pair))]
+    info = add_counts(info, info_x)
+    infos = [info, over_core(info)]
 
     a2, b0, a1_odd, w_pair, w_staged, infos = tie((a2, b0, a1_odd, w_pair, w_staged, infos))
     a4 = over_seq(a2, two_on)
@@ -396,7 +398,7 @@
     crossed = over_seq(a2, even_to_odd + odd_to_even)
     d0 = over_core(b0)
     q_own, q_pair, *state, key_cache, value_cache = own_block(
-        *infos[:2], seg, gain, (tokens, b0, c0, d0), w_staged, w_pair)
+        *infos, seg, gain, (tokens, b0, c0, d0), w_staged, w_pair)
 
     crossed, b2, a4, b0_sent, wo_sent, state[0] = tie((crossed, b2, a4, b0, w_out, state[0]))
     over_y = over_seq(pick(b0_sent, a4), even_to_odd + odd_to_even)

time: 95.1 us -> 99.3 us (1.044)
  starting transfers between devices: 29.6 us -> 31.5 us
    ppermute x6, waiting for transfers between devices: 7.36 us -> 1.93 us  [over_core(): return lax.ppermute(value, 'head', [(i, i ^ 1) for i in range(4)])]
    ppermute x6, waiting for transfers between devices: 12.9 us -> 16 us  [over_x(): return lax.ppermute(value, 'head', [(i, i ^ 2) for i in range(4)])]
    ppermute x1, waiting for transfers between devices: 3.76 us -> 6.26 us  [on_device(): lax.ppermute(seg, ('seq', 'head'), [(4 * i + head, 4 * (i + head + 1) + h...]
    ppermute x1, starting transfers between devices: 3.42 us -> 5.6 us  [on_device(): lax.ppermute(seg, ('seq', 'head'), [(4 * i + head, 4 * (i + head + 1) + h...]
    ppermute x7, starting transfers between devices: 17 us -> 15.3 us  [over_seq(): return lax.ppermute(value, 'seq', pairs)]
    ppermute x6, starting transfers between devices: 8.41 us -> 9.86 us  [over_x(): return lax.ppermute(value, 'head', [(i, i ^ 2) for i in range(4)])]
  transfers between devices with their start and end apart: 20 -> 20, of which waited for: 9 -> 7; matrix products, arithmetic and copies ran while one was open for 0% -> 0% of each run, Pallas kernels for 34% -> 34%
where the time goes in v7:
time: 99.3 us; the launch traced here: 97.9 us
  Pallas kernels  33.7 us (34%)
  starting transfers between devices  31.5 us (32%)
  waiting for transfers between devices  26.1 us (26%)
  local copies, waits for them, and re-layouts  4.76 us (5%)
    pallas_call x3, Pallas kernels, earlier_pieces(): pl.pallas_call(body, out_shape=shapes, in_specs=[VMEM] * (12 + count), ou...  20.7 us
    ppermute x6, waiting for transfers between devices, over_x(): return lax.ppermute(value, 'head', [(i, i ^ 2) for i in range(4)])  16 us
    ppermute x7, starting transfers between devices, over_seq(): return lax.ppermute(value, 'seq', pairs)  15.3 us
    pallas_call x1, Pallas kernels, own_block(): pl.pallas_call(body, out_shape=(jax.ShapeDtypeStruct((width, block), BF16...  10.1 us
    ppermute x6, starting transfers between devices, over_x(): return lax.ppermute(value, 'head', [(i, i ^ 2) for i in range(4)])  9.86 us
    ppermute x1, waiting for transfers between devices, on_device(): lax.ppermute(seg, ('seq', 'head'), [(4 * i + head, 4 * (i + head + 1) + h...  6.26 us
    ppermute x1, starting transfers between devices, on_device(): lax.ppermute(seg, ('seq', 'head'), [(4 * i + head, 4 * (i + head + 1) + h...  5.6 us
    unnamed x14, local copies, waits for them, and re-layouts  4.72 us
  transfers between devices with their start and end apart: 20, of which 7 were waited for; matrix products, arithmetic and copies ran while one was open for 0% of the time, Pallas kernels for 34%

profile of v7, /device:TPU:12, one launch (start us, length us, event | category | flops | bytes accessed | tf_op | source)
XLA Modules:
  0.0 97.9 jit_solution(654685211085198958)
XLA Ops:
  0.6 0.1 collective-permute-start.3
  0.7 1.3 %collective-permute-start.2 = (bf16[128,2048]{1,0:T(8,128)(2,1)}, bf16[128,2048]{1,0:T(8,128)(2,1)S(1)}, u32[]{:S(2)}, u32[]{:S(2)}) collective-permute-start(bf16[128,2048]{1,0:T(8,128)(2,1)} %refs_0_.1), channel_id=1, source_target_pairs={{0,4},{8,12},{16,20},{24,28},{1,5},{9,13},{17,21},{25,29},{2,6},{1... | collective-permute-start | bytes 1572872 | tf_op jit(solution)/shard_map/ppermute | solution.py:369
  2.0 1.6 %collective-permute-start.1 = (bf16[128,2048]{1,0:T(8,128)(2,1)}, bf16[128,2048]{1,0:T(8,128)(2,1)S(1)}, u32[]{:S(2)}, u32[]{:S(2)}) collective-permute-start(bf16[128,2048]{1,0:T(8,128)(2,1)} %refs_0_.1), channel_id=1, source_target_pairs={{0,2},{1,3},{2,0},{3,1},{4,6},{5,7},{6,4},{7,5},{8,10},{9,11},{10,... | collective-permute-start | bytes 1572872 | tf_op jit(solution)/shard_map/ppermute | solution.py:366
  3.6 3.5 %collective-permute-start = (bf16[128,2048]{1,0:T(8,128)(2,1)}, bf16[128,2048]{1,0:T(8,128)(2,1)S(1)}, u32[]{:S(2)}, u32[]{:S(2)}) collective-permute-start(bf16[128,2048]{1,0:T(8,128)(2,1)} %refs_0_.1), channel_id=1, source_target_pairs={{0,8},{4,12},{8,16},{12,20},{16,24},{20,28},{1,9},{5,13},{9,17},{1... | collective-permute-start | bytes 1572872 | tf_op jit(solution)/shard_map/ppermute | solution.py:369
  7.0 5.6 %collective-permute-start.4 = (s32[4,128]{1,0:T(4,128)}, s32[4,128]{1,0:T(4,128)S(1)}, u32[]{:S(2)}, u32[]{:S(2)}) collective-permute-start(s32[4,128]{1,0:T(4,128)} %bitcast.9), channel_id=1, source_target_pairs={{0,4},{4,8},{8,12},{12,16},{16,20},{20,24},{24,28},{1,9},{5,13},{9... | collective-permute-start | bytes 6152 | tf_op jit(solution)/shard_map/ppermute | solution.py:379
  12.7 6.3 %collective-permute-done.4.far_ref = s32[4,128]{1,0:T(4,128)S(1)} collective-permute-done((s32[4,128]{1,0:T(4,128)}, s32[4,128]{1,0:T(4,128)S(1)}, u32[]{:S(2)}, u32[]{:S(2)}) %collective-permute-start.4) | collective-permute-done | bytes 2080 | tf_op jit(solution)/shard_map/ppermute | solution.py:379
  18.9 0.7 copy-done.4
  19.6 0.7 copy-done.6
  20.3 0.7 shard_map.85.mine_ref
  21.0 3.3 %collective-permute-start.5 = (f32[8,128]{1,0:T(8,128)S(1)}, f32[8,128]{1,0:T(8,128)S(1)}, u32[]{:S(2)}, u32[]{:S(2)}) collective-permute-start(f32[8,128]{1,0:T(8,128)S(1)} %shard_map.85.mine_ref), channel_id=1, source_target_pairs={{0,2},{1,3},{2,0},{3,1},{4,6},{5,7},{6,4},{7,5},{8,10},{9,11},{10,... | collective-permute-start | bytes 12296 | tf_op jit(solution)/shard_map/ppermute | solution.py:366
  24.2 1.6 %collective-permute-done.5.other_ref = f32[8,128]{1,0:T(8,128)S(1)} collective-permute-done((f32[8,128]{1,0:T(8,128)S(1)}, f32[8,128]{1,0:T(8,128)S(1)}, u32[]{:S(2)}, u32[]{:S(2)}) %collective-permute-start.5) | collective-permute-done | bytes 4128 | tf_op jit(solution)/shard_map/ppermute | solution.py:366
  25.8 0.0 collective-permute-start.6
  25.8 2.8 %copy-done.1 = bf16[2048,3,512]{2,0,1:T(8,128)(2,1)S(1)} copy-done((bf16[2048,3,512]{2,0,1:T(8,128)(2,1)S(1)}, bf16[2048,3,512]{2,0,1:T(8,128)(2,1)}, u32[]{:S(2)}) %copy-start.1) | copy-done | bytes 6291480
  28.6 0.4 shard_map.86.w0.refs_5_.refs_3_.refs_2_
  29.0 0.0 collective-permute-done.6.s1
  29.0 0.6 copy-done.2
  29.6 0.5 collective-permute-start.10
  30.1 0.0 collective-permute-done.2.refs_4_
  30.1 0.0 collective-permute-done.1.b.even_ref
  30.1 0.0 collective-permute-done.refs_0_
  30.2 0.1 collective-permute-start.11
  30.2 3.5 %collective-permute-start.9 = (bf16[128,2048]{1,0:T(8,128)(2,1)S(1)}, bf16[128,2048]{1,0:T(8,128)(2,1)S(1)}, u32[]{:S(2)}, u32[]{:S(2)}) collective-permute-start(bf16[128,2048]{1,0:T(8,128)(2,1)S(1)} %collective-permute-done.refs_0_), channel_id=1, source_target_pairs={{0,8},{4,12},{8,16},{12,20},{16,24},{20,28},{1,9},{5,13},{9,17},{1... | collective-permute-start | bytes 1572872 | tf_op jit(solution)/shard_map/ppermute | solution.py:369
  33.8 2.1 %collective-permute-start.8 = (bf16[128,2048]{1,0:T(8,128)(2,1)S(1)}, bf16[128,2048]{1,0:T(8,128)(2,1)S(1)}, u32[]{:S(2)}, u32[]{:S(2)}) collective-permute-start(bf16[128,2048]{1,0:T(8,128)(2,1)S(1)} %collective-permute-done.refs_0_), channel_id=1, source_target_pairs={{0,2},{1,3},{2,0},{3,1},{4,6},{5,7},{6,4},{7,5},{8,10},{9,11},{10,... | collective-permute-start | bytes 1572872 | tf_op jit(solution)/shard_map/ppermute | solution.py:366
  35.8 0.0 collective-permute-done.10.c
  35.8 0.0 collective-permute-done.11.d
  35.9 0.0 copy-start
  35.9 10.1 %shard_map.88 = (bf16[512,512]{1,0:T(8,128)(2,1)S(1)}, bf16[512,512]{1,0:T(8,128)(2,1)S(1)}, f32[8,512]{1,0:T(8,128)S(1)}, f32[512,512]{1,0:T(8,128)S(1)}, f32[8...) custom-call(f32[8,128]{1,0:T(8,128)S(1)} %shard_map.87.s0, ...), custom_call_target="tpu_custom_call" | custom-call | flops 5368709120 | bytes 1048576 | tf_op jit(solution)/shard_map/pallas_call | solution.py:209
  46.0 0.4 collective-permute-done.9.odd_ref.refs_2_
  46.5 1.7 %collective-permute-done.8.refs_1_ = bf16[128,2048]{1,0:T(8,128)(2,1)S(1)} collective-permute-done((bf16[128,2048]{1,0:T(8,128)(2,1)S(1)}, bf16[128,2048]{1,0:T(8,128)(2,1)S(1)}, u32[]{:S(2)}, u32[]{:S(2)}) %collective-permute-start.8) | collective-permute-done | bytes 524320 | tf_op jit(solution)/shard_map/ppermute | solution.py:366
  48.1 1.5 %collective-permute-done.7.refs_3_ = bf16[128,2048]{1,0:T(8,128)(2,1)S(1)} collective-permute-done((bf16[128,2048]{1,0:T(8,128)(2,1)S(1)}, bf16[128,2048]{1,0:T(8,128)(2,1)S(1)}, u32[]{:S(2)}, u32[]{:S(2)}) %collective-permute-start.7) | collective-permute-done | bytes 524320 | tf_op jit(solution)/shard_map/ppermute | solution.py:369
  49.6 0.3 collective-permute-start.12
  50.0 0.8 collective-permute-start.13
  50.8 3.5 %collective-permute-start.14 = (bf16[128,2048]{1,0:T(8,128)(2,1)S(1)}, bf16[128,2048]{1,0:T(8,128)(2,1)S(1)}, u32[]{:S(2)}, u32[]{:S(2)}) collective-permute-start(bf16[128,2048]{1,0:T(8,128)(2,1)S(1)} %collective-permute-done.8.refs_1_), channel_id=1, source_target_pairs={{0,8},{4,12},{8,16},{12,20},{16,24},{20,28},{1,9},{5,13},{9,17},{1... | collective-permute-start | bytes 1572872 | tf_op jit(solution)/shard_map/ppermute | solution.py:369
  54.3 12.3 %shard_map.90 = (f32[8,512]{1,0:T(8,128)S(1)}, f32[512,512]{1,0:T(8,128)S(1)}, f32[8,512]{1,0:T(8,128)S(1)}, f32[512,512]{1,0:T(8,128)S(1)}) custom-call(f32[8,128]{1,0:T(8,128)S(1)} %shard_map.87.s0, f32[8,128]{1,0:T(8,128)S(1)} %collective-permute-done.6.s1, s32[4,128]{1,0:T(4,128)S(1)} %bitcast.12, f32[1,2048]{1,0:T(1,128)S(1)} %bitcast.6, ...), custom_call_target="tpu_custom_call" | custom-call | flops 5368709120 | bytes 1048576 | tf_op jit(solution)/shard_map/pallas_call | solution.py:311
  66.6 0.0 collective-permute-done.12.refs_2_
  66.6 0.0 collective-permute-done.14.refs_0_
  66.7 3.2 %collective-permute-start.16 = (bf16[64,2048]{1,0:T(8,128)(2,1)S(1)}, bf16[64,2048]{1,0:T(8,128)(2,1)S(1)}, u32[]{:S(2)}, u32[]{:S(2)}) collective-permute-start(bf16[64,2048]{1,0:T(8,128)(2,1)S(1)} %slice.7), channel_id=1, source_target_pairs={{4,0},{12,8},{20,16},{28,24},{5,1},{13,9},{21,17},{29,25},{6,2},{1... | collective-permute-start | bytes 786440 | tf_op jit(solution)/shard_map/ppermute | solution.py:369
  69.8 1.7 %collective-permute-start.15 = (bf16[64,2048]{1,0:T(8,128)(2,1)S(1)}, bf16[64,2048]{1,0:T(8,128)(2,1)S(1)}, u32[]{:S(2)}, u32[]{:S(2)}) collective-permute-start(bf16[64,2048]{1,0:T(8,128)(2,1)S(1)} %slice.6), channel_id=1, source_target_pairs={{0,2},{1,3},{2,0},{3,1},{4,6},{5,7},{6,4},{7,5},{8,10},{9,11},{10,... | collective-permute-start | bytes 786440 | tf_op jit(solution)/shard_map/ppermute | solution.py:366
  71.6 8.1 %shard_map.91 = (f32[8,512]{1,0:T(8,128)S(1)}, f32[512,512]{1,0:T(8,128)S(1)}, f32[8,512]{1,0:T(8,128)S(1)}, f32[512,512]{1,0:T(8,128)S(1)}) custom-call(f32[8,128]{1,0:T(8,128)S(1)} %shard_map.87.s0, f32[8,128]{1,0:T(8,128)S(1)} %collective-permute-done.6.s1, s32[4,128]{1,0:T(4,128)S(1)} %bitcast.13, f32[1,2048]{1,0:T(1,128)S(1)} %bitcast.7, ...), custom_call_target="tpu_custom_call" | custom-call | flops 3221225472 | bytes 1048576 | tf_op jit(solution)/shard_map/pallas_call | solution.py:311
  79.6 0.0 collective-permute-done.15.refs_0_
  79.6 0.4 shard_map.92
  80.1 0.1 collective-permute-start.17
  80.1 1.9 %collective-permute-done.17.got_ref = bf16[1056,256]{1,0:T(8,128)(2,1)S(1)} collective-permute-done((bf16[1056,256]{1,0:T(8,128)(2,1)S(1)}, bf16[1056,256]{1,0:T(8,128)(2,1)S(1)}, u32[]{:S(2)}, u32[]{:S(2)}) %collective-permute-start.17) | collective-permute-done | bytes 540704 | tf_op jit(solution)/shard_map/ppermute | solution.py:363
  82.1 0.8 shard_map.94
  82.9 0.4 collective-permute-start.19
  83.3 0.8 shard_map.93
  84.2 12.8 %collective-permute-done.19 = bf16[128,2048]{1,0:T(8,128)(2,1)S(1)} collective-permute-done((bf16[128,2048]{1,0:T(8,128)(2,1)S(1)}, bf16[128,2048]{1,0:T(8,128)(2,1)S(1)}, u32[]{:S(2)}, u32[]{:S(2)}) %collective-permute-start.19) | collective-permute-done | bytes 524320 | tf_op jit(solution)/shard_map/ppermute | solution.py:366
  96.9 0.9 add_convert_fusion
  (19 shorter events, 0.1 us)
Async XLA Ops:
  0.6 29.5 %collective-permute-start.3 = (bf16[3,2048,512]{2,1,0:T(8,128)(2,1)}, bf16[3,2048,512]{2,1,0:T(8,128)(2,1)S(1)}, u32[]{:S(2)}, u32[]{:S(2)}) collective-permute-start(bf16[3,2048,512]{2,1,0:T(8,128)(2,1)} %bitcast.3), channel_id=1, source_target_pairs={{0,1},{1,0},{2,3},{3,2},{4,5},{5,4},{6,7},{7,6},{8,9},{9,8},{10,11... | collective-permute-start | bytes 18874376 | tf_op jit(solution)/shard_map/ppermute | solution.py:363
  0.7 29.4 %collective-permute-start.2 = (bf16[128,2048]{1,0:T(8,128)(2,1)}, bf16[128,2048]{1,0:T(8,128)(2,1)S(1)}, u32[]{:S(2)}, u32[]{:S(2)}) collective-permute-start(bf16[128,2048]{1,0:T(8,128)(2,1)} %refs_0_.1), channel_id=1, source_target_pairs={{0,4},{8,12},{16,20},{24,28},{1,5},{9,13},{17,21},{25,29},{2,6},{1... | collective-permute-start | bytes 1572872 | tf_op jit(solution)/shard_map/ppermute | solution.py:369
  2.0 28.1 %collective-permute-start.1 = (bf16[128,2048]{1,0:T(8,128)(2,1)}, bf16[128,2048]{1,0:T(8,128)(2,1)S(1)}, u32[]{:S(2)}, u32[]{:S(2)}) collective-permute-start(bf16[128,2048]{1,0:T(8,128)(2,1)} %refs_0_.1), channel_id=1, source_target_pairs={{0,2},{1,3},{2,0},{3,1},{4,6},{5,7},{6,4},{7,5},{8,10},{9,11},{10,... | collective-permute-start | bytes 1572872 | tf_op jit(solution)/shard_map/ppermute | solution.py:366
  3.6 26.6 %collective-permute-start = (bf16[128,2048]{1,0:T(8,128)(2,1)}, bf16[128,2048]{1,0:T(8,128)(2,1)S(1)}, u32[]{:S(2)}, u32[]{:S(2)}) collective-permute-start(bf16[128,2048]{1,0:T(8,128)(2,1)} %refs_0_.1), channel_id=1, source_target_pairs={{0,8},{4,12},{8,16},{12,20},{16,24},{20,28},{1,9},{5,13},{9,17},{1... | collective-permute-start | bytes 1572872 | tf_op jit(solution)/shard_map/ppermute | solution.py:369
  7.0 11.9 %collective-permute-start.4 = (s32[4,128]{1,0:T(4,128)}, s32[4,128]{1,0:T(4,128)S(1)}, u32[]{:S(2)}, u32[]{:S(2)}) collective-permute-start(s32[4,128]{1,0:T(4,128)} %bitcast.9), channel_id=1, source_target_pairs={{0,4},{4,8},{8,12},{12,16},{16,20},{20,24},{24,28},{1,9},{5,13},{9... | collective-permute-start | bytes 6152 | tf_op jit(solution)/shard_map/ppermute | solution.py:379
  18.9 0.7 copy-start.4
  19.6 0.7 copy-start.6
  21.0 4.8 %collective-permute-start.5 = (f32[8,128]{1,0:T(8,128)S(1)}, f32[8,128]{1,0:T(8,128)S(1)}, u32[]{:S(2)}, u32[]{:S(2)}) collective-permute-start(f32[8,128]{1,0:T(8,128)S(1)} %shard_map.85.mine_ref), channel_id=1, source_target_pairs={{0,2},{1,3},{2,0},{3,1},{4,6},{5,7},{6,4},{7,5},{8,10},{9,11},{10,... | collective-permute-start | bytes 12296 | tf_op jit(solution)/shard_map/ppermute | solution.py:366
  25.8 3.2 %collective-permute-start.6 = (f32[8,128]{1,0:T(8,128)S(1)}, f32[8,128]{1,0:T(8,128)S(1)}, u32[]{:S(2)}, u32[]{:S(2)}) collective-permute-start(f32[8,128]{1,0:T(8,128)S(1)} %shard_map.87.s0), channel_id=1, source_target_pairs={{0,1},{1,0},{2,3},{3,2},{4,5},{5,4},{6,7},{7,6},{8,9},{9,8},{10,11... | collective-permute-start | bytes 12296 | tf_op jit(solution)/shard_map/ppermute | solution.py:363
  25.8 2.8 %copy-start.1 = (bf16[2048,3,512]{2,0,1:T(8,128)(2,1)S(1)}, bf16[2048,3,512]{2,0,1:T(8,128)(2,1)}, u32[]{:S(2)}) copy-start(bf16[2048,3,512]{2,0,1:T(8,128)(2,1)} %param.8) | copy-start | bytes 18874372
  28.6 1.0 %copy-start.2 = (bf16[128,2048]{1,0:T(8,128)(2,1)S(1)}, bf16[128,2048]{1,0:T(8,128)(2,1)}, u32[]{:S(2)}) copy-start(bf16[128,2048]{1,0:T(8,128)(2,1)} %refs_0_.1) | copy-start | bytes 1572868
  28.6 7.3 %copy-start.3 = (f32[2048]{0:T(1024)S(1)}, f32[2048]{0:T(1024)}, u32[]{:S(2)}) copy-start(f32[2048]{0:T(1024)} %param.7) | copy-start | bytes 24580
  28.6 7.3 %copy-start.5 = (s32[512]{0:T(512)S(1)}, s32[512]{0:T(512)}, u32[]{:S(2)}) copy-start(s32[512]{0:T(512)} %param.11) | copy-start | bytes 6148
  29.6 6.2 %collective-permute-start.10 = (bf16[128,2048]{1,0:T(8,128)(2,1)S(1)}, bf16[128,2048]{1,0:T(8,128)(2,1)S(1)}, u32[]{:S(2)}, u32[]{:S(2)}) collective-permute-start(bf16[128,2048]{1,0:T(8,128)(2,1)S(1)} %copy-done.2), channel_id=1, source_target_pairs={{0,1},{1,0},{2,3},{3,2},{4,5},{5,4},{6,7},{7,6},{8,9},{9,8},{10,11... | collective-permute-start | bytes 1572872 | tf_op jit(solution)/shard_map/ppermute | solution.py:363
  30.2 5.7 %collective-permute-start.11 = (bf16[128,2048]{1,0:T(8,128)(2,1)S(1)}, bf16[128,2048]{1,0:T(8,128)(2,1)S(1)}, u32[]{:S(2)}, u32[]{:S(2)}) collective-permute-start(bf16[128,2048]{1,0:T(8,128)(2,1)S(1)} %collective-permute-done.1.b.even_ref), channel_id=1, source_target_pairs={{0,1},{1,0},{2,3},{3,2},{4,5},{5,4},{6,7},{7,6},{8,9},{9,8},{10,11... | collective-permute-start | bytes 1572872 | tf_op jit(solution)/shard_map/ppermute | solution.py:363
  30.2 16.2 %collective-permute-start.9 = (bf16[128,2048]{1,0:T(8,128)(2,1)S(1)}, bf16[128,2048]{1,0:T(8,128)(2,1)S(1)}, u32[]{:S(2)}, u32[]{:S(2)}) collective-permute-start(bf16[128,2048]{1,0:T(8,128)(2,1)S(1)} %collective-permute-done.refs_0_), channel_id=1, source_target_pairs={{0,8},{4,12},{8,16},{12,20},{16,24},{20,28},{1,9},{5,13},{9,17},{1... | collective-permute-start | bytes 1572872 | tf_op jit(solution)/shard_map/ppermute | solution.py:369
  33.8 14.4 %collective-permute-start.8 = (bf16[128,2048]{1,0:T(8,128)(2,1)S(1)}, bf16[128,2048]{1,0:T(8,128)(2,1)S(1)}, u32[]{:S(2)}, u32[]{:S(2)}) collective-permute-start(bf16[128,2048]{1,0:T(8,128)(2,1)S(1)} %collective-permute-done.refs_0_), channel_id=1, source_target_pairs={{0,2},{1,3},{2,0},{3,1},{4,6},{5,7},{6,4},{7,5},{8,10},{9,11},{10,... | collective-permute-start | bytes 1572872 | tf_op jit(solution)/shard_map/ppermute | solution.py:366
  35.8 13.8 %collective-permute-start.7 = (bf16[128,2048]{1,0:T(8,128)(2,1)S(1)}, bf16[128,2048]{1,0:T(8,128)(2,1)S(1)}, u32[]{:S(2)}, u32[]{:S(2)}) collective-permute-start(bf16[128,2048]{1,0:T(8,128)(2,1)S(1)} %collective-permute-done.refs_0_), channel_id=1, source_target_pairs={{0,4},{8,12},{16,20},{24,28},{4,0},{12,8},{20,16},{28,24},{1,5},{9... | collective-permute-start | bytes 1572872 | tf_op jit(solution)/shard_map/ppermute | solution.py:369
  35.9 13.7 %copy-start = (bf16[512,2048]{1,0:T(8,128)(2,1)S(1)}, bf16[512,2048]{1,0:T(8,128)(2,1)}, u32[]{:S(2)}) copy-start(bf16[512,2048]{1,0:T(8,128)(2,1)} %w0.3) | copy-start | bytes 6291460
  49.6 32.5 %collective-permute-start.18 = (bf16[512,2048]{1,0:T(8,128)(2,1)S(1)}, bf16[512,2048]{1,0:T(8,128)(2,1)S(1)}, u32[]{:S(2)}, u32[]{:S(2)}) collective-permute-start(bf16[512,2048]{1,0:T(8,128)(2,1)S(1)} %copy-done), channel_id=1, source_target_pairs={{0,1},{1,0},{2,3},{3,2},{4,5},{5,4},{6,7},{7,6},{8,9},{9,8},{10,11... | collective-permute-start | bytes 6291464 | tf_op jit(solution)/shard_map/ppermute | solution.py:363
  49.6 16.9 %collective-permute-start.12 = (bf16[128,2048]{1,0:T(8,128)(2,1)S(1)}, bf16[128,2048]{1,0:T(8,128)(2,1)S(1)}, u32[]{:S(2)}, u32[]{:S(2)}) collective-permute-start(bf16[128,2048]{1,0:T(8,128)(2,1)S(1)} %shard_map.89), channel_id=1, source_target_pairs={{0,4},{8,12},{16,20},{24,28},{4,0},{12,8},{20,16},{28,24},{1,5},{9... | collective-permute-start | bytes 1572872 | tf_op jit(solution)/shard_map/ppermute | solution.py:369
  50.0 16.6 %collective-permute-start.13 = (bf16[128,2048]{1,0:T(8,128)(2,1)S(1)}, bf16[128,2048]{1,0:T(8,128)(2,1)S(1)}, u32[]{:S(2)}, u32[]{:S(2)}) collective-permute-start(bf16[128,2048]{1,0:T(8,128)(2,1)S(1)} %collective-permute-done.7.refs_3_), channel_id=1, source_target_pairs={{0,2},{1,3},{2,0},{3,1},{4,6},{5,7},{6,4},{7,5},{8,10},{9,11},{10,... | collective-permute-start | bytes 1572872 | tf_op jit(solution)/shard_map/ppermute | solution.py:366
  50.8 15.8 %collective-permute-start.14 = (bf16[128,2048]{1,0:T(8,128)(2,1)S(1)}, bf16[128,2048]{1,0:T(8,128)(2,1)S(1)}, u32[]{:S(2)}, u32[]{:S(2)}) collective-permute-start(bf16[128,2048]{1,0:T(8,128)(2,1)S(1)} %collective-permute-done.8.refs_1_), channel_id=1, source_target_pairs={{0,8},{4,12},{8,16},{12,20},{16,24},{20,28},{1,9},{5,13},{9,17},{1... | collective-permute-start | bytes 1572872 | tf_op jit(solution)/shard_map/ppermute | solution.py:369
  66.7 13.0 %collective-permute-start.16 = (bf16[64,2048]{1,0:T(8,128)(2,1)S(1)}, bf16[64,2048]{1,0:T(8,128)(2,1)S(1)}, u32[]{:S(2)}, u32[]{:S(2)}) collective-permute-start(bf16[64,2048]{1,0:T(8,128)(2,1)S(1)} %slice.7), channel_id=1, source_target_pairs={{4,0},{12,8},{20,16},{28,24},{5,1},{13,9},{21,17},{29,25},{6,2},{1... | collective-permute-start | bytes 786440 | tf_op jit(solution)/shard_map/ppermute | solution.py:369
  69.8 9.8 %collective-permute-start.15 = (bf16[64,2048]{1,0:T(8,128)(2,1)S(1)}, bf16[64,2048]{1,0:T(8,128)(2,1)S(1)}, u32[]{:S(2)}, u32[]{:S(2)}) collective-permute-start(bf16[64,2048]{1,0:T(8,128)(2,1)S(1)} %slice.6), channel_id=1, source_target_pairs={{0,2},{1,3},{2,0},{3,1},{4,6},{5,7},{6,4},{7,5},{8,10},{9,11},{10,... | collective-permute-start | bytes 786440 | tf_op jit(solution)/shard_map/ppermute | solution.py:366
  80.1 2.0 %collective-permute-start.17 = (bf16[1056,256]{1,0:T(8,128)(2,1)S(1)}, bf16[1056,256]{1,0:T(8,128)(2,1)S(1)}, u32[]{:S(2)}, u32[]{:S(2)}) collective-permute-start(bf16[1056,256]{1,0:T(8,128)(2,1)S(1)} %get-tuple-element.75), channel_id=1, source_target_pairs={{0,1},{1,0},{2,3},{3,2},{4,5},{5,4},{6,7},{7,6},{8,9},{9,8},{10,11... | collective-permute-start | bytes 1622024 | tf_op jit(solution)/shard_map/ppermute | solution.py:363
  82.9 14.0 %collective-permute-start.19 = (bf16[128,2048]{1,0:T(8,128)(2,1)S(1)}, bf16[128,2048]{1,0:T(8,128)(2,1)S(1)}, u32[]{:S(2)}, u32[]{:S(2)}) collective-permute-start(bf16[128,2048]{1,0:T(8,128)(2,1)S(1)} %shard_map.94), channel_id=1, source_target_pairs={{0,2},{1,3},{2,0},{3,1},{4,6},{5,7},{6,4},{7,5},{8,10},{9,11},{10,... | collective-permute-start | bytes 1572872 | tf_op jit(solution)/shard_map/ppermute | solution.py:366

commit v8 on v7

--- a/solution.py
+++ b/solution.py
@@ -45,39 +45,6 @@
     centred = inputs - jnp.mean(inputs, axis=-1, keepdims=True)
     variance = jnp.mean(centred * centred, axis=-1, keepdims=True)
     return (centred * lax.rsqrt(variance + EPSILON) * gain).astype(BF16)
-
-
-def count_back(slopes, seg, far_seg):
-    def body(slopes_ref, seg_ref, far_ref, out_ref):
-        there = lax.axis_index("seq") >= lax.axis_index("head") + 1
-        same = jnp.where((far_ref[...] == seg_ref[0:1, 0:1]) & there, 1, 0)
-        for head in range(4):
-            out_ref[head : head + 1, :] = jnp.full((1, PIECE), slopes_ref[head], F32)
-        out_ref[4:8, :] = jnp.full((4, PIECE), jnp.sum(same).astype(F32), F32)
-
-    return pl.pallas_call(
-        body,
-        out_shape=jax.ShapeDtypeStruct((8, PIECE), F32),
-        in_specs=[SMEM, VMEM, VMEM],
-        out_specs=VMEM,
-        compiler_params=params(4),
-        cost_estimate=cost(0, 2**13),
-    )(slopes, seg, far_seg)
-
-
-def add_counts(mine, other):
-    def body(mine_ref, other_ref, out_ref):
-        out_ref[0:4, :] = mine_ref[0:4, :]
-        out_ref[4:8, :] = mine_ref[4:8, :] + other_ref[4:8, :]
-
-    return pl.pallas_call(
-        body,
-        out_shape=jax.ShapeDtypeStruct(mine.shape, F32),
-        in_specs=[VMEM, VMEM],
-        out_specs=VMEM,
-        compiler_params=params(4),
-        cost_estimate=cost(0, 2**13),
-    )(mine, other)
 
 
 def stage(weights):
@@ -161,7 +128,7 @@
     for head in range(heads):
         cols = slice(head * HD, (head + 1) * HD)
         wide = pl.ds(head * HD, HD)
-        bias = dist_ref[...] * (slopes_ref[head : head + 1, :] * LOG2E)
+        bias = dist_ref[...] * (slopes_ref[head] * LOG2E)
         bias = jnp.concatenate([bias] * (q_ref.shape[1] // PIECE), axis=1)
         scores = dot(k_rows[:, cols], q_ref[wide, :]) * (HD**-0.5 * LOG2E)
         scores = scores + bias + mask_ref[...]
@@ -184,7 +151,7 @@
     return (jax.ShapeDtypeStruct((8, block), F32), jax.ShapeDtypeStruct((width, block), F32))
 
 
-def own_block(info, info_pair, seg, gain, pieces, w_own, w_pair):
+def own_block(slopes, slopes_pair, seg, gain, pieces, w_own, w_pair):
     depth, width = w_own.shape[1:]
     block = 4 * PIECE
 
@@ -212,7 +179,7 @@
             jax.ShapeDtypeStruct((block, width), BF16),
             jax.ShapeDtypeStruct((block, width), BF16),
         ),
-        in_specs=[VMEM] * 10,
+        in_specs=[SMEM] * 2 + [VMEM] * 8,
         out_specs=(VMEM,) * 8,
         scratch_shapes=[
             pltpu.VMEM((block, depth), BF16),
@@ -221,7 +188,7 @@
         ],
         compiler_params=params(OWN_MIB),
         cost_estimate=cost(5 * block * depth * width, 2**20, 0),
-    )(info, info_pair, seg, gain, *pieces, w_own, w_pair)
+    )(slopes, slopes_pair, seg, gain, *pieces, w_own, w_pair)
 
 
 def write_closed(states, send_ref, lse_ref, out_ref):
@@ -246,7 +213,7 @@
     send_ref[pl.ds(2 * width, 32), :] = jnp.concatenate(parts, axis=0).astype(BF16)
 
 
-def earlier_pieces(which, closing, infos, seg, gain, pieces, w_own, w_pair, q_own, q_pair, state):
+def earlier_pieces(which, closing, slopes, slopes_pair, seg, segs, gain, pieces, w_own, w_pair, q_own, q_pair, state):
     depth, width = w_own.shape[1:]
     block = 4 * PIECE
     count = len(pieces)
@@ -254,6 +221,7 @@
     n_out = 3 if closing else 4
 
     def body(s0, s1, seg_ref, gain_ref, *refs):
+        seg_refs, refs = refs[: len(segs)], refs[len(segs) :]
         sources, refs = refs[:count], refs[count:]
         (w0, w1, q0, q1), before, refs = refs[:4], (refs[4:6], refs[6:8]), refs[8:]
         outs, (x, mask, dist, *inner) = refs[:n_out], refs[n_out:]
@@ -261,8 +229,10 @@
         after = (after[0:2], after[2:4])
         block_num = lax.axis_index("seq")
         block_base = block_num * block
-        counts = s0[4:5, :] + s1[4:5, :]
-        start = block_base - jnp.max(counts).astype(jnp.int32)
+        same = jnp.zeros(seg_ref.shape, jnp.int32)
+        for back, ref in enumerate(seg_refs, 1):
+            same = same + jnp.where((ref[...] == seg_ref[0:1, 0:1]) & (block_num >= back), 1, 0)
+        start = block_base - jnp.sum(same)
 
         def key_base(i):
             def base(back, place):
@@ -311,12 +281,12 @@
     return pl.pallas_call(
         body,
         out_shape=shapes,
-        in_specs=[VMEM] * (12 + count),
+        in_specs=[SMEM] * 2 + [VMEM] * (10 + len(segs) + count),
         out_specs=(VMEM,) * n_out,
         scratch_shapes=scratch,
         compiler_params=params(EARLIER_MIB),
         cost_estimate=cost(4 * rows * depth * width, 2**20, 0),
-    )(*infos, seg, gain, *pieces, w_own, w_pair, q_own, q_pair, *state)
+    )(slopes, slopes_pair, seg, gain, *segs, *pieces, w_own, w_pair, q_own, q_pair, *state)
 
 
 def project(place, lse, out, got, wo_own, wo_pair, tokens):
@@ -376,51 +346,53 @@
     w_all = jnp.transpose(w_qkv, (1, 0, 2))
     seg = seg_ids.reshape(4, PIECE)
     gain = ln_gain.reshape(1, -1)
-    far_seg = lax.ppermute(
-        seg, ("seq", "head"),
-        [(4 * i + head, 4 * (i + head + 1) + head) for head in range(SPAN) for i in range(blocks - head - 1)])
     w_pair = over_core(w_all)
 
     a2 = over_seq(tokens, two_on)
     b0 = over_x(tokens)
     a1_odd = over_seq(tokens, even_to_odd)
     c0 = over_core(tokens)
-    info = count_back(slopes, seg, far_seg)
-    info_x = over_x(info)
-    info_x, w_staged = tie((info_x, w_all))
+    slopes_sent, w_staged, c0 = tie((slopes, w_all, c0))
+    slopes_pair = over_core(slopes_sent)
+    seg_sent, slopes_pair = tie((seg, slopes_pair))
+    seg1 = over_seq(seg_sent, [(i, i + 1) for i in range(blocks - 1)])
     w_staged = stage(w_staged)
-    info = add_counts(info, info_x)
-    infos = [info, over_core(info)]
-
-    a2, b0, a1_odd, w_pair, w_staged, infos = tie((a2, b0, a1_odd, w_pair, w_staged, infos))
+
+    a2, b0, a1_odd, w_pair, w_staged, slopes_pair, seg1 = tie(
+        (a2, b0, a1_odd, w_pair, w_staged, slopes_pair, seg1))
     a4 = over_seq(a2, two_on)
     b2 = over_x(a2)
     crossed = over_seq(a2, even_to_odd + odd_to_even)
     d0 = over_core(b0)
+    seg23 = over_seq(jnp.concatenate([seg, seg1], axis=0), two_on)
+    segs = [seg1, seg23[:4], seg23[4:]]
     q_own, q_pair, *state, key_cache, value_cache = own_block(
-        *infos, seg, gain, (tokens, b0, c0, d0), w_staged, w_pair)
-
-    crossed, b2, a4, b0_sent, wo_sent, state[0] = tie((crossed, b2, a4, b0, w_out, state[0]))
+        slopes, slopes_pair, seg, gain, (tokens, b0, c0, d0), w_staged, w_pair)
+
+    crossed, b2, a4, b0_sent, wo_sent, segs, state[0] = tie((crossed, b2, a4, b0, w_out, segs, state[0]))
     over_y = over_seq(pick(b0_sent, a4), even_to_odd + odd_to_even)
     x_third = over_x(crossed)
     b4 = over_seq(b2, two_on)
+    seg4 = over_seq(segs[1], two_on)
     wo_pair = over_core(wo_sent)
 
-    def merge(closing, pieces, which, state):
+    def merge(closing, segs, pieces, which, state):
         return earlier_pieces(
-            which, closing, infos, seg, gain, pieces, w_staged, w_pair, q_own, q_pair, state)
+            which, closing, slopes, slopes_pair, seg, segs, gain, pieces, w_staged, w_pair, q_own, q_pair, state)
 
     state = merge(
-        False, (a2, b2, a4, crossed, a1_odd),
-        (((2, 0),) * 2, ((2, 1),) * 2, ((4, 0),) * 2, ((1, 0), (3, 0)), ((0, 0), (1, 0))), state)
-
-    over_y, x_third, b4, held = tie((over_y, x_third, b4, state[0]))
+        False, segs, (a2, b2, crossed, a1_odd),
+        (((2, 0),) * 2, ((2, 1),) * 2, ((1, 0), (3, 0)), ((0, 0), (1, 0))), state)
+
+    over_y, x_third, b4, seg4, held = tie((over_y, x_third, b4, seg4, state[0]))
+    segs = [*segs, seg4]
     state = (held, *state[1:])
     b3_top = over_x(over_y[: PIECE // 2])
     b3_rest = over_seq(b4[PIECE // 2 :], odd_to_even)
     state = merge(
-        False, (b4, x_third, over_y), (((4, 1),) * 2, ((1, 1), (3, 1)), ((3, 0), (1, 1))), state)
-    send, lse, out = merge(True, (b3_top, b3_rest), (((3, 1), (0, 0)),), state)
+        False, segs, (a4, b4, x_third, over_y),
+        (((4, 0),) * 2, ((4, 1),) * 2, ((1, 1), (3, 1)), ((3, 0), (1, 1))), state)
+    send, lse, out = merge(True, segs, (b3_top, b3_rest), (((3, 1), (0, 0)),), state)
     got = over_core(send)
     y_pair = project(1, lse, out, got, w_out, wo_pair, None)
     y_got = over_x(y_pair)

time: 99.3 us -> 93.4 us (0.941); the launches traced: 97.9 us -> 93.1 us
  Pallas kernels: 33.7 us -> 25.5 us
  waiting for transfers between devices: 26.1 us -> 32.1 us
  local copies, waits for them, and re-layouts: 4.76 us -> 2.94 us
    ppermute x7 -> x10, starting transfers between devices: 15.3 us -> 25.6 us  [over_seq(): return lax.ppermute(value, 'seq', pairs)]
    ppermute x7 -> x10, waiting for transfers between devices: 1.91 us -> 11.5 us  [over_seq(): return lax.ppermute(value, 'seq', pairs)]
    pallas_call x5 -> x3, Pallas kernels: 21.4 us -> 12.8 us  [earlier_pieces(): pl.pallas_call(body, out_shape=shapes, in_specs=[SMEM] * 2 + [VMEM] * (10...]
    ppermute x1 -> x0, waiting for transfers between devices: 6.26 us -> none  [on_device(): lax.ppermute(seg, ('seq', 'head'), [(4 * i + head, 4 * (i + head + 1) + h...]
    ppermute x1 -> x0, starting transfers between devices: 5.6 us -> none  [on_device(): lax.ppermute(seg, ('seq', 'head'), [(4 * i + head, 4 * (i + head + 1) + h...]
    ppermute x6 -> x5, starting transfers between devices: 9.86 us -> 4.32 us  [over_x(): return lax.ppermute(value, 'head', [(i, i ^ 2) for i in range(4)])]
    ppermute x6, waiting for transfers between devices: 1.93 us -> 7.33 us  [over_core(): return lax.ppermute(value, 'head', [(i, i ^ 1) for i in range(4)])]
    ppermute x6 -> x5, waiting for transfers between devices: 16 us -> 13.3 us  [over_x(): return lax.ppermute(value, 'head', [(i, i ^ 2) for i in range(4)])]
  transfers between devices with their start and end apart: 20 -> 21, of which waited for: 7 -> 7; matrix products, arithmetic and copies ran while one was open for 0% -> 0% of each run, Pallas kernels for 34% -> 27%
where the time goes in v8:
time: 93.4 us; the launch traced here: 93.1 us
  waiting for transfers between devices  32.1 us (34%)
  starting transfers between devices  30.7 us (33%)
  Pallas kernels  25.5 us (27%)
  local copies, waits for them, and re-layouts  2.94 us (3%)
  other arithmetic  0.94 us (1%)
    ppermute x10, starting transfers between devices, over_seq(): return lax.ppermute(value, 'seq', pairs)  25.6 us
    ppermute x5, waiting for transfers between devices, over_x(): return lax.ppermute(value, 'head', [(i, i ^ 2) for i in range(4)])  13.3 us
    pallas_call x3, Pallas kernels, earlier_pieces(): pl.pallas_call(body, out_shape=shapes, in_specs=[SMEM] * 2 + [VMEM] * (10...  12.8 us
    ppermute x10, waiting for transfers between devices, over_seq(): return lax.ppermute(value, 'seq', pairs)  11.5 us
    pallas_call x1, Pallas kernels, own_block(): pl.pallas_call(body, out_shape=(jax.ShapeDtypeStruct((width, block), BF16...  10.6 us
    ppermute x6, waiting for transfers between devices, over_core(): return lax.ppermute(value, 'head', [(i, i ^ 1) for i in range(4)])  7.33 us
    ppermute x5, starting transfers between devices, over_x(): return lax.ppermute(value, 'head', [(i, i ^ 2) for i in range(4)])  4.32 us
    unnamed x12, local copies, waits for them, and re-layouts  2.89 us
  transfers between devices with their start and end apart: 21, of which 7 were waited for; matrix products, arithmetic and copies ran while one was open for 0% of the time, Pallas kernels for 27%

profile of v8, /device:TPU:12, one launch (start us, length us, event | category | flops | bytes accessed | tf_op | source)
XLA Modules:
  0.0 93.1 jit_solution(14556761806932920439)
XLA Ops:
  0.6 0.1 collective-permute-start.3
  0.7 0.5 collective-permute-start.4
  1.2 1.3 %collective-permute-start.2 = (bf16[128,2048]{1,0:T(8,128)(2,1)}, bf16[128,2048]{1,0:T(8,128)(2,1)S(1)}, u32[]{:S(2)}, u32[]{:S(2)}) collective-permute-start(bf16[128,2048]{1,0:T(8,128)(2,1)} %refs_0_.1), channel_id=1, source_target_pairs={{0,4},{8,12},{16,20},{24,28},{1,5},{9,13},{17,21},{25,29},{2,6},{1... | collective-permute-start | bytes 1572872 | tf_op jit(solution)/shard_map/ppermute | solution.py:339
  2.5 1.6 %collective-permute-start.1 = (bf16[128,2048]{1,0:T(8,128)(2,1)}, bf16[128,2048]{1,0:T(8,128)(2,1)S(1)}, u32[]{:S(2)}, u32[]{:S(2)}) collective-permute-start(bf16[128,2048]{1,0:T(8,128)(2,1)} %refs_0_.1), channel_id=1, source_target_pairs={{0,2},{1,3},{2,0},{3,1},{4,6},{5,7},{6,4},{7,5},{8,10},{9,11},{10,... | collective-permute-start | bytes 1572872 | tf_op jit(solution)/shard_map/ppermute | solution.py:336
  4.1 3.5 %collective-permute-start = (bf16[128,2048]{1,0:T(8,128)(2,1)}, bf16[128,2048]{1,0:T(8,128)(2,1)S(1)}, u32[]{:S(2)}, u32[]{:S(2)}) collective-permute-start(bf16[128,2048]{1,0:T(8,128)(2,1)} %refs_0_.1), channel_id=1, source_target_pairs={{0,8},{4,12},{8,16},{12,20},{16,24},{20,28},{1,9},{5,13},{9,17},{1... | collective-permute-start | bytes 1572872 | tf_op jit(solution)/shard_map/ppermute | solution.py:339
  7.5 4.3 %collective-permute-done.4.c = bf16[128,2048]{1,0:T(8,128)(2,1)S(1)} collective-permute-done((bf16[128,2048]{1,0:T(8,128)(2,1)}, bf16[128,2048]{1,0:T(8,128)(2,1)S(1)}, u32[]{:S(2)}, u32[]{:S(2)}) %collective-permute-start.4) | collective-permute-done | bytes 524320 | tf_op jit(solution)/shard_map/ppermute | solution.py:333
  11.8 0.1 collective-permute-start.5
  12.0 1.1 %collective-permute-done.5.s1 = f32[4]{0:T(128)S(1)} collective-permute-done((f32[4]{0:T(128)}, f32[4]{0:T(128)S(1)}, u32[]{:S(2)}, u32[]{:S(2)}) %collective-permute-start.5) | collective-permute-done | bytes 48 | tf_op jit(solution)/shard_map/ppermute | solution.py:333
  13.1 3.4 %collective-permute-start.6 = (s32[4,128]{1,0:T(4,128)}, s32[4,128]{1,0:T(4,128)S(1)}, u32[]{:S(2)}, u32[]{:S(2)}) collective-permute-start(s32[4,128]{1,0:T(4,128)} %bitcast.9), channel_id=1, source_target_pairs={{0,4},{4,8},{8,12},{12,16},{16,20},{20,24},{24,28},{1,5},{5,9},{9,... | collective-permute-start | bytes 6152 | tf_op jit(solution)/shard_map/ppermute | solution.py:339
  16.5 2.8 %copy-done.1 = bf16[2048,3,512]{2,0,1:T(8,128)(2,1)S(1)} copy-done((bf16[2048,3,512]{2,0,1:T(8,128)(2,1)S(1)}, bf16[2048,3,512]{2,0,1:T(8,128)(2,1)}, u32[]{:S(2)}) %copy-start.1) | copy-done | bytes 6291480
  19.3 0.4 shard_map.85.w0.refs_7_.refs_8_.refs_6_
  19.7 0.0 collective-permute-done.2.refs_6_
  19.7 0.0 collective-permute-done.1.b.even_ref
  19.8 0.0 collective-permute-done.refs_3_
  19.8 0.0 collective-permute-done.6.refs_0_
  19.8 0.0 collective-permute-done.3.w1.refs_8_.refs_9_.refs_7_
  19.8 0.1 collective-permute-start.11
  19.9 0.1 copy-done.4
  20.0 3.5 %collective-permute-start.10 = (s32[8,128]{1,0:T(8,128)S(1)}, s32[8,128]{1,0:T(8,128)S(1)}, u32[]{:S(2)}, u32[]{:S(2)}) collective-permute-start(s32[8,128]{1,0:T(8,128)S(1)} %pad_add_fusion), channel_id=1, source_target_pairs={{0,8},{4,12},{8,16},{12,20},{16,24},{20,28},{1,9},{5,13},{9,17},{1... | collective-permute-start | bytes 12296 | tf_op jit(solution)/shard_map/ppermute | solution.py:339
  23.5 3.4 %collective-permute-start.9 = (bf16[128,2048]{1,0:T(8,128)(2,1)S(1)}, bf16[128,2048]{1,0:T(8,128)(2,1)S(1)}, u32[]{:S(2)}, u32[]{:S(2)}) collective-permute-start(bf16[128,2048]{1,0:T(8,128)(2,1)S(1)} %collective-permute-done.refs_3_), channel_id=1, source_target_pairs={{0,8},{4,12},{8,16},{12,20},{16,24},{20,28},{1,9},{5,13},{9,17},{1... | collective-permute-start | bytes 1572872 | tf_op jit(solution)/shard_map/ppermute | solution.py:339
  26.8 0.6 collective-permute-start.8
  27.4 2.4 %collective-permute-start.7 = (bf16[128,2048]{1,0:T(8,128)(2,1)S(1)}, bf16[128,2048]{1,0:T(8,128)(2,1)S(1)}, u32[]{:S(2)}, u32[]{:S(2)}) collective-permute-start(bf16[128,2048]{1,0:T(8,128)(2,1)S(1)} %collective-permute-done.refs_3_), channel_id=1, source_target_pairs={{0,4},{8,12},{16,20},{24,28},{4,0},{12,8},{20,16},{28,24},{1,5},{9... | collective-permute-start | bytes 1572872 | tf_op jit(solution)/shard_map/ppermute | solution.py:339
  29.8 0.0 collective-permute-done.10
  29.8 0.0 collective-permute-done.11.d
  29.8 0.0 copy-start
  29.8 10.6 %shard_map.86 = (bf16[512,512]{1,0:T(8,128)(2,1)S(1)}, bf16[512,512]{1,0:T(8,128)(2,1)S(1)}, f32[8,512]{1,0:T(8,128)S(1)}, f32[512,512]{1,0:T(8,128)S(1)}, f32[8...) custom-call(f32[4]{0:T(128)S(1)} %copy-done.5, ...), custom_call_target="tpu_custom_call" | custom-call | flops 5368709120 | bytes 1048576 | tf_op jit(solution)/shard_map/pallas_call | solution.py:176
  40.5 0.0 collective-permute-done.9.odd_ref.refs_4_
  40.5 0.2 collective-permute-done.8.refs_4_
  40.6 0.9 collective-permute-done.7.refs_5_
  41.6 1.8 %collective-permute-start.12 = (bf16[128,2048]{1,0:T(8,128)(2,1)S(1)}, bf16[128,2048]{1,0:T(8,128)(2,1)S(1)}, u32[]{:S(2)}, u32[]{:S(2)}) collective-permute-start(bf16[128,2048]{1,0:T(8,128)(2,1)S(1)} %shard_map.87), channel_id=1, source_target_pairs={{0,4},{8,12},{16,20},{24,28},{4,0},{12,8},{20,16},{28,24},{1,5},{9... | collective-permute-start | bytes 1572872 | tf_op jit(solution)/shard_map/ppermute | solution.py:339
  43.4 1.5 %collective-permute-start.13 = (bf16[128,2048]{1,0:T(8,128)(2,1)S(1)}, bf16[128,2048]{1,0:T(8,128)(2,1)S(1)}, u32[]{:S(2)}, u32[]{:S(2)}) collective-permute-start(bf16[128,2048]{1,0:T(8,128)(2,1)S(1)} %collective-permute-done.7.refs_5_), channel_id=1, source_target_pairs={{0,2},{1,3},{2,0},{3,1},{4,6},{5,7},{6,4},{7,5},{8,10},{9,11},{10,... | collective-permute-start | bytes 1572872 | tf_op jit(solution)/shard_map/ppermute | solution.py:336
  44.9 2.2 %collective-permute-start.14 = (bf16[128,2048]{1,0:T(8,128)(2,1)S(1)}, bf16[128,2048]{1,0:T(8,128)(2,1)S(1)}, u32[]{:S(2)}, u32[]{:S(2)}) collective-permute-start(bf16[128,2048]{1,0:T(8,128)(2,1)S(1)} %collective-permute-done.8.refs_4_), channel_id=1, source_target_pairs={{0,8},{4,12},{8,16},{12,20},{16,24},{20,28},{1,9},{5,13},{9,17},{1... | collective-permute-start | bytes 1572872 | tf_op jit(solution)/shard_map/ppermute | solution.py:339
  47.1 1.9 %collective-permute-start.15 = (s32[4,128]{1,0:T(4,128)S(1)}, s32[4,128]{1,0:T(4,128)S(1)}, u32[]{:S(2)}, u32[]{:S(2)}) collective-permute-start(s32[4,128]{1,0:T(4,128)S(1)} %get-tuple-element.61.refs_1_), channel_id=1, source_target_pairs={{0,8},{4,12},{8,16},{12,20},{16,24},{20,28},{1,9},{5,13},{9,17},{1... | collective-permute-start | bytes 6152 | tf_op jit(solution)/shard_map/ppermute | solution.py:339
  49.0 1.0 %shard_map.88 = (f32[8,512]{1,0:T(8,128)S(1)}, f32[512,512]{1,0:T(8,128)S(1)}, f32[8,512]{1,0:T(8,128)S(1)}, f32[512,512]{1,0:T(8,128)S(1)}) custom-call(f32[4]{0:T(128)S(1)} %copy-done.5, f32[4]{0:T(128)S(1)} %collective-permute-done.5.s1, s32[4,128]{1,0:T(4,128)S(1)} %bitcast.12, f32[1,2048]{1,0:T(1,128)S(1)} %bitcast.6, ...), custom_call_target="tpu_custom_call" | custom-call | flops 4294967296 | bytes 1048576 | tf_op jit(solution)/shard_map/pallas_call | solution.py:281
  50.0 10.5 %collective-permute-done.15.refs_3_ = s32[4,128]{1,0:T(4,128)S(1)} collective-permute-done((s32[4,128]{1,0:T(4,128)S(1)}, s32[4,128]{1,0:T(4,128)S(1)}, u32[]{:S(2)}, u32[]{:S(2)}) %collective-permute-start.15) | collective-permute-done | bytes 2080 | tf_op jit(solution)/shard_map/ppermute | solution.py:339
  60.6 0.0 collective-permute-done.13.refs_6_
  60.6 0.0 collective-permute-done.14.refs_5_
  60.6 2.3 %collective-permute-start.17 = (bf16[64,2048]{1,0:T(8,128)(2,1)S(1)}, bf16[64,2048]{1,0:T(8,128)(2,1)S(1)}, u32[]{:S(2)}, u32[]{:S(2)}) collective-permute-start(bf16[64,2048]{1,0:T(8,128)(2,1)S(1)} %slice.15), channel_id=1, source_target_pairs={{4,0},{12,8},{20,16},{28,24},{5,1},{13,9},{21,17},{29,25},{6,2},{1... | collective-permute-start | bytes 786440 | tf_op jit(solution)/shard_map/ppermute | solution.py:339
  62.9 0.6 collective-permute-start.16
  63.5 10.7 %shard_map.89 = (f32[8,512]{1,0:T(8,128)S(1)}, f32[512,512]{1,0:T(8,128)S(1)}, f32[8,512]{1,0:T(8,128)S(1)}, f32[512,512]{1,0:T(8,128)S(1)}) custom-call(f32[4]{0:T(128)S(1)} %copy-done.5, f32[4]{0:T(128)S(1)} %collective-permute-done.5.s1, s32[4,128]{1,0:T(4,128)S(1)} %bitcast.13, f32[1,2048]{1,0:T(1,128)S(1)} %bitcast.7, ...), custom_call_target="tpu_custom_call" | custom-call | flops 4294967296 | bytes 1048576 | tf_op jit(solution)/shard_map/pallas_call | solution.py:281
  74.3 1.0 %shard_map.90 = (bf16[1056,256]{1,0:T(8,128)(2,1)S(1)}, f32[8,256]{1,0:T(8,128)S(1)}, f32[1024,256]{1,0:T(8,128)S(1)}) custom-call(f32[4]{0:T(128)S(1)} %copy-done.5, f32[4]{0:T(128)S(1)} %collective-permute-done.5.s1, s32[4,128]{1,0:T(4,128)S(1)} %bitcast.14, f32[1,2048]{1,0:T(1,128)S(1)} %bitcast.8, s32[4,128]{1,0:T(4,128)S(1)} %collective-permute-done.6.refs_0_, ...), custom_call_target="tpu_custom_call" | custom-call | flops 1073741824 | bytes 1048576 | tf_op jit(solution)/shard_map/pallas_call | solution.py:281
  75.3 0.1 collective-permute-start.18
  75.4 1.9 %collective-permute-done.18.got_ref = bf16[1056,256]{1,0:T(8,128)(2,1)S(1)} collective-permute-done((bf16[1056,256]{1,0:T(8,128)(2,1)S(1)}, bf16[1056,256]{1,0:T(8,128)(2,1)S(1)}, u32[]{:S(2)}, u32[]{:S(2)}) %collective-permute-start.18) | collective-permute-done | bytes 540704 | tf_op jit(solution)/shard_map/ppermute | solution.py:333
  77.3 0.8 shard_map.92
  78.1 0.1 collective-permute-start.20
  78.2 0.8 shard_map.91
  79.0 13.1 %collective-permute-done.20 = bf16[128,2048]{1,0:T(8,128)(2,1)S(1)} collective-permute-done((bf16[128,2048]{1,0:T(8,128)(2,1)S(1)}, bf16[128,2048]{1,0:T(8,128)(2,1)S(1)}, u32[]{:S(2)}, u32[]{:S(2)}) %collective-permute-start.20) | collective-permute-done | bytes 524320 | tf_op jit(solution)/shard_map/ppermute | solution.py:336
  92.1 0.9 %add_convert_fusion = bf16[128,2048]{1,0:T(8,128)(2,1)} fusion(f32[128,2048]{1,0:T(8,128)S(1)} %shard_map.91, bf16[128,2048]{1,0:T(8,128)(2,1)S(1)} %collective-permute-done.20), kind=kLoop, calls=%fused_computation | loop fusion | flops 786432 | bytes 2097152 | tf_op jit(solution)/shard_map/convert_element_type | solution.py:400
  (19 shorter events, 0.1 us)
Async XLA Ops:
  0.6 19.2 %collective-permute-start.3 = (bf16[3,2048,512]{2,1,0:T(8,128)(2,1)}, bf16[3,2048,512]{2,1,0:T(8,128)(2,1)S(1)}, u32[]{:S(2)}, u32[]{:S(2)}) collective-permute-start(bf16[3,2048,512]{2,1,0:T(8,128)(2,1)} %bitcast.3), channel_id=1, source_target_pairs={{0,1},{1,0},{2,3},{3,2},{4,5},{5,4},{6,7},{7,6},{8,9},{9,8},{10,11... | collective-permute-start | bytes 18874376 | tf_op jit(solution)/shard_map/ppermute | solution.py:333
  0.7 11.1 %collective-permute-start.4 = (bf16[128,2048]{1,0:T(8,128)(2,1)}, bf16[128,2048]{1,0:T(8,128)(2,1)S(1)}, u32[]{:S(2)}, u32[]{:S(2)}) collective-permute-start(bf16[128,2048]{1,0:T(8,128)(2,1)} %refs_0_.1), channel_id=1, source_target_pairs={{0,1},{1,0},{2,3},{3,2},{4,5},{5,4},{6,7},{7,6},{8,9},{9,8},{10,11... | collective-permute-start | bytes 1572872 | tf_op jit(solution)/shard_map/ppermute | solution.py:333
  1.2 18.5 %collective-permute-start.2 = (bf16[128,2048]{1,0:T(8,128)(2,1)}, bf16[128,2048]{1,0:T(8,128)(2,1)S(1)}, u32[]{:S(2)}, u32[]{:S(2)}) collective-permute-start(bf16[128,2048]{1,0:T(8,128)(2,1)} %refs_0_.1), channel_id=1, source_target_pairs={{0,4},{8,12},{16,20},{24,28},{1,5},{9,13},{17,21},{25,29},{2,6},{1... | collective-permute-start | bytes 1572872 | tf_op jit(solution)/shard_map/ppermute | solution.py:339
  2.5 17.2 %collective-permute-start.1 = (bf16[128,2048]{1,0:T(8,128)(2,1)}, bf16[128,2048]{1,0:T(8,128)(2,1)S(1)}, u32[]{:S(2)}, u32[]{:S(2)}) collective-permute-start(bf16[128,2048]{1,0:T(8,128)(2,1)} %refs_0_.1), channel_id=1, source_target_pairs={{0,2},{1,3},{2,0},{3,1},{4,6},{5,7},{6,4},{7,5},{8,10},{9,11},{10,... | collective-permute-start | bytes 1572872 | tf_op jit(solution)/shard_map/ppermute | solution.py:336
  4.1 15.7 %collective-permute-start = (bf16[128,2048]{1,0:T(8,128)(2,1)}, bf16[128,2048]{1,0:T(8,128)(2,1)S(1)}, u32[]{:S(2)}, u32[]{:S(2)}) collective-permute-start(bf16[128,2048]{1,0:T(8,128)(2,1)} %refs_0_.1), channel_id=1, source_target_pairs={{0,8},{4,12},{8,16},{12,20},{16,24},{20,28},{1,9},{5,13},{9,17},{1... | collective-permute-start | bytes 1572872 | tf_op jit(solution)/shard_map/ppermute | solution.py:339
  11.8 1.3 %collective-permute-start.5 = (f32[4]{0:T(128)}, f32[4]{0:T(128)S(1)}, u32[]{:S(2)}, u32[]{:S(2)}) collective-permute-start(f32[4]{0:T(128)} %s0.7), channel_id=1, source_target_pairs={{0,1},{1,0},{2,3},{3,2},{4,5},{5,4},{6,7},{7,6},{8,9},{9,8},{10,11... | collective-permute-start | bytes 56 | tf_op jit(solution)/shard_map/ppermute | solution.py:333
  13.1 6.7 %collective-permute-start.6 = (s32[4,128]{1,0:T(4,128)}, s32[4,128]{1,0:T(4,128)S(1)}, u32[]{:S(2)}, u32[]{:S(2)}) collective-permute-start(s32[4,128]{1,0:T(4,128)} %bitcast.9), channel_id=1, source_target_pairs={{0,4},{4,8},{8,12},{12,16},{16,20},{20,24},{24,28},{1,5},{5,9},{9,... | collective-permute-start | bytes 6152 | tf_op jit(solution)/shard_map/ppermute | solution.py:339
  16.5 2.8 %copy-start.1 = (bf16[2048,3,512]{2,0,1:T(8,128)(2,1)S(1)}, bf16[2048,3,512]{2,0,1:T(8,128)(2,1)}, u32[]{:S(2)}) copy-start(bf16[2048,3,512]{2,0,1:T(8,128)(2,1)} %param.8) | copy-start | bytes 18874372
  19.3 0.7 copy-start.4
  19.3 10.5 %copy-start.2 = (bf16[128,2048]{1,0:T(8,128)(2,1)S(1)}, bf16[128,2048]{1,0:T(8,128)(2,1)}, u32[]{:S(2)}) copy-start(bf16[128,2048]{1,0:T(8,128)(2,1)} %refs_0_.1) | copy-start | bytes 1572868
  19.3 10.5 %copy-start.3 = (f32[2048]{0:T(1024)S(1)}, f32[2048]{0:T(1024)}, u32[]{:S(2)}) copy-start(f32[2048]{0:T(1024)} %param.7) | copy-start | bytes 24580
  19.3 10.5 %copy-start.5 = (f32[4]{0:T(128)S(1)}, f32[4]{0:T(128)}, u32[]{:S(2)}) copy-start(f32[4]{0:T(128)} %s0.7) | copy-start | bytes 52
  19.8 10.0 %collective-permute-start.11 = (bf16[128,2048]{1,0:T(8,128)(2,1)S(1)}, bf16[128,2048]{1,0:T(8,128)(2,1)S(1)}, u32[]{:S(2)}, u32[]{:S(2)}) collective-permute-start(bf16[128,2048]{1,0:T(8,128)(2,1)S(1)} %collective-permute-done.1.b.even_ref), channel_id=1, source_target_pairs={{0,1},{1,0},{2,3},{3,2},{4,5},{5,4},{6,7},{7,6},{8,9},{9,8},{10,11... | collective-permute-start | bytes 1572872 | tf_op jit(solution)/shard_map/ppermute | solution.py:333
  20.0 9.8 %collective-permute-start.10 = (s32[8,128]{1,0:T(8,128)S(1)}, s32[8,128]{1,0:T(8,128)S(1)}, u32[]{:S(2)}, u32[]{:S(2)}) collective-permute-start(s32[8,128]{1,0:T(8,128)S(1)} %pad_add_fusion), channel_id=1, source_target_pairs={{0,8},{4,12},{8,16},{12,20},{16,24},{20,28},{1,9},{5,13},{9,17},{1... | collective-permute-start | bytes 12296 | tf_op jit(solution)/shard_map/ppermute | solution.py:339
  23.5 17.0 %collective-permute-start.9 = (bf16[128,2048]{1,0:T(8,128)(2,1)S(1)}, bf16[128,2048]{1,0:T(8,128)(2,1)S(1)}, u32[]{:S(2)}, u32[]{:S(2)}) collective-permute-start(bf16[128,2048]{1,0:T(8,128)(2,1)S(1)} %collective-permute-done.refs_3_), channel_id=1, source_target_pairs={{0,8},{4,12},{8,16},{12,20},{16,24},{20,28},{1,9},{5,13},{9,17},{1... | collective-permute-start | bytes 1572872 | tf_op jit(solution)/shard_map/ppermute | solution.py:339
  26.8 13.8 %collective-permute-start.8 = (bf16[128,2048]{1,0:T(8,128)(2,1)S(1)}, bf16[128,2048]{1,0:T(8,128)(2,1)S(1)}, u32[]{:S(2)}, u32[]{:S(2)}) collective-permute-start(bf16[128,2048]{1,0:T(8,128)(2,1)S(1)} %collective-permute-done.refs_3_), channel_id=1, source_target_pairs={{0,2},{1,3},{2,0},{3,1},{4,6},{5,7},{6,4},{7,5},{8,10},{9,11},{10,... | collective-permute-start | bytes 1572872 | tf_op jit(solution)/shard_map/ppermute | solution.py:336
  27.4 14.1 %collective-permute-start.7 = (bf16[128,2048]{1,0:T(8,128)(2,1)S(1)}, bf16[128,2048]{1,0:T(8,128)(2,1)S(1)}, u32[]{:S(2)}, u32[]{:S(2)}) collective-permute-start(bf16[128,2048]{1,0:T(8,128)(2,1)S(1)} %collective-permute-done.refs_3_), channel_id=1, source_target_pairs={{0,4},{8,12},{16,20},{24,28},{4,0},{12,8},{20,16},{28,24},{1,5},{9... | collective-permute-start | bytes 1572872 | tf_op jit(solution)/shard_map/ppermute | solution.py:339
  29.8 11.7 %copy-start = (bf16[512,2048]{1,0:T(8,128)(2,1)S(1)}, bf16[512,2048]{1,0:T(8,128)(2,1)}, u32[]{:S(2)}) copy-start(bf16[512,2048]{1,0:T(8,128)(2,1)} %w0.3) | copy-start | bytes 6291460
  41.5 35.7 %collective-permute-start.19 = (bf16[512,2048]{1,0:T(8,128)(2,1)S(1)}, bf16[512,2048]{1,0:T(8,128)(2,1)S(1)}, u32[]{:S(2)}, u32[]{:S(2)}) collective-permute-start(bf16[512,2048]{1,0:T(8,128)(2,1)S(1)} %copy-done), channel_id=1, source_target_pairs={{0,1},{1,0},{2,3},{3,2},{4,5},{5,4},{6,7},{7,6},{8,9},{9,8},{10,11... | collective-permute-start | bytes 6291464 | tf_op jit(solution)/shard_map/ppermute | solution.py:333
  41.6 19.0 %collective-permute-start.12 = (bf16[128,2048]{1,0:T(8,128)(2,1)S(1)}, bf16[128,2048]{1,0:T(8,128)(2,1)S(1)}, u32[]{:S(2)}, u32[]{:S(2)}) collective-permute-start(bf16[128,2048]{1,0:T(8,128)(2,1)S(1)} %shard_map.87), channel_id=1, source_target_pairs={{0,4},{8,12},{16,20},{24,28},{4,0},{12,8},{20,16},{28,24},{1,5},{9... | collective-permute-start | bytes 1572872 | tf_op jit(solution)/shard_map/ppermute | solution.py:339
  43.4 17.2 %collective-permute-start.13 = (bf16[128,2048]{1,0:T(8,128)(2,1)S(1)}, bf16[128,2048]{1,0:T(8,128)(2,1)S(1)}, u32[]{:S(2)}, u32[]{:S(2)}) collective-permute-start(bf16[128,2048]{1,0:T(8,128)(2,1)S(1)} %collective-permute-done.7.refs_5_), channel_id=1, source_target_pairs={{0,2},{1,3},{2,0},{3,1},{4,6},{5,7},{6,4},{7,5},{8,10},{9,11},{10,... | collective-permute-start | bytes 1572872 | tf_op jit(solution)/shard_map/ppermute | solution.py:336
  44.9 15.7 %collective-permute-start.14 = (bf16[128,2048]{1,0:T(8,128)(2,1)S(1)}, bf16[128,2048]{1,0:T(8,128)(2,1)S(1)}, u32[]{:S(2)}, u32[]{:S(2)}) collective-permute-start(bf16[128,2048]{1,0:T(8,128)(2,1)S(1)} %collective-permute-done.8.refs_4_), channel_id=1, source_target_pairs={{0,8},{4,12},{8,16},{12,20},{16,24},{20,28},{1,9},{5,13},{9,17},{1... | collective-permute-start | bytes 1572872 | tf_op jit(solution)/shard_map/ppermute | solution.py:339
  47.1 13.5 %collective-permute-start.15 = (s32[4,128]{1,0:T(4,128)S(1)}, s32[4,128]{1,0:T(4,128)S(1)}, u32[]{:S(2)}, u32[]{:S(2)}) collective-permute-start(s32[4,128]{1,0:T(4,128)S(1)} %get-tuple-element.61.refs_1_), channel_id=1, source_target_pairs={{0,8},{4,12},{8,16},{12,20},{16,24},{20,28},{1,9},{5,13},{9,17},{1... | collective-permute-start | bytes 6152 | tf_op jit(solution)/shard_map/ppermute | solution.py:339
  60.6 13.6 %collective-permute-start.17 = (bf16[64,2048]{1,0:T(8,128)(2,1)S(1)}, bf16[64,2048]{1,0:T(8,128)(2,1)S(1)}, u32[]{:S(2)}, u32[]{:S(2)}) collective-permute-start(bf16[64,2048]{1,0:T(8,128)(2,1)S(1)} %slice.15), channel_id=1, source_target_pairs={{4,0},{12,8},{20,16},{28,24},{5,1},{13,9},{21,17},{29,25},{6,2},{1... | collective-permute-start | bytes 786440 | tf_op jit(solution)/shard_map/ppermute | solution.py:339
  62.9 11.3 %collective-permute-start.16 = (bf16[64,2048]{1,0:T(8,128)(2,1)S(1)}, bf16[64,2048]{1,0:T(8,128)(2,1)S(1)}, u32[]{:S(2)}, u32[]{:S(2)}) collective-permute-start(bf16[64,2048]{1,0:T(8,128)(2,1)S(1)} %slice.14), channel_id=1, source_target_pairs={{0,2},{1,3},{2,0},{3,1},{4,6},{5,7},{6,4},{7,5},{8,10},{9,11},{10,... | collective-permute-start | bytes 786440 | tf_op jit(solution)/shard_map/ppermute | solution.py:336
  75.3 2.0 %collective-permute-start.18 = (bf16[1056,256]{1,0:T(8,128)(2,1)S(1)}, bf16[1056,256]{1,0:T(8,128)(2,1)S(1)}, u32[]{:S(2)}, u32[]{:S(2)}) collective-permute-start(bf16[1056,256]{1,0:T(8,128)(2,1)S(1)} %get-tuple-element.89), channel_id=1, source_target_pairs={{0,1},{1,0},{2,3},{3,2},{4,5},{5,4},{6,7},{7,6},{8,9},{9,8},{10,11... | collective-permute-start | bytes 1622024 | tf_op jit(solution)/shard_map/ppermute | solution.py:333
  78.1 14.0 %collective-permute-start.20 = (bf16[128,2048]{1,0:T(8,128)(2,1)S(1)}, bf16[128,2048]{1,0:T(8,128)(2,1)S(1)}, u32[]{:S(2)}, u32[]{:S(2)}) collective-permute-start(bf16[128,2048]{1,0:T(8,128)(2,1)S(1)} %shard_map.92), channel_id=1, source_target_pairs={{0,2},{1,3},{2,0},{3,1},{4,6},{5,7},{6,4},{7,5},{8,10},{9,11},{10,... | collective-permute-start | bytes 1572872 | tf_op jit(solution)/shard_map/ppermute | solution.py:336

commit v9 on v8

--- a/solution.py
+++ b/solution.py
@@ -128,7 +128,7 @@
     for head in range(heads):
         cols = slice(head * HD, (head + 1) * HD)
         wide = pl.ds(head * HD, HD)
-        bias = dist_ref[...] * (slopes_ref[head] * LOG2E)
+        bias = dist_ref[...] * (slopes_ref[head : head + 1, :] * LOG2E)
         bias = jnp.concatenate([bias] * (q_ref.shape[1] // PIECE), axis=1)
         scores = dot(k_rows[:, cols], q_ref[wide, :]) * (HD**-0.5 * LOG2E)
         scores = scores + bias + mask_ref[...]
@@ -156,8 +156,11 @@
     block = 4 * PIECE
 
     def body(s0, s1, seg_ref, gain_ref, a, b, c, d, w0, w1, q0, q1, stat0, acc0, stat1, acc1, k_cache, v_cache,
-             x, mask, dist):
+             slopes_out, x, mask, dist):
         set_own_masks(seg_ref, mask, dist)
+        for head in range(4):
+            slopes_out[head : head + 1, :] = jnp.full((1, PIECE), s0[head], F32)
+            slopes_out[4 + head : 5 + head, :] = jnp.full((1, PIECE), s1[head], F32)
         for place, piece in enumerate((a, b, c, d)):
             x[pl.ds(place * PIECE, PIECE), :] = normalise(piece[...], gain_ref[...])
         for group, (w, q, stat, acc) in enumerate(((w0, q0, stat0, acc0), (w1, q1, stat1, acc1))):
@@ -171,16 +174,17 @@
                     k_cache[to, :] = keys[place * PIECE : (place + 1) * PIECE]
                     v_cache[to, :] = values[place * PIECE : (place + 1) * PIECE].astype(BF16)
             v_t = values[: 2 * PIECE].T.astype(BF16)
-            attend(keys[: 2 * PIECE], v_t, q, (s0, s1)[group], mask, dist, None, stat, acc)
+            attend(keys[: 2 * PIECE], v_t, q, slopes_out.at[pl.ds(4 * group, 4)], mask, dist, None, stat, acc)
 
     return pl.pallas_call(
         body,
         out_shape=(jax.ShapeDtypeStruct((width, block), BF16),) * 2 + state_shapes(width, block) * 2 + (
             jax.ShapeDtypeStruct((block, width), BF16),
             jax.ShapeDtypeStruct((block, width), BF16),
+            jax.ShapeDtypeStruct((8, PIECE), F32),
         ),
         in_specs=[SMEM] * 2 + [VMEM] * 8,
-        out_specs=(VMEM,) * 8,
+        out_specs=(VMEM,) * 9,
         scratch_shapes=[
             pltpu.VMEM((block, depth), BF16),
             pltpu.VMEM((2 * PIECE, block), F32),
@@ -213,14 +217,14 @@
     send_ref[pl.ds(2 * width, 32), :] = jnp.concatenate(parts, axis=0).astype(BF16)
 
 
-def earlier_pieces(which, closing, slopes, slopes_pair, seg, segs, gain, pieces, w_own, w_pair, q_own, q_pair, state):
+def earlier_pieces(which, closing, slopes8, seg, segs, gain, pieces, w_own, w_pair, q_own, q_pair, state):
     depth, width = w_own.shape[1:]
     block = 4 * PIECE
     count = len(pieces)
     rows = len(which) * PIECE
     n_out = 3 if closing else 4
 
-    def body(s0, s1, seg_ref, gain_ref, *refs):
+    def body(slopes_ref, seg_ref, gain_ref, *refs):
         seg_refs, refs = refs[: len(segs)], refs[len(segs) :]
         sources, refs = refs[:count], refs[count:]
         (w0, w1, q0, q1), before, refs = refs[:4], (refs[4:6], refs[6:8]), refs[8:]
@@ -254,7 +258,7 @@
             for group, (w, q) in enumerate(((w0, q0), (w1, q1))):
                 keys = dot(x[...], w[1]).astype(BF16)
                 v_t = dot(x[...], w[2]).T.astype(BF16)
-                attend(keys, v_t, q, (s0, s1)[group], mask, dist, before[group], *after[group])
+                attend(keys, v_t, q, slopes_ref.at[pl.ds(4 * group, 4)], mask, dist, before[group], *after[group])
 
         @pl.when(jnp.logical_not(live))
         def _():
@@ -281,12 +285,12 @@
     return pl.pallas_call(
         body,
         out_shape=shapes,
-        in_specs=[SMEM] * 2 + [VMEM] * (10 + len(segs) + count),
+        in_specs=[VMEM] * (11 + len(segs) + count),
         out_specs=(VMEM,) * n_out,
         scratch_shapes=scratch,
         compiler_params=params(EARLIER_MIB),
         cost_estimate=cost(4 * rows * depth * width, 2**20, 0),
-    )(slopes, slopes_pair, seg, gain, *segs, *pieces, w_own, w_pair, q_own, q_pair, *state)
+    )(slopes8, seg, gain, *segs, *pieces, w_own, w_pair, q_own, q_pair, *state)
 
 
 def project(place, lse, out, got, wo_own, wo_pair, tokens):
@@ -364,21 +368,22 @@
     b2 = over_x(a2)
     crossed = over_seq(a2, even_to_odd + odd_to_even)
     d0 = over_core(b0)
-    seg23 = over_seq(jnp.concatenate([seg, seg1], axis=0), two_on)
+    seg1_sent, wo_sent, d0 = tie((seg1, w_out, d0))
+    seg23 = over_seq(jnp.concatenate([seg, seg1_sent], axis=0), two_on)
+    wo_pair = over_core(wo_sent)
     segs = [seg1, seg23[:4], seg23[4:]]
-    q_own, q_pair, *state, key_cache, value_cache = own_block(
+    q_own, q_pair, *state, key_cache, value_cache, slopes8 = own_block(
         slopes, slopes_pair, seg, gain, (tokens, b0, c0, d0), w_staged, w_pair)
 
-    crossed, b2, a4, b0_sent, wo_sent, segs, state[0] = tie((crossed, b2, a4, b0, w_out, segs, state[0]))
+    crossed, b2, a4, b0_sent, segs, state[0] = tie((crossed, b2, a4, b0, segs, state[0]))
     over_y = over_seq(pick(b0_sent, a4), even_to_odd + odd_to_even)
     x_third = over_x(crossed)
     b4 = over_seq(b2, two_on)
     seg4 = over_seq(segs[1], two_on)
-    wo_pair = over_core(wo_sent)
 
     def merge(closing, segs, pieces, which, state):
         return earlier_pieces(
-            which, closing, slopes, slopes_pair, seg, segs, gain, pieces, w_staged, w_pair, q_own, q_pair, state)
+            which, closing, slopes8, seg, segs, gain, pieces, w_staged, w_pair, q_own, q_pair, state)
 
     state = merge(
         False, segs, (a2, b2, crossed, a1_odd),

time: 93.4 us -> 90.8 us (0.972)
  waiting for transfers between devices: 32.1 us -> 23.5 us
  Pallas kernels: 25.5 us -> 33.2 us
  starting transfers between devices: 30.7 us -> 28.6 us
    ppermute x10, waiting for transfers between devices: 11.5 us -> 3.61 us  [over_seq(): return lax.ppermute(value, 'seq', pairs)]
    pallas_call x3, Pallas kernels: 12.8 us -> 20.6 us  [earlier_pieces(): pl.pallas_call(body, out_shape=shapes, in_specs=[VMEM] * (11 + len(segs)...]
    ppermute x10, starting transfers between devices: 25.6 us -> 23.5 us  [over_seq(): return lax.ppermute(value, 'seq', pairs)]
  transfers between devices with their start and end apart: 21 -> 21, of which waited for: 7 -> 6; matrix products, arithmetic and copies ran while one was open for 0% -> 0% of each run, Pallas kernels for 27% -> 36%
where the time goes in v9:
time: 90.8 us; the launch traced here: 90 us
  Pallas kernels  33.2 us (37%)
  starting transfers between devices  28.6 us (31%)
  waiting for transfers between devices  23.5 us (26%)
  local copies, waits for them, and re-layouts  2.84 us (3%)
  other arithmetic  0.94 us (1%)
  between operations  0.91 us (1%)
    ppermute x10, starting transfers between devices, over_seq(): return lax.ppermute(value, 'seq', pairs)  23.5 us
    pallas_call x3, Pallas kernels, earlier_pieces(): pl.pallas_call(body, out_shape=shapes, in_specs=[VMEM] * (11 + len(segs)...  20.6 us
    ppermute x5, waiting for transfers between devices, over_x(): return lax.ppermute(value, 'head', [(i, i ^ 2) for i in range(4)])  12.6 us
    pallas_call x1, Pallas kernels, own_block(): pl.pallas_call(body, out_shape=(jax.ShapeDtypeStruct((width, block), BF16...  10.5 us
    ppermute x6, waiting for transfers between devices, over_core(): return lax.ppermute(value, 'head', [(i, i ^ 1) for i in range(4)])  7.33 us
    ppermute x5, starting transfers between devices, over_x(): return lax.ppermute(value, 'head', [(i, i ^ 2) for i in range(4)])  4.25 us
    ppermute x10, waiting for transfers between devices, over_seq(): return lax.ppermute(value, 'seq', pairs)  3.61 us
    unnamed x12, local copies, waits for them, and re-layouts  2.8 us
  transfers between devices with their start and end apart: 21, of which 6 were waited for; matrix products, arithmetic and copies ran while one was open for 0% of the time, Pallas kernels for 36%

profile of v9, /device:TPU:12, one launch (start us, length us, event | category | flops | bytes accessed | tf_op | source)
XLA Modules:
  0.0 90.0 jit_solution(13685633830345054719)
XLA Ops:
  0.6 0.1 collective-permute-start.3
  0.7 0.5 collective-permute-start.4
  1.2 3.5 %collective-permute-start = (bf16[128,2048]{1,0:T(8,128)(2,1)}, bf16[128,2048]{1,0:T(8,128)(2,1)S(1)}, u32[]{:S(2)}, u32[]{:S(2)}) collective-permute-start(bf16[128,2048]{1,0:T(8,128)(2,1)} %refs_0_.1), channel_id=1, source_target_pairs={{0,8},{4,12},{8,16},{12,20},{16,24},{20,28},{1,9},{5,13},{9,17},{1... | collective-permute-start | bytes 1572872 | tf_op jit(solution)/shard_map/ppermute | solution.py:343
  4.7 1.6 %collective-permute-start.1 = (bf16[128,2048]{1,0:T(8,128)(2,1)}, bf16[128,2048]{1,0:T(8,128)(2,1)S(1)}, u32[]{:S(2)}, u32[]{:S(2)}) collective-permute-start(bf16[128,2048]{1,0:T(8,128)(2,1)} %refs_0_.1), channel_id=1, source_target_pairs={{0,2},{1,3},{2,0},{3,1},{4,6},{5,7},{6,4},{7,5},{8,10},{9,11},{10,... | collective-permute-start | bytes 1572872 | tf_op jit(solution)/shard_map/ppermute | solution.py:340
  6.2 1.3 %collective-permute-start.2 = (bf16[128,2048]{1,0:T(8,128)(2,1)}, bf16[128,2048]{1,0:T(8,128)(2,1)S(1)}, u32[]{:S(2)}, u32[]{:S(2)}) collective-permute-start(bf16[128,2048]{1,0:T(8,128)(2,1)} %refs_0_.1), channel_id=1, source_target_pairs={{0,4},{8,12},{16,20},{24,28},{1,5},{9,13},{17,21},{25,29},{2,6},{1... | collective-permute-start | bytes 1572872 | tf_op jit(solution)/shard_map/ppermute | solution.py:343
  7.5 4.3 %collective-permute-done.4.c = bf16[128,2048]{1,0:T(8,128)(2,1)S(1)} collective-permute-done((bf16[128,2048]{1,0:T(8,128)(2,1)}, bf16[128,2048]{1,0:T(8,128)(2,1)S(1)}, u32[]{:S(2)}, u32[]{:S(2)}) %collective-permute-start.4) | collective-permute-done | bytes 524320 | tf_op jit(solution)/shard_map/ppermute | solution.py:337
  11.8 0.1 collective-permute-start.5
  12.0 1.1 %collective-permute-done.5.s1 = f32[4]{0:T(128)S(1)} collective-permute-done((f32[4]{0:T(128)}, f32[4]{0:T(128)S(1)}, u32[]{:S(2)}, u32[]{:S(2)}) %collective-permute-start.5) | collective-permute-done | bytes 48 | tf_op jit(solution)/shard_map/ppermute | solution.py:337
  13.1 3.5 %collective-permute-start.6 = (s32[4,128]{1,0:T(4,128)}, s32[4,128]{1,0:T(4,128)S(1)}, u32[]{:S(2)}, u32[]{:S(2)}) collective-permute-start(s32[4,128]{1,0:T(4,128)} %bitcast.9), channel_id=1, source_target_pairs={{0,4},{4,8},{8,12},{12,16},{16,20},{20,24},{24,28},{1,5},{5,9},{9,... | collective-permute-start | bytes 6152 | tf_op jit(solution)/shard_map/ppermute | solution.py:343
  16.6 2.8 %copy-done.1 = bf16[2048,3,512]{2,0,1:T(8,128)(2,1)S(1)} copy-done((bf16[2048,3,512]{2,0,1:T(8,128)(2,1)S(1)}, bf16[2048,3,512]{2,0,1:T(8,128)(2,1)}, u32[]{:S(2)}) %copy-start.1) | copy-done | bytes 6291480
  19.4 0.4 shard_map.85.w0.refs_7_.refs_8_.refs_6_
  19.9 0.0 collective-permute-done.refs_3_
  19.9 0.0 collective-permute-done.1.b.even_ref
  19.9 1.8 %collective-permute-done.2.refs_6_ = bf16[128,2048]{1,0:T(8,128)(2,1)S(1)} collective-permute-done((bf16[128,2048]{1,0:T(8,128)(2,1)}, bf16[128,2048]{1,0:T(8,128)(2,1)S(1)}, u32[]{:S(2)}, u32[]{:S(2)}) %collective-permute-start.2) | collective-permute-done | bytes 524320 | tf_op jit(solution)/shard_map/ppermute | solution.py:343
  21.7 0.0 collective-permute-done.6.refs_0_
  21.7 0.0 collective-permute-done.3.w1.refs_8_.refs_9_.refs_7_
  21.7 0.0 collective-permute-start.7
  21.7 3.5 %collective-permute-start.10 = (bf16[128,2048]{1,0:T(8,128)(2,1)S(1)}, bf16[128,2048]{1,0:T(8,128)(2,1)S(1)}, u32[]{:S(2)}, u32[]{:S(2)}) collective-permute-start(bf16[128,2048]{1,0:T(8,128)(2,1)S(1)} %collective-permute-done.refs_3_), channel_id=1, source_target_pairs={{0,8},{4,12},{8,16},{12,20},{16,24},{20,28},{1,9},{5,13},{9,17},{1... | collective-permute-start | bytes 1572872 | tf_op jit(solution)/shard_map/ppermute | solution.py:343
  25.2 0.1 collective-permute-start.8
  25.3 0.6 collective-permute-start.9
  25.9 0.0 collective-permute-done.7.d
  25.9 3.1 %collective-permute-start.11 = (s32[8,128]{1,0:T(8,128)S(1)}, s32[8,128]{1,0:T(8,128)S(1)}, u32[]{:S(2)}, u32[]{:S(2)}) collective-permute-start(s32[8,128]{1,0:T(8,128)S(1)} %pad_add_fusion), channel_id=1, source_target_pairs={{0,8},{4,12},{8,16},{12,20},{16,24},{20,28},{1,9},{5,13},{9,17},{1... | collective-permute-start | bytes 12296 | tf_op jit(solution)/shard_map/ppermute | solution.py:343
  29.1 0.1 collective-permute-start.19
  29.2 10.5 %shard_map.86 = (bf16[512,512]{1,0:T(8,128)(2,1)S(1)}, bf16[512,512]{1,0:T(8,128)(2,1)S(1)}, f32[8,512]{1,0:T(8,128)S(1)}, f32[512,512]{1,0:T(8,128)S(1)}, f32[8...) custom-call(f32[4]{0:T(128)S(1)} %copy-done.5, ...), custom_call_target="tpu_custom_call" | custom-call | flops 5368709120 | bytes 1048576 | tf_op jit(solution)/shard_map/pallas_call | solution.py:179
  39.7 0.0 collective-permute-done.11
  39.7 0.0 collective-permute-done.10.odd_ref.refs_4_
  39.7 0.0 collective-permute-done.8.refs_5_
  39.7 0.1 shard_map.87
  39.8 1.4 %collective-permute-start.12 = (bf16[128,2048]{1,0:T(8,128)(2,1)S(1)}, bf16[128,2048]{1,0:T(8,128)(2,1)S(1)}, u32[]{:S(2)}, u32[]{:S(2)}) collective-permute-start(bf16[128,2048]{1,0:T(8,128)(2,1)S(1)} %shard_map.87), channel_id=1, source_target_pairs={{0,4},{8,12},{16,20},{24,28},{4,0},{12,8},{20,16},{28,24},{1,5},{9... | collective-permute-start | bytes 1572872 | tf_op jit(solution)/shard_map/ppermute | solution.py:343
  41.2 0.9 collective-permute-start.13
  42.1 1.9 %collective-permute-start.14 = (bf16[128,2048]{1,0:T(8,128)(2,1)S(1)}, bf16[128,2048]{1,0:T(8,128)(2,1)S(1)}, u32[]{:S(2)}, u32[]{:S(2)}) collective-permute-start(bf16[128,2048]{1,0:T(8,128)(2,1)S(1)} %collective-permute-done.9.refs_4_), channel_id=1, source_target_pairs={{0,8},{4,12},{8,16},{12,20},{16,24},{20,28},{1,9},{5,13},{9,17},{1... | collective-permute-start | bytes 1572872 | tf_op jit(solution)/shard_map/ppermute | solution.py:343
  44.0 1.9 %collective-permute-start.15 = (s32[4,128]{1,0:T(4,128)S(1)}, s32[4,128]{1,0:T(4,128)S(1)}, u32[]{:S(2)}, u32[]{:S(2)}) collective-permute-start(s32[4,128]{1,0:T(4,128)S(1)} %get-tuple-element.67.refs_1_), channel_id=1, source_target_pairs={{0,8},{4,12},{8,16},{12,20},{16,24},{20,28},{1,9},{5,13},{9,17},{1... | collective-permute-start | bytes 6152 | tf_op jit(solution)/shard_map/ppermute | solution.py:343
  45.9 10.1 %shard_map.88 = (f32[8,512]{1,0:T(8,128)S(1)}, f32[512,512]{1,0:T(8,128)S(1)}, f32[8,512]{1,0:T(8,128)S(1)}, f32[512,512]{1,0:T(8,128)S(1)}) custom-call(f32[8,128]{1,0:T(8,128)S(1)} %get-tuple-element.62.slopes_ref, s32[4,128]{1,0:T(4,128)S(1)} %bitcast.12, f32[1,2048]{1,0:T(1,128)S(1)} %bitcast.6, s32[4,128]{1,0:T(4,128)S(1)} %collective-permute-done.6.refs_0_, ...), custom_call_target="tpu_custom_call" | custom-call | flops 4294967296 | bytes 1048576 | tf_op jit(solution)/shard_map/pallas_call | solution.py:285
  56.0 1.8 %collective-permute-done.15.refs_3_ = s32[4,128]{1,0:T(4,128)S(1)} collective-permute-done((s32[4,128]{1,0:T(4,128)S(1)}, s32[4,128]{1,0:T(4,128)S(1)}, u32[]{:S(2)}, u32[]{:S(2)}) %collective-permute-start.15) | collective-permute-done | bytes 2080 | tf_op jit(solution)/shard_map/ppermute | solution.py:343
  57.7 0.0 collective-permute-done.14.refs_5_
  57.8 0.6 collective-permute-start.16
  58.4 3.2 %collective-permute-start.17 = (bf16[64,2048]{1,0:T(8,128)(2,1)S(1)}, bf16[64,2048]{1,0:T(8,128)(2,1)S(1)}, u32[]{:S(2)}, u32[]{:S(2)}) collective-permute-start(bf16[64,2048]{1,0:T(8,128)(2,1)S(1)} %slice.15), channel_id=1, source_target_pairs={{4,0},{12,8},{20,16},{28,24},{5,1},{13,9},{21,17},{29,25},{6,2},{1... | collective-permute-start | bytes 786440 | tf_op jit(solution)/shard_map/ppermute | solution.py:343
  61.6 10.1 %shard_map.89 = (f32[8,512]{1,0:T(8,128)S(1)}, f32[512,512]{1,0:T(8,128)S(1)}, f32[8,512]{1,0:T(8,128)S(1)}, f32[512,512]{1,0:T(8,128)S(1)}) custom-call(f32[8,128]{1,0:T(8,128)S(1)} %get-tuple-element.62.slopes_ref, s32[4,128]{1,0:T(4,128)S(1)} %bitcast.13, f32[1,2048]{1,0:T(1,128)S(1)} %bitcast.7, s32[4,128]{1,0:T(4,128)S(1)} %collective-permute-done.6.refs_0_, ...), custom_call_target="tpu_custom_call" | custom-call | flops 4294967296 | bytes 1048576 | tf_op jit(solution)/shard_map/pallas_call | solution.py:285
  71.7 0.0 collective-permute-done.17.refs_5_
  71.7 0.5 shard_map.90
  72.2 0.1 collective-permute-start.18
  72.3 1.9 %collective-permute-done.18.got_ref = bf16[1056,256]{1,0:T(8,128)(2,1)S(1)} collective-permute-done((bf16[1056,256]{1,0:T(8,128)(2,1)S(1)}, bf16[1056,256]{1,0:T(8,128)(2,1)S(1)}, u32[]{:S(2)}, u32[]{:S(2)}) %collective-permute-start.18) | collective-permute-done | bytes 540704 | tf_op jit(solution)/shard_map/ppermute | solution.py:337
  74.2 0.0 collective-permute-done.19.w1
  74.2 0.8 shard_map.92
  75.0 0.6 collective-permute-start.20
  75.6 0.8 shard_map.91
  76.5 12.6 %collective-permute-done.20 = bf16[128,2048]{1,0:T(8,128)(2,1)S(1)} collective-permute-done((bf16[128,2048]{1,0:T(8,128)(2,1)S(1)}, bf16[128,2048]{1,0:T(8,128)(2,1)S(1)}, u32[]{:S(2)}, u32[]{:S(2)}) %collective-permute-start.20) | collective-permute-done | bytes 524320 | tf_op jit(solution)/shard_map/ppermute | solution.py:340
  89.1 0.9 %add_convert_fusion = bf16[128,2048]{1,0:T(8,128)(2,1)} fusion(f32[128,2048]{1,0:T(8,128)S(1)} %shard_map.91, bf16[128,2048]{1,0:T(8,128)(2,1)S(1)} %collective-permute-done.20), kind=kLoop, calls=%fused_computation | loop fusion | flops 786432 | bytes 2097152 | tf_op jit(solution)/shard_map/convert_element_type | solution.py:405
  (19 shorter events, 0.1 us)
Async XLA Ops:
  0.6 21.1 %collective-permute-start.3 = (bf16[3,2048,512]{2,1,0:T(8,128)(2,1)}, bf16[3,2048,512]{2,1,0:T(8,128)(2,1)S(1)}, u32[]{:S(2)}, u32[]{:S(2)}) collective-permute-start(bf16[3,2048,512]{2,1,0:T(8,128)(2,1)} %bitcast.3), channel_id=1, source_target_pairs={{0,1},{1,0},{2,3},{3,2},{4,5},{5,4},{6,7},{7,6},{8,9},{9,8},{10,11... | collective-permute-start | bytes 18874376 | tf_op jit(solution)/shard_map/ppermute | solution.py:337
  0.7 11.1 %collective-permute-start.4 = (bf16[128,2048]{1,0:T(8,128)(2,1)}, bf16[128,2048]{1,0:T(8,128)(2,1)S(1)}, u32[]{:S(2)}, u32[]{:S(2)}) collective-permute-start(bf16[128,2048]{1,0:T(8,128)(2,1)} %refs_0_.1), channel_id=1, source_target_pairs={{0,1},{1,0},{2,3},{3,2},{4,5},{5,4},{6,7},{7,6},{8,9},{9,8},{10,11... | collective-permute-start | bytes 1572872 | tf_op jit(solution)/shard_map/ppermute | solution.py:337
  1.2 18.7 %collective-permute-start = (bf16[128,2048]{1,0:T(8,128)(2,1)}, bf16[128,2048]{1,0:T(8,128)(2,1)S(1)}, u32[]{:S(2)}, u32[]{:S(2)}) collective-permute-start(bf16[128,2048]{1,0:T(8,128)(2,1)} %refs_0_.1), channel_id=1, source_target_pairs={{0,8},{4,12},{8,16},{12,20},{16,24},{20,28},{1,9},{5,13},{9,17},{1... | collective-permute-start | bytes 1572872 | tf_op jit(solution)/shard_map/ppermute | solution.py:343
  4.7 15.2 %collective-permute-start.1 = (bf16[128,2048]{1,0:T(8,128)(2,1)}, bf16[128,2048]{1,0:T(8,128)(2,1)S(1)}, u32[]{:S(2)}, u32[]{:S(2)}) collective-permute-start(bf16[128,2048]{1,0:T(8,128)(2,1)} %refs_0_.1), channel_id=1, source_target_pairs={{0,2},{1,3},{2,0},{3,1},{4,6},{5,7},{6,4},{7,5},{8,10},{9,11},{10,... | collective-permute-start | bytes 1572872 | tf_op jit(solution)/shard_map/ppermute | solution.py:340
  6.2 15.5 %collective-permute-start.2 = (bf16[128,2048]{1,0:T(8,128)(2,1)}, bf16[128,2048]{1,0:T(8,128)(2,1)S(1)}, u32[]{:S(2)}, u32[]{:S(2)}) collective-permute-start(bf16[128,2048]{1,0:T(8,128)(2,1)} %refs_0_.1), channel_id=1, source_target_pairs={{0,4},{8,12},{16,20},{24,28},{1,5},{9,13},{17,21},{25,29},{2,6},{1... | collective-permute-start | bytes 1572872 | tf_op jit(solution)/shard_map/ppermute | solution.py:343
  11.8 1.3 %collective-permute-start.5 = (f32[4]{0:T(128)}, f32[4]{0:T(128)S(1)}, u32[]{:S(2)}, u32[]{:S(2)}) collective-permute-start(f32[4]{0:T(128)} %s0.1), channel_id=1, source_target_pairs={{0,1},{1,0},{2,3},{3,2},{4,5},{5,4},{6,7},{7,6},{8,9},{9,8},{10,11... | collective-permute-start | bytes 56 | tf_op jit(solution)/shard_map/ppermute | solution.py:337
  13.1 16.0 %copy-start = (bf16[512,2048]{1,0:T(8,128)(2,1)S(1)}, bf16[512,2048]{1,0:T(8,128)(2,1)}, u32[]{:S(2)}) copy-start(bf16[512,2048]{1,0:T(8,128)(2,1)} %w0.3) | copy-start | bytes 6291460
  13.1 8.7 %collective-permute-start.6 = (s32[4,128]{1,0:T(4,128)}, s32[4,128]{1,0:T(4,128)S(1)}, u32[]{:S(2)}, u32[]{:S(2)}) collective-permute-start(s32[4,128]{1,0:T(4,128)} %bitcast.9), channel_id=1, source_target_pairs={{0,4},{4,8},{8,12},{12,16},{16,20},{20,24},{24,28},{1,5},{5,9},{9,... | collective-permute-start | bytes 6152 | tf_op jit(solution)/shard_map/ppermute | solution.py:343
  16.6 2.8 %copy-start.1 = (bf16[2048,3,512]{2,0,1:T(8,128)(2,1)S(1)}, bf16[2048,3,512]{2,0,1:T(8,128)(2,1)}, u32[]{:S(2)}) copy-start(bf16[2048,3,512]{2,0,1:T(8,128)(2,1)} %param.8) | copy-start | bytes 18874372
  19.4 6.5 %copy-start.4 = (s32[512]{0:T(512)S(1)}, s32[512]{0:T(512)}, u32[]{:S(2)}) copy-start(s32[512]{0:T(512)} %param.11) | copy-start | bytes 6148
  19.4 9.7 %copy-start.2 = (bf16[128,2048]{1,0:T(8,128)(2,1)S(1)}, bf16[128,2048]{1,0:T(8,128)(2,1)}, u32[]{:S(2)}) copy-start(bf16[128,2048]{1,0:T(8,128)(2,1)} %refs_0_.1) | copy-start | bytes 1572868
  19.4 9.7 %copy-start.3 = (f32[2048]{0:T(1024)S(1)}, f32[2048]{0:T(1024)}, u32[]{:S(2)}) copy-start(f32[2048]{0:T(1024)} %param.7) | copy-start | bytes 24580
  19.4 9.8 %copy-start.5 = (f32[4]{0:T(128)S(1)}, f32[4]{0:T(128)}, u32[]{:S(2)}) copy-start(f32[4]{0:T(128)} %s0.1) | copy-start | bytes 52
  21.7 4.2 %collective-permute-start.7 = (bf16[128,2048]{1,0:T(8,128)(2,1)S(1)}, bf16[128,2048]{1,0:T(8,128)(2,1)S(1)}, u32[]{:S(2)}, u32[]{:S(2)}) collective-permute-start(bf16[128,2048]{1,0:T(8,128)(2,1)S(1)} %collective-permute-done.1.b.even_ref), channel_id=1, source_target_pairs={{0,1},{1,0},{2,3},{3,2},{4,5},{5,4},{6,7},{7,6},{8,9},{9,8},{10,11... | collective-permute-start | bytes 1572872 | tf_op jit(solution)/shard_map/ppermute | solution.py:337
  21.7 17.9 %collective-permute-start.10 = (bf16[128,2048]{1,0:T(8,128)(2,1)S(1)}, bf16[128,2048]{1,0:T(8,128)(2,1)S(1)}, u32[]{:S(2)}, u32[]{:S(2)}) collective-permute-start(bf16[128,2048]{1,0:T(8,128)(2,1)S(1)} %collective-permute-done.refs_3_), channel_id=1, source_target_pairs={{0,8},{4,12},{8,16},{12,20},{16,24},{20,28},{1,9},{5,13},{9,17},{1... | collective-permute-start | bytes 1572872 | tf_op jit(solution)/shard_map/ppermute | solution.py:343
  25.2 14.5 %collective-permute-start.8 = (bf16[128,2048]{1,0:T(8,128)(2,1)S(1)}, bf16[128,2048]{1,0:T(8,128)(2,1)S(1)}, u32[]{:S(2)}, u32[]{:S(2)}) collective-permute-start(bf16[128,2048]{1,0:T(8,128)(2,1)S(1)} %collective-permute-done.refs_3_), channel_id=1, source_target_pairs={{0,4},{8,12},{16,20},{24,28},{4,0},{12,8},{20,16},{28,24},{1,5},{9... | collective-permute-start | bytes 1572872 | tf_op jit(solution)/shard_map/ppermute | solution.py:343
  25.3 14.4 %collective-permute-start.9 = (bf16[128,2048]{1,0:T(8,128)(2,1)S(1)}, bf16[128,2048]{1,0:T(8,128)(2,1)S(1)}, u32[]{:S(2)}, u32[]{:S(2)}) collective-permute-start(bf16[128,2048]{1,0:T(8,128)(2,1)S(1)} %collective-permute-done.refs_3_), channel_id=1, source_target_pairs={{0,2},{1,3},{2,0},{3,1},{4,6},{5,7},{6,4},{7,5},{8,10},{9,11},{10,... | collective-permute-start | bytes 1572872 | tf_op jit(solution)/shard_map/ppermute | solution.py:340
  25.9 13.8 %collective-permute-start.11 = (s32[8,128]{1,0:T(8,128)S(1)}, s32[8,128]{1,0:T(8,128)S(1)}, u32[]{:S(2)}, u32[]{:S(2)}) collective-permute-start(s32[8,128]{1,0:T(8,128)S(1)} %pad_add_fusion), channel_id=1, source_target_pairs={{0,8},{4,12},{8,16},{12,20},{16,24},{20,28},{1,9},{5,13},{9,17},{1... | collective-permute-start | bytes 12296 | tf_op jit(solution)/shard_map/ppermute | solution.py:343
  29.1 45.1 %collective-permute-start.19 = (bf16[512,2048]{1,0:T(8,128)(2,1)S(1)}, bf16[512,2048]{1,0:T(8,128)(2,1)S(1)}, u32[]{:S(2)}, u32[]{:S(2)}) collective-permute-start(bf16[512,2048]{1,0:T(8,128)(2,1)S(1)} %copy-done), channel_id=1, source_target_pairs={{0,1},{1,0},{2,3},{3,2},{4,5},{5,4},{6,7},{7,6},{8,9},{9,8},{10,11... | collective-permute-start | bytes 6291464 | tf_op jit(solution)/shard_map/ppermute | solution.py:337
  39.8 18.0 %collective-permute-start.12 = (bf16[128,2048]{1,0:T(8,128)(2,1)S(1)}, bf16[128,2048]{1,0:T(8,128)(2,1)S(1)}, u32[]{:S(2)}, u32[]{:S(2)}) collective-permute-start(bf16[128,2048]{1,0:T(8,128)(2,1)S(1)} %shard_map.87), channel_id=1, source_target_pairs={{0,4},{8,12},{16,20},{24,28},{4,0},{12,8},{20,16},{28,24},{1,5},{9... | collective-permute-start | bytes 1572872 | tf_op jit(solution)/shard_map/ppermute | solution.py:343
  41.2 16.5 %collective-permute-start.13 = (bf16[128,2048]{1,0:T(8,128)(2,1)S(1)}, bf16[128,2048]{1,0:T(8,128)(2,1)S(1)}, u32[]{:S(2)}, u32[]{:S(2)}) collective-permute-start(bf16[128,2048]{1,0:T(8,128)(2,1)S(1)} %collective-permute-done.8.refs_5_), channel_id=1, source_target_pairs={{0,2},{1,3},{2,0},{3,1},{4,6},{5,7},{6,4},{7,5},{8,10},{9,11},{10,... | collective-permute-start | bytes 1572872 | tf_op jit(solution)/shard_map/ppermute | solution.py:340
  42.1 15.7 %collective-permute-start.14 = (bf16[128,2048]{1,0:T(8,128)(2,1)S(1)}, bf16[128,2048]{1,0:T(8,128)(2,1)S(1)}, u32[]{:S(2)}, u32[]{:S(2)}) collective-permute-start(bf16[128,2048]{1,0:T(8,128)(2,1)S(1)} %collective-permute-done.9.refs_4_), channel_id=1, source_target_pairs={{0,8},{4,12},{8,16},{12,20},{16,24},{20,28},{1,9},{5,13},{9,17},{1... | collective-permute-start | bytes 1572872 | tf_op jit(solution)/shard_map/ppermute | solution.py:343
  44.0 13.7 %collective-permute-start.15 = (s32[4,128]{1,0:T(4,128)S(1)}, s32[4,128]{1,0:T(4,128)S(1)}, u32[]{:S(2)}, u32[]{:S(2)}) collective-permute-start(s32[4,128]{1,0:T(4,128)S(1)} %get-tuple-element.67.refs_1_), channel_id=1, source_target_pairs={{0,8},{4,12},{8,16},{12,20},{16,24},{20,28},{1,9},{5,13},{9,17},{1... | collective-permute-start | bytes 6152 | tf_op jit(solution)/shard_map/ppermute | solution.py:343
  57.8 13.9 %collective-permute-start.16 = (bf16[64,2048]{1,0:T(8,128)(2,1)S(1)}, bf16[64,2048]{1,0:T(8,128)(2,1)S(1)}, u32[]{:S(2)}, u32[]{:S(2)}) collective-permute-start(bf16[64,2048]{1,0:T(8,128)(2,1)S(1)} %slice.14), channel_id=1, source_target_pairs={{0,2},{1,3},{2,0},{3,1},{4,6},{5,7},{6,4},{7,5},{8,10},{9,11},{10,... | collective-permute-start | bytes 786440 | tf_op jit(solution)/shard_map/ppermute | solution.py:340
  58.4 13.3 %collective-permute-start.17 = (bf16[64,2048]{1,0:T(8,128)(2,1)S(1)}, bf16[64,2048]{1,0:T(8,128)(2,1)S(1)}, u32[]{:S(2)}, u32[]{:S(2)}) collective-permute-start(bf16[64,2048]{1,0:T(8,128)(2,1)S(1)} %slice.15), channel_id=1, source_target_pairs={{4,0},{12,8},{20,16},{28,24},{5,1},{13,9},{21,17},{29,25},{6,2},{1... | collective-permute-start | bytes 786440 | tf_op jit(solution)/shard_map/ppermute | solution.py:343
  72.2 2.0 %collective-permute-start.18 = (bf16[1056,256]{1,0:T(8,128)(2,1)S(1)}, bf16[1056,256]{1,0:T(8,128)(2,1)S(1)}, u32[]{:S(2)}, u32[]{:S(2)}) collective-permute-start(bf16[1056,256]{1,0:T(8,128)(2,1)S(1)} %get-tuple-element.95), channel_id=1, source_target_pairs={{0,1},{1,0},{2,3},{3,2},{4,5},{5,4},{6,7},{7,6},{8,9},{9,8},{10,11... | collective-permute-start | bytes 1622024 | tf_op jit(solution)/shard_map/ppermute | solution.py:337
  75.0 14.0 %collective-permute-start.20 = (bf16[128,2048]{1,0:T(8,128)(2,1)S(1)}, bf16[128,2048]{1,0:T(8,128)(2,1)S(1)}, u32[]{:S(2)}, u32[]{:S(2)}) collective-permute-start(bf16[128,2048]{1,0:T(8,128)(2,1)S(1)} %shard_map.92), channel_id=1, source_target_pairs={{0,2},{1,3},{2,0},{3,1},{4,6},{5,7},{6,4},{7,5},{8,10},{9,11},{10,... | collective-permute-start | bytes 1572872 | tf_op jit(solution)/shard_map/ppermute | solution.py:340

commit v10 on v9

--- a/solution.py
+++ b/solution.py
@@ -356,11 +356,10 @@
     b0 = over_x(tokens)
     a1_odd = over_seq(tokens, even_to_odd)
     c0 = over_core(tokens)
-    slopes_sent, w_staged, c0 = tie((slopes, w_all, c0))
+    slopes_sent, w_staged, c0 = tie((slopes, stage(w_all), c0))
     slopes_pair = over_core(slopes_sent)
     seg_sent, slopes_pair = tie((seg, slopes_pair))
     seg1 = over_seq(seg_sent, [(i, i + 1) for i in range(blocks - 1)])
-    w_staged = stage(w_staged)
 
     a2, b0, a1_odd, w_pair, w_staged, slopes_pair, seg1 = tie(
         (a2, b0, a1_odd, w_pair, w_staged, slopes_pair, seg1))
@@ -368,35 +367,35 @@
     b2 = over_x(a2)
     crossed = over_seq(a2, even_to_odd + odd_to_even)
     d0 = over_core(b0)
-    seg1_sent, wo_sent, d0 = tie((seg1, w_out, d0))
+    seg1_sent, seg_sent, d0 = tie((seg1, seg, d0))
     seg23 = over_seq(jnp.concatenate([seg, seg1_sent], axis=0), two_on)
-    wo_pair = over_core(wo_sent)
-    segs = [seg1, seg23[:4], seg23[4:]]
+    seg4 = over_seq(seg_sent, [(i, i + SPAN) for i in range(blocks - SPAN)])
+    segs = [seg1, seg23[:4], seg23[4:], seg4]
     q_own, q_pair, *state, key_cache, value_cache, slopes8 = own_block(
         slopes, slopes_pair, seg, gain, (tokens, b0, c0, d0), w_staged, w_pair)
 
     crossed, b2, a4, b0_sent, segs, state[0] = tie((crossed, b2, a4, b0, segs, state[0]))
-    over_y = over_seq(pick(b0_sent, a4), even_to_odd + odd_to_even)
+    picked = pick(b0_sent, a4)
+    over_y = over_seq(picked, even_to_odd + odd_to_even)
     x_third = over_x(crossed)
     b4 = over_seq(b2, two_on)
-    seg4 = over_seq(segs[1], two_on)
+    wo_sent, picked = tie((w_out, picked))
+    wo_pair = over_core(wo_sent)
 
     def merge(closing, segs, pieces, which, state):
         return earlier_pieces(
             which, closing, slopes8, seg, segs, gain, pieces, w_staged, w_pair, q_own, q_pair, state)
 
     state = merge(
-        False, segs, (a2, b2, crossed, a1_odd),
-        (((2, 0),) * 2, ((2, 1),) * 2, ((1, 0), (3, 0)), ((0, 0), (1, 0))), state)
-
-    over_y, x_third, b4, seg4, held = tie((over_y, x_third, b4, seg4, state[0]))
-    segs = [*segs, seg4]
+        False, segs, (a2, b2, a4, crossed, a1_odd),
+        (((2, 0),) * 2, ((2, 1),) * 2, ((4, 0),) * 2, ((1, 0), (3, 0)), ((0, 0), (1, 0))), state)
+
+    over_y, x_third, b4, held = tie((over_y, x_third, b4, state[0]))
     state = (held, *state[1:])
     b3_top = over_x(over_y[: PIECE // 2])
     b3_rest = over_seq(b4[PIECE // 2 :], odd_to_even)
     state = merge(
-        False, segs, (a4, b4, x_third, over_y),
-        (((4, 0),) * 2, ((4, 1),) * 2, ((1, 1), (3, 1)), ((3, 0), (1, 1))), state)
+        False, segs, (b4, x_third, over_y), (((4, 1),) * 2, ((1, 1), (3, 1)), ((3, 0), (1, 1))), state)
     send, lse, out = merge(True, segs, (b3_top, b3_rest), (((3, 1), (0, 0)),), state)
     got = over_core(send)
     y_pair = project(1, lse, out, got, w_out, wo_pair, None)

time: 90.8 us -> 90.1 us (level)
  waiting for transfers between devices: 23.5 us -> 19.5 us
  starting transfers between devices: 28.6 us -> 32.4 us
    ppermute x6, waiting for transfers between devices: 7.33 us -> 3.97 us  [over_core(): return lax.ppermute(value, 'head', [(i, i ^ 1) for i in range(4)])]
    ppermute x10, starting transfers between devices: 23.5 us -> 25.6 us  [over_seq(): return lax.ppermute(value, 'seq', pairs)]
    ppermute x5, starting transfers between devices: 4.25 us -> 5.87 us  [over_x(): return lax.ppermute(value, 'head', [(i, i ^ 2) for i in range(4)])]
    ppermute x5, waiting for transfers between devices: 12.6 us -> 11.6 us  [over_x(): return lax.ppermute(value, 'head', [(i, i ^ 2) for i in range(4)])]
where the time goes in v10:
time: 90.1 us; the launch traced here: 89.8 us
  Pallas kernels  33.3 us (37%)
  starting transfers between devices  32.4 us (36%)
  waiting for transfers between devices  19.5 us (22%)
  local copies, waits for them, and re-layouts  2.84 us (3%)
  between operations  0.94 us (1%)
    ppermute x10, starting transfers between devices, over_seq(): return lax.ppermute(value, 'seq', pairs)  25.6 us
    pallas_call x3, Pallas kernels, earlier_pieces(): pl.pallas_call(body, out_shape=shapes, in_specs=[VMEM] * (11 + len(segs)...  20.6 us
    ppermute x5, waiting for transfers between devices, over_x(): return lax.ppermute(value, 'head', [(i, i ^ 2) for i in range(4)])  11.6 us
    pallas_call x1, Pallas kernels, own_block(): pl.pallas_call(body, out_shape=(jax.ShapeDtypeStruct((width, block), BF16...  10.5 us
    ppermute x5, starting transfers between devices, over_x(): return lax.ppermute(value, 'head', [(i, i ^ 2) for i in range(4)])  5.87 us
    ppermute x6, waiting for transfers between devices, over_core(): return lax.ppermute(value, 'head', [(i, i ^ 1) for i in range(4)])  3.97 us
    ppermute x10, waiting for transfers between devices, over_seq(): return lax.ppermute(value, 'seq', pairs)  3.89 us
    unnamed x12, local copies, waits for them, and re-layouts  2.8 us
  transfers between devices with their start and end apart: 21, of which 6 were waited for; matrix products, arithmetic and copies ran while one was open for 0% of the time, Pallas kernels for 36%

profile of v10, /device:TPU:12, one launch (start us, length us, event | category | flops | bytes accessed | tf_op | source)
XLA Modules:
  0.0 89.8 jit_solution(2699055599307156577)
XLA Ops:
  0.6 0.1 collective-permute-start.3
  0.7 0.5 collective-permute-start.4
  1.2 1.3 %collective-permute-start.2 = (bf16[128,2048]{1,0:T(8,128)(2,1)}, bf16[128,2048]{1,0:T(8,128)(2,1)S(1)}, u32[]{:S(2)}, u32[]{:S(2)}) collective-permute-start(bf16[128,2048]{1,0:T(8,128)(2,1)} %refs_0_.1), channel_id=1, source_target_pairs={{0,4},{8,12},{16,20},{24,28},{1,5},{9,13},{17,21},{25,29},{2,6},{1... | collective-permute-start | bytes 1572872 | tf_op jit(solution)/shard_map/ppermute | solution.py:343
  2.5 1.6 %collective-permute-start.1 = (bf16[128,2048]{1,0:T(8,128)(2,1)}, bf16[128,2048]{1,0:T(8,128)(2,1)S(1)}, u32[]{:S(2)}, u32[]{:S(2)}) collective-permute-start(bf16[128,2048]{1,0:T(8,128)(2,1)} %refs_0_.1), channel_id=1, source_target_pairs={{0,2},{1,3},{2,0},{3,1},{4,6},{5,7},{6,4},{7,5},{8,10},{9,11},{10,... | collective-permute-start | bytes 1572872 | tf_op jit(solution)/shard_map/ppermute | solution.py:340
  4.1 3.5 %collective-permute-start = (bf16[128,2048]{1,0:T(8,128)(2,1)}, bf16[128,2048]{1,0:T(8,128)(2,1)S(1)}, u32[]{:S(2)}, u32[]{:S(2)}) collective-permute-start(bf16[128,2048]{1,0:T(8,128)(2,1)} %refs_0_.1), channel_id=1, source_target_pairs={{0,8},{4,12},{8,16},{12,20},{16,24},{20,28},{1,9},{5,13},{9,17},{1... | collective-permute-start | bytes 1572872 | tf_op jit(solution)/shard_map/ppermute | solution.py:343
  7.6 2.8 %copy-done.1 = bf16[2048,3,512]{2,0,1:T(8,128)(2,1)S(1)} copy-done((bf16[2048,3,512]{2,0,1:T(8,128)(2,1)S(1)}, bf16[2048,3,512]{2,0,1:T(8,128)(2,1)}, u32[]{:S(2)}) %copy-start.1) | copy-done | bytes 6291480
  10.3 0.4 shard_map.85.w0.refs_9_.refs_7_.refs_6_
  10.8 1.1 %collective-permute-done.4.c = bf16[128,2048]{1,0:T(8,128)(2,1)S(1)} collective-permute-done((bf16[128,2048]{1,0:T(8,128)(2,1)}, bf16[128,2048]{1,0:T(8,128)(2,1)S(1)}, u32[]{:S(2)}, u32[]{:S(2)}) %collective-permute-start.4) | collective-permute-done | bytes 524320 | tf_op jit(solution)/shard_map/ppermute | solution.py:337
  11.8 0.1 collective-permute-start.5
  12.0 1.0 %collective-permute-done.5.s1 = f32[4]{0:T(128)S(1)} collective-permute-done((f32[4]{0:T(128)S(1)}, f32[4]{0:T(128)S(1)}, u32[]{:S(2)}, u32[]{:S(2)}) %collective-permute-start.5) | collective-permute-done | bytes 48 | tf_op jit(solution)/shard_map/ppermute | solution.py:337
  13.0 4.6 %collective-permute-start.6 = (s32[4,128]{1,0:T(4,128)S(1)}, s32[4,128]{1,0:T(4,128)S(1)}, u32[]{:S(2)}, u32[]{:S(2)}) collective-permute-start(s32[4,128]{1,0:T(4,128)S(1)} %bitcast.9), channel_id=1, source_target_pairs={{0,4},{4,8},{8,12},{12,16},{16,20},{20,24},{24,28},{1,5},{5,9},{9,... | collective-permute-start | bytes 6152 | tf_op jit(solution)/shard_map/ppermute | solution.py:343
  17.6 0.0 collective-permute-done.2.refs_8_
  17.6 0.0 collective-permute-done.1.b.even_ref
  17.6 2.2 %collective-permute-done.refs_4_ = bf16[128,2048]{1,0:T(8,128)(2,1)S(1)} collective-permute-done((bf16[128,2048]{1,0:T(8,128)(2,1)}, bf16[128,2048]{1,0:T(8,128)(2,1)S(1)}, u32[]{:S(2)}, u32[]{:S(2)}) %collective-permute-start) | collective-permute-done | bytes 524320 | tf_op jit(solution)/shard_map/ppermute | solution.py:343
  19.8 0.0 collective-permute-done.6.refs_0_
  19.8 0.0 collective-permute-done.3.w1.refs_10_.refs_8_.refs_7_
  19.8 0.0 collective-permute-start.7
  19.8 3.5 %collective-permute-start.10 = (bf16[128,2048]{1,0:T(8,128)(2,1)S(1)}, bf16[128,2048]{1,0:T(8,128)(2,1)S(1)}, u32[]{:S(2)}, u32[]{:S(2)}) collective-permute-start(bf16[128,2048]{1,0:T(8,128)(2,1)S(1)} %collective-permute-done.refs_4_), channel_id=1, source_target_pairs={{0,8},{4,12},{8,16},{12,20},{16,24},{20,28},{1,9},{5,13},{9,17},{1... | collective-permute-start | bytes 1572872 | tf_op jit(solution)/shard_map/ppermute | solution.py:343
  23.3 0.6 collective-permute-start.9
  23.9 2.4 %collective-permute-start.8 = (bf16[128,2048]{1,0:T(8,128)(2,1)S(1)}, bf16[128,2048]{1,0:T(8,128)(2,1)S(1)}, u32[]{:S(2)}, u32[]{:S(2)}) collective-permute-start(bf16[128,2048]{1,0:T(8,128)(2,1)S(1)} %collective-permute-done.refs_4_), channel_id=1, source_target_pairs={{0,4},{8,12},{16,20},{24,28},{4,0},{12,8},{20,16},{28,24},{1,5},{9... | collective-permute-start | bytes 1572872 | tf_op jit(solution)/shard_map/ppermute | solution.py:343
  26.3 0.0 collective-permute-done.7.d
  26.3 2.3 %collective-permute-start.12 = (s32[4,128]{1,0:T(4,128)S(1)}, s32[4,128]{1,0:T(4,128)S(1)}, u32[]{:S(2)}, u32[]{:S(2)}) collective-permute-start(s32[4,128]{1,0:T(4,128)S(1)} %bitcast.11), channel_id=1, source_target_pairs={{0,16},{4,20},{8,24},{12,28},{1,17},{5,21},{9,25},{13,29},{2,18},{... | collective-permute-start | bytes 6152 | tf_op jit(solution)/shard_map/ppermute | solution.py:343
  28.6 2.5 %collective-permute-start.11 = (s32[8,128]{1,0:T(8,128)S(1)}, s32[8,128]{1,0:T(8,128)S(1)}, u32[]{:S(2)}, u32[]{:S(2)}) collective-permute-start(s32[8,128]{1,0:T(8,128)S(1)} %pad_add_fusion), channel_id=1, source_target_pairs={{0,8},{4,12},{8,16},{12,20},{16,24},{20,28},{1,9},{5,13},{9,17},{1... | collective-permute-start | bytes 12296 | tf_op jit(solution)/shard_map/ppermute | solution.py:343
  31.1 0.0 copy-start
  31.1 10.5 %shard_map.86 = (bf16[512,512]{1,0:T(8,128)(2,1)S(1)}, bf16[512,512]{1,0:T(8,128)(2,1)S(1)}, f32[8,512]{1,0:T(8,128)S(1)}, f32[512,512]{1,0:T(8,128)S(1)}, f32[8...) custom-call(f32[4]{0:T(128)S(1)} %copy-done.5, ...), custom_call_target="tpu_custom_call" | custom-call | flops 5368709120 | bytes 1048576 | tf_op jit(solution)/shard_map/pallas_call | solution.py:179
  41.6 0.0 collective-permute-done.11
  41.6 0.0 collective-permute-done.10.odd_ref.refs_6_
  41.6 0.0 collective-permute-done.9.refs_5_
  41.7 0.1 shard_map.87
  41.7 0.1 collective-permute-start.19
  41.8 0.1 collective-permute-start.13
  41.9 1.6 %collective-permute-start.14 = (bf16[128,2048]{1,0:T(8,128)(2,1)S(1)}, bf16[128,2048]{1,0:T(8,128)(2,1)S(1)}, u32[]{:S(2)}, u32[]{:S(2)}) collective-permute-start(bf16[128,2048]{1,0:T(8,128)(2,1)S(1)} %collective-permute-done.8.refs_7_), channel_id=1, source_target_pairs={{0,2},{1,3},{2,0},{3,1},{4,6},{5,7},{6,4},{7,5},{8,10},{9,11},{10,... | collective-permute-start | bytes 1572872 | tf_op jit(solution)/shard_map/ppermute | solution.py:340
  43.4 1.9 %collective-permute-start.15 = (bf16[128,2048]{1,0:T(8,128)(2,1)S(1)}, bf16[128,2048]{1,0:T(8,128)(2,1)S(1)}, u32[]{:S(2)}, u32[]{:S(2)}) collective-permute-start(bf16[128,2048]{1,0:T(8,128)(2,1)S(1)} %collective-permute-done.9.refs_5_), channel_id=1, source_target_pairs={{0,8},{4,12},{8,16},{12,20},{16,24},{20,28},{1,9},{5,13},{9,17},{1... | collective-permute-start | bytes 1572872 | tf_op jit(solution)/shard_map/ppermute | solution.py:343
  45.4 12.2 %shard_map.88 = (f32[8,512]{1,0:T(8,128)S(1)}, f32[512,512]{1,0:T(8,128)S(1)}, f32[8,512]{1,0:T(8,128)S(1)}, f32[512,512]{1,0:T(8,128)S(1)}) custom-call(f32[8,128]{1,0:T(8,128)S(1)} %get-tuple-element.63.slopes_ref, s32[4,128]{1,0:T(4,128)S(1)} %bitcast.13, f32[1,2048]{1,0:T(1,128)S(1)} %bitcast.6, s32[4,128]{1,0:T(4,128)S(1)} %collective-permute-done.6.refs_0_, ...), custom_call_target="tpu_custom_call" | custom-call | flops 5368709120 | bytes 1048576 | tf_op jit(solution)/shard_map/pallas_call | solution.py:285
  57.6 1.7 %collective-permute-done.15.refs_4_ = bf16[128,2048]{1,0:T(8,128)(2,1)S(1)} collective-permute-done((bf16[128,2048]{1,0:T(8,128)(2,1)S(1)}, bf16[128,2048]{1,0:T(8,128)(2,1)S(1)}, u32[]{:S(2)}, u32[]{:S(2)}) %collective-permute-start.15) | collective-permute-done | bytes 524320 | tf_op jit(solution)/shard_map/ppermute | solution.py:343
  59.3 3.7 %collective-permute-start.17 = (bf16[64,2048]{1,0:T(8,128)(2,1)S(1)}, bf16[64,2048]{1,0:T(8,128)(2,1)S(1)}, u32[]{:S(2)}, u32[]{:S(2)}) collective-permute-start(bf16[64,2048]{1,0:T(8,128)(2,1)S(1)} %slice.15), channel_id=1, source_target_pairs={{4,0},{12,8},{20,16},{28,24},{5,1},{13,9},{21,17},{29,25},{6,2},{1... | collective-permute-start | bytes 786440 | tf_op jit(solution)/shard_map/ppermute | solution.py:343
  63.0 0.6 collective-permute-start.16
  63.6 8.0 %shard_map.89 = (f32[8,512]{1,0:T(8,128)S(1)}, f32[512,512]{1,0:T(8,128)S(1)}, f32[8,512]{1,0:T(8,128)S(1)}, f32[512,512]{1,0:T(8,128)S(1)}) custom-call(f32[8,128]{1,0:T(8,128)S(1)} %get-tuple-element.63.slopes_ref, s32[4,128]{1,0:T(4,128)S(1)} %bitcast.14, f32[1,2048]{1,0:T(1,128)S(1)} %bitcast.7, s32[4,128]{1,0:T(4,128)S(1)} %collective-permute-done.6.refs_0_, ...), custom_call_target="tpu_custom_call" | custom-call | flops 3221225472 | bytes 1048576 | tf_op jit(solution)/shard_map/pallas_call | solution.py:285
  71.6 0.0 collective-permute-done.17.refs_5_
  71.6 0.5 shard_map.90
  72.1 0.1 collective-permute-start.18
  72.1 1.9 %collective-permute-done.18.got_ref = bf16[1056,256]{1,0:T(8,128)(2,1)S(1)} collective-permute-done((bf16[1056,256]{1,0:T(8,128)(2,1)S(1)}, bf16[1056,256]{1,0:T(8,128)(2,1)S(1)}, u32[]{:S(2)}, u32[]{:S(2)}) %collective-permute-start.18) | collective-permute-done | bytes 540704 | tf_op jit(solution)/shard_map/ppermute | solution.py:337
  74.1 0.0 collective-permute-done.19.w1
  74.1 0.8 shard_map.92
  74.9 1.6 %collective-permute-start.20 = (bf16[128,2048]{1,0:T(8,128)(2,1)S(1)}, bf16[128,2048]{1,0:T(8,128)(2,1)S(1)}, u32[]{:S(2)}, u32[]{:S(2)}) collective-permute-start(bf16[128,2048]{1,0:T(8,128)(2,1)S(1)} %shard_map.92), channel_id=1, source_target_pairs={{0,2},{1,3},{2,0},{3,1},{4,6},{5,7},{6,4},{7,5},{8,10},{9,11},{10,... | collective-permute-start | bytes 1572872 | tf_op jit(solution)/shard_map/ppermute | solution.py:340
  76.4 0.8 shard_map.91
  77.3 11.6 %collective-permute-done.20 = bf16[128,2048]{1,0:T(8,128)(2,1)S(1)} collective-permute-done((bf16[128,2048]{1,0:T(8,128)(2,1)S(1)}, bf16[128,2048]{1,0:T(8,128)(2,1)S(1)}, u32[]{:S(2)}, u32[]{:S(2)}) %collective-permute-start.20) | collective-permute-done | bytes 524320 | tf_op jit(solution)/shard_map/ppermute | solution.py:340
  88.9 0.9 add_convert_fusion
  (19 shorter events, 0.1 us)
Async XLA Ops:
  0.6 11.2 %copy-start.5 = (f32[4]{0:T(128)S(1)}, f32[4]{0:T(128)}, u32[]{:S(2)}) copy-start(f32[4]{0:T(128)} %s0.1) | copy-start | bytes 52
  0.6 19.2 %collective-permute-start.3 = (bf16[3,2048,512]{2,1,0:T(8,128)(2,1)}, bf16[3,2048,512]{2,1,0:T(8,128)(2,1)S(1)}, u32[]{:S(2)}, u32[]{:S(2)}) collective-permute-start(bf16[3,2048,512]{2,1,0:T(8,128)(2,1)} %bitcast.3), channel_id=1, source_target_pairs={{0,1},{1,0},{2,3},{3,2},{4,5},{5,4},{6,7},{7,6},{8,9},{9,8},{10,11... | collective-permute-start | bytes 18874376 | tf_op jit(solution)/shard_map/ppermute | solution.py:337
  0.7 11.1 %collective-permute-start.4 = (bf16[128,2048]{1,0:T(8,128)(2,1)}, bf16[128,2048]{1,0:T(8,128)(2,1)S(1)}, u32[]{:S(2)}, u32[]{:S(2)}) collective-permute-start(bf16[128,2048]{1,0:T(8,128)(2,1)} %refs_0_.1), channel_id=1, source_target_pairs={{0,1},{1,0},{2,3},{3,2},{4,5},{5,4},{6,7},{7,6},{8,9},{9,8},{10,11... | collective-permute-start | bytes 1572872 | tf_op jit(solution)/shard_map/ppermute | solution.py:337
  1.2 16.4 %collective-permute-start.2 = (bf16[128,2048]{1,0:T(8,128)(2,1)}, bf16[128,2048]{1,0:T(8,128)(2,1)S(1)}, u32[]{:S(2)}, u32[]{:S(2)}) collective-permute-start(bf16[128,2048]{1,0:T(8,128)(2,1)} %refs_0_.1), channel_id=1, source_target_pairs={{0,4},{8,12},{16,20},{24,28},{1,5},{9,13},{17,21},{25,29},{2,6},{1... | collective-permute-start | bytes 1572872 | tf_op jit(solution)/shard_map/ppermute | solution.py:343
  2.5 15.1 %collective-permute-start.1 = (bf16[128,2048]{1,0:T(8,128)(2,1)}, bf16[128,2048]{1,0:T(8,128)(2,1)S(1)}, u32[]{:S(2)}, u32[]{:S(2)}) collective-permute-start(bf16[128,2048]{1,0:T(8,128)(2,1)} %refs_0_.1), channel_id=1, source_target_pairs={{0,2},{1,3},{2,0},{3,1},{4,6},{5,7},{6,4},{7,5},{8,10},{9,11},{10,... | collective-permute-start | bytes 1572872 | tf_op jit(solution)/shard_map/ppermute | solution.py:340
  4.1 15.7 %collective-permute-start = (bf16[128,2048]{1,0:T(8,128)(2,1)}, bf16[128,2048]{1,0:T(8,128)(2,1)S(1)}, u32[]{:S(2)}, u32[]{:S(2)}) collective-permute-start(bf16[128,2048]{1,0:T(8,128)(2,1)} %refs_0_.1), channel_id=1, source_target_pairs={{0,8},{4,12},{8,16},{12,20},{16,24},{20,28},{1,9},{5,13},{9,17},{1... | collective-permute-start | bytes 1572872 | tf_op jit(solution)/shard_map/ppermute | solution.py:343
  7.5 2.8 %copy-start.1 = (bf16[2048,3,512]{2,0,1:T(8,128)(2,1)S(1)}, bf16[2048,3,512]{2,0,1:T(8,128)(2,1)}, u32[]{:S(2)}) copy-start(bf16[2048,3,512]{2,0,1:T(8,128)(2,1)} %param.8) | copy-start | bytes 18874372
  10.3 2.6 %copy-start.4 = (s32[512]{0:T(512)S(1)}, s32[512]{0:T(512)}, u32[]{:S(2)}) copy-start(s32[512]{0:T(512)} %param.11) | copy-start | bytes 6148
  10.3 20.8 %copy-start.2 = (bf16[128,2048]{1,0:T(8,128)(2,1)S(1)}, bf16[128,2048]{1,0:T(8,128)(2,1)}, u32[]{:S(2)}) copy-start(bf16[128,2048]{1,0:T(8,128)(2,1)} %refs_0_.1) | copy-start | bytes 1572868
  10.3 20.8 %copy-start.3 = (f32[2048]{0:T(1024)S(1)}, f32[2048]{0:T(1024)}, u32[]{:S(2)}) copy-start(f32[2048]{0:T(1024)} %param.7) | copy-start | bytes 24580
  11.8 1.1 %collective-permute-start.5 = (f32[4]{0:T(128)S(1)}, f32[4]{0:T(128)S(1)}, u32[]{:S(2)}, u32[]{:S(2)}) collective-permute-start(f32[4]{0:T(128)S(1)} %copy-done.5), channel_id=1, source_target_pairs={{0,1},{1,0},{2,3},{3,2},{4,5},{5,4},{6,7},{7,6},{8,9},{9,8},{10,11... | collective-permute-start | bytes 56 | tf_op jit(solution)/shard_map/ppermute | solution.py:337
  13.0 6.9 %collective-permute-start.6 = (s32[4,128]{1,0:T(4,128)S(1)}, s32[4,128]{1,0:T(4,128)S(1)}, u32[]{:S(2)}, u32[]{:S(2)}) collective-permute-start(s32[4,128]{1,0:T(4,128)S(1)} %bitcast.9), channel_id=1, source_target_pairs={{0,4},{4,8},{8,12},{12,16},{16,20},{20,24},{24,28},{1,5},{5,9},{9,... | collective-permute-start | bytes 6152 | tf_op jit(solution)/shard_map/ppermute | solution.py:343
  19.8 6.5 %collective-permute-start.7 = (bf16[128,2048]{1,0:T(8,128)(2,1)S(1)}, bf16[128,2048]{1,0:T(8,128)(2,1)S(1)}, u32[]{:S(2)}, u32[]{:S(2)}) collective-permute-start(bf16[128,2048]{1,0:T(8,128)(2,1)S(1)} %collective-permute-done.1.b.even_ref), channel_id=1, source_target_pairs={{0,1},{1,0},{2,3},{3,2},{4,5},{5,4},{6,7},{7,6},{8,9},{9,8},{10,11... | collective-permute-start | bytes 1572872 | tf_op jit(solution)/shard_map/ppermute | solution.py:337
  19.8 21.8 %collective-permute-start.10 = (bf16[128,2048]{1,0:T(8,128)(2,1)S(1)}, bf16[128,2048]{1,0:T(8,128)(2,1)S(1)}, u32[]{:S(2)}, u32[]{:S(2)}) collective-permute-start(bf16[128,2048]{1,0:T(8,128)(2,1)S(1)} %collective-permute-done.refs_4_), channel_id=1, source_target_pairs={{0,8},{4,12},{8,16},{12,20},{16,24},{20,28},{1,9},{5,13},{9,17},{1... | collective-permute-start | bytes 1572872 | tf_op jit(solution)/shard_map/ppermute | solution.py:343
  23.3 18.3 %collective-permute-start.9 = (bf16[128,2048]{1,0:T(8,128)(2,1)S(1)}, bf16[128,2048]{1,0:T(8,128)(2,1)S(1)}, u32[]{:S(2)}, u32[]{:S(2)}) collective-permute-start(bf16[128,2048]{1,0:T(8,128)(2,1)S(1)} %collective-permute-done.refs_4_), channel_id=1, source_target_pairs={{0,2},{1,3},{2,0},{3,1},{4,6},{5,7},{6,4},{7,5},{8,10},{9,11},{10,... | collective-permute-start | bytes 1572872 | tf_op jit(solution)/shard_map/ppermute | solution.py:340
  23.9 17.7 %collective-permute-start.8 = (bf16[128,2048]{1,0:T(8,128)(2,1)S(1)}, bf16[128,2048]{1,0:T(8,128)(2,1)S(1)}, u32[]{:S(2)}, u32[]{:S(2)}) collective-permute-start(bf16[128,2048]{1,0:T(8,128)(2,1)S(1)} %collective-permute-done.refs_4_), channel_id=1, source_target_pairs={{0,4},{8,12},{16,20},{24,28},{4,0},{12,8},{20,16},{28,24},{1,5},{9... | collective-permute-start | bytes 1572872 | tf_op jit(solution)/shard_map/ppermute | solution.py:343
  26.3 15.4 %collective-permute-start.12 = (s32[4,128]{1,0:T(4,128)S(1)}, s32[4,128]{1,0:T(4,128)S(1)}, u32[]{:S(2)}, u32[]{:S(2)}) collective-permute-start(s32[4,128]{1,0:T(4,128)S(1)} %bitcast.11), channel_id=1, source_target_pairs={{0,16},{4,20},{8,24},{12,28},{1,17},{5,21},{9,25},{13,29},{2,18},{... | collective-permute-start | bytes 6152 | tf_op jit(solution)/shard_map/ppermute | solution.py:343
  28.6 13.0 %collective-permute-start.11 = (s32[8,128]{1,0:T(8,128)S(1)}, s32[8,128]{1,0:T(8,128)S(1)}, u32[]{:S(2)}, u32[]{:S(2)}) collective-permute-start(s32[8,128]{1,0:T(8,128)S(1)} %pad_add_fusion), channel_id=1, source_target_pairs={{0,8},{4,12},{8,16},{12,20},{16,24},{20,28},{1,9},{5,13},{9,17},{1... | collective-permute-start | bytes 12296 | tf_op jit(solution)/shard_map/ppermute | solution.py:343
  31.1 10.6 %copy-start = (bf16[512,2048]{1,0:T(8,128)(2,1)S(1)}, bf16[512,2048]{1,0:T(8,128)(2,1)}, u32[]{:S(2)}) copy-start(bf16[512,2048]{1,0:T(8,128)(2,1)} %w0.3) | copy-start | bytes 6291460
  41.7 32.3 %collective-permute-start.19 = (bf16[512,2048]{1,0:T(8,128)(2,1)S(1)}, bf16[512,2048]{1,0:T(8,128)(2,1)S(1)}, u32[]{:S(2)}, u32[]{:S(2)}) collective-permute-start(bf16[512,2048]{1,0:T(8,128)(2,1)S(1)} %copy-done), channel_id=1, source_target_pairs={{0,1},{1,0},{2,3},{3,2},{4,5},{5,4},{6,7},{7,6},{8,9},{9,8},{10,11... | collective-permute-start | bytes 6291464 | tf_op jit(solution)/shard_map/ppermute | solution.py:337
  41.8 15.7 %collective-permute-start.13 = (bf16[128,2048]{1,0:T(8,128)(2,1)S(1)}, bf16[128,2048]{1,0:T(8,128)(2,1)S(1)}, u32[]{:S(2)}, u32[]{:S(2)}) collective-permute-start(bf16[128,2048]{1,0:T(8,128)(2,1)S(1)} %shard_map.87), channel_id=1, source_target_pairs={{0,4},{8,12},{16,20},{24,28},{4,0},{12,8},{20,16},{28,24},{1,5},{9... | collective-permute-start | bytes 1572872 | tf_op jit(solution)/shard_map/ppermute | solution.py:343
  41.9 15.7 %collective-permute-start.14 = (bf16[128,2048]{1,0:T(8,128)(2,1)S(1)}, bf16[128,2048]{1,0:T(8,128)(2,1)S(1)}, u32[]{:S(2)}, u32[]{:S(2)}) collective-permute-start(bf16[128,2048]{1,0:T(8,128)(2,1)S(1)} %collective-permute-done.8.refs_7_), channel_id=1, source_target_pairs={{0,2},{1,3},{2,0},{3,1},{4,6},{5,7},{6,4},{7,5},{8,10},{9,11},{10,... | collective-permute-start | bytes 1572872 | tf_op jit(solution)/shard_map/ppermute | solution.py:340
  43.4 15.8 %collective-permute-start.15 = (bf16[128,2048]{1,0:T(8,128)(2,1)S(1)}, bf16[128,2048]{1,0:T(8,128)(2,1)S(1)}, u32[]{:S(2)}, u32[]{:S(2)}) collective-permute-start(bf16[128,2048]{1,0:T(8,128)(2,1)S(1)} %collective-permute-done.9.refs_5_), channel_id=1, source_target_pairs={{0,8},{4,12},{8,16},{12,20},{16,24},{20,28},{1,9},{5,13},{9,17},{1... | collective-permute-start | bytes 1572872 | tf_op jit(solution)/shard_map/ppermute | solution.py:343
  59.3 12.3 %collective-permute-start.17 = (bf16[64,2048]{1,0:T(8,128)(2,1)S(1)}, bf16[64,2048]{1,0:T(8,128)(2,1)S(1)}, u32[]{:S(2)}, u32[]{:S(2)}) collective-permute-start(bf16[64,2048]{1,0:T(8,128)(2,1)S(1)} %slice.15), channel_id=1, source_target_pairs={{4,0},{12,8},{20,16},{28,24},{5,1},{13,9},{21,17},{29,25},{6,2},{1... | collective-permute-start | bytes 786440 | tf_op jit(solution)/shard_map/ppermute | solution.py:343
  63.0 8.6 %collective-permute-start.16 = (bf16[64,2048]{1,0:T(8,128)(2,1)S(1)}, bf16[64,2048]{1,0:T(8,128)(2,1)S(1)}, u32[]{:S(2)}, u32[]{:S(2)}) collective-permute-start(bf16[64,2048]{1,0:T(8,128)(2,1)S(1)} %slice.14), channel_id=1, source_target_pairs={{0,2},{1,3},{2,0},{3,1},{4,6},{5,7},{6,4},{7,5},{8,10},{9,11},{10,... | collective-permute-start | bytes 786440 | tf_op jit(solution)/shard_map/ppermute | solution.py:340
  72.1 2.0 %collective-permute-start.18 = (bf16[1056,256]{1,0:T(8,128)(2,1)S(1)}, bf16[1056,256]{1,0:T(8,128)(2,1)S(1)}, u32[]{:S(2)}, u32[]{:S(2)}) collective-permute-start(bf16[1056,256]{1,0:T(8,128)(2,1)S(1)} %get-tuple-element.97), channel_id=1, source_target_pairs={{0,1},{1,0},{2,3},{3,2},{4,5},{5,4},{6,7},{7,6},{8,9},{9,8},{10,11... | collective-permute-start | bytes 1622024 | tf_op jit(solution)/shard_map/ppermute | solution.py:337
  74.9 14.0 %collective-permute-start.20 = (bf16[128,2048]{1,0:T(8,128)(2,1)S(1)}, bf16[128,2048]{1,0:T(8,128)(2,1)S(1)}, u32[]{:S(2)}, u32[]{:S(2)}) collective-permute-start(bf16[128,2048]{1,0:T(8,128)(2,1)S(1)} %shard_map.92), channel_id=1, source_target_pairs={{0,2},{1,3},{2,0},{3,1},{4,6},{5,7},{6,4},{7,5},{8,10},{9,11},{10,... | collective-permute-start | bytes 1572872 | tf_op jit(solution)/shard_map/ppermute | solution.py:340

commit v11 on v10

--- a/solution.py
+++ b/solution.py
@@ -17,7 +17,6 @@
 
 BF16 = jnp.bfloat16
 F32 = jnp.float32
-SMEM = pl.BlockSpec(memory_space=pltpu.SMEM)
 HBM = pl.BlockSpec(memory_space=pltpu.HBM)
 VMEM = pl.BlockSpec(memory_space=pltpu.VMEM)
 
@@ -159,8 +158,8 @@
              slopes_out, x, mask, dist):
         set_own_masks(seg_ref, mask, dist)
         for head in range(4):
-            slopes_out[head : head + 1, :] = jnp.full((1, PIECE), s0[head], F32)
-            slopes_out[4 + head : 5 + head, :] = jnp.full((1, PIECE), s1[head], F32)
+            slopes_out[head : head + 1, :] = jnp.broadcast_to(s0[0:1, head : head + 1], (1, PIECE))
+            slopes_out[4 + head : 5 + head, :] = jnp.broadcast_to(s1[0:1, head : head + 1], (1, PIECE))
         for place, piece in enumerate((a, b, c, d)):
             x[pl.ds(place * PIECE, PIECE), :] = normalise(piece[...], gain_ref[...])
         for group, (w, q, stat, acc) in enumerate(((w0, q0, stat0, acc0), (w1, q1, stat1, acc1))):
@@ -183,7 +182,7 @@
             jax.ShapeDtypeStruct((block, width), BF16),
             jax.ShapeDtypeStruct((8, PIECE), F32),
         ),
-        in_specs=[SMEM] * 2 + [VMEM] * 8,
+        in_specs=[VMEM] * 10,
         out_specs=(VMEM,) * 9,
         scratch_shapes=[
             pltpu.VMEM((block, depth), BF16),
@@ -349,6 +348,7 @@
     tie = lax.optimization_barrier
     w_all = jnp.transpose(w_qkv, (1, 0, 2))
     seg = seg_ids.reshape(4, PIECE)
+    slopes = slopes.reshape(1, -1)
     gain = ln_gain.reshape(1, -1)
     w_pair = over_core(w_all)
 
@@ -379,8 +379,6 @@
     over_y = over_seq(picked, even_to_odd + odd_to_even)
     x_third = over_x(crossed)
     b4 = over_seq(b2, two_on)
-    wo_sent, picked = tie((w_out, picked))
-    wo_pair = over_core(wo_sent)
 
     def merge(closing, segs, pieces, which, state):
         return earlier_pieces(
@@ -390,10 +388,11 @@
         False, segs, (a2, b2, a4, crossed, a1_odd),
         (((2, 0),) * 2, ((2, 1),) * 2, ((4, 0),) * 2, ((1, 0), (3, 0)), ((0, 0), (1, 0))), state)
 
-    over_y, x_third, b4, held = tie((over_y, x_third, b4, state[0]))
+    over_y, x_third, b4, wo_sent, held = tie((over_y, x_third, b4, w_out, state[0]))
     state = (held, *state[1:])
     b3_top = over_x(over_y[: PIECE // 2])
     b3_rest = over_seq(b4[PIECE // 2 :], odd_to_even)
+    wo_pair = over_core(wo_sent)
     state = merge(
         False, segs, (b4, x_third, over_y), (((4, 1),) * 2, ((1, 1), (3, 1)), ((3, 0), (1, 1))), state)
     send, lse, out = merge(True, segs, (b3_top, b3_rest), (((3, 1), (0, 0)),), state)

time: 90.1 us -> 88.7 us (0.984)
  Pallas kernels: 33.3 us -> 21 us
  waiting for transfers between devices: 19.5 us -> 30.2 us
    pallas_call x3, Pallas kernels: 20.6 us -> 8.93 us  [earlier_pieces(): pl.pallas_call(body, out_shape=shapes, in_specs=[VMEM] * (11 + len(segs)...]
    ppermute x10, waiting for transfers between devices: 3.89 us -> 14.1 us  [over_seq(): return lax.ppermute(value, 'seq', pairs)]
  transfers between devices with their start and end apart: 21 -> 21, of which waited for: 6 -> 8; matrix products, arithmetic and copies ran while one was open for 0% -> 0% of each run, Pallas kernels for 36% -> 23%
where the time goes in v11:
time: 88.7 us; the launch traced here: 88.1 us
  starting transfers between devices  32.2 us (36%)
  waiting for transfers between devices  30.2 us (34%)
  Pallas kernels  21 us (24%)
  local copies, waits for them, and re-layouts  2.84 us (3%)
  other arithmetic  0.94 us (1%)
  between operations  0.91 us (1%)
    ppermute x10, starting transfers between devices, over_seq(): return lax.ppermute(value, 'seq', pairs)  26 us
    ppermute x10, waiting for transfers between devices, over_seq(): return lax.ppermute(value, 'seq', pairs)  14.1 us
    ppermute x5, waiting for transfers between devices, over_x(): return lax.ppermute(value, 'head', [(i, i ^ 2) for i in range(4)])  12.1 us
    pallas_call x1, Pallas kernels, own_block(): pl.pallas_call(body, out_shape=(jax.ShapeDtypeStruct((width, block), BF16...  9.92 us
    pallas_call x3, Pallas kernels, earlier_pieces(): pl.pallas_call(body, out_shape=shapes, in_specs=[VMEM] * (11 + len(segs)...  8.93 us
    ppermute x5, starting transfers between devices, over_x(): return lax.ppermute(value, 'head', [(i, i ^ 2) for i in range(4)])  5.45 us
    ppermute x6, waiting for transfers between devices, over_core(): return lax.ppermute(value, 'head', [(i, i ^ 1) for i in range(4)])  3.97 us
    unnamed x12, local copies, waits for them, and re-layouts  2.8 us
  transfers between devices with their start and end apart: 21, of which 8 were waited for; matrix products, arithmetic and copies ran while one was open for 0% of the time, Pallas kernels for 23%

profile of v11, /device:TPU:12, one launch (start us, length us, event | category | flops | bytes accessed | tf_op | source)
XLA Modules:
  0.0 88.1 jit_solution(9995272877199313915)
XLA Ops:
  0.6 0.1 collective-permute-start.3
  0.7 0.5 collective-permute-start.4
  1.2 1.3 %collective-permute-start.2 = (bf16[128,2048]{1,0:T(8,128)(2,1)}, bf16[128,2048]{1,0:T(8,128)(2,1)S(1)}, u32[]{:S(2)}, u32[]{:S(2)}) collective-permute-start(bf16[128,2048]{1,0:T(8,128)(2,1)} %refs_0_.1), channel_id=1, source_target_pairs={{0,4},{8,12},{16,20},{24,28},{1,5},{9,13},{17,21},{25,29},{2,6},{1... | collective-permute-start | bytes 1572872 | tf_op jit(solution)/shard_map/ppermute | solution.py:342
  2.5 1.6 %collective-permute-start.1 = (bf16[128,2048]{1,0:T(8,128)(2,1)}, bf16[128,2048]{1,0:T(8,128)(2,1)S(1)}, u32[]{:S(2)}, u32[]{:S(2)}) collective-permute-start(bf16[128,2048]{1,0:T(8,128)(2,1)} %refs_0_.1), channel_id=1, source_target_pairs={{0,2},{1,3},{2,0},{3,1},{4,6},{5,7},{6,4},{7,5},{8,10},{9,11},{10,... | collective-permute-start | bytes 1572872 | tf_op jit(solution)/shard_map/ppermute | solution.py:339
  4.1 3.5 %collective-permute-start = (bf16[128,2048]{1,0:T(8,128)(2,1)}, bf16[128,2048]{1,0:T(8,128)(2,1)S(1)}, u32[]{:S(2)}, u32[]{:S(2)}) collective-permute-start(bf16[128,2048]{1,0:T(8,128)(2,1)} %refs_0_.1), channel_id=1, source_target_pairs={{0,8},{4,12},{8,16},{12,20},{16,24},{20,28},{1,9},{5,13},{9,17},{1... | collective-permute-start | bytes 1572872 | tf_op jit(solution)/shard_map/ppermute | solution.py:342
  7.6 2.8 %copy-done.1 = bf16[2048,3,512]{2,0,1:T(8,128)(2,1)S(1)} copy-done((bf16[2048,3,512]{2,0,1:T(8,128)(2,1)S(1)}, bf16[2048,3,512]{2,0,1:T(8,128)(2,1)}, u32[]{:S(2)}) %copy-start.1) | copy-done | bytes 6291480
  10.3 0.4 shard_map.85.w0.refs_9_.refs_7_.refs_6_
  10.8 1.1 %collective-permute-done.4.c = bf16[128,2048]{1,0:T(8,128)(2,1)S(1)} collective-permute-done((bf16[128,2048]{1,0:T(8,128)(2,1)}, bf16[128,2048]{1,0:T(8,128)(2,1)S(1)}, u32[]{:S(2)}, u32[]{:S(2)}) %collective-permute-start.4) | collective-permute-done | bytes 524320 | tf_op jit(solution)/shard_map/ppermute | solution.py:336
  11.8 0.1 collective-permute-start.5
  12.0 1.0 %collective-permute-done.5.s1 = f32[1,4]{1,0:T(1,128)S(1)} collective-permute-done((f32[1,4]{1,0:T(1,128)S(1)}, f32[1,4]{1,0:T(1,128)S(1)}, u32[]{:S(2)}, u32[]{:S(2)}) %collective-permute-start.5) | collective-permute-done | bytes 48 | tf_op jit(solution)/shard_map/ppermute | solution.py:336
  13.0 4.6 %collective-permute-start.6 = (s32[4,128]{1,0:T(4,128)S(1)}, s32[4,128]{1,0:T(4,128)S(1)}, u32[]{:S(2)}, u32[]{:S(2)}) collective-permute-start(s32[4,128]{1,0:T(4,128)S(1)} %bitcast.10), channel_id=1, source_target_pairs={{0,4},{4,8},{8,12},{12,16},{16,20},{20,24},{24,28},{1,5},{5,9},{9,... | collective-permute-start | bytes 6152 | tf_op jit(solution)/shard_map/ppermute | solution.py:342
  17.6 0.0 collective-permute-done.2.refs_8_
  17.6 0.0 collective-permute-done.1.b.even_ref
  17.6 2.2 %collective-permute-done.refs_4_ = bf16[128,2048]{1,0:T(8,128)(2,1)S(1)} collective-permute-done((bf16[128,2048]{1,0:T(8,128)(2,1)}, bf16[128,2048]{1,0:T(8,128)(2,1)S(1)}, u32[]{:S(2)}, u32[]{:S(2)}) %collective-permute-start) | collective-permute-done | bytes 524320 | tf_op jit(solution)/shard_map/ppermute | solution.py:342
  19.8 0.0 collective-permute-done.6.refs_0_
  19.8 0.0 collective-permute-done.3.w1.refs_10_.refs_8_.refs_7_
  19.8 3.5 %collective-permute-start.10 = (bf16[128,2048]{1,0:T(8,128)(2,1)S(1)}, bf16[128,2048]{1,0:T(8,128)(2,1)S(1)}, u32[]{:S(2)}, u32[]{:S(2)}) collective-permute-start(bf16[128,2048]{1,0:T(8,128)(2,1)S(1)} %collective-permute-done.refs_4_), channel_id=1, source_target_pairs={{0,8},{4,12},{8,16},{12,20},{16,24},{20,28},{1,9},{5,13},{9,17},{1... | collective-permute-start | bytes 1572872 | tf_op jit(solution)/shard_map/ppermute | solution.py:342
  23.3 0.6 collective-permute-start.9
  23.9 2.4 %collective-permute-start.8 = (bf16[128,2048]{1,0:T(8,128)(2,1)S(1)}, bf16[128,2048]{1,0:T(8,128)(2,1)S(1)}, u32[]{:S(2)}, u32[]{:S(2)}) collective-permute-start(bf16[128,2048]{1,0:T(8,128)(2,1)S(1)} %collective-permute-done.refs_4_), channel_id=1, source_target_pairs={{0,4},{8,12},{16,20},{24,28},{4,0},{12,8},{20,16},{28,24},{1,5},{9... | collective-permute-start | bytes 1572872 | tf_op jit(solution)/shard_map/ppermute | solution.py:342
  26.3 2.3 %collective-permute-start.12 = (s32[4,128]{1,0:T(4,128)S(1)}, s32[4,128]{1,0:T(4,128)S(1)}, u32[]{:S(2)}, u32[]{:S(2)}) collective-permute-start(s32[4,128]{1,0:T(4,128)S(1)} %bitcast.12), channel_id=1, source_target_pairs={{0,16},{4,20},{8,24},{12,28},{1,17},{5,21},{9,25},{13,29},{2,18},{... | collective-permute-start | bytes 6152 | tf_op jit(solution)/shard_map/ppermute | solution.py:342
  28.6 2.5 %collective-permute-start.11 = (s32[8,128]{1,0:T(8,128)S(1)}, s32[8,128]{1,0:T(8,128)S(1)}, u32[]{:S(2)}, u32[]{:S(2)}) collective-permute-start(s32[8,128]{1,0:T(8,128)S(1)} %pad_add_fusion), channel_id=1, source_target_pairs={{0,8},{4,12},{8,16},{12,20},{16,24},{20,28},{1,9},{5,13},{9,17},{1... | collective-permute-start | bytes 12296 | tf_op jit(solution)/shard_map/ppermute | solution.py:342
  31.1 9.9 %shard_map.86 = (bf16[512,512]{1,0:T(8,128)(2,1)S(1)}, bf16[512,512]{1,0:T(8,128)(2,1)S(1)}, f32[8,512]{1,0:T(8,128)S(1)}, f32[512,512]{1,0:T(8,128)S(1)}, f32[8...) custom-call(f32[1,4]{1,0:T(1,128)S(1)} %bitcast.18, ...), custom_call_target="tpu_custom_call" | custom-call | flops 5368709120 | bytes 1048576 | tf_op jit(solution)/shard_map/pallas_call | solution.py:178
  41.0 0.0 collective-permute-done.11
  41.0 0.0 collective-permute-done.10.odd_ref.refs_6_
  41.0 0.0 collective-permute-done.9.refs_5_
  41.1 0.0 collective-permute-done.12.refs_3_
  41.1 0.1 shard_map.87
  41.1 0.1 collective-permute-start.13
  41.2 1.6 %collective-permute-start.14 = (bf16[128,2048]{1,0:T(8,128)(2,1)S(1)}, bf16[128,2048]{1,0:T(8,128)(2,1)S(1)}, u32[]{:S(2)}, u32[]{:S(2)}) collective-permute-start(bf16[128,2048]{1,0:T(8,128)(2,1)S(1)} %collective-permute-done.8.refs_7_), channel_id=1, source_target_pairs={{0,2},{1,3},{2,0},{3,1},{4,6},{5,7},{6,4},{7,5},{8,10},{9,11},{10,... | collective-permute-start | bytes 1572872 | tf_op jit(solution)/shard_map/ppermute | solution.py:339
  42.8 2.3 %collective-permute-start.15 = (bf16[128,2048]{1,0:T(8,128)(2,1)S(1)}, bf16[128,2048]{1,0:T(8,128)(2,1)S(1)}, u32[]{:S(2)}, u32[]{:S(2)}) collective-permute-start(bf16[128,2048]{1,0:T(8,128)(2,1)S(1)} %collective-permute-done.9.refs_5_), channel_id=1, source_target_pairs={{0,8},{4,12},{8,16},{12,20},{16,24},{20,28},{1,9},{5,13},{9,17},{1... | collective-permute-start | bytes 1572872 | tf_op jit(solution)/shard_map/ppermute | solution.py:342
  45.1 0.0 copy-start
  45.1 0.5 shard_map.88
  45.6 8.8 %collective-permute-done.13.refs_6_ = bf16[128,2048]{1,0:T(8,128)(2,1)S(1)} collective-permute-done((bf16[128,2048]{1,0:T(8,128)(2,1)S(1)}, bf16[128,2048]{1,0:T(8,128)(2,1)S(1)}, u32[]{:S(2)}, u32[]{:S(2)}) %collective-permute-start.13) | collective-permute-done | bytes 524320 | tf_op jit(solution)/shard_map/ppermute | solution.py:342
  54.4 0.1 collective-permute-done.14.refs_5_
  54.5 3.1 %collective-permute-done.15.refs_4_ = bf16[128,2048]{1,0:T(8,128)(2,1)S(1)} collective-permute-done((bf16[128,2048]{1,0:T(8,128)(2,1)S(1)}, bf16[128,2048]{1,0:T(8,128)(2,1)S(1)}, u32[]{:S(2)}, u32[]{:S(2)}) %collective-permute-start.15) | collective-permute-done | bytes 524320 | tf_op jit(solution)/shard_map/ppermute | solution.py:342
  57.6 0.0 collective-permute-start.19
  57.6 3.6 %collective-permute-start.17 = (bf16[64,2048]{1,0:T(8,128)(2,1)S(1)}, bf16[64,2048]{1,0:T(8,128)(2,1)S(1)}, u32[]{:S(2)}, u32[]{:S(2)}) collective-permute-start(bf16[64,2048]{1,0:T(8,128)(2,1)S(1)} %slice.15), channel_id=1, source_target_pairs={{4,0},{12,8},{20,16},{28,24},{5,1},{13,9},{21,17},{29,25},{6,2},{1... | collective-permute-start | bytes 786440 | tf_op jit(solution)/shard_map/ppermute | solution.py:342
  61.2 0.6 collective-permute-start.16
  61.8 8.0 %shard_map.89 = (f32[8,512]{1,0:T(8,128)S(1)}, f32[512,512]{1,0:T(8,128)S(1)}, f32[8,512]{1,0:T(8,128)S(1)}, f32[512,512]{1,0:T(8,128)S(1)}) custom-call(f32[8,128]{1,0:T(8,128)S(1)} %get-tuple-element.63.slopes_ref, s32[4,128]{1,0:T(4,128)S(1)} %bitcast.15, f32[1,2048]{1,0:T(1,128)S(1)} %bitcast.8, s32[4,128]{1,0:T(4,128)S(1)} %collective-permute-done.6.refs_0_, ...), custom_call_target="tpu_custom_call" | custom-call | flops 3221225472 | bytes 1048576 | tf_op jit(solution)/shard_map/pallas_call | solution.py:284
  69.8 0.5 shard_map.90
  70.3 0.1 collective-permute-start.18
  70.4 1.9 %collective-permute-done.18.got_ref = bf16[1056,256]{1,0:T(8,128)(2,1)S(1)} collective-permute-done((bf16[1056,256]{1,0:T(8,128)(2,1)S(1)}, bf16[1056,256]{1,0:T(8,128)(2,1)S(1)}, u32[]{:S(2)}, u32[]{:S(2)}) %collective-permute-start.18) | collective-permute-done | bytes 540704 | tf_op jit(solution)/shard_map/ppermute | solution.py:336
  72.3 0.0 collective-permute-done.19.w1
  72.3 0.8 shard_map.92
  73.1 1.1 %collective-permute-start.20 = (bf16[128,2048]{1,0:T(8,128)(2,1)S(1)}, bf16[128,2048]{1,0:T(8,128)(2,1)S(1)}, u32[]{:S(2)}, u32[]{:S(2)}) collective-permute-start(bf16[128,2048]{1,0:T(8,128)(2,1)S(1)} %shard_map.92), channel_id=1, source_target_pairs={{0,2},{1,3},{2,0},{3,1},{4,6},{5,7},{6,4},{7,5},{8,10},{9,11},{10,... | collective-permute-start | bytes 1572872 | tf_op jit(solution)/shard_map/ppermute | solution.py:339
  74.3 0.8 shard_map.91
  75.1 12.1 %collective-permute-done.20 = bf16[128,2048]{1,0:T(8,128)(2,1)S(1)} collective-permute-done((bf16[128,2048]{1,0:T(8,128)(2,1)S(1)}, bf16[128,2048]{1,0:T(8,128)(2,1)S(1)}, u32[]{:S(2)}, u32[]{:S(2)}) %collective-permute-start.20) | collective-permute-done | bytes 524320 | tf_op jit(solution)/shard_map/ppermute | solution.py:339
  87.1 0.9 %add_convert_fusion = bf16[128,2048]{1,0:T(8,128)(2,1)} fusion(f32[128,2048]{1,0:T(8,128)S(1)} %shard_map.91, bf16[128,2048]{1,0:T(8,128)(2,1)S(1)} %collective-permute-done.20), kind=kLoop, calls=%fused_computation | loop fusion | flops 786432 | bytes 2097152 | tf_op jit(solution)/shard_map/convert_element_type | solution.py:403
  (19 shorter events, 0.1 us)
Async XLA Ops:
  0.6 11.2 %copy-start.5 = (f32[4]{0:T(128)S(1)}, f32[4]{0:T(128)}, u32[]{:S(2)}) copy-start(f32[4]{0:T(128)} %param.9) | copy-start | bytes 52
  0.6 19.2 %collective-permute-start.3 = (bf16[3,2048,512]{2,1,0:T(8,128)(2,1)}, bf16[3,2048,512]{2,1,0:T(8,128)(2,1)S(1)}, u32[]{:S(2)}, u32[]{:S(2)}) collective-permute-start(bf16[3,2048,512]{2,1,0:T(8,128)(2,1)} %bitcast.4), channel_id=1, source_target_pairs={{0,1},{1,0},{2,3},{3,2},{4,5},{5,4},{6,7},{7,6},{8,9},{9,8},{10,11... | collective-permute-start | bytes 18874376 | tf_op jit(solution)/shard_map/ppermute | solution.py:336
  0.7 11.1 %collective-permute-start.4 = (bf16[128,2048]{1,0:T(8,128)(2,1)}, bf16[128,2048]{1,0:T(8,128)(2,1)S(1)}, u32[]{:S(2)}, u32[]{:S(2)}) collective-permute-start(bf16[128,2048]{1,0:T(8,128)(2,1)} %refs_0_.1), channel_id=1, source_target_pairs={{0,1},{1,0},{2,3},{3,2},{4,5},{5,4},{6,7},{7,6},{8,9},{9,8},{10,11... | collective-permute-start | bytes 1572872 | tf_op jit(solution)/shard_map/ppermute | solution.py:336
  1.2 16.4 %collective-permute-start.2 = (bf16[128,2048]{1,0:T(8,128)(2,1)}, bf16[128,2048]{1,0:T(8,128)(2,1)S(1)}, u32[]{:S(2)}, u32[]{:S(2)}) collective-permute-start(bf16[128,2048]{1,0:T(8,128)(2,1)} %refs_0_.1), channel_id=1, source_target_pairs={{0,4},{8,12},{16,20},{24,28},{1,5},{9,13},{17,21},{25,29},{2,6},{1... | collective-permute-start | bytes 1572872 | tf_op jit(solution)/shard_map/ppermute | solution.py:342
  2.5 15.1 %collective-permute-start.1 = (bf16[128,2048]{1,0:T(8,128)(2,1)}, bf16[128,2048]{1,0:T(8,128)(2,1)S(1)}, u32[]{:S(2)}, u32[]{:S(2)}) collective-permute-start(bf16[128,2048]{1,0:T(8,128)(2,1)} %refs_0_.1), channel_id=1, source_target_pairs={{0,2},{1,3},{2,0},{3,1},{4,6},{5,7},{6,4},{7,5},{8,10},{9,11},{10,... | collective-permute-start | bytes 1572872 | tf_op jit(solution)/shard_map/ppermute | solution.py:339
  4.1 15.7 %collective-permute-start = (bf16[128,2048]{1,0:T(8,128)(2,1)}, bf16[128,2048]{1,0:T(8,128)(2,1)S(1)}, u32[]{:S(2)}, u32[]{:S(2)}) collective-permute-start(bf16[128,2048]{1,0:T(8,128)(2,1)} %refs_0_.1), channel_id=1, source_target_pairs={{0,8},{4,12},{8,16},{12,20},{16,24},{20,28},{1,9},{5,13},{9,17},{1... | collective-permute-start | bytes 1572872 | tf_op jit(solution)/shard_map/ppermute | solution.py:342
  7.5 2.8 %copy-start.1 = (bf16[2048,3,512]{2,0,1:T(8,128)(2,1)S(1)}, bf16[2048,3,512]{2,0,1:T(8,128)(2,1)}, u32[]{:S(2)}) copy-start(bf16[2048,3,512]{2,0,1:T(8,128)(2,1)} %param.8) | copy-start | bytes 18874372
  10.3 2.6 %copy-start.4 = (s32[512]{0:T(512)S(1)}, s32[512]{0:T(512)}, u32[]{:S(2)}) copy-start(s32[512]{0:T(512)} %param.11) | copy-start | bytes 6148
  10.3 20.8 %copy-start.2 = (bf16[128,2048]{1,0:T(8,128)(2,1)S(1)}, bf16[128,2048]{1,0:T(8,128)(2,1)}, u32[]{:S(2)}) copy-start(bf16[128,2048]{1,0:T(8,128)(2,1)} %refs_0_.1) | copy-start | bytes 1572868
  10.3 20.8 %copy-start.3 = (f32[2048]{0:T(1024)S(1)}, f32[2048]{0:T(1024)}, u32[]{:S(2)}) copy-start(f32[2048]{0:T(1024)} %param.7) | copy-start | bytes 24580
  11.8 1.1 %collective-permute-start.5 = (f32[1,4]{1,0:T(1,128)S(1)}, f32[1,4]{1,0:T(1,128)S(1)}, u32[]{:S(2)}, u32[]{:S(2)}) collective-permute-start(f32[1,4]{1,0:T(1,128)S(1)} %bitcast.17), channel_id=1, source_target_pairs={{0,1},{1,0},{2,3},{3,2},{4,5},{5,4},{6,7},{7,6},{8,9},{9,8},{10,11... | collective-permute-start | bytes 56 | tf_op jit(solution)/shard_map/ppermute | solution.py:336
  13.0 6.9 %collective-permute-start.6 = (s32[4,128]{1,0:T(4,128)S(1)}, s32[4,128]{1,0:T(4,128)S(1)}, u32[]{:S(2)}, u32[]{:S(2)}) collective-permute-start(s32[4,128]{1,0:T(4,128)S(1)} %bitcast.10), channel_id=1, source_target_pairs={{0,4},{4,8},{8,12},{12,16},{16,20},{20,24},{24,28},{1,5},{5,9},{9,... | collective-permute-start | bytes 6152 | tf_op jit(solution)/shard_map/ppermute | solution.py:342
  19.8 6.5 %collective-permute-start.7 = (bf16[128,2048]{1,0:T(8,128)(2,1)S(1)}, bf16[128,2048]{1,0:T(8,128)(2,1)S(1)}, u32[]{:S(2)}, u32[]{:S(2)}) collective-permute-start(bf16[128,2048]{1,0:T(8,128)(2,1)S(1)} %collective-permute-done.1.b.even_ref), channel_id=1, source_target_pairs={{0,1},{1,0},{2,3},{3,2},{4,5},{5,4},{6,7},{7,6},{8,9},{9,8},{10,11... | collective-permute-start | bytes 1572872 | tf_op jit(solution)/shard_map/ppermute | solution.py:336
  19.8 21.2 %collective-permute-start.10 = (bf16[128,2048]{1,0:T(8,128)(2,1)S(1)}, bf16[128,2048]{1,0:T(8,128)(2,1)S(1)}, u32[]{:S(2)}, u32[]{:S(2)}) collective-permute-start(bf16[128,2048]{1,0:T(8,128)(2,1)S(1)} %collective-permute-done.refs_4_), channel_id=1, source_target_pairs={{0,8},{4,12},{8,16},{12,20},{16,24},{20,28},{1,9},{5,13},{9,17},{1... | collective-permute-start | bytes 1572872 | tf_op jit(solution)/shard_map/ppermute | solution.py:342
  23.3 17.7 %collective-permute-start.9 = (bf16[128,2048]{1,0:T(8,128)(2,1)S(1)}, bf16[128,2048]{1,0:T(8,128)(2,1)S(1)}, u32[]{:S(2)}, u32[]{:S(2)}) collective-permute-start(bf16[128,2048]{1,0:T(8,128)(2,1)S(1)} %collective-permute-done.refs_4_), channel_id=1, source_target_pairs={{0,2},{1,3},{2,0},{3,1},{4,6},{5,7},{6,4},{7,5},{8,10},{9,11},{10,... | collective-permute-start | bytes 1572872 | tf_op jit(solution)/shard_map/ppermute | solution.py:339
  23.9 17.1 %collective-permute-start.8 = (bf16[128,2048]{1,0:T(8,128)(2,1)S(1)}, bf16[128,2048]{1,0:T(8,128)(2,1)S(1)}, u32[]{:S(2)}, u32[]{:S(2)}) collective-permute-start(bf16[128,2048]{1,0:T(8,128)(2,1)S(1)} %collective-permute-done.refs_4_), channel_id=1, source_target_pairs={{0,4},{8,12},{16,20},{24,28},{4,0},{12,8},{20,16},{28,24},{1,5},{9... | collective-permute-start | bytes 1572872 | tf_op jit(solution)/shard_map/ppermute | solution.py:342
  26.3 14.8 %collective-permute-start.12 = (s32[4,128]{1,0:T(4,128)S(1)}, s32[4,128]{1,0:T(4,128)S(1)}, u32[]{:S(2)}, u32[]{:S(2)}) collective-permute-start(s32[4,128]{1,0:T(4,128)S(1)} %bitcast.12), channel_id=1, source_target_pairs={{0,16},{4,20},{8,24},{12,28},{1,17},{5,21},{9,25},{13,29},{2,18},{... | collective-permute-start | bytes 6152 | tf_op jit(solution)/shard_map/ppermute | solution.py:342
  28.6 12.4 %collective-permute-start.11 = (s32[8,128]{1,0:T(8,128)S(1)}, s32[8,128]{1,0:T(8,128)S(1)}, u32[]{:S(2)}, u32[]{:S(2)}) collective-permute-start(s32[8,128]{1,0:T(8,128)S(1)} %pad_add_fusion), channel_id=1, source_target_pairs={{0,8},{4,12},{8,16},{12,20},{16,24},{20,28},{1,9},{5,13},{9,17},{1... | collective-permute-start | bytes 12296 | tf_op jit(solution)/shard_map/ppermute | solution.py:342
  41.1 13.3 %collective-permute-start.13 = (bf16[128,2048]{1,0:T(8,128)(2,1)S(1)}, bf16[128,2048]{1,0:T(8,128)(2,1)S(1)}, u32[]{:S(2)}, u32[]{:S(2)}) collective-permute-start(bf16[128,2048]{1,0:T(8,128)(2,1)S(1)} %shard_map.87), channel_id=1, source_target_pairs={{0,4},{8,12},{16,20},{24,28},{4,0},{12,8},{20,16},{28,24},{1,5},{9... | collective-permute-start | bytes 1572872 | tf_op jit(solution)/shard_map/ppermute | solution.py:342
  41.2 13.3 %collective-permute-start.14 = (bf16[128,2048]{1,0:T(8,128)(2,1)S(1)}, bf16[128,2048]{1,0:T(8,128)(2,1)S(1)}, u32[]{:S(2)}, u32[]{:S(2)}) collective-permute-start(bf16[128,2048]{1,0:T(8,128)(2,1)S(1)} %collective-permute-done.8.refs_7_), channel_id=1, source_target_pairs={{0,2},{1,3},{2,0},{3,1},{4,6},{5,7},{6,4},{7,5},{8,10},{9,11},{10,... | collective-permute-start | bytes 1572872 | tf_op jit(solution)/shard_map/ppermute | solution.py:339
  42.8 14.8 %collective-permute-start.15 = (bf16[128,2048]{1,0:T(8,128)(2,1)S(1)}, bf16[128,2048]{1,0:T(8,128)(2,1)S(1)}, u32[]{:S(2)}, u32[]{:S(2)}) collective-permute-start(bf16[128,2048]{1,0:T(8,128)(2,1)S(1)} %collective-permute-done.9.refs_5_), channel_id=1, source_target_pairs={{0,8},{4,12},{8,16},{12,20},{16,24},{20,28},{1,9},{5,13},{9,17},{1... | collective-permute-start | bytes 1572872 | tf_op jit(solution)/shard_map/ppermute | solution.py:342
  45.1 12.5 %copy-start = (bf16[512,2048]{1,0:T(8,128)(2,1)S(1)}, bf16[512,2048]{1,0:T(8,128)(2,1)}, u32[]{:S(2)}) copy-start(bf16[512,2048]{1,0:T(8,128)(2,1)} %w0.3) | copy-start | bytes 6291460
  57.6 14.7 %collective-permute-start.19 = (bf16[512,2048]{1,0:T(8,128)(2,1)S(1)}, bf16[512,2048]{1,0:T(8,128)(2,1)S(1)}, u32[]{:S(2)}, u32[]{:S(2)}) collective-permute-start(bf16[512,2048]{1,0:T(8,128)(2,1)S(1)} %copy-done), channel_id=1, source_target_pairs={{0,1},{1,0},{2,3},{3,2},{4,5},{5,4},{6,7},{7,6},{8,9},{9,8},{10,11... | collective-permute-start | bytes 6291464 | tf_op jit(solution)/shard_map/ppermute | solution.py:336
  57.6 12.2 %collective-permute-start.17 = (bf16[64,2048]{1,0:T(8,128)(2,1)S(1)}, bf16[64,2048]{1,0:T(8,128)(2,1)S(1)}, u32[]{:S(2)}, u32[]{:S(2)}) collective-permute-start(bf16[64,2048]{1,0:T(8,128)(2,1)S(1)} %slice.15), channel_id=1, source_target_pairs={{4,0},{12,8},{20,16},{28,24},{5,1},{13,9},{21,17},{29,25},{6,2},{1... | collective-permute-start | bytes 786440 | tf_op jit(solution)/shard_map/ppermute | solution.py:342
  61.2 8.6 %collective-permute-start.16 = (bf16[64,2048]{1,0:T(8,128)(2,1)S(1)}, bf16[64,2048]{1,0:T(8,128)(2,1)S(1)}, u32[]{:S(2)}, u32[]{:S(2)}) collective-permute-start(bf16[64,2048]{1,0:T(8,128)(2,1)S(1)} %slice.14), channel_id=1, source_target_pairs={{0,2},{1,3},{2,0},{3,1},{4,6},{5,7},{6,4},{7,5},{8,10},{9,11},{10,... | collective-permute-start | bytes 786440 | tf_op jit(solution)/shard_map/ppermute | solution.py:339
  70.3 2.0 %collective-permute-start.18 = (bf16[1056,256]{1,0:T(8,128)(2,1)S(1)}, bf16[1056,256]{1,0:T(8,128)(2,1)S(1)}, u32[]{:S(2)}, u32[]{:S(2)}) collective-permute-start(bf16[1056,256]{1,0:T(8,128)(2,1)S(1)} %get-tuple-element.97), channel_id=1, source_target_pairs={{0,1},{1,0},{2,3},{3,2},{4,5},{5,4},{6,7},{7,6},{8,9},{9,8},{10,11... | collective-permute-start | bytes 1622024 | tf_op jit(solution)/shard_map/ppermute | solution.py:336
  73.1 14.0 %collective-permute-start.20 = (bf16[128,2048]{1,0:T(8,128)(2,1)S(1)}, bf16[128,2048]{1,0:T(8,128)(2,1)S(1)}, u32[]{:S(2)}, u32[]{:S(2)}) collective-permute-start(bf16[128,2048]{1,0:T(8,128)(2,1)S(1)} %shard_map.92), channel_id=1, source_target_pairs={{0,2},{1,3},{2,0},{3,1},{4,6},{5,7},{6,4},{7,5},{8,10},{9,11},{10,... | collective-permute-start | bytes 1572872 | tf_op jit(solution)/shard_map/ppermute | solution.py:339

commit v12 on v11

--- a/solution.py
+++ b/solution.py
@@ -390,7 +390,9 @@
 
     over_y, x_third, b4, wo_sent, held = tie((over_y, x_third, b4, w_out, state[0]))
     state = (held, *state[1:])
-    b3_top = over_x(over_y[: PIECE // 2])
+    b3_top = lax.ppermute(
+        over_y[: PIECE // 2], ("seq", "head"),
+        [(4 * i + head, 4 * i + (head ^ 2)) for i in range(0, blocks, 2) for head in range(4)])
     b3_rest = over_seq(b4[PIECE // 2 :], odd_to_even)
     wo_pair = over_core(wo_sent)
     state = merge(

time: 88.7 us -> 89.8 us (1.012); the launches traced: 88.1 us -> 88.3 us
  Pallas kernels: 21 us -> 32.6 us
  waiting for transfers between devices: 30.2 us -> 19 us
    pallas_call x3, Pallas kernels: 8.93 us -> 20.6 us  [earlier_pieces(): pl.pallas_call(body, out_shape=shapes, in_specs=[VMEM] * (11 + len(segs)...]
    ppermute x10, waiting for transfers between devices: 14.1 us -> 2.5 us  [over_seq(): return lax.ppermute(value, 'seq', pairs)]
    ppermute x5 -> x4, starting transfers between devices: 5.45 us -> 4.31 us  [over_x(): return lax.ppermute(value, 'head', [(i, i ^ 2) for i in range(4)])]
    ppermute x5 -> x4, waiting for transfers between devices: 12.1 us -> 12.7 us  [over_x(): return lax.ppermute(value, 'head', [(i, i ^ 2) for i in range(4)])]
  transfers between devices with their start and end apart: 21 -> 21, of which waited for: 8 -> 6; matrix products, arithmetic and copies ran while one was open for 0% -> 0% of each run, Pallas kernels for 23% -> 36%
where the time goes in v12:
time: 89.8 us; the launch traced here: 88.3 us
  Pallas kernels  32.6 us (36%)
  starting transfers between devices  32 us (36%)
  waiting for transfers between devices  19 us (21%)
  local copies, waits for them, and re-layouts  2.84 us (3%)
  other arithmetic  0.94 us (1%)
  between operations  0.93 us (1%)
    ppermute x10, starting transfers between devices, over_seq(): return lax.ppermute(value, 'seq', pairs)  26 us
    pallas_call x3, Pallas kernels, earlier_pieces(): pl.pallas_call(body, out_shape=shapes, in_specs=[VMEM] * (11 + len(segs)...  20.6 us
    ppermute x4, waiting for transfers between devices, over_x(): return lax.ppermute(value, 'head', [(i, i ^ 2) for i in range(4)])  12.7 us
    pallas_call x1, Pallas kernels, own_block(): pl.pallas_call(body, out_shape=(jax.ShapeDtypeStruct((width, block), BF16...  9.92 us
    ppermute x4, starting transfers between devices, over_x(): return lax.ppermute(value, 'head', [(i, i ^ 2) for i in range(4)])  4.31 us
    ppermute x6, waiting for transfers between devices, over_core(): return lax.ppermute(value, 'head', [(i, i ^ 1) for i in range(4)])  3.76 us
    unnamed x12, local copies, waits for them, and re-layouts  2.8 us
    ppermute x10, waiting for transfers between devices, over_seq(): return lax.ppermute(value, 'seq', pairs)  2.5 us
  transfers between devices with their start and end apart: 21, of which 6 were waited for; matrix products, arithmetic and copies ran while one was open for 0% of the time, Pallas kernels for 36%

profile of v12, /device:TPU:12, one launch (start us, length us, event | category | flops | bytes accessed | tf_op | source)
XLA Modules:
  0.0 88.3 jit_solution(11549262423368489218)
XLA Ops:
  0.6 0.1 collective-permute-start.3
  0.7 0.5 collective-permute-start.4
  1.2 1.3 %collective-permute-start.2 = (bf16[128,2048]{1,0:T(8,128)(2,1)}, bf16[128,2048]{1,0:T(8,128)(2,1)S(1)}, u32[]{:S(2)}, u32[]{:S(2)}) collective-permute-start(bf16[128,2048]{1,0:T(8,128)(2,1)} %refs_0_.1), channel_id=1, source_target_pairs={{0,4},{8,12},{16,20},{24,28},{1,5},{9,13},{17,21},{25,29},{2,6},{1... | collective-permute-start | bytes 1572872 | tf_op jit(solution)/shard_map/ppermute | solution.py:342
  2.5 1.6 %collective-permute-start.1 = (bf16[128,2048]{1,0:T(8,128)(2,1)}, bf16[128,2048]{1,0:T(8,128)(2,1)S(1)}, u32[]{:S(2)}, u32[]{:S(2)}) collective-permute-start(bf16[128,2048]{1,0:T(8,128)(2,1)} %refs_0_.1), channel_id=1, source_target_pairs={{0,2},{1,3},{2,0},{3,1},{4,6},{5,7},{6,4},{7,5},{8,10},{9,11},{10,... | collective-permute-start | bytes 1572872 | tf_op jit(solution)/shard_map/ppermute | solution.py:339
  4.1 3.5 %collective-permute-start = (bf16[128,2048]{1,0:T(8,128)(2,1)}, bf16[128,2048]{1,0:T(8,128)(2,1)S(1)}, u32[]{:S(2)}, u32[]{:S(2)}) collective-permute-start(bf16[128,2048]{1,0:T(8,128)(2,1)} %refs_0_.1), channel_id=1, source_target_pairs={{0,8},{4,12},{8,16},{12,20},{16,24},{20,28},{1,9},{5,13},{9,17},{1... | collective-permute-start | bytes 1572872 | tf_op jit(solution)/shard_map/ppermute | solution.py:342
  7.6 2.8 %copy-done.1 = bf16[2048,3,512]{2,0,1:T(8,128)(2,1)S(1)} copy-done((bf16[2048,3,512]{2,0,1:T(8,128)(2,1)S(1)}, bf16[2048,3,512]{2,0,1:T(8,128)(2,1)}, u32[]{:S(2)}) %copy-start.1) | copy-done | bytes 6291480
  10.3 0.4 shard_map.85.w0.refs_9_.refs_7_.refs_6_
  10.8 1.1 %collective-permute-done.4.c = bf16[128,2048]{1,0:T(8,128)(2,1)S(1)} collective-permute-done((bf16[128,2048]{1,0:T(8,128)(2,1)}, bf16[128,2048]{1,0:T(8,128)(2,1)S(1)}, u32[]{:S(2)}, u32[]{:S(2)}) %collective-permute-start.4) | collective-permute-done | bytes 524320 | tf_op jit(solution)/shard_map/ppermute | solution.py:336
  11.8 0.1 collective-permute-start.5
  12.0 1.0 %collective-permute-done.5.s1 = f32[1,4]{1,0:T(1,128)S(1)} collective-permute-done((f32[1,4]{1,0:T(1,128)S(1)}, f32[1,4]{1,0:T(1,128)S(1)}, u32[]{:S(2)}, u32[]{:S(2)}) %collective-permute-start.5) | collective-permute-done | bytes 48 | tf_op jit(solution)/shard_map/ppermute | solution.py:336
  13.0 4.6 %collective-permute-start.6 = (s32[4,128]{1,0:T(4,128)S(1)}, s32[4,128]{1,0:T(4,128)S(1)}, u32[]{:S(2)}, u32[]{:S(2)}) collective-permute-start(s32[4,128]{1,0:T(4,128)S(1)} %bitcast.10), channel_id=1, source_target_pairs={{0,4},{4,8},{8,12},{12,16},{16,20},{20,24},{24,28},{1,5},{5,9},{9,... | collective-permute-start | bytes 6152 | tf_op jit(solution)/shard_map/ppermute | solution.py:342
  17.6 0.0 collective-permute-done.2.refs_8_
  17.6 0.0 collective-permute-done.1.b.even_ref
  17.6 2.2 %collective-permute-done.refs_4_ = bf16[128,2048]{1,0:T(8,128)(2,1)S(1)} collective-permute-done((bf16[128,2048]{1,0:T(8,128)(2,1)}, bf16[128,2048]{1,0:T(8,128)(2,1)S(1)}, u32[]{:S(2)}, u32[]{:S(2)}) %collective-permute-start) | collective-permute-done | bytes 524320 | tf_op jit(solution)/shard_map/ppermute | solution.py:342
  19.8 0.0 collective-permute-done.6.refs_0_
  19.8 0.0 collective-permute-done.3.w1.refs_10_.refs_8_.refs_7_
  19.8 0.0 collective-permute-start.7
  19.8 3.5 %collective-permute-start.10 = (bf16[128,2048]{1,0:T(8,128)(2,1)S(1)}, bf16[128,2048]{1,0:T(8,128)(2,1)S(1)}, u32[]{:S(2)}, u32[]{:S(2)}) collective-permute-start(bf16[128,2048]{1,0:T(8,128)(2,1)S(1)} %collective-permute-done.refs_4_), channel_id=1, source_target_pairs={{0,8},{4,12},{8,16},{12,20},{16,24},{20,28},{1,9},{5,13},{9,17},{1... | collective-permute-start | bytes 1572872 | tf_op jit(solution)/shard_map/ppermute | solution.py:342
  23.3 0.6 collective-permute-start.9
  23.9 2.4 %collective-permute-start.8 = (bf16[128,2048]{1,0:T(8,128)(2,1)S(1)}, bf16[128,2048]{1,0:T(8,128)(2,1)S(1)}, u32[]{:S(2)}, u32[]{:S(2)}) collective-permute-start(bf16[128,2048]{1,0:T(8,128)(2,1)S(1)} %collective-permute-done.refs_4_), channel_id=1, source_target_pairs={{0,4},{8,12},{16,20},{24,28},{4,0},{12,8},{20,16},{28,24},{1,5},{9... | collective-permute-start | bytes 1572872 | tf_op jit(solution)/shard_map/ppermute | solution.py:342
  26.3 2.3 %collective-permute-start.12 = (s32[4,128]{1,0:T(4,128)S(1)}, s32[4,128]{1,0:T(4,128)S(1)}, u32[]{:S(2)}, u32[]{:S(2)}) collective-permute-start(s32[4,128]{1,0:T(4,128)S(1)} %bitcast.12), channel_id=1, source_target_pairs={{0,16},{4,20},{8,24},{12,28},{1,17},{5,21},{9,25},{13,29},{2,18},{... | collective-permute-start | bytes 6152 | tf_op jit(solution)/shard_map/ppermute | solution.py:342
  28.6 2.5 %collective-permute-start.11 = (s32[8,128]{1,0:T(8,128)S(1)}, s32[8,128]{1,0:T(8,128)S(1)}, u32[]{:S(2)}, u32[]{:S(2)}) collective-permute-start(s32[8,128]{1,0:T(8,128)S(1)} %pad_add_fusion), channel_id=1, source_target_pairs={{0,8},{4,12},{8,16},{12,20},{16,24},{20,28},{1,9},{5,13},{9,17},{1... | collective-permute-start | bytes 12296 | tf_op jit(solution)/shard_map/ppermute | solution.py:342
  31.1 9.9 %shard_map.86 = (bf16[512,512]{1,0:T(8,128)(2,1)S(1)}, bf16[512,512]{1,0:T(8,128)(2,1)S(1)}, f32[8,512]{1,0:T(8,128)S(1)}, f32[512,512]{1,0:T(8,128)S(1)}, f32[8...) custom-call(f32[1,4]{1,0:T(1,128)S(1)} %bitcast.18, ...), custom_call_target="tpu_custom_call" | custom-call | flops 5368709120 | bytes 1048576 | tf_op jit(solution)/shard_map/pallas_call | solution.py:178
  41.0 0.0 collective-permute-done.11
  41.0 0.0 collective-permute-done.10.odd_ref.refs_6_
  41.0 0.0 collective-permute-done.9.refs_5_
  41.1 0.1 shard_map.87
  41.1 0.1 collective-permute-start.13
  41.2 1.6 %collective-permute-start.14 = (bf16[128,2048]{1,0:T(8,128)(2,1)S(1)}, bf16[128,2048]{1,0:T(8,128)(2,1)S(1)}, u32[]{:S(2)}, u32[]{:S(2)}) collective-permute-start(bf16[128,2048]{1,0:T(8,128)(2,1)S(1)} %collective-permute-done.8.refs_7_), channel_id=1, source_target_pairs={{0,2},{1,3},{2,0},{3,1},{4,6},{5,7},{6,4},{7,5},{8,10},{9,11},{10,... | collective-permute-start | bytes 1572872 | tf_op jit(solution)/shard_map/ppermute | solution.py:339
  42.8 2.3 %collective-permute-start.15 = (bf16[128,2048]{1,0:T(8,128)(2,1)S(1)}, bf16[128,2048]{1,0:T(8,128)(2,1)S(1)}, u32[]{:S(2)}, u32[]{:S(2)}) collective-permute-start(bf16[128,2048]{1,0:T(8,128)(2,1)S(1)} %collective-permute-done.9.refs_5_), channel_id=1, source_target_pairs={{0,8},{4,12},{8,16},{12,20},{16,24},{20,28},{1,9},{5,13},{9,17},{1... | collective-permute-start | bytes 1572872 | tf_op jit(solution)/shard_map/ppermute | solution.py:342
  45.1 0.0 copy-start
  45.1 12.1 %shard_map.88 = (f32[8,512]{1,0:T(8,128)S(1)}, f32[512,512]{1,0:T(8,128)S(1)}, f32[8,512]{1,0:T(8,128)S(1)}, f32[512,512]{1,0:T(8,128)S(1)}) custom-call(f32[8,128]{1,0:T(8,128)S(1)} %get-tuple-element.63.slopes_ref, s32[4,128]{1,0:T(4,128)S(1)} %bitcast.14, f32[1,2048]{1,0:T(1,128)S(1)} %bitcast.7, s32[4,128]{1,0:T(4,128)S(1)} %collective-permute-done.6.refs_0_, ...), custom_call_target="tpu_custom_call" | custom-call | flops 5368709120 | bytes 1048576 | tf_op jit(solution)/shard_map/pallas_call | solution.py:284
  57.3 0.0 collective-permute-done.14.refs_5_
  57.3 0.3 collective-permute-done.15.refs_4_
  57.6 0.0 collective-permute-start.19
  57.6 3.6 %collective-permute-start.17 = (bf16[64,2048]{1,0:T(8,128)(2,1)S(1)}, bf16[64,2048]{1,0:T(8,128)(2,1)S(1)}, u32[]{:S(2)}, u32[]{:S(2)}) collective-permute-start(bf16[64,2048]{1,0:T(8,128)(2,1)S(1)} %slice.15), channel_id=1, source_target_pairs={{4,0},{12,8},{20,16},{28,24},{5,1},{13,9},{21,17},{29,25},{6,2},{1... | collective-permute-start | bytes 786440 | tf_op jit(solution)/shard_map/ppermute | solution.py:342
  61.2 0.7 collective-permute-start.16
  61.9 8.0 %shard_map.89 = (f32[8,512]{1,0:T(8,128)S(1)}, f32[512,512]{1,0:T(8,128)S(1)}, f32[8,512]{1,0:T(8,128)S(1)}, f32[512,512]{1,0:T(8,128)S(1)}) custom-call(f32[8,128]{1,0:T(8,128)S(1)} %get-tuple-element.63.slopes_ref, s32[4,128]{1,0:T(4,128)S(1)} %bitcast.15, f32[1,2048]{1,0:T(1,128)S(1)} %bitcast.8, s32[4,128]{1,0:T(4,128)S(1)} %collective-permute-done.6.refs_0_, ...), custom_call_target="tpu_custom_call" | custom-call | flops 3221225472 | bytes 1048576 | tf_op jit(solution)/shard_map/pallas_call | solution.py:284
  69.9 0.0 collective-permute-done.17.refs_5_
  69.9 0.0 collective-permute-done.16.refs_4_
  69.9 0.5 shard_map.90
  70.4 0.3 collective-permute-start.18
  70.7 1.7 %collective-permute-done.18.got_ref = bf16[1056,256]{1,0:T(8,128)(2,1)S(1)} collective-permute-done((bf16[1056,256]{1,0:T(8,128)(2,1)S(1)}, bf16[1056,256]{1,0:T(8,128)(2,1)S(1)}, u32[]{:S(2)}, u32[]{:S(2)}) %collective-permute-start.18) | collective-permute-done | bytes 540704 | tf_op jit(solution)/shard_map/ppermute | solution.py:336
  72.4 0.8 shard_map.92
  73.2 0.6 collective-permute-start.20
  73.8 0.8 shard_map.91
  74.6 12.7 %collective-permute-done.20 = bf16[128,2048]{1,0:T(8,128)(2,1)S(1)} collective-permute-done((bf16[128,2048]{1,0:T(8,128)(2,1)S(1)}, bf16[128,2048]{1,0:T(8,128)(2,1)S(1)}, u32[]{:S(2)}, u32[]{:S(2)}) %collective-permute-start.20) | collective-permute-done | bytes 524320 | tf_op jit(solution)/shard_map/ppermute | solution.py:339
  87.3 0.9 %add_convert_fusion = bf16[128,2048]{1,0:T(8,128)(2,1)} fusion(f32[128,2048]{1,0:T(8,128)S(1)} %shard_map.91, bf16[128,2048]{1,0:T(8,128)(2,1)S(1)} %collective-permute-done.20), kind=kLoop, calls=%fused_computation | loop fusion | flops 786432 | bytes 2097152 | tf_op jit(solution)/shard_map/convert_element_type | solution.py:405
  (19 shorter events, 0.1 us)
Async XLA Ops:
  0.6 11.2 %copy-start.5 = (f32[4]{0:T(128)S(1)}, f32[4]{0:T(128)}, u32[]{:S(2)}) copy-start(f32[4]{0:T(128)} %param.9) | copy-start | bytes 52
  0.6 19.2 %collective-permute-start.3 = (bf16[3,2048,512]{2,1,0:T(8,128)(2,1)}, bf16[3,2048,512]{2,1,0:T(8,128)(2,1)S(1)}, u32[]{:S(2)}, u32[]{:S(2)}) collective-permute-start(bf16[3,2048,512]{2,1,0:T(8,128)(2,1)} %bitcast.4), channel_id=1, source_target_pairs={{0,1},{1,0},{2,3},{3,2},{4,5},{5,4},{6,7},{7,6},{8,9},{9,8},{10,11... | collective-permute-start | bytes 18874376 | tf_op jit(solution)/shard_map/ppermute | solution.py:336
  0.7 11.1 %collective-permute-start.4 = (bf16[128,2048]{1,0:T(8,128)(2,1)}, bf16[128,2048]{1,0:T(8,128)(2,1)S(1)}, u32[]{:S(2)}, u32[]{:S(2)}) collective-permute-start(bf16[128,2048]{1,0:T(8,128)(2,1)} %refs_0_.1), channel_id=1, source_target_pairs={{0,1},{1,0},{2,3},{3,2},{4,5},{5,4},{6,7},{7,6},{8,9},{9,8},{10,11... | collective-permute-start | bytes 1572872 | tf_op jit(solution)/shard_map/ppermute | solution.py:336
  1.2 16.4 %collective-permute-start.2 = (bf16[128,2048]{1,0:T(8,128)(2,1)}, bf16[128,2048]{1,0:T(8,128)(2,1)S(1)}, u32[]{:S(2)}, u32[]{:S(2)}) collective-permute-start(bf16[128,2048]{1,0:T(8,128)(2,1)} %refs_0_.1), channel_id=1, source_target_pairs={{0,4},{8,12},{16,20},{24,28},{1,5},{9,13},{17,21},{25,29},{2,6},{1... | collective-permute-start | bytes 1572872 | tf_op jit(solution)/shard_map/ppermute | solution.py:342
  2.5 15.1 %collective-permute-start.1 = (bf16[128,2048]{1,0:T(8,128)(2,1)}, bf16[128,2048]{1,0:T(8,128)(2,1)S(1)}, u32[]{:S(2)}, u32[]{:S(2)}) collective-permute-start(bf16[128,2048]{1,0:T(8,128)(2,1)} %refs_0_.1), channel_id=1, source_target_pairs={{0,2},{1,3},{2,0},{3,1},{4,6},{5,7},{6,4},{7,5},{8,10},{9,11},{10,... | collective-permute-start | bytes 1572872 | tf_op jit(solution)/shard_map/ppermute | solution.py:339
  4.1 15.7 %collective-permute-start = (bf16[128,2048]{1,0:T(8,128)(2,1)}, bf16[128,2048]{1,0:T(8,128)(2,1)S(1)}, u32[]{:S(2)}, u32[]{:S(2)}) collective-permute-start(bf16[128,2048]{1,0:T(8,128)(2,1)} %refs_0_.1), channel_id=1, source_target_pairs={{0,8},{4,12},{8,16},{12,20},{16,24},{20,28},{1,9},{5,13},{9,17},{1... | collective-permute-start | bytes 1572872 | tf_op jit(solution)/shard_map/ppermute | solution.py:342
  7.5 2.8 %copy-start.1 = (bf16[2048,3,512]{2,0,1:T(8,128)(2,1)S(1)}, bf16[2048,3,512]{2,0,1:T(8,128)(2,1)}, u32[]{:S(2)}) copy-start(bf16[2048,3,512]{2,0,1:T(8,128)(2,1)} %param.8) | copy-start | bytes 18874372
  10.3 2.6 %copy-start.4 = (s32[512]{0:T(512)S(1)}, s32[512]{0:T(512)}, u32[]{:S(2)}) copy-start(s32[512]{0:T(512)} %param.11) | copy-start | bytes 6148
  10.3 20.8 %copy-start.2 = (bf16[128,2048]{1,0:T(8,128)(2,1)S(1)}, bf16[128,2048]{1,0:T(8,128)(2,1)}, u32[]{:S(2)}) copy-start(bf16[128,2048]{1,0:T(8,128)(2,1)} %refs_0_.1) | copy-start | bytes 1572868
  10.3 20.8 %copy-start.3 = (f32[2048]{0:T(1024)S(1)}, f32[2048]{0:T(1024)}, u32[]{:S(2)}) copy-start(f32[2048]{0:T(1024)} %param.7) | copy-start | bytes 24580
  11.8 1.1 %collective-permute-start.5 = (f32[1,4]{1,0:T(1,128)S(1)}, f32[1,4]{1,0:T(1,128)S(1)}, u32[]{:S(2)}, u32[]{:S(2)}) collective-permute-start(f32[1,4]{1,0:T(1,128)S(1)} %bitcast.17), channel_id=1, source_target_pairs={{0,1},{1,0},{2,3},{3,2},{4,5},{5,4},{6,7},{7,6},{8,9},{9,8},{10,11... | collective-permute-start | bytes 56 | tf_op jit(solution)/shard_map/ppermute | solution.py:336
  13.0 6.9 %collective-permute-start.6 = (s32[4,128]{1,0:T(4,128)S(1)}, s32[4,128]{1,0:T(4,128)S(1)}, u32[]{:S(2)}, u32[]{:S(2)}) collective-permute-start(s32[4,128]{1,0:T(4,128)S(1)} %bitcast.10), channel_id=1, source_target_pairs={{0,4},{4,8},{8,12},{12,16},{16,20},{20,24},{24,28},{1,5},{5,9},{9,... | collective-permute-start | bytes 6152 | tf_op jit(solution)/shard_map/ppermute | solution.py:342
  19.8 6.5 %collective-permute-start.7 = (bf16[128,2048]{1,0:T(8,128)(2,1)S(1)}, bf16[128,2048]{1,0:T(8,128)(2,1)S(1)}, u32[]{:S(2)}, u32[]{:S(2)}) collective-permute-start(bf16[128,2048]{1,0:T(8,128)(2,1)S(1)} %collective-permute-done.1.b.even_ref), channel_id=1, source_target_pairs={{0,1},{1,0},{2,3},{3,2},{4,5},{5,4},{6,7},{7,6},{8,9},{9,8},{10,11... | collective-permute-start | bytes 1572872 | tf_op jit(solution)/shard_map/ppermute | solution.py:336
  19.8 21.2 %collective-permute-start.10 = (bf16[128,2048]{1,0:T(8,128)(2,1)S(1)}, bf16[128,2048]{1,0:T(8,128)(2,1)S(1)}, u32[]{:S(2)}, u32[]{:S(2)}) collective-permute-start(bf16[128,2048]{1,0:T(8,128)(2,1)S(1)} %collective-permute-done.refs_4_), channel_id=1, source_target_pairs={{0,8},{4,12},{8,16},{12,20},{16,24},{20,28},{1,9},{5,13},{9,17},{1... | collective-permute-start | bytes 1572872 | tf_op jit(solution)/shard_map/ppermute | solution.py:342
  23.3 17.7 %collective-permute-start.9 = (bf16[128,2048]{1,0:T(8,128)(2,1)S(1)}, bf16[128,2048]{1,0:T(8,128)(2,1)S(1)}, u32[]{:S(2)}, u32[]{:S(2)}) collective-permute-start(bf16[128,2048]{1,0:T(8,128)(2,1)S(1)} %collective-permute-done.refs_4_), channel_id=1, source_target_pairs={{0,2},{1,3},{2,0},{3,1},{4,6},{5,7},{6,4},{7,5},{8,10},{9,11},{10,... | collective-permute-start | bytes 1572872 | tf_op jit(solution)/shard_map/ppermute | solution.py:339
  23.9 17.1 %collective-permute-start.8 = (bf16[128,2048]{1,0:T(8,128)(2,1)S(1)}, bf16[128,2048]{1,0:T(8,128)(2,1)S(1)}, u32[]{:S(2)}, u32[]{:S(2)}) collective-permute-start(bf16[128,2048]{1,0:T(8,128)(2,1)S(1)} %collective-permute-done.refs_4_), channel_id=1, source_target_pairs={{0,4},{8,12},{16,20},{24,28},{4,0},{12,8},{20,16},{28,24},{1,5},{9... | collective-permute-start | bytes 1572872 | tf_op jit(solution)/shard_map/ppermute | solution.py:342
  26.3 14.8 %collective-permute-start.12 = (s32[4,128]{1,0:T(4,128)S(1)}, s32[4,128]{1,0:T(4,128)S(1)}, u32[]{:S(2)}, u32[]{:S(2)}) collective-permute-start(s32[4,128]{1,0:T(4,128)S(1)} %bitcast.12), channel_id=1, source_target_pairs={{0,16},{4,20},{8,24},{12,28},{1,17},{5,21},{9,25},{13,29},{2,18},{... | collective-permute-start | bytes 6152 | tf_op jit(solution)/shard_map/ppermute | solution.py:342
  28.6 12.4 %collective-permute-start.11 = (s32[8,128]{1,0:T(8,128)S(1)}, s32[8,128]{1,0:T(8,128)S(1)}, u32[]{:S(2)}, u32[]{:S(2)}) collective-permute-start(s32[8,128]{1,0:T(8,128)S(1)} %pad_add_fusion), channel_id=1, source_target_pairs={{0,8},{4,12},{8,16},{12,20},{16,24},{20,28},{1,9},{5,13},{9,17},{1... | collective-permute-start | bytes 12296 | tf_op jit(solution)/shard_map/ppermute | solution.py:342
  41.1 16.2 %collective-permute-start.13 = (bf16[128,2048]{1,0:T(8,128)(2,1)S(1)}, bf16[128,2048]{1,0:T(8,128)(2,1)S(1)}, u32[]{:S(2)}, u32[]{:S(2)}) collective-permute-start(bf16[128,2048]{1,0:T(8,128)(2,1)S(1)} %shard_map.87), channel_id=1, source_target_pairs={{0,4},{8,12},{16,20},{24,28},{4,0},{12,8},{20,16},{28,24},{1,5},{9... | collective-permute-start | bytes 1572872 | tf_op jit(solution)/shard_map/ppermute | solution.py:342
  41.2 16.1 %collective-permute-start.14 = (bf16[128,2048]{1,0:T(8,128)(2,1)S(1)}, bf16[128,2048]{1,0:T(8,128)(2,1)S(1)}, u32[]{:S(2)}, u32[]{:S(2)}) collective-permute-start(bf16[128,2048]{1,0:T(8,128)(2,1)S(1)} %collective-permute-done.8.refs_7_), channel_id=1, source_target_pairs={{0,2},{1,3},{2,0},{3,1},{4,6},{5,7},{6,4},{7,5},{8,10},{9,11},{10,... | collective-permute-start | bytes 1572872 | tf_op jit(solution)/shard_map/ppermute | solution.py:339
  42.8 14.8 %collective-permute-start.15 = (bf16[128,2048]{1,0:T(8,128)(2,1)S(1)}, bf16[128,2048]{1,0:T(8,128)(2,1)S(1)}, u32[]{:S(2)}, u32[]{:S(2)}) collective-permute-start(bf16[128,2048]{1,0:T(8,128)(2,1)S(1)} %collective-permute-done.9.refs_5_), channel_id=1, source_target_pairs={{0,8},{4,12},{8,16},{12,20},{16,24},{20,28},{1,9},{5,13},{9,17},{1... | collective-permute-start | bytes 1572872 | tf_op jit(solution)/shard_map/ppermute | solution.py:342
  45.1 12.5 %copy-start = (bf16[512,2048]{1,0:T(8,128)(2,1)S(1)}, bf16[512,2048]{1,0:T(8,128)(2,1)}, u32[]{:S(2)}) copy-start(bf16[512,2048]{1,0:T(8,128)(2,1)} %w0.3) | copy-start | bytes 6291460
  57.6 14.8 %collective-permute-start.19 = (bf16[512,2048]{1,0:T(8,128)(2,1)S(1)}, bf16[512,2048]{1,0:T(8,128)(2,1)S(1)}, u32[]{:S(2)}, u32[]{:S(2)}) collective-permute-start(bf16[512,2048]{1,0:T(8,128)(2,1)S(1)} %copy-done), channel_id=1, source_target_pairs={{0,1},{1,0},{2,3},{3,2},{4,5},{5,4},{6,7},{7,6},{8,9},{9,8},{10,11... | collective-permute-start | bytes 6291464 | tf_op jit(solution)/shard_map/ppermute | solution.py:336
  57.6 12.3 %collective-permute-start.17 = (bf16[64,2048]{1,0:T(8,128)(2,1)S(1)}, bf16[64,2048]{1,0:T(8,128)(2,1)S(1)}, u32[]{:S(2)}, u32[]{:S(2)}) collective-permute-start(bf16[64,2048]{1,0:T(8,128)(2,1)S(1)} %slice.15), channel_id=1, source_target_pairs={{4,0},{12,8},{20,16},{28,24},{5,1},{13,9},{21,17},{29,25},{6,2},{1... | collective-permute-start | bytes 786440 | tf_op jit(solution)/shard_map/ppermute | solution.py:342
  61.2 8.7 %collective-permute-start.16 = (bf16[64,2048]{1,0:T(8,128)(2,1)S(1)}, bf16[64,2048]{1,0:T(8,128)(2,1)S(1)}, u32[]{:S(2)}, u32[]{:S(2)}) collective-permute-start(bf16[64,2048]{1,0:T(8,128)(2,1)S(1)} %slice.14), channel_id=1, source_target_pairs={{0,2},{1,3},{2,0},{3,1},{8,10},{9,11},{10,8},{11,9},{16,18},{17,19... | collective-permute-start | bytes 786440 | tf_op jit(solution)/shard_map/ppermute | solution.py:393
  70.4 2.0 %collective-permute-start.18 = (bf16[1056,256]{1,0:T(8,128)(2,1)S(1)}, bf16[1056,256]{1,0:T(8,128)(2,1)S(1)}, u32[]{:S(2)}, u32[]{:S(2)}) collective-permute-start(bf16[1056,256]{1,0:T(8,128)(2,1)S(1)} %get-tuple-element.97), channel_id=1, source_target_pairs={{0,1},{1,0},{2,3},{3,2},{4,5},{5,4},{6,7},{7,6},{8,9},{9,8},{10,11... | collective-permute-start | bytes 1622024 | tf_op jit(solution)/shard_map/ppermute | solution.py:336
  73.2 14.1 %collective-permute-start.20 = (bf16[128,2048]{1,0:T(8,128)(2,1)S(1)}, bf16[128,2048]{1,0:T(8,128)(2,1)S(1)}, u32[]{:S(2)}, u32[]{:S(2)}) collective-permute-start(bf16[128,2048]{1,0:T(8,128)(2,1)S(1)} %shard_map.92), channel_id=1, source_target_pairs={{0,2},{1,3},{2,0},{3,1},{4,6},{5,7},{6,4},{7,5},{8,10},{9,11},{10,... | collective-permute-start | bytes 1572872 | tf_op jit(solution)/shard_map/ppermute | solution.py:339
